TPU v7x, 32 devices: a whole 2x2x4 slice. The times are simulated.
32 devices in a mesh: tm: 4 (over y, x), space: 8 (over z, core).
Axes of the slice: x: 2, y: 2, z: 4, core: 2. Of those that a mesh axis runs over, the one named last changes fastest.
Arguments:
- snapshots: bfloat16 [2048, 16384], P('tm', 'space'), may hold values from -13 to 13
- modes_basis: bfloat16 [16384, 64], P('space'), may hold values from -0.046875 to 0.046875
- reg_weights: float32 [2144], replicated, may hold values from 0.3 to 3
Outputs:
- reduced: float32 [2048, 64], P('tm')
- time_rates: float32 [2048, 64], P('tm')
- normal: float32 [2144, 2144], P('tm', 'space')
- right_side: float32 [2144, 64], P('tm')
All inputs are finite; a program needn't handle non-finite values.
Results may differ from a plain program's by a relative error of at most 0.0043.
Values sent between devices are 32-bit elements; how exact they have to be, the bound alone decides.
No kernel may reach another device: no remote copies, remote signals or barrier semaphores. Data moves between devices by JAX's collectives and lax.ppermute only.
A program may use at most 128 MiB of HBM per device.

v0:
```python
import functools

import jax
import jax.numpy as jnp
from jax import lax
from jax.experimental import pallas as pl
from jax.experimental.pallas import tpu as pltpu
from jax.sharding import PartitionSpec as P

NT = (((1,), (1,)), ((), ()))


def round_up(value, step):
    return (value + step - 1) // step * step


def selectors(first, rows, modes, depth):
    feature = first + lax.broadcasted_iota(jnp.int32, (rows, 1), 0)
    mode = lax.broadcasted_iota(jnp.int32, (1, modes), 1)
    start = modes + mode * modes - (mode * (mode - 1)) // 2
    gap = feature - start
    holds = (gap >= 0) & (gap < modes - mode)
    left = jnp.sum(jnp.where(holds, mode, 0), axis=1, keepdims=True)
    right = left + jnp.sum(jnp.where(holds, gap, 0), axis=1, keepdims=True)
    linear = feature < modes
    left = jnp.where(linear, feature, left)
    right = jnp.where(linear, modes, right)
    lane = lax.broadcasted_iota(jnp.int32, (1, depth), 1)
    held = jnp.where(lane < 3 * modes, lax.rem(lane, modes), lane - 2 * modes)
    return (
        jnp.where(held == left, 1.0, 0.0).astype(jnp.bfloat16),
        jnp.where(held == right, 1.0, 0.0).astype(jnp.bfloat16),
    )


def parts_of(block, depth):
    modes, snaps = block.shape
    high = block.astype(jnp.bfloat16)
    rest = block - high.astype(jnp.float32)
    middle = rest.astype(jnp.bfloat16)
    low = (rest - middle.astype(jnp.float32)).astype(jnp.bfloat16)
    tail = depth - 3 * modes
    ones = jnp.where(lax.broadcasted_iota(jnp.int32, (tail, snaps), 0) == 0, 1.0, 0.0)
    return jnp.concatenate([high, middle, low, ones.astype(jnp.bfloat16)], axis=0)


def picked(left, right, parts):
    first = jnp.dot(left, parts, preferred_element_type=jnp.float32)
    second = jnp.dot(right, parts, preferred_element_type=jnp.float32)
    return (first * second).astype(jnp.bfloat16)


def normal_kernel(
    groups, row_block, col_block, place_ref, all_ref, reg_ref,
    reduced_ref, rates_ref, normal_ref, right_ref, col_scratch, acc_scratch,
):
    time_idx = place_ref[0]
    space_idx = place_ref[1]
    modes, snaps = all_ref.shape[1:]
    count = groups * snaps
    rows = round_up(row_block, 16)
    cols = round_up(col_block, 16)
    depth = round_up(3 * modes + 1, 128)
    row_left, row_right = selectors(time_idx * row_block, rows, modes, depth)
    col_left, col_right = selectors(space_idx * col_block, cols, modes, depth)
    lane = lax.broadcasted_iota(jnp.int32, (1, snaps), 1)
    for group in range(groups):
        block = all_ref[group]
        before = all_ref[max(group - 1, 0)][:, snaps - 1 : snaps]
        after = all_ref[min(group + 1, groups - 1)][:, 0:1]
        low = jnp.where(lane == 0, before, pltpu.roll(block, 1, 1))
        high = jnp.where(lane == snaps - 1, after, pltpu.roll(block, snaps - 1, 1))
        rates = (high - low) * 0.5
        if group == 0:
            rates = jnp.where(lane == 0, high - block, rates)
        if group == groups - 1:
            rates = jnp.where(lane == snaps - 1, block - low, rates)

        @pl.when(time_idx == group)
        def _():
            reduced_ref[...] = block.T
            rates_ref[...] = rates.T

        parts = parts_of(block, depth)
        col_scratch[:cols] = picked(col_left, col_right, parts)
        col_scratch[cols:] = rates.astype(jnp.bfloat16)
        row_features = picked(row_left, row_right, parts)
        term = lax.dot_general(row_features, col_scratch[...], NT, preferred_element_type=jnp.float32)
        if group == 0:
            acc_scratch[...] = term
        else:
            acc_scratch[...] += term
    scale = 1.0 / count
    row_ids = time_idx * row_block + lax.broadcasted_iota(jnp.int32, (row_block, col_block), 0)
    col_ids = space_idx * col_block + lax.broadcasted_iota(jnp.int32, (row_block, col_block), 1)
    diagonal = jnp.where(row_ids == col_ids, reg_ref[...], 0.0)
    normal_ref[...] = acc_scratch[:row_block, :col_block] * scale + diagonal
    right_ref[...] = acc_scratch[:row_block, cols:] * scale


def local(snapshots, modes_basis, reg_weights):
    feature_count = reg_weights.shape[0]
    snaps_dev = snapshots.shape[0]
    modes = modes_basis.shape[1]
    tm_count = lax.axis_size("tm")
    space_count = lax.axis_size("space")
    row_block = feature_count // tm_count
    col_block = feature_count // space_count
    time_idx = lax.axis_index("tm")
    space_idx = lax.axis_index("space")
    partial_value = lax.dot_general(
        modes_basis, snapshots, (((0,), (1,)), ((), ())), preferred_element_type=jnp.float32
    )
    spread = lax.all_to_all(partial_value, "space", 0, 0, tiled=True)
    share = jnp.sum(spread.reshape(space_count, modes // space_count, snaps_dev), axis=0)
    copies = jnp.broadcast_to(share[None], (space_count,) + share.shape).reshape(modes, snaps_dev)
    own = lax.all_to_all(copies, "space", 0, 0, tiled=True)
    slots = [own]
    for step in range(1, tm_count):
        slots.append(lax.ppermute(own, "tm", [(i, i ^ step) for i in range(tm_count)]))
    stacked = jnp.stack(slots)
    order = jnp.bitwise_xor(time_idx, jnp.arange(tm_count))
    everyone = jnp.take(stacked, order, axis=0)
    reg_cols = lax.dynamic_slice_in_dim(reg_weights, space_idx * col_block, col_block, 0)[None]
    place = jnp.stack([time_idx, space_idx]).astype(jnp.int32)
    rows = round_up(row_block, 16)
    cols = round_up(col_block, 16)
    vmem = pl.BlockSpec(memory_space=pltpu.VMEM)
    return pl.pallas_call(
        functools.partial(normal_kernel, tm_count, row_block, col_block),
        out_shape=(
            jax.ShapeDtypeStruct((snaps_dev, modes), jnp.float32),
            jax.ShapeDtypeStruct((snaps_dev, modes), jnp.float32),
            jax.ShapeDtypeStruct((row_block, col_block), jnp.float32),
            jax.ShapeDtypeStruct((row_block, modes), jnp.float32),
        ),
        in_specs=[pl.BlockSpec(memory_space=pltpu.SMEM), vmem, vmem],
        out_specs=(vmem,) * 4,
        scratch_shapes=[
            pltpu.VMEM((cols + modes, snaps_dev), jnp.bfloat16),
            pltpu.VMEM((rows, cols + modes), jnp.float32),
        ],
        compiler_params=pltpu.CompilerParams(vmem_limit_bytes=48 * 1024 * 1024),
        name="normal_block",
    )(place, everyone, reg_cols)


def solution(mesh):
    return jax.shard_map(
        local,
        mesh=mesh,
        in_specs=(P("tm", "space"), P("space", None), P()),
        out_specs=(P("tm", None), P("tm", None), P("tm", "space"), P("tm", None)),
        check_vma=False,
    )
```

profile of v0, /device:TPU:0, one launch (start us, length us, event | category | flops | bytes accessed | tf_op | source)
XLA Modules:
  0.0 47.3 jit_solution(12245972179031902447)
XLA Ops:
  0.6 0.0 copy-start
  0.6 1.6 %copy-done = bf16[512,2048]{1,0:T(8,128)(2,1)S(1)} copy-done((bf16[512,2048]{1,0:T(8,128)(2,1)S(1)}, bf16[512,2048]{1,0:T(8,128)(2,1)}, u32[]{:S(2)}) %copy-start) | copy-done | bytes 2097176
  2.2 1.7 %convolution_bitcast_fusion = f32[8,8,512]{2,1,0:T(8,128)S(1)} fusion(bf16[2048,64]{0,1:T(8,128)(2,1)} %param.4, bf16[512,2048]{1,0:T(8,128)(2,1)S(1)} %copy-done), kind=kOutput, calls=%fused_computation.1 | convolution fusion | flops 134217728 | bytes 2490368 | tf_op jit(solution)/shard_map/dot_general | solution.py:111
  3.9 12.9 %all_to_all.18 = f32[8,8,512]{2,1,0:T(8,128)S(1)} all-to-all(f32[8,8,512]{2,1,0:T(8,128)S(1)} %convolution_bitcast_fusion), channel_id=1, replica_groups=mesh['tm'=4,'space'=8] {'space'}, dimensions={0} | all-to-all | bytes 262144 | tf_op jit(solution)/shard_map/all_to_all | solution.py:114
  16.9 0.7 %broadcast_in_dim.20 = f32[8,8,512]{2,1,0:T(8,128)} broadcast(f32[8,512]{1,0:T(8,128)S(1)} %reduce_sum.9), dimensions={1,2} | broadcast | bytes 147456 | tf_op jit(solution)/shard_map/broadcast_in_dim | solution.py:116
  17.5 3.4 %all-to-all-start.1 = ((f32[8,8,512]{2,1,0:T(8,128)}), f32[8,8,512]{2,1,0:T(8,128)S(1)}, u32[]{:S(2)}, u32[]{:S(2)}) async-start(f32[8,8,512]{2,1,0:T(8,128)} %broadcast_in_dim.20), calls=%async_computation.1 | async-start | bytes 262144 | tf_op jit(solution)/shard_map/all_to_all | solution.py:117
  20.9 6.7 %all-to-all-done.1 = f32[8,8,512]{2,1,0:T(8,128)S(1)} async-done(((f32[8,8,512]{2,1,0:T(8,128)}), f32[8,8,512]{2,1,0:T(8,128)S(1)}, u32[]{:S(2)}, u32[]{:S(2)}) %all-to-all-start.1) | async-done | bytes 131104 | tf_op jit(solution)/shard_map/all_to_all | solution.py:117
  27.6 2.4 %collective-permute-start.2 = (f32[64,512]{1,0:T(8,128)S(1)}, f32[64,512]{1,0:T(8,128)S(1)}, u32[]{:S(2)}, u32[]{:S(2)}) collective-permute-start(f32[64,512]{1,0:T(8,128)S(1)} %bitcast.13), channel_id=1, source_target_pairs={{0,24},{8,16},{16,8},{24,0},{1,25},{9,17},{17,9},{25,1},{2,26},{10... | collective-permute-start | bytes 393224 | tf_op jit(solution)/shard_map/ppermute | solution.py:120
  30.1 0.5 %collective-permute-start.1 = (f32[64,512]{1,0:T(8,128)S(1)}, f32[64,512]{1,0:T(8,128)S(1)}, u32[]{:S(2)}, u32[]{:S(2)}) collective-permute-start(f32[64,512]{1,0:T(8,128)S(1)} %bitcast.14), channel_id=1, source_target_pairs={{0,16},{8,24},{16,0},{24,8},{1,17},{9,25},{17,1},{25,9},{2,18},{10... | collective-permute-start | bytes 393224 | tf_op jit(solution)/shard_map/ppermute | solution.py:120
  30.6 0.5 %collective-permute-start = (f32[64,512]{1,0:T(8,128)S(1)}, f32[64,512]{1,0:T(8,128)S(1)}, u32[]{:S(2)}, u32[]{:S(2)}) collective-permute-start(f32[64,512]{1,0:T(8,128)S(1)} %bitcast.15), channel_id=1, source_target_pairs={{0,8},{8,0},{16,24},{24,16},{1,9},{9,1},{17,25},{25,17},{2,10},{10... | collective-permute-start | bytes 393224 | tf_op jit(solution)/shard_map/ppermute | solution.py:120
  31.1 0.1 pad_add_fusion.place_ref
  31.2 0.8 %dynamic_slice.3 = f32[268]{0:T(512)S(1)} dynamic-slice(f32[2144]{0:T(1024)} %param.5, s32[]{:T(128)S(6)} %select_n.26), dynamic_slice_sizes={268} | dynamic-slice | bytes 2148 | tf_op jit(solution)/shard_map/dynamic_slice | solution.py:124
  32.0 2.0 %collective-permute-done.2 = f32[64,512]{1,0:T(8,128)S(1)} collective-permute-done((f32[64,512]{1,0:T(8,128)S(1)}, f32[64,512]{1,0:T(8,128)S(1)}, u32[]{:S(2)}, u32[]{:S(2)}) %collective-permute-start.2) | collective-permute-done | bytes 131104 | tf_op jit(solution)/shard_map/ppermute | solution.py:120
  34.0 2.3 %collective-permute-done.1 = f32[64,512]{1,0:T(8,128)S(1)} collective-permute-done((f32[64,512]{1,0:T(8,128)S(1)}, f32[64,512]{1,0:T(8,128)S(1)}, u32[]{:S(2)}, u32[]{:S(2)}) %collective-permute-start.1) | collective-permute-done | bytes 131104 | tf_op jit(solution)/shard_map/ppermute | solution.py:120
  36.3 0.1 collective-permute-done
  36.4 0.6 %gather_fusion = f32[4,64,512]{2,1,0:T(8,128)S(1)} fusion(f32[4,64,512]{2,1,0:T(8,128)S(1)} %pad_maximum_fusion, s32[1024]{0:T(1024)S(1)} %pad_clamp_fusion), kind=kCustom, calls=%fused_computation | custom fusion | bytes 1048592 | tf_op jit(solution)/shard_map/jit(_take)/gather | solution.py:123
  37.0 0.1 broadcast_select_fusion.all_ref
  37.1 5.1 %normal_block.1 = (f32[512,64]{1,0:T(8,128)S(1)}, f32[512,64]{1,0:T(8,128)S(1)}, f32[536,268]{1,0:T(8,128)S(1)}, f32[536,64]{1,0:T(8,128)S(1)}) custom-call(s32[2]{0:T(128)S(1)} %pad_add_fusion.place_ref, f32[4,64,512]{2,1,0:T(8,128)S(1)} %broadcast_select_fusion.all_ref, f32[1,268]{1,0:T(1,128)S(1)} %broadcast_in_dim.22.reg_ref), custom_call_target="tpu_custom_call" | custom-call | tf_op jit(solution)/shard_map/normal_block/pallas_call | solution.py:129
  42.2 0.0 copy-start.1
  42.2 0.7 %copy-done.1 = f32[512,64]{1,0:T(8,128)} copy-done((f32[512,64]{1,0:T(8,128)}, f32[512,64]{1,0:T(8,128)S(1)}, u32[]{:S(2)}) %copy-start.1) | copy-done | bytes 131096
  42.9 1.7 %copy.7 = f32[512,64]{0,1:T(8,128)} copy(f32[512,64]{1,0:T(8,128)} %copy-done.1) | data formatting | bytes 262144 | tf_op jit(solution)/shard_map/normal_block/pallas_call | solution.py:129
  44.6 0.8 %copy.8 = f32[512,64]{0,1:T(8,128)} copy(f32[512,64]{1,0:T(8,128)S(1)} %get-tuple-element.5) | data formatting | bytes 262144 | tf_op jit(solution)/shard_map/normal_block/pallas_call | solution.py:129
  45.4 0.8 %copy.10 = f32[536,64]{0,1:T(8,128)} copy(f32[536,64]{1,0:T(8,128)S(1)} %get-tuple-element.7) | data formatting | bytes 274432 | tf_op jit(solution)/shard_map/normal_block/pallas_call | solution.py:129
  46.2 1.2 %copy.9 = f32[536,268]{0,1:T(8,128)} copy(f32[536,268]{1,0:T(8,128)S(1)} %get-tuple-element.6) | data formatting | bytes 1149184 | tf_op jit(solution)/shard_map/normal_block/pallas_call | solution.py:129
  (6 shorter events, 0.1 us)
Async XLA Ops:
  0.6 1.6 %copy-start = (bf16[512,2048]{1,0:T(8,128)(2,1)S(1)}, bf16[512,2048]{1,0:T(8,128)(2,1)}, u32[]{:S(2)}) copy-start(bf16[512,2048]{1,0:T(8,128)(2,1)} %param.3) | copy-start | bytes 6291460
  17.5 10.1 %all-to-all-start.1 = ((f32[8,8,512]{2,1,0:T(8,128)}), f32[8,8,512]{2,1,0:T(8,128)S(1)}, u32[]{:S(2)}, u32[]{:S(2)}) async-start(f32[8,8,512]{2,1,0:T(8,128)} %broadcast_in_dim.20), calls=%async_computation.1 | async-start | bytes 262144 | tf_op jit(solution)/shard_map/all_to_all | solution.py:117
  27.6 6.4 %collective-permute-start.2 = (f32[64,512]{1,0:T(8,128)S(1)}, f32[64,512]{1,0:T(8,128)S(1)}, u32[]{:S(2)}, u32[]{:S(2)}) collective-permute-start(f32[64,512]{1,0:T(8,128)S(1)} %bitcast.13), channel_id=1, source_target_pairs={{0,24},{8,16},{16,8},{24,0},{1,25},{9,17},{17,9},{25,1},{2,26},{10... | collective-permute-start | bytes 393224 | tf_op jit(solution)/shard_map/ppermute | solution.py:120
  30.1 6.2 %collective-permute-start.1 = (f32[64,512]{1,0:T(8,128)S(1)}, f32[64,512]{1,0:T(8,128)S(1)}, u32[]{:S(2)}, u32[]{:S(2)}) collective-permute-start(f32[64,512]{1,0:T(8,128)S(1)} %bitcast.14), channel_id=1, source_target_pairs={{0,16},{8,24},{16,0},{24,8},{1,17},{9,25},{17,1},{25,9},{2,18},{10... | collective-permute-start | bytes 393224 | tf_op jit(solution)/shard_map/ppermute | solution.py:120
  30.6 5.8 %collective-permute-start = (f32[64,512]{1,0:T(8,128)S(1)}, f32[64,512]{1,0:T(8,128)S(1)}, u32[]{:S(2)}, u32[]{:S(2)}) collective-permute-start(f32[64,512]{1,0:T(8,128)S(1)} %bitcast.15), channel_id=1, source_target_pairs={{0,8},{8,0},{16,24},{24,16},{1,9},{9,1},{17,25},{25,17},{2,10},{10... | collective-permute-start | bytes 393224 | tf_op jit(solution)/shard_map/ppermute | solution.py:120
  42.2 0.7 %copy-start.1 = (f32[512,64]{1,0:T(8,128)}, f32[512,64]{1,0:T(8,128)S(1)}, u32[]{:S(2)}) copy-start(f32[512,64]{1,0:T(8,128)S(1)} %get-tuple-element.4) | copy-start | bytes 393220
where the time goes:
time: 47.7 us; the launch traced here: 47.3 us
  blocking collectives  12.9 us (27%)
  waiting for transfers between devices  11.1 us (23%)
  local copies, waits for them, and re-layouts  8.78 us (18%)
  starting transfers between devices  6.86 us (14%)
  Pallas kernels  5.06 us (11%)
  matrix products  1.71 us (4%)
  between operations  0.7 us (1%)
    all_to_all x1, blocking collectives, local(): spread = lax.all_to_all(partial_value, 'space', 0, 0, tiled=True)  12.9 us
    all_to_all x1, waiting for transfers between devices, local(): own = lax.all_to_all(copies, 'space', 0, 0, tiled=True)  6.68 us
    pallas_call x1, Pallas kernels, local(): pl.pallas_call(functools.partial(normal_kernel, tm_count, row_block, col_...  5.06 us
    pallas_call x4, local copies, waits for them, and re-layouts, local(): pl.pallas_call(functools.partial(normal_kernel, tm_count, row_block, col_...  4.46 us
    ppermute x3, waiting for transfers between devices, local(): lax.ppermute(own, 'tm', [(i, i ^ step) for i in range(tm_count)])  4.39 us
    ppermute x3, starting transfers between devices, local(): lax.ppermute(own, 'tm', [(i, i ^ step) for i in range(tm_count)])  3.49 us
    all_to_all x1, starting transfers between devices, local(): own = lax.all_to_all(copies, 'space', 0, 0, tiled=True)  3.37 us
    unnamed x4, local copies, waits for them, and re-layouts  2.29 us
  transfers between devices with their start and end apart: 4, of which 4 were waited for; matrix products, arithmetic and copies ran while one was open for 2% of the time, Pallas kernels for 0%

commit v1 on v0

v1 whole, which is shorter than its diff:
```python
import functools

import jax
import jax.numpy as jnp
from jax import lax
from jax.experimental import pallas as pl
from jax.experimental.pallas import tpu as pltpu
from jax.sharding import PartitionSpec as P

NT = (((1,), (1,)), ((), ()))


def round_up(value, step):
    return (value + step - 1) // step * step


def tree_sum(terms):
    while len(terms) > 1:
        terms = [terms[i] + terms[i + 1] for i in range(0, len(terms), 2)]
    return terms[0]


def selectors(first, rows, modes, depth):
    feature = first + lax.broadcasted_iota(jnp.int32, (rows, 1), 0)
    mode = lax.broadcasted_iota(jnp.int32, (1, modes), 1)
    start = modes + mode * modes - (mode * (mode - 1)) // 2
    gap = feature - start
    holds = (gap >= 0) & (gap < modes - mode)
    left = jnp.sum(jnp.where(holds, mode, 0), axis=1, keepdims=True)
    right = left + jnp.sum(jnp.where(holds, gap, 0), axis=1, keepdims=True)
    linear = feature < modes
    left = jnp.where(linear, feature, left)
    right = jnp.where(linear, modes, right)
    lane = lax.broadcasted_iota(jnp.int32, (1, depth), 1)
    held = jnp.where(lane < 3 * modes, lax.rem(lane, modes), lane - 2 * modes)
    return (
        jnp.where(held == left, 1.0, 0.0).astype(jnp.bfloat16),
        jnp.where(held == right, 1.0, 0.0).astype(jnp.bfloat16),
    )


def parts_of(block, depth):
    modes, snaps = block.shape
    high = block.astype(jnp.bfloat16)
    rest = block - high.astype(jnp.float32)
    middle = rest.astype(jnp.bfloat16)
    low = (rest - middle.astype(jnp.float32)).astype(jnp.bfloat16)
    tail = depth - 3 * modes
    ones = jnp.where(lax.broadcasted_iota(jnp.int32, (tail, snaps), 0) == 0, 1.0, 0.0)
    return jnp.concatenate([high, middle, low, ones.astype(jnp.bfloat16)], axis=0)


def picked(left, right, parts):
    first = jnp.dot(left, parts, preferred_element_type=jnp.float32)
    second = jnp.dot(right, parts, preferred_element_type=jnp.float32)
    return (first * second).astype(jnp.bfloat16)


def project_kernel(place_ref, basis_ref, snaps_ref, keep_ref, give_ref, basis, held, basis_sem, sems):
    core = place_ref[1] % 2
    _, chunks, half, step = held.shape
    basis_copy = pltpu.make_async_copy(basis_ref, basis, basis_sem)
    basis_copy.start()
    copies = []
    for side in range(2):
        first = pl.multiple_of((core if side else 1 - core) * half, half)
        for chunk in range(chunks):
            copies.append(
                pltpu.make_async_copy(
                    snaps_ref.at[pl.ds(first, half), pl.ds(chunk * step, step)],
                    held.at[side, chunk],
                    sems.at[side, chunk],
                )
            )
            copies[-1].start()
    basis_copy.wait()
    for side, out_ref in enumerate((give_ref, keep_ref)):
        for copy in copies[side * chunks : (side + 1) * chunks]:
            copy.wait()
        terms = [
            lax.dot_general(
                held[side, chunk],
                basis[:, chunk * step : (chunk + 1) * step],
                NT,
                preferred_element_type=jnp.float32,
            )
            for chunk in range(chunks)
        ]
        out_ref[...] = tree_sum(terms).T


def project(place, snapshots, basis):
    snaps, states = snapshots.shape
    modes = basis.shape[0]
    half = snaps // 2
    chunks = 4
    hbm = pl.BlockSpec(memory_space=pltpu.HBM)
    vmem = pl.BlockSpec(memory_space=pltpu.VMEM)
    block = jax.ShapeDtypeStruct((modes, half), jnp.float32)
    return pl.pallas_call(
        project_kernel,
        out_shape=(block, block),
        in_specs=[pl.BlockSpec(memory_space=pltpu.SMEM), hbm, hbm],
        out_specs=(vmem, vmem),
        scratch_shapes=[
            pltpu.VMEM(basis.shape, basis.dtype),
            pltpu.VMEM((2, chunks, half, states // chunks), snapshots.dtype),
            pltpu.SemaphoreType.DMA,
            pltpu.SemaphoreType.DMA((2, chunks)),
        ],
        compiler_params=pltpu.CompilerParams(vmem_limit_bytes=55000 * 1024),
        name="project",
    )(place, basis, snapshots)


def selector_kernel(row_block, col_block, modes, place_ref, left_ref, right_ref):
    cols = round_up(col_block, 16)
    rows = left_ref.shape[0] - cols
    depth = left_ref.shape[1]
    for at, size, first in (
        (0, cols, place_ref[1] * col_block),
        (cols, rows, place_ref[0] * row_block),
    ):
        left, right = selectors(first, size, modes, depth)
        left_ref[at : at + size] = left
        right_ref[at : at + size] = right


def inner_rates(block, half):
    snaps = block.shape[1]
    lane = lax.rem(lax.broadcasted_iota(jnp.int32, (1, snaps), 1), half)
    rates = (pltpu.roll(block, snaps - 1, 1) - pltpu.roll(block, 1, 1)) * 0.5
    return jnp.where((lane == 0) | (lane == half - 1), 0.0, rates)


def column_side(left_ref, right_ref, parts, rates, cols, col_scratch):
    col_scratch[:cols, : rates.shape[1]] = picked(left_ref[:cols], right_ref[:cols], parts)
    col_scratch[cols:, : rates.shape[1]] = rates.astype(jnp.bfloat16)


def terms_of(left_ref, right_ref, block, half, cols, col_scratch):
    parts = parts_of(block, left_ref.shape[1])
    column_side(left_ref, right_ref, parts, inner_rates(block, half), cols, col_scratch)
    row_features = picked(left_ref[cols:], right_ref[cols:], parts)
    return lax.dot_general(
        col_scratch[:, : block.shape[1]], row_features, NT, preferred_element_type=jnp.float32
    )


def stack_kernel(cols, has_before, left_ref, right_ref, *refs):
    block_ref, acc_ref, col_scratch = refs[-3:]
    count, _, half = block_ref.shape
    block = jnp.concatenate([block_ref[slot] for slot in range(count)], axis=1)
    term = terms_of(left_ref, right_ref, block, half, cols, col_scratch)
    acc_ref[...] = refs[0][...] + term if has_before else term


def slot_offset(slot, core, bits):
    plain = sum(((slot >> k) & 1) << k for k in range(bits))
    turned = sum(((slot >> k) & 1) << ((k + 1) % bits) for k in range(bits))
    return jnp.where(core == 0, plain, turned)


def edge_columns(time_idx, core, mine_ref, other_ref, starts, ends):
    groups, modes, half = mine_ref.shape
    width = starts.shape[2]
    for slot in range(groups):
        for source, side in ((mine_ref, core), (other_ref, 1 - core)):
            at = 2 * (time_idx ^ slot_offset(slot, side, (groups - 1).bit_length())) + side
            starts[at] = source[slot, :, :width]
            ends[at] = source[slot, :, half - width :]
    lane = lax.broadcasted_iota(jnp.int32, (1, width), 1)
    heads = jnp.zeros((modes, width), jnp.float32)
    tails = jnp.zeros((modes, width), jnp.float32)
    count = 2 * groups
    for at in range(count):
        pair = (lane == 2 * at) | (lane == 2 * at + 1)
        heads = jnp.where(pair, pltpu.roll(starts[at], 2 * at, 1), heads)
        tails = jnp.where(pair, pltpu.roll(ends[at], (2 * at + 2) % width, 1), tails)
    after = pltpu.roll(heads, width - 1, 1)
    before = pltpu.roll(tails, 1, 1)
    rates = (after - before) * 0.5
    rates = jnp.where(lane == 0, after - heads, rates)
    rates = jnp.where(lane == 2 * count - 1, tails - before, rates)
    edge = jnp.where(lax.rem(lane, 2) == 0, heads, tails)
    inside = lane < 2 * count
    return jnp.where(inside, edge, 0.0), jnp.where(inside, rates, 0.0)


def last_kernel(
    row_block, col_block, row_chunk, place_ref, left_ref, right_ref, before_ref, reg_ref, mine_ref,
    other_ref, reduced_ref, rates_ref, normal_ref, right_side_ref, starts, ends, col_scratch,
    reduced_out, rates_out, normal_out, right_side_out, sems,
):
    time_idx = place_ref[0]
    space_idx = place_ref[1]
    core = space_idx % 2
    groups, modes, half = mine_ref.shape
    snaps = 2 * half
    cols = round_up(col_block, 16)
    depth = left_ref.shape[1]
    copies = []

    def send(source, target):
        copies.append(pltpu.make_async_copy(source, target, sems.at[len(copies)]))
        copies[-1].start()

    edge, edge_rates = edge_columns(time_idx, core, mine_ref, other_ref, starts, ends)
    first = pl.multiple_of(core * half, half)
    second = pl.multiple_of((1 - core) * half, half)
    reduced_out[:, pl.ds(first, half)] = mine_ref[0]
    reduced_out[:, pl.ds(second, half)] = other_ref[0]
    send(reduced_out, reduced_ref)
    own = reduced_out[...]
    width = edge.shape[1]
    own_edges = pltpu.roll(edge_rates, lax.rem(width - 4 * time_idx, width), 1)
    lane = lax.broadcasted_iota(jnp.int32, (1, snaps), 1)
    rates = jnp.where(lane == 0, own_edges[:, 0:1], inner_rates(own, snaps))
    rates_out[...] = jnp.where(lane == snaps - 1, own_edges[:, 3:4], rates)
    send(rates_out, rates_ref)

    block = jnp.concatenate([other_ref[slot] for slot in range(groups)], axis=1)
    parts = parts_of(block, depth)
    edge_parts = parts_of(edge, depth)
    column_side(left_ref, right_ref, parts, inner_rates(block, half), cols, col_scratch)
    edge_rates = edge_rates.astype(jnp.bfloat16)
    scale = 1.0 / (groups * snaps)
    for at in range(0, row_block, row_chunk):
        size = min(row_chunk, row_block - at)
        padded = round_up(size, 16)
        pick = slice(cols + at, cols + at + padded)
        features = picked(left_ref[pick], right_ref[pick], parts)
        edge_features = picked(left_ref[pick], right_ref[pick], edge_parts)
        total = before_ref[:, at : at + padded] + lax.dot_general(
            col_scratch[...], features, NT, preferred_element_type=jnp.float32
        )
        edge_total = lax.dot_general(edge_rates, edge_features, NT, preferred_element_type=jnp.float32)
        col_ids = space_idx * col_block + lax.broadcasted_iota(jnp.int32, (col_block, size), 0)
        row_ids = time_idx * row_block + at + lax.broadcasted_iota(jnp.int32, (col_block, size), 1)
        diagonal = jnp.where(row_ids == col_ids, reg_ref[:, at : at + size], 0.0)
        normal_out[:, at : at + size] = total[:col_block, :size] * scale + diagonal
        right_side_out[:, at : at + size] = (total[cols:] + edge_total)[:, :size] * scale
        send(normal_out.at[:, at : at + size], normal_ref.at[:, at : at + size])
    send(right_side_out, right_side_ref)
    for copy in copies:
        copy.wait()


def swapped(value, axis, distance):
    return lax.ppermute(value, axis, [(i, i ^ distance) for i in range(lax.axis_size(axis))])


def exchanged(value, axis, step, bits, first_bit):
    space_count = lax.axis_size("space")
    tm_count = lax.axis_size("tm")
    perm = []
    for time in range(tm_count):
        for space in range(space_count):
            distance = 1 << (first_bit + (step + space % 2) % bits)
            if axis == "tm":
                target = (time ^ distance) * space_count + space
            else:
                target = time * space_count + (space ^ distance)
            perm.append((time * space_count + space, target))
    return lax.ppermute(value, ("tm", "space"), perm)


def local(snapshots, modes_basis, reg_weights):
    feature_count = reg_weights.shape[0]
    snaps_dev = snapshots.shape[0]
    modes = modes_basis.shape[1]
    tm_count = lax.axis_size("tm")
    space_count = lax.axis_size("space")
    row_block = feature_count // tm_count
    col_block = feature_count // space_count
    rows = round_up(row_block, 16)
    cols = round_up(col_block, 16)
    depth = round_up(3 * modes + 1, 128)
    time_idx = lax.axis_index("tm")
    space_idx = lax.axis_index("space")
    place = jnp.stack([time_idx, space_idx]).astype(jnp.int32)
    smem = pl.BlockSpec(memory_space=pltpu.SMEM)
    vmem = pl.BlockSpec(memory_space=pltpu.VMEM)
    params = pltpu.CompilerParams(vmem_limit_bytes=32 * 1024 * 1024)

    keep, give = project(place, snapshots, modes_basis.T)
    half = keep + swapped(give, "space", 1)
    after, half = lax.optimization_barrier((place, half))
    selector = jax.ShapeDtypeStruct((cols + rows, depth), jnp.bfloat16)
    left, right = pl.pallas_call(
        functools.partial(selector_kernel, row_block, col_block, modes),
        out_shape=(selector, selector),
        in_specs=[smem],
        out_specs=(vmem, vmem),
        compiler_params=params,
        cost_estimate=pl.CostEstimate(flops=10**6, bytes_accessed=10**6, transcendentals=0),
        name="selectors",
    )(after)
    first_row = after[0] * row_block
    reg_rows = lax.dynamic_slice_in_dim(reg_weights, first_row, row_block, 0)[None]

    total = half
    space_bits = (space_count - 1).bit_length() - 1
    for step in range(space_bits):
        total = total + exchanged(total, "space", step, space_bits, 1)
    total, left, right, reg_rows = lax.optimization_barrier((total, left, right, reg_rows))

    acc_shape = jax.ShapeDtypeStruct((cols + modes, rows), jnp.float32)

    def cost(count):
        flops = 2 * count * (2 * depth * (cols + rows) + (cols + modes) * rows)
        return pl.CostEstimate(flops=flops, bytes_accessed=2 * 10**6, transcendentals=0)

    def col_scratch(count):
        return pltpu.VMEM((cols + modes, count), jnp.bfloat16)

    half_snaps = snaps_dev // 2
    def add_terms(acc, block):
        count = block.shape[0] * half_snaps
        before = [] if acc is None else [acc]
        return pl.pallas_call(
            functools.partial(stack_kernel, cols, len(before)),
            out_shape=acc_shape,
            in_specs=[vmem] * (3 + len(before)),
            out_specs=vmem,
            scratch_shapes=[col_scratch(count)],
            input_output_aliases={2: 0} if before else {},
            compiler_params=params,
            cost_estimate=cost(count),
            name="stack_terms",
        )(left, right, *before, block)

    acc = None
    new = total[None]
    mine = new
    time_bits = (tm_count - 1).bit_length()
    for step in range(time_bits):
        got = exchanged(mine, "tm", step, time_bits, 0)
        acc = add_terms(acc, new)
        got, acc = lax.optimization_barrier((got, acc))
        new = got
        mine = jnp.concatenate([mine, got])
    other = swapped(mine, "space", 1)
    acc = add_terms(acc, new)
    width = 128
    row_chunk = 256
    chunks = pl.cdiv(row_block, row_chunk)
    out_shapes = (
        jax.ShapeDtypeStruct((modes, snaps_dev), jnp.float32),
        jax.ShapeDtypeStruct((modes, snaps_dev), jnp.float32),
        jax.ShapeDtypeStruct((col_block, row_block), jnp.float32),
        jax.ShapeDtypeStruct((modes, row_block), jnp.float32),
    )
    outs = pl.pallas_call(
        functools.partial(last_kernel, row_block, col_block, row_chunk),
        out_shape=out_shapes,
        in_specs=[smem] + [vmem] * 6,
        out_specs=(pl.BlockSpec(memory_space=pltpu.HBM),) * 4,
        scratch_shapes=[
            pltpu.VMEM((2 * tm_count, modes, width), jnp.float32),
            pltpu.VMEM((2 * tm_count, modes, width), jnp.float32),
            col_scratch(tm_count * half_snaps),
            *[pltpu.VMEM(shape.shape, shape.dtype) for shape in out_shapes],
            pltpu.SemaphoreType.DMA((3 + chunks,)),
        ],
        compiler_params=params,
        cost_estimate=cost(tm_count * half_snaps),
        name="last_half",
    )(place, left, right, acc, reg_rows, mine, other)
    return tuple(out.T for out in outs)


def solution(mesh):
    return jax.shard_map(
        local,
        mesh=mesh,
        in_specs=(P("tm", "space"), P("space", None), P()),
        out_specs=(P("tm", None), P("tm", None), P("tm", "space"), P("tm", None)),
        check_vma=False,
    )
```

time: 47.7 us -> 32.1 us (0.67)
  blocking collectives: 12.9 us -> 0 us
  local copies, waits for them, and re-layouts: 8.78 us -> 0.78 us
  Pallas kernels: 5.06 us -> 10.3 us
  starting transfers between devices: 6.86 us -> 9.92 us
  matrix products: 1.71 us -> 0 us
  waiting for transfers between devices: 11.1 us -> 10 us
    all_to_all x1 -> x0, blocking collectives: 12.9 us -> none  [local(): spread = lax.all_to_all(partial_value, 'space', 0, 0, tiled=True)]
    all_to_all x1 -> x0, waiting for transfers between devices: 6.68 us -> none  [local(): own = lax.all_to_all(copies, 'space', 0, 0, tiled=True)]
    ppermute x3 -> x6, starting transfers between devices: 3.49 us -> 9.92 us  [the longest x4 9.33 us: exchanged(): return lax.ppermute(value, ('tm', 'space'), perm)]
    ppermute x3 -> x6, waiting for transfers between devices: 4.39 us -> 10 us  [the longest x4 8.61 us: exchanged(): return lax.ppermute(value, ('tm', 'space'), perm)]
    pallas_call x1 -> x6, Pallas kernels: 5.06 us -> 10.3 us  [the longest x1 3.6 us: project(): pl.pallas_call(project_kernel, out_shape=(block, block), in_specs=[pl.Blo...]
    pallas_call x4 -> x0, local copies, waits for them, and re-layouts: 4.46 us -> none  [local(): pl.pallas_call(functools.partial(normal_kernel, tm_count, row_block, col_...]
    all_to_all x1 -> x0, starting transfers between devices: 3.37 us -> none  [local(): own = lax.all_to_all(copies, 'space', 0, 0, tiled=True)]
    unnamed x4 -> x0, local copies, waits for them, and re-layouts: 2.29 us -> none
  transfers between devices with their start and end apart: 4 -> 6, of which waited for: 4 -> 6; matrix products, arithmetic and copies ran while one was open for 2% -> 2% of each run, Pallas kernels for 0% -> 11%
where the time goes in v1:
time: 32.1 us; the launch traced here: 31.9 us
  Pallas kernels  10.3 us (32%)
  waiting for transfers between devices  10 us (31%)
  starting transfers between devices  9.92 us (31%)
  local copies, waits for them, and re-layouts  0.78 us (2%)
  between operations  0.75 us (2%)
    ppermute x4, starting transfers between devices, exchanged(): return lax.ppermute(value, ('tm', 'space'), perm)  9.33 us
    ppermute x4, waiting for transfers between devices, exchanged(): return lax.ppermute(value, ('tm', 'space'), perm)  8.61 us
    pallas_call x1, Pallas kernels, project(): pl.pallas_call(project_kernel, out_shape=(block, block), in_specs=[pl.Blo...  3.6 us
    pallas_call x1, Pallas kernels, local(): pl.pallas_call(functools.partial(last_kernel, row_block, col_block, row_c...  3.24 us
    pallas_call x3, Pallas kernels, add_terms(): pl.pallas_call(functools.partial(stack_kernel, cols, len(before)), out_sh...  2.29 us
    ppermute x2, waiting for transfers between devices, swapped(): lax.ppermute(value, axis, [(i, i ^ distance) for i in range(lax.axis_size...  1.43 us
    pallas_call x1, Pallas kernels, local(): pl.pallas_call(functools.partial(selector_kernel, row_block, col_block, m...  1.14 us
    dynamic_slice x1, local copies, waits for them, and re-layouts, local(): lax.dynamic_slice_in_dim(reg_weights, first_row, row_block, 0)[None]  0.78 us
  transfers between devices with their start and end apart: 6, of which 6 were waited for; matrix products, arithmetic and copies ran while one was open for 2% of the time, Pallas kernels for 11%

profile of v1, /device:TPU:0, one launch (start us, length us, event | category | flops | bytes accessed | tf_op | source)
XLA Modules:
  0.0 31.9 jit_solution(4069178338263272793)
XLA Ops:
  0.6 0.1 pad_add_fusion.place_ref
  0.7 3.6 %project.1 = (f32[64,256]{1,0:T(8,128)S(1)}, f32[64,256]{1,0:T(8,128)S(1)}) custom-call(s32[2]{0:T(128)S(1)} %pad_add_fusion.place_ref, bf16[64,2048]{1,0:T(8,128)(2,1)} %bitcast.15, bf16[512,2048]{1,0:T(8,128)(2,1)} %snaps_ref.1), custom_call_target="tpu_custom_call" | custom-call | tf_op jit(solution)/shard_map/project/pallas_call | solution.py:100
  4.3 0.5 %collective-permute-start = (f32[64,256]{1,0:T(8,128)S(1)}, f32[64,256]{1,0:T(8,128)S(1)}, u32[]{:S(2)}, u32[]{:S(2)}) collective-permute-start(f32[64,256]{1,0:T(8,128)S(1)} %get-tuple-element.23), channel_id=1, source_target_pairs={{0,1},{1,0},{2,3},{3,2},{4,5},{5,4},{6,7},{7,6},{8,9},{9,8},{10,11... | collective-permute-start | bytes 196616 | tf_op jit(solution)/shard_map/ppermute | solution.py:250
  4.8 0.9 %collective-permute-done = f32[64,256]{1,0:T(8,128)S(1)} collective-permute-done((f32[64,256]{1,0:T(8,128)S(1)}, f32[64,256]{1,0:T(8,128)S(1)}, u32[]{:S(2)}, u32[]{:S(2)}) %collective-permute-start) | collective-permute-done | bytes 65568 | tf_op jit(solution)/shard_map/ppermute | solution.py:250
  5.8 3.0 %collective-permute-start.1 = (f32[64,256]{1,0:T(8,128)S(1)}, f32[64,256]{1,0:T(8,128)S(1)}, u32[]{:S(2)}, u32[]{:S(2)}) collective-permute-start(f32[64,256]{1,0:T(8,128)S(1)} %add.12), channel_id=1, source_target_pairs={{0,2},{1,5},{2,0},{3,7},{4,6},{5,1},{6,4},{7,3},{8,10},{9,13},{10,... | collective-permute-start | bytes 196616 | tf_op jit(solution)/shard_map/ppermute | solution.py:265
  8.7 2.9 %collective-permute-done.1 = f32[64,256]{1,0:T(8,128)S(1)} collective-permute-done((f32[64,256]{1,0:T(8,128)S(1)}, f32[64,256]{1,0:T(8,128)S(1)}, u32[]{:S(2)}, u32[]{:S(2)}) %collective-permute-start.1) | collective-permute-done | bytes 65568 | tf_op jit(solution)/shard_map/ppermute | solution.py:265
  11.7 2.4 %collective-permute-start.2 = (f32[64,256]{1,0:T(8,128)S(1)}, f32[64,256]{1,0:T(8,128)S(1)}, u32[]{:S(2)}, u32[]{:S(2)}) collective-permute-start(f32[64,256]{1,0:T(8,128)S(1)} %add.13), channel_id=1, source_target_pairs={{0,4},{1,3},{2,6},{3,1},{4,0},{5,7},{6,2},{7,5},{8,12},{9,11},{10,... | collective-permute-start | bytes 196616 | tf_op jit(solution)/shard_map/ppermute | solution.py:265
  14.1 0.8 %dynamic_slice.3 = f32[536]{0:T(1024)S(1)} dynamic-slice(f32[2144]{0:T(1024)} %param.5, s32[]{:T(128)S(6)} %select_n.3), dynamic_slice_sizes={536} | dynamic-slice | bytes 4292 | tf_op jit(solution)/shard_map/dynamic_slice | solution.py:300
  14.9 1.1 %selectors.1 = (bf16[816,256]{1,0:T(8,128)(2,1)S(1)}, bf16[816,256]{1,0:T(8,128)(2,1)S(1)}) custom-call(s32[2]{0:T(128)S(1)} %pad_add_fusion.place_ref), custom_call_target="tpu_custom_call" | custom-call | flops 1000000 | bytes 1000000 | tf_op jit(solution)/shard_map/selectors/pallas_call | solution.py:290
  16.1 0.9 %collective-permute-done.2 = f32[64,256]{1,0:T(8,128)S(1)} collective-permute-done((f32[64,256]{1,0:T(8,128)S(1)}, f32[64,256]{1,0:T(8,128)S(1)}, u32[]{:S(2)}, u32[]{:S(2)}) %collective-permute-start.2) | collective-permute-done | bytes 65568 | tf_op jit(solution)/shard_map/ppermute | solution.py:265
  16.9 2.0 %collective-permute-start.3 = (f32[1,64,256]{2,1,0:T(8,128)S(1)}, f32[1,64,256]{2,1,0:T(8,128)S(1)}, u32[]{:S(2)}, u32[]{:S(2)}) collective-permute-start(f32[1,64,256]{2,1,0:T(8,128)S(1)} %bitcast.10), channel_id=1, source_target_pairs={{0,8},{1,17},{2,10},{3,19},{4,12},{5,21},{6,14},{7,23},{8,0},{9,25... | collective-permute-start | bytes 196616 | tf_op jit(solution)/shard_map/ppermute | solution.py:265
  18.9 0.6 %stack_terms.3.refs_0_ = f32[336,544]{1,0:T(8,128)S(1)} custom-call(bf16[816,256]{1,0:T(8,128)(2,1)S(1)} %get-tuple-element.28.left_ref, bf16[816,256]{1,0:T(8,128)(2,1)S(1)} %get-tuple-element.29.right_ref, f32[1,64,256]{2,1,0:T(8,128)S(1)} %bitcast.11), custom_call_target="tpu_custom_call" | custom-call | flops 307494912 | bytes 2000000 | tf_op jit(solution)/shard_map/stack_terms/pallas_call | solution.py:321
  19.6 2.4 %collective-permute-done.3.refs_1_ = f32[1,64,256]{2,1,0:T(8,128)S(1)} collective-permute-done((f32[1,64,256]{2,1,0:T(8,128)S(1)}, f32[1,64,256]{2,1,0:T(8,128)S(1)}, u32[]{:S(2)}, u32[]{:S(2)}) %collective-permute-start.3) | collective-permute-done | bytes 65568 | tf_op jit(solution)/shard_map/ppermute | solution.py:265
  22.0 1.9 %collective-permute-start.4 = (f32[2,64,256]{2,1,0:T(8,128)S(1)}, f32[2,64,256]{2,1,0:T(8,128)S(1)}, u32[]{:S(2)}, u32[]{:S(2)}) collective-permute-start(f32[2,64,256]{2,1,0:T(8,128)S(1)} %pad_maximum_fusion.1), channel_id=1, source_target_pairs={{0,16},{1,9},{2,18},{3,11},{4,20},{5,13},{6,22},{7,15},{8,24},{9,1... | collective-permute-start | bytes 393224 | tf_op jit(solution)/shard_map/ppermute | solution.py:265
  23.9 0.7 %stack_terms.4.refs_0_ = f32[336,544]{1,0:T(8,128)S(1)} custom-call(bf16[816,256]{1,0:T(8,128)(2,1)S(1)} %get-tuple-element.28.left_ref, bf16[816,256]{1,0:T(8,128)(2,1)S(1)} %get-tuple-element.29.right_ref, f32[336,544]{1,0:T(8,128)S(1)} %stack_terms.3.refs_0_, f32[1,64,256]{2,1,0:T(8,128)S(1)} %collective-permute-done.3.refs_1_), custom_call_target="tpu_custom_call", output_to_operand_aliasing={{}: (2, {})} | custom-call | flops 307494912 | bytes 2000000 | tf_op jit(solution)/shard_map/stack_terms/pallas_call | solution.py:321
  24.6 2.4 %collective-permute-done.4.refs_1_ = f32[2,64,256]{2,1,0:T(8,128)S(1)} collective-permute-done((f32[2,64,256]{2,1,0:T(8,128)S(1)}, f32[2,64,256]{2,1,0:T(8,128)S(1)}, u32[]{:S(2)}, u32[]{:S(2)}) %collective-permute-start.4) | collective-permute-done | bytes 131104 | tf_op jit(solution)/shard_map/ppermute | solution.py:265
  27.0 0.1 collective-permute-start.5
  27.1 1.0 %stack_terms.5.before_ref = f32[336,544]{1,0:T(8,128)S(1)} custom-call(bf16[816,256]{1,0:T(8,128)(2,1)S(1)} %get-tuple-element.28.left_ref, bf16[816,256]{1,0:T(8,128)(2,1)S(1)} %get-tuple-element.29.right_ref, f32[336,544]{1,0:T(8,128)S(1)} %stack_terms.4.refs_0_, f32[2,64,256]{2,1,0:T(8,128)S(1)} %collective-permute-done.4.refs_1_), custom_call_target="tpu_custom_call", output_to_operand_aliasing={{}: (2, {})} | custom-call | flops 614989824 | bytes 2000000 | tf_op jit(solution)/shard_map/stack_terms/pallas_call | solution.py:321
  28.1 0.5 %collective-permute-done.5.other_ref = f32[4,64,256]{2,1,0:T(8,128)S(1)} collective-permute-done((f32[4,64,256]{2,1,0:T(8,128)S(1)}, f32[4,64,256]{2,1,0:T(8,128)S(1)}, u32[]{:S(2)}, u32[]{:S(2)}) %collective-permute-start.5) | collective-permute-done | bytes 262176 | tf_op jit(solution)/shard_map/ppermute | solution.py:250
  28.6 3.2 %last_half.1 = (f32[64,512]{1,0:T(8,128)}, f32[64,512]{1,0:T(8,128)}, f32[268,536]{1,0:T(8,128)}, f32[64,536]{1,0:T(8,128)}) custom-call(s32[2]{0:T(128)S(1)} %pad_add_fusion.place_ref, bf16[816,256]{1,0:T(8,128)(2,1)S(1)} %get-tuple-element.28.left_ref, bf16[816,256]{1,0:T(8,128)(2,1)S(1)} %get-tuple-element.29.right_ref, ...), custom_call_target="tpu_custom_call" | custom-call | flops 1229979648 | bytes 2000000 | tf_op jit(solution)/shard_map/last_half/pallas_call | solution.py:354
  (6 shorter events, 0.1 us)
Async XLA Ops:
  4.3 1.4 %collective-permute-start = (f32[64,256]{1,0:T(8,128)S(1)}, f32[64,256]{1,0:T(8,128)S(1)}, u32[]{:S(2)}, u32[]{:S(2)}) collective-permute-start(f32[64,256]{1,0:T(8,128)S(1)} %get-tuple-element.23), channel_id=1, source_target_pairs={{0,1},{1,0},{2,3},{3,2},{4,5},{5,4},{6,7},{7,6},{8,9},{9,8},{10,11... | collective-permute-start | bytes 196616 | tf_op jit(solution)/shard_map/ppermute | solution.py:250
  5.8 5.9 %collective-permute-start.1 = (f32[64,256]{1,0:T(8,128)S(1)}, f32[64,256]{1,0:T(8,128)S(1)}, u32[]{:S(2)}, u32[]{:S(2)}) collective-permute-start(f32[64,256]{1,0:T(8,128)S(1)} %add.12), channel_id=1, source_target_pairs={{0,2},{1,5},{2,0},{3,7},{4,6},{5,1},{6,4},{7,3},{8,10},{9,13},{10,... | collective-permute-start | bytes 196616 | tf_op jit(solution)/shard_map/ppermute | solution.py:265
  11.7 5.2 %collective-permute-start.2 = (f32[64,256]{1,0:T(8,128)S(1)}, f32[64,256]{1,0:T(8,128)S(1)}, u32[]{:S(2)}, u32[]{:S(2)}) collective-permute-start(f32[64,256]{1,0:T(8,128)S(1)} %add.13), channel_id=1, source_target_pairs={{0,4},{1,3},{2,6},{3,1},{4,0},{5,7},{6,2},{7,5},{8,12},{9,11},{10,... | collective-permute-start | bytes 196616 | tf_op jit(solution)/shard_map/ppermute | solution.py:265
  16.9 5.0 %collective-permute-start.3 = (f32[1,64,256]{2,1,0:T(8,128)S(1)}, f32[1,64,256]{2,1,0:T(8,128)S(1)}, u32[]{:S(2)}, u32[]{:S(2)}) collective-permute-start(f32[1,64,256]{2,1,0:T(8,128)S(1)} %bitcast.10), channel_id=1, source_target_pairs={{0,8},{1,17},{2,10},{3,19},{4,12},{5,21},{6,14},{7,23},{8,0},{9,25... | collective-permute-start | bytes 196616 | tf_op jit(solution)/shard_map/ppermute | solution.py:265
  22.0 5.0 %collective-permute-start.4 = (f32[2,64,256]{2,1,0:T(8,128)S(1)}, f32[2,64,256]{2,1,0:T(8,128)S(1)}, u32[]{:S(2)}, u32[]{:S(2)}) collective-permute-start(f32[2,64,256]{2,1,0:T(8,128)S(1)} %pad_maximum_fusion.1), channel_id=1, source_target_pairs={{0,16},{1,9},{2,18},{3,11},{4,20},{5,13},{6,22},{7,15},{8,24},{9,1... | collective-permute-start | bytes 393224 | tf_op jit(solution)/shard_map/ppermute | solution.py:265
  27.0 1.6 %collective-permute-start.5 = (f32[4,64,256]{2,1,0:T(8,128)S(1)}, f32[4,64,256]{2,1,0:T(8,128)S(1)}, u32[]{:S(2)}, u32[]{:S(2)}) collective-permute-start(f32[4,64,256]{2,1,0:T(8,128)S(1)} %pad_maximum_fusion.mine_ref), channel_id=1, source_target_pairs={{0,1},{1,0},{2,3},{3,2},{4,5},{5,4},{6,7},{7,6},{8,9},{9,8},{10,11... | collective-permute-start | bytes 786440 | tf_op jit(solution)/shard_map/ppermute | solution.py:250

commit v2 on v1

--- a/solution.py
+++ b/solution.py
@@ -58,45 +58,43 @@
 
 def project_kernel(place_ref, basis_ref, snaps_ref, keep_ref, give_ref, basis, held, basis_sem, sems):
     core = place_ref[1] % 2
-    _, chunks, half, step = held.shape
+    chunks, size, states = held.shape
+    half = chunks // 2 * size
     basis_copy = pltpu.make_async_copy(basis_ref, basis, basis_sem)
     basis_copy.start()
     copies = []
-    for side in range(2):
-        first = pl.multiple_of((core if side else 1 - core) * half, half)
-        for chunk in range(chunks):
-            copies.append(
-                pltpu.make_async_copy(
-                    snaps_ref.at[pl.ds(first, half), pl.ds(chunk * step, step)],
-                    held.at[side, chunk],
-                    sems.at[side, chunk],
-                )
-            )
-            copies[-1].start()
+    for chunk in range(chunks):
+        side, at = divmod(chunk * size, half)
+        first = pl.multiple_of((core if side else 1 - core) * half + at, size)
+        copies.append(
+            pltpu.make_async_copy(snaps_ref.at[pl.ds(first, size)], held.at[chunk], sems.at[chunk])
+        )
+        copies[-1].start()
     basis_copy.wait()
-    for side, out_ref in enumerate((give_ref, keep_ref)):
-        for copy in copies[side * chunks : (side + 1) * chunks]:
-            copy.wait()
+    pieces = 4
+    step = states // pieces
+    for chunk in range(chunks):
+        copies[chunk].wait()
         terms = [
             lax.dot_general(
-                held[side, chunk],
-                basis[:, chunk * step : (chunk + 1) * step],
+                basis[:, piece * step : (piece + 1) * step],
+                held[chunk, :, piece * step : (piece + 1) * step],
                 NT,
                 preferred_element_type=jnp.float32,
             )
-            for chunk in range(chunks)
+            for piece in range(pieces)
         ]
-        out_ref[...] = tree_sum(terms).T
+        side, at = divmod(chunk * size, half)
+        (keep_ref if side else give_ref)[:, at : at + size] = tree_sum(terms)
 
 
 def project(place, snapshots, basis):
     snaps, states = snapshots.shape
     modes = basis.shape[0]
-    half = snaps // 2
-    chunks = 4
+    size = 128
     hbm = pl.BlockSpec(memory_space=pltpu.HBM)
     vmem = pl.BlockSpec(memory_space=pltpu.VMEM)
-    block = jax.ShapeDtypeStruct((modes, half), jnp.float32)
+    block = jax.ShapeDtypeStruct((modes, snaps // 2), jnp.float32)
     return pl.pallas_call(
         project_kernel,
         out_shape=(block, block),
@@ -104,9 +102,9 @@
         out_specs=(vmem, vmem),
         scratch_shapes=[
             pltpu.VMEM(basis.shape, basis.dtype),
-            pltpu.VMEM((2, chunks, half, states // chunks), snapshots.dtype),
+            pltpu.VMEM((snaps // size, size, states), snapshots.dtype),
             pltpu.SemaphoreType.DMA,
-            pltpu.SemaphoreType.DMA((2, chunks)),
+            pltpu.SemaphoreType.DMA((snaps // size,)),
         ],
         compiler_params=pltpu.CompilerParams(vmem_limit_bytes=55000 * 1024),
         name="project",
@@ -147,32 +145,32 @@
     )
 
 
-def stack_kernel(cols, has_before, left_ref, right_ref, *refs):
-    block_ref, acc_ref, col_scratch = refs[-3:]
-    count, _, half = block_ref.shape
-    block = jnp.concatenate([block_ref[slot] for slot in range(count)], axis=1)
+def joined(refs):
+    halves = []
+    for ref in refs:
+        halves.extend([ref[...]] if len(ref.shape) == 2 else [ref[slot] for slot in range(ref.shape[0])])
+    return jnp.concatenate(halves, axis=1)
+
+
+def halves_kernel(cols, has_before, left_ref, right_ref, *refs):
+    before_ref, refs = (refs[0], refs[1:]) if has_before else (None, refs)
+    block_refs, acc_ref, col_scratch = refs[:-2], refs[-2], refs[-1]
+    half = block_refs[0].shape[-1]
+    block = joined(block_refs)
     term = terms_of(left_ref, right_ref, block, half, cols, col_scratch)
-    acc_ref[...] = refs[0][...] + term if has_before else term
-
-
-def slot_offset(slot, core, bits):
-    plain = sum(((slot >> k) & 1) << k for k in range(bits))
-    turned = sum(((slot >> k) & 1) << ((k + 1) % bits) for k in range(bits))
-    return jnp.where(core == 0, plain, turned)
-
-
-def edge_columns(time_idx, core, mine_ref, other_ref, starts, ends):
-    groups, modes, half = mine_ref.shape
-    width = starts.shape[2]
-    for slot in range(groups):
-        for source, side in ((mine_ref, core), (other_ref, 1 - core)):
-            at = 2 * (time_idx ^ slot_offset(slot, side, (groups - 1).bit_length())) + side
-            starts[at] = source[slot, :, :width]
-            ends[at] = source[slot, :, half - width :]
+    acc_ref[...] = before_ref[...] + term if has_before else term
+
+
+def edge_columns(time_idx, core, halves, starts, ends):
+    count, modes, width = starts.shape
+    for offset, side, load in halves:
+        block = load()
+        at = 2 * (time_idx ^ offset) + side
+        starts[at] = block[:, :width]
+        ends[at] = block[:, block.shape[1] - width :]
     lane = lax.broadcasted_iota(jnp.int32, (1, width), 1)
     heads = jnp.zeros((modes, width), jnp.float32)
     tails = jnp.zeros((modes, width), jnp.float32)
-    count = 2 * groups
     for at in range(count):
         pair = (lane == 2 * at) | (lane == 2 * at + 1)
         heads = jnp.where(pair, pltpu.roll(starts[at], 2 * at, 1), heads)
@@ -188,14 +186,15 @@
 
 
 def last_kernel(
-    row_block, col_block, row_chunk, place_ref, left_ref, right_ref, before_ref, reg_ref, mine_ref,
-    other_ref, reduced_ref, rates_ref, normal_ref, right_side_ref, starts, ends, col_scratch,
-    reduced_out, rates_out, normal_out, right_side_out, sems,
+    row_block, col_block, row_chunk, offsets, place_ref, left_ref, right_ref, before_ref, reg_ref, early_ref,
+    early_other_ref, late_ref, late_other_ref, reduced_ref, rates_ref, normal_ref, right_side_ref, starts,
+    ends, col_scratch, reduced_out, rates_out, normal_out, right_side_out, sems,
 ):
     time_idx = place_ref[0]
     space_idx = place_ref[1]
     core = space_idx % 2
-    groups, modes, half = mine_ref.shape
+    early, modes, half = early_ref.shape
+    groups = early + late_ref.shape[0]
     snaps = 2 * half
     cols = round_up(col_block, 16)
     depth = left_ref.shape[1]
@@ -205,12 +204,15 @@
         copies.append(pltpu.make_async_copy(source, target, sems.at[len(copies)]))
         copies[-1].start()
 
-    edge, edge_rates = edge_columns(time_idx, core, mine_ref, other_ref, starts, ends)
-    first = pl.multiple_of(core * half, half)
-    second = pl.multiple_of((1 - core) * half, half)
-    reduced_out[:, pl.ds(first, half)] = mine_ref[0]
-    reduced_out[:, pl.ds(second, half)] = other_ref[0]
+    reduced_out[:, pl.ds(pl.multiple_of(core * half, half), half)] = early_ref[0]
+    reduced_out[:, pl.ds(pl.multiple_of((1 - core) * half, half), half)] = early_other_ref[0]
     send(reduced_out, reduced_ref)
+    halves = []
+    for slot, offset in enumerate(offsets):
+        for side, pair in ((core, (early_ref, late_ref)), (1 - core, (early_other_ref, late_other_ref))):
+            ref, at = (pair[0], slot) if slot < early else (pair[1], slot - early)
+            halves.append((offset, side, functools.partial(lambda ref, at: ref[at], ref, at)))
+    edge, edge_rates = edge_columns(time_idx, core, halves, starts, ends)
     own = reduced_out[...]
     width = edge.shape[1]
     own_edges = pltpu.roll(edge_rates, lax.rem(width - 4 * time_idx, width), 1)
@@ -219,19 +221,18 @@
     rates_out[...] = jnp.where(lane == snaps - 1, own_edges[:, 3:4], rates)
     send(rates_out, rates_ref)
 
-    block = jnp.concatenate([other_ref[slot] for slot in range(groups)], axis=1)
+    block = joined([late_other_ref])
     parts = parts_of(block, depth)
+    column_side(left_ref, right_ref, parts, inner_rates(block, half), cols, col_scratch)
+    scale = 1.0 / (groups * snaps)
+    chunks = [(at, min(row_chunk, row_block - at)) for at in range(0, row_block, row_chunk)]
     edge_parts = parts_of(edge, depth)
-    column_side(left_ref, right_ref, parts, inner_rates(block, half), cols, col_scratch)
     edge_rates = edge_rates.astype(jnp.bfloat16)
-    scale = 1.0 / (groups * snaps)
-    for at in range(0, row_block, row_chunk):
-        size = min(row_chunk, row_block - at)
-        padded = round_up(size, 16)
-        pick = slice(cols + at, cols + at + padded)
+    for at, size in chunks:
+        pick = slice(cols + at, cols + at + round_up(size, 16))
         features = picked(left_ref[pick], right_ref[pick], parts)
         edge_features = picked(left_ref[pick], right_ref[pick], edge_parts)
-        total = before_ref[:, at : at + padded] + lax.dot_general(
+        total = before_ref[:, at : at + features.shape[0]] + lax.dot_general(
             col_scratch[...], features, NT, preferred_element_type=jnp.float32
         )
         edge_total = lax.dot_general(edge_rates, edge_features, NT, preferred_element_type=jnp.float32)
@@ -248,21 +249,6 @@
 
 def swapped(value, axis, distance):
     return lax.ppermute(value, axis, [(i, i ^ distance) for i in range(lax.axis_size(axis))])
-
-
-def exchanged(value, axis, step, bits, first_bit):
-    space_count = lax.axis_size("space")
-    tm_count = lax.axis_size("tm")
-    perm = []
-    for time in range(tm_count):
-        for space in range(space_count):
-            distance = 1 << (first_bit + (step + space % 2) % bits)
-            if axis == "tm":
-                target = (time ^ distance) * space_count + space
-            else:
-                target = time * space_count + (space ^ distance)
-            perm.append((time * space_count + space, target))
-    return lax.ppermute(value, ("tm", "space"), perm)
 
 
 def local(snapshots, modes_basis, reg_weights):
@@ -299,12 +285,11 @@
     first_row = after[0] * row_block
     reg_rows = lax.dynamic_slice_in_dim(reg_weights, first_row, row_block, 0)[None]
 
-    total = half
-    space_bits = (space_count - 1).bit_length() - 1
-    for step in range(space_bits):
-        total = total + exchanged(total, "space", step, space_bits, 1)
-    total, left, right, reg_rows = lax.optimization_barrier((total, left, right, reg_rows))
-
+    terms = [half] + [swapped(half, "space", step) for step in range(2, space_count, 2)]
+    while len(terms) > 1:
+        terms = [terms[i] + terms[i + 1] for i in range(0, len(terms), 2)]
+    mine, left, right, reg_rows = lax.optimization_barrier((terms[0], left, right, reg_rows))
+    arriving = [(step, swapped(mine, "tm", step)) for step in range(tm_count - 1, 0, -1)]
     acc_shape = jax.ShapeDtypeStruct((cols + modes, rows), jnp.float32)
 
     def cost(count):
@@ -315,33 +300,33 @@
         return pltpu.VMEM((cols + modes, count), jnp.bfloat16)
 
     half_snaps = snaps_dev // 2
-    def add_terms(acc, block):
-        count = block.shape[0] * half_snaps
+
+    def add_terms(acc, blocks):
+        count = sum(block.size for block in blocks) // modes
         before = [] if acc is None else [acc]
         return pl.pallas_call(
-            functools.partial(stack_kernel, cols, len(before)),
+            functools.partial(halves_kernel, cols, len(before)),
             out_shape=acc_shape,
-            in_specs=[vmem] * (3 + len(before)),
+            in_specs=[vmem] * (2 + len(before) + len(blocks)),
             out_specs=vmem,
             scratch_shapes=[col_scratch(count)],
             input_output_aliases={2: 0} if before else {},
             compiler_params=params,
             cost_estimate=cost(count),
-            name="stack_terms",
-        )(left, right, *before, block)
-
-    acc = None
-    new = total[None]
-    mine = new
-    time_bits = (tm_count - 1).bit_length()
-    for step in range(time_bits):
-        got = exchanged(mine, "tm", step, time_bits, 0)
-        acc = add_terms(acc, new)
-        got, acc = lax.optimization_barrier((got, acc))
-        new = got
-        mine = jnp.concatenate([mine, got])
-    other = swapped(mine, "space", 1)
-    acc = add_terms(acc, new)
+            name="halves",
+        )(left, right, *before, *blocks)
+
+    offsets = [0] + [offset for offset, _ in arriving]
+    early = [mine, arriving[0][1]]
+    late = [got for _, got in arriving[1:]]
+    acc = add_terms(None, [mine])
+    early_stack = jnp.stack(early)
+    early_other = swapped(early_stack, "space", 1)
+    acc = add_terms(acc, early[1:])
+    acc, *late = lax.optimization_barrier((acc, *late))
+    late_stack = jnp.stack(late)
+    late_other = swapped(late_stack, "space", 1)
+    acc = add_terms(acc, [early_other, late_stack])
     width = 128
     row_chunk = 256
     chunks = pl.cdiv(row_block, row_chunk)
@@ -352,21 +337,21 @@
         jax.ShapeDtypeStruct((modes, row_block), jnp.float32),
     )
     outs = pl.pallas_call(
-        functools.partial(last_kernel, row_block, col_block, row_chunk),
+        functools.partial(last_kernel, row_block, col_block, row_chunk, offsets),
         out_shape=out_shapes,
-        in_specs=[smem] + [vmem] * 6,
+        in_specs=[smem] + [vmem] * 8,
         out_specs=(pl.BlockSpec(memory_space=pltpu.HBM),) * 4,
         scratch_shapes=[
             pltpu.VMEM((2 * tm_count, modes, width), jnp.float32),
             pltpu.VMEM((2 * tm_count, modes, width), jnp.float32),
-            col_scratch(tm_count * half_snaps),
+            col_scratch(len(late) * half_snaps),
             *[pltpu.VMEM(shape.shape, shape.dtype) for shape in out_shapes],
             pltpu.SemaphoreType.DMA((3 + chunks,)),
         ],
         compiler_params=params,
-        cost_estimate=cost(tm_count * half_snaps),
+        cost_estimate=cost(len(late) * half_snaps),
         name="last_half",
-    )(place, left, right, acc, reg_rows, mine, other)
+    )(place, left, right, acc, reg_rows, early_stack, early_other, late_stack, late_other)
     return tuple(out.T for out in outs)
 
 

time: 32.1 us -> 28.2 us (0.88)
  waiting for transfers between devices: 10 us -> 6.52 us
  Pallas kernels: 10.3 us -> 9.92 us
    ppermute x4 -> x0, starting transfers between devices: 9.33 us -> none  [exchanged(): return lax.ppermute(value, ('tm', 'space'), perm)]
    ppermute x2 -> x9, starting transfers between devices: 0.59 us -> 9.87 us  [swapped(): lax.ppermute(value, axis, [(i, i ^ distance) for i in range(lax.axis_size...]
    ppermute x4 -> x0, waiting for transfers between devices: 8.61 us -> none  [exchanged(): return lax.ppermute(value, ('tm', 'space'), perm)]
    ppermute x2 -> x9, waiting for transfers between devices: 1.43 us -> 6.52 us  [swapped(): lax.ppermute(value, axis, [(i, i ^ distance) for i in range(lax.axis_size...]
    pallas_call x1, Pallas kernels: 3.24 us -> 2.52 us  [local(): pl.pallas_call(functools.partial(last_kernel, row_block, col_block, row_c...]
    pallas_call x3, Pallas kernels: 2.29 us -> 2.94 us  [add_terms(): pl.pallas_call(functools.partial(halves_kernel, cols, len(before)), out_s...]
  transfers between devices with their start and end apart: 6 -> 9, of which waited for: 6 -> 4; matrix products, arithmetic and copies ran while one was open for 2% -> 3% of each run, Pallas kernels for 11% -> 15%
where the time goes in v2:
time: 28.2 us; the launch traced here: 28 us
  Pallas kernels  9.92 us (35%)
  starting transfers between devices  9.87 us (35%)
  waiting for transfers between devices  6.52 us (23%)
  local copies, waits for them, and re-layouts  0.78 us (3%)
  between operations  0.76 us (3%)
    ppermute x9, starting transfers between devices, swapped(): lax.ppermute(value, axis, [(i, i ^ distance) for i in range(lax.axis_size...  9.87 us
    ppermute x9, waiting for transfers between devices, swapped(): lax.ppermute(value, axis, [(i, i ^ distance) for i in range(lax.axis_size...  6.52 us
    pallas_call x1, Pallas kernels, project(): pl.pallas_call(project_kernel, out_shape=(block, block), in_specs=[pl.Blo...  3.33 us
    pallas_call x3, Pallas kernels, add_terms(): pl.pallas_call(functools.partial(halves_kernel, cols, len(before)), out_s...  2.94 us
    pallas_call x1, Pallas kernels, local(): pl.pallas_call(functools.partial(last_kernel, row_block, col_block, row_c...  2.52 us
    pallas_call x1, Pallas kernels, local(): pl.pallas_call(functools.partial(selector_kernel, row_block, col_block, m...  1.14 us
    dynamic_slice x1, local copies, waits for them, and re-layouts, local(): lax.dynamic_slice_in_dim(reg_weights, first_row, row_block, 0)[None]  0.78 us
  transfers between devices with their start and end apart: 9, of which 4 were waited for; matrix products, arithmetic and copies ran while one was open for 3% of the time, Pallas kernels for 15%

profile of v2, /device:TPU:0, one launch (start us, length us, event | category | flops | bytes accessed | tf_op | source)
XLA Modules:
  0.0 28.0 jit_solution(4147912806167925290)
XLA Ops:
  0.6 0.1 pad_add_fusion.place_ref
  0.7 3.3 %project.1 = (f32[64,256]{1,0:T(8,128)S(1)}, f32[64,256]{1,0:T(8,128)S(1)}) custom-call(s32[2]{0:T(128)S(1)} %pad_add_fusion.place_ref, bf16[64,2048]{1,0:T(8,128)(2,1)} %bitcast.16, bf16[512,2048]{1,0:T(8,128)(2,1)} %snaps_ref.1), custom_call_target="tpu_custom_call" | custom-call | tf_op jit(solution)/shard_map/project/pallas_call | solution.py:98
  4.0 0.5 %collective-permute-start = (f32[64,256]{1,0:T(8,128)S(1)}, f32[64,256]{1,0:T(8,128)S(1)}, u32[]{:S(2)}, u32[]{:S(2)}) collective-permute-start(f32[64,256]{1,0:T(8,128)S(1)} %get-tuple-element.22), channel_id=1, source_target_pairs={{0,1},{1,0},{2,3},{3,2},{4,5},{5,4},{6,7},{7,6},{8,9},{9,8},{10,11... | collective-permute-start | bytes 196616 | tf_op jit(solution)/shard_map/ppermute | solution.py:251
  4.6 0.9 %collective-permute-done = f32[64,256]{1,0:T(8,128)S(1)} collective-permute-done((f32[64,256]{1,0:T(8,128)S(1)}, f32[64,256]{1,0:T(8,128)S(1)}, u32[]{:S(2)}, u32[]{:S(2)}) %collective-permute-start) | collective-permute-done | bytes 65568 | tf_op jit(solution)/shard_map/ppermute | solution.py:251
  5.5 5.0 %collective-permute-start.3 = (f32[64,256]{1,0:T(8,128)S(1)}, f32[64,256]{1,0:T(8,128)S(1)}, u32[]{:S(2)}, u32[]{:S(2)}) collective-permute-start(f32[64,256]{1,0:T(8,128)S(1)} %add.15), channel_id=1, source_target_pairs={{0,6},{1,7},{2,4},{3,5},{4,2},{5,3},{6,0},{7,1},{8,14},{9,15},{10,... | collective-permute-start | bytes 196616 | tf_op jit(solution)/shard_map/ppermute | solution.py:251
  10.5 0.0 collective-permute-start.2
  10.5 0.6 %collective-permute-start.1 = (f32[64,256]{1,0:T(8,128)S(1)}, f32[64,256]{1,0:T(8,128)S(1)}, u32[]{:S(2)}, u32[]{:S(2)}) collective-permute-start(f32[64,256]{1,0:T(8,128)S(1)} %add.15), channel_id=1, source_target_pairs={{0,2},{1,3},{2,0},{3,1},{4,6},{5,7},{6,4},{7,5},{8,10},{9,11},{10,... | collective-permute-start | bytes 196616 | tf_op jit(solution)/shard_map/ppermute | solution.py:251
  11.2 0.8 %dynamic_slice.3 = f32[536]{0:T(1024)S(1)} dynamic-slice(f32[2144]{0:T(1024)} %param.5, s32[]{:T(128)S(6)} %select_n.3), dynamic_slice_sizes={536} | dynamic-slice | bytes 4292 | tf_op jit(solution)/shard_map/dynamic_slice | solution.py:286
  12.0 1.1 %selectors.1 = (bf16[816,256]{1,0:T(8,128)(2,1)S(1)}, bf16[816,256]{1,0:T(8,128)(2,1)S(1)}) custom-call(s32[2]{0:T(128)S(1)} %pad_add_fusion.place_ref), custom_call_target="tpu_custom_call" | custom-call | flops 1000000 | bytes 1000000 | tf_op jit(solution)/shard_map/selectors/pallas_call | solution.py:276
  13.1 0.0 collective-permute-done.3
  13.1 3.2 %collective-permute-done.2 = f32[64,256]{1,0:T(8,128)S(1)} collective-permute-done((f32[64,256]{1,0:T(8,128)S(1)}, f32[64,256]{1,0:T(8,128)S(1)}, u32[]{:S(2)}, u32[]{:S(2)}) %collective-permute-start.2) | collective-permute-done | bytes 65568 | tf_op jit(solution)/shard_map/ppermute | solution.py:251
  16.4 0.0 collective-permute-done.1
  16.4 2.5 %collective-permute-start.4 = (f32[64,256]{1,0:T(8,128)S(1)}, f32[64,256]{1,0:T(8,128)S(1)}, u32[]{:S(2)}, u32[]{:S(2)}) collective-permute-start(f32[64,256]{1,0:T(8,128)S(1)} %add_add_fusion.refs_0_), channel_id=1, source_target_pairs={{0,24},{8,16},{16,8},{24,0},{1,25},{9,17},{17,9},{25,1},{2,26},{10... | collective-permute-start | bytes 196616 | tf_op jit(solution)/shard_map/ppermute | solution.py:251
  18.9 0.5 %collective-permute-start.6 = (f32[64,256]{1,0:T(8,128)S(1)}, f32[64,256]{1,0:T(8,128)S(1)}, u32[]{:S(2)}, u32[]{:S(2)}) collective-permute-start(f32[64,256]{1,0:T(8,128)S(1)} %add_add_fusion.refs_0_), channel_id=1, source_target_pairs={{0,8},{8,0},{16,24},{24,16},{1,9},{9,1},{17,25},{25,17},{2,10},{10... | collective-permute-start | bytes 196616 | tf_op jit(solution)/shard_map/ppermute | solution.py:251
  19.5 0.5 %collective-permute-start.5 = (f32[64,256]{1,0:T(8,128)S(1)}, f32[64,256]{1,0:T(8,128)S(1)}, u32[]{:S(2)}, u32[]{:S(2)}) collective-permute-start(f32[64,256]{1,0:T(8,128)S(1)} %add_add_fusion.refs_0_), channel_id=1, source_target_pairs={{0,16},{8,24},{16,0},{24,8},{1,17},{9,25},{17,1},{25,9},{2,18},{10... | collective-permute-start | bytes 196616 | tf_op jit(solution)/shard_map/ppermute | solution.py:251
  20.0 0.6 %halves.3.refs_0_ = f32[336,544]{1,0:T(8,128)S(1)} custom-call(bf16[816,256]{1,0:T(8,128)(2,1)S(1)} %get-tuple-element.27.left_ref, bf16[816,256]{1,0:T(8,128)(2,1)S(1)} %get-tuple-element.28.right_ref, f32[64,256]{1,0:T(8,128)S(1)} %add_add_fusion.refs_0_), custom_call_target="tpu_custom_call" | custom-call | flops 307494912 | bytes 2000000 | tf_op jit(solution)/shard_map/halves/pallas_call | solution.py:307
  20.6 1.8 %collective-permute-done.4.refs_1_ = f32[64,256]{1,0:T(8,128)S(1)} collective-permute-done((f32[64,256]{1,0:T(8,128)S(1)}, f32[64,256]{1,0:T(8,128)S(1)}, u32[]{:S(2)}, u32[]{:S(2)}) %collective-permute-start.4) | collective-permute-done | bytes 65568 | tf_op jit(solution)/shard_map/ppermute | solution.py:251
  22.4 0.1 collective-permute-start.7
  22.5 0.7 %halves.4.refs_0_ = f32[336,544]{1,0:T(8,128)S(1)} custom-call(bf16[816,256]{1,0:T(8,128)(2,1)S(1)} %get-tuple-element.27.left_ref, bf16[816,256]{1,0:T(8,128)(2,1)S(1)} %get-tuple-element.28.right_ref, f32[336,544]{1,0:T(8,128)S(1)} %halves.3.refs_0_, f32[64,256]{1,0:T(8,128)S(1)} %collective-permute-done.4.refs_1_), custom_call_target="tpu_custom_call", output_to_operand_aliasing={{}: (2, {})} | custom-call | flops 307494912 | bytes 2000000 | tf_op jit(solution)/shard_map/halves/pallas_call | solution.py:307
  23.1 0.0 collective-permute-done.6
  23.2 0.5 %collective-permute-done.5 = f32[64,256]{1,0:T(8,128)S(1)} collective-permute-done((f32[64,256]{1,0:T(8,128)S(1)}, f32[64,256]{1,0:T(8,128)S(1)}, u32[]{:S(2)}, u32[]{:S(2)}) %collective-permute-start.5) | collective-permute-done | bytes 65568 | tf_op jit(solution)/shard_map/ppermute | solution.py:251
  23.7 0.1 collective-permute-start.8
  23.8 0.0 collective-permute-done.7.refs_1_.early_other_ref
  23.8 1.6 %halves.5.before_ref = f32[336,544]{1,0:T(8,128)S(1)} custom-call(bf16[816,256]{1,0:T(8,128)(2,1)S(1)} %get-tuple-element.27.left_ref, bf16[816,256]{1,0:T(8,128)(2,1)S(1)} %get-tuple-element.28.right_ref, f32[336,544]{1,0:T(8,128)S(1)} %halves.4.refs_0_, ...), custom_call_target="tpu_custom_call", output_to_operand_aliasing={{}: (2, {})} | custom-call | flops 1229979648 | bytes 2000000 | tf_op jit(solution)/shard_map/halves/pallas_call | solution.py:307
  25.5 0.0 collective-permute-done.8.late_other_ref
  25.5 2.5 %last_half.1 = (f32[64,512]{1,0:T(8,128)}, f32[64,512]{1,0:T(8,128)}, f32[268,536]{1,0:T(8,128)}, f32[64,536]{1,0:T(8,128)}) custom-call(s32[2]{0:T(128)S(1)} %pad_add_fusion.place_ref, bf16[816,256]{1,0:T(8,128)(2,1)S(1)} %get-tuple-element.27.left_ref, bf16[816,256]{1,0:T(8,128)(2,1)S(1)} %get-tuple-element.28.right_ref, f32[336,544]{1,0:T(8,128)S(1)} %halves.5.before_ref, ...), custom_call_target="tpu_custom_call" | custom-call | flops 614989824 | bytes 2000000 | tf_op jit(solution)/shard_map/last_half/pallas_call | solution.py:339
  (5 shorter events, 0.1 us)
Async XLA Ops:
  4.0 1.4 %collective-permute-start = (f32[64,256]{1,0:T(8,128)S(1)}, f32[64,256]{1,0:T(8,128)S(1)}, u32[]{:S(2)}, u32[]{:S(2)}) collective-permute-start(f32[64,256]{1,0:T(8,128)S(1)} %get-tuple-element.22), channel_id=1, source_target_pairs={{0,1},{1,0},{2,3},{3,2},{4,5},{5,4},{6,7},{7,6},{8,9},{9,8},{10,11... | collective-permute-start | bytes 196616 | tf_op jit(solution)/shard_map/ppermute | solution.py:251
  5.5 7.7 %collective-permute-start.3 = (f32[64,256]{1,0:T(8,128)S(1)}, f32[64,256]{1,0:T(8,128)S(1)}, u32[]{:S(2)}, u32[]{:S(2)}) collective-permute-start(f32[64,256]{1,0:T(8,128)S(1)} %add.15), channel_id=1, source_target_pairs={{0,6},{1,7},{2,4},{3,5},{4,2},{5,3},{6,0},{7,1},{8,14},{9,15},{10,... | collective-permute-start | bytes 196616 | tf_op jit(solution)/shard_map/ppermute | solution.py:251
  10.5 5.9 %collective-permute-start.2 = (f32[64,256]{1,0:T(8,128)S(1)}, f32[64,256]{1,0:T(8,128)S(1)}, u32[]{:S(2)}, u32[]{:S(2)}) collective-permute-start(f32[64,256]{1,0:T(8,128)S(1)} %add.15), channel_id=1, source_target_pairs={{0,4},{1,5},{2,6},{3,7},{4,0},{5,1},{6,2},{7,3},{8,12},{9,13},{10,... | collective-permute-start | bytes 196616 | tf_op jit(solution)/shard_map/ppermute | solution.py:251
  10.5 5.9 %collective-permute-start.1 = (f32[64,256]{1,0:T(8,128)S(1)}, f32[64,256]{1,0:T(8,128)S(1)}, u32[]{:S(2)}, u32[]{:S(2)}) collective-permute-start(f32[64,256]{1,0:T(8,128)S(1)} %add.15), channel_id=1, source_target_pairs={{0,2},{1,3},{2,0},{3,1},{4,6},{5,7},{6,4},{7,5},{8,10},{9,11},{10,... | collective-permute-start | bytes 196616 | tf_op jit(solution)/shard_map/ppermute | solution.py:251
  16.4 6.0 %collective-permute-start.4 = (f32[64,256]{1,0:T(8,128)S(1)}, f32[64,256]{1,0:T(8,128)S(1)}, u32[]{:S(2)}, u32[]{:S(2)}) collective-permute-start(f32[64,256]{1,0:T(8,128)S(1)} %add_add_fusion.refs_0_), channel_id=1, source_target_pairs={{0,24},{8,16},{16,8},{24,0},{1,25},{9,17},{17,9},{25,1},{2,26},{10... | collective-permute-start | bytes 196616 | tf_op jit(solution)/shard_map/ppermute | solution.py:251
  18.9 4.3 %collective-permute-start.6 = (f32[64,256]{1,0:T(8,128)S(1)}, f32[64,256]{1,0:T(8,128)S(1)}, u32[]{:S(2)}, u32[]{:S(2)}) collective-permute-start(f32[64,256]{1,0:T(8,128)S(1)} %add_add_fusion.refs_0_), channel_id=1, source_target_pairs={{0,8},{8,0},{16,24},{24,16},{1,9},{9,1},{17,25},{25,17},{2,10},{10... | collective-permute-start | bytes 196616 | tf_op jit(solution)/shard_map/ppermute | solution.py:251
  19.5 4.3 %collective-permute-start.5 = (f32[64,256]{1,0:T(8,128)S(1)}, f32[64,256]{1,0:T(8,128)S(1)}, u32[]{:S(2)}, u32[]{:S(2)}) collective-permute-start(f32[64,256]{1,0:T(8,128)S(1)} %add_add_fusion.refs_0_), channel_id=1, source_target_pairs={{0,16},{8,24},{16,0},{24,8},{1,17},{9,25},{17,1},{25,9},{2,18},{10... | collective-permute-start | bytes 196616 | tf_op jit(solution)/shard_map/ppermute | solution.py:251
  22.4 1.4 %collective-permute-start.7 = (f32[2,64,256]{2,1,0:T(8,128)S(1)}, f32[2,64,256]{2,1,0:T(8,128)S(1)}, u32[]{:S(2)}, u32[]{:S(2)}) collective-permute-start(f32[2,64,256]{2,1,0:T(8,128)S(1)} %pad_maximum_fusion.early_ref), channel_id=1, source_target_pairs={{0,1},{1,0},{2,3},{3,2},{4,5},{5,4},{6,7},{7,6},{8,9},{9,8},{10,11... | collective-permute-start | bytes 393224 | tf_op jit(solution)/shard_map/ppermute | solution.py:251
  23.7 1.7 %collective-permute-start.8 = (f32[2,64,256]{2,1,0:T(8,128)S(1)}, f32[2,64,256]{2,1,0:T(8,128)S(1)}, u32[]{:S(2)}, u32[]{:S(2)}) collective-permute-start(f32[2,64,256]{2,1,0:T(8,128)S(1)} %pad_maximum_fusion.1.refs_2_.late_ref), channel_id=1, source_target_pairs={{0,1},{1,0},{2,3},{3,2},{4,5},{5,4},{6,7},{7,6},{8,9},{9,8},{10,11... | collective-permute-start | bytes 393224 | tf_op jit(solution)/shard_map/ppermute | solution.py:251

commit v3 on v2

--- a/solution.py
+++ b/solution.py
@@ -60,21 +60,29 @@
     core = place_ref[1] % 2
     chunks, size, states = held.shape
     half = chunks // 2 * size
+    parts = sems.shape[1]
+    rows = size // parts
     basis_copy = pltpu.make_async_copy(basis_ref, basis, basis_sem)
-    basis_copy.start()
+    basis_copy.start(priority=1)
     copies = []
     for chunk in range(chunks):
         side, at = divmod(chunk * size, half)
-        first = pl.multiple_of((core if side else 1 - core) * half + at, size)
-        copies.append(
-            pltpu.make_async_copy(snaps_ref.at[pl.ds(first, size)], held.at[chunk], sems.at[chunk])
-        )
-        copies[-1].start()
+        first = (core if side else 1 - core) * half + at
+        for part in range(parts):
+            copies.append(
+                pltpu.make_async_copy(
+                    snaps_ref.at[pl.ds(pl.multiple_of(first + part * rows, rows), rows)],
+                    held.at[chunk, pl.ds(part * rows, rows)],
+                    sems.at[chunk, part],
+                )
+            )
+            copies[-1].start(priority=part % 2)
     basis_copy.wait()
     pieces = 4
     step = states // pieces
     for chunk in range(chunks):
-        copies[chunk].wait()
+        for copy in copies[chunk * parts : (chunk + 1) * parts]:
+            copy.wait()
         terms = [
             lax.dot_general(
                 basis[:, piece * step : (piece + 1) * step],
@@ -104,7 +112,7 @@
             pltpu.VMEM(basis.shape, basis.dtype),
             pltpu.VMEM((snaps // size, size, states), snapshots.dtype),
             pltpu.SemaphoreType.DMA,
-            pltpu.SemaphoreType.DMA((snaps // size,)),
+            pltpu.SemaphoreType.DMA((snaps // size, 2)),
         ],
         compiler_params=pltpu.CompilerParams(vmem_limit_bytes=55000 * 1024),
         name="project",
@@ -155,10 +163,24 @@
 def halves_kernel(cols, has_before, left_ref, right_ref, *refs):
     before_ref, refs = (refs[0], refs[1:]) if has_before else (None, refs)
     block_refs, acc_ref, col_scratch = refs[:-2], refs[-2], refs[-1]
-    half = block_refs[0].shape[-1]
     block = joined(block_refs)
-    term = terms_of(left_ref, right_ref, block, half, cols, col_scratch)
+    term = terms_of(left_ref, right_ref, block, block_refs[0].shape[-1], cols, col_scratch)
     acc_ref[...] = before_ref[...] + term if has_before else term
+
+
+def own_kernel(
+    cols, place_ref, left_ref, right_ref, before_ref, early_ref, other_ref, late_ref, acc_ref, reduced_ref,
+    col_scratch, reduced_out, sem,
+):
+    core = place_ref[1] % 2
+    half = early_ref.shape[-1]
+    reduced_out[:, pl.ds(pl.multiple_of(core * half, half), half)] = early_ref[0]
+    reduced_out[:, pl.ds(pl.multiple_of((1 - core) * half, half), half)] = other_ref[0]
+    copy = pltpu.make_async_copy(reduced_out, reduced_ref, sem)
+    copy.start()
+    block = joined([other_ref, late_ref])
+    acc_ref[...] = before_ref[...] + terms_of(left_ref, right_ref, block, half, cols, col_scratch)
+    copy.wait()
 
 
 def edge_columns(time_idx, core, halves, starts, ends):
@@ -186,9 +208,9 @@
 
 
 def last_kernel(
-    row_block, col_block, row_chunk, offsets, place_ref, left_ref, right_ref, before_ref, reg_ref, early_ref,
-    early_other_ref, late_ref, late_other_ref, reduced_ref, rates_ref, normal_ref, right_side_ref, starts,
-    ends, col_scratch, reduced_out, rates_out, normal_out, right_side_out, sems,
+    row_block, col_block, chunks, offsets, place_ref, left_ref, right_ref, before_ref, reg_ref, early_ref,
+    early_other_ref, late_ref, late_other_ref, rates_ref, normal_ref, right_side_ref, starts, ends,
+    col_scratch, rates_out, normal_out, right_side_out, sems,
 ):
     time_idx = place_ref[0]
     space_idx = place_ref[1]
@@ -204,16 +226,15 @@
         copies.append(pltpu.make_async_copy(source, target, sems.at[len(copies)]))
         copies[-1].start()
 
-    reduced_out[:, pl.ds(pl.multiple_of(core * half, half), half)] = early_ref[0]
-    reduced_out[:, pl.ds(pl.multiple_of((1 - core) * half, half), half)] = early_other_ref[0]
-    send(reduced_out, reduced_ref)
+    rates_out[:, pl.ds(pl.multiple_of(core * half, half), half)] = early_ref[0]
+    rates_out[:, pl.ds(pl.multiple_of((1 - core) * half, half), half)] = early_other_ref[0]
     halves = []
     for slot, offset in enumerate(offsets):
         for side, pair in ((core, (early_ref, late_ref)), (1 - core, (early_other_ref, late_other_ref))):
             ref, at = (pair[0], slot) if slot < early else (pair[1], slot - early)
             halves.append((offset, side, functools.partial(lambda ref, at: ref[at], ref, at)))
     edge, edge_rates = edge_columns(time_idx, core, halves, starts, ends)
-    own = reduced_out[...]
+    own = rates_out[...]
     width = edge.shape[1]
     own_edges = pltpu.roll(edge_rates, lax.rem(width - 4 * time_idx, width), 1)
     lane = lax.broadcasted_iota(jnp.int32, (1, snaps), 1)
@@ -225,7 +246,6 @@
     parts = parts_of(block, depth)
     column_side(left_ref, right_ref, parts, inner_rates(block, half), cols, col_scratch)
     scale = 1.0 / (groups * snaps)
-    chunks = [(at, min(row_chunk, row_block - at)) for at in range(0, row_block, row_chunk)]
     edge_parts = parts_of(edge, depth)
     edge_rates = edge_rates.astype(jnp.bfloat16)
     for at, size in chunks:
@@ -242,7 +262,7 @@
         normal_out[:, at : at + size] = total[:col_block, :size] * scale + diagonal
         right_side_out[:, at : at + size] = (total[cols:] + edge_total)[:, :size] * scale
         send(normal_out.at[:, at : at + size], normal_ref.at[:, at : at + size])
-    send(right_side_out, right_side_ref)
+        send(right_side_out.at[:, at : at + size], right_side_ref.at[:, at : at + size])
     for copy in copies:
         copy.wait()
 
@@ -267,6 +287,7 @@
     place = jnp.stack([time_idx, space_idx]).astype(jnp.int32)
     smem = pl.BlockSpec(memory_space=pltpu.SMEM)
     vmem = pl.BlockSpec(memory_space=pltpu.VMEM)
+    hbm = pl.BlockSpec(memory_space=pltpu.HBM)
     params = pltpu.CompilerParams(vmem_limit_bytes=32 * 1024 * 1024)
 
     keep, give = project(place, snapshots, modes_basis.T)
@@ -326,33 +347,50 @@
     acc, *late = lax.optimization_barrier((acc, *late))
     late_stack = jnp.stack(late)
     late_other = swapped(late_stack, "space", 1)
-    acc = add_terms(acc, [early_other, late_stack])
+    block_shape = jax.ShapeDtypeStruct((modes, snaps_dev), jnp.float32)
+    count = tm_count * half_snaps
+    acc, reduced = pl.pallas_call(
+        functools.partial(own_kernel, cols),
+        out_shape=(acc_shape, block_shape),
+        in_specs=[smem] + [vmem] * 6,
+        out_specs=(vmem, hbm),
+        scratch_shapes=[
+            col_scratch(count),
+            pltpu.VMEM(block_shape.shape, block_shape.dtype),
+            pltpu.SemaphoreType.DMA,
+        ],
+        input_output_aliases={3: 0},
+        compiler_params=params,
+        cost_estimate=cost(count),
+        name="own_and_late",
+    )(place, left, right, acc, early_stack, early_other, late_stack)
     width = 128
-    row_chunk = 256
-    chunks = pl.cdiv(row_block, row_chunk)
+    starts = list(range(0, row_block - width, 2 * width))
+    starts = [0] + [start - width for start in starts[1:]] if len(starts) > 1 else [0]
+    ends = starts[1:] + [row_block]
+    chunks = [(start, end - start) for start, end in zip(starts, ends)][::-1]
     out_shapes = (
-        jax.ShapeDtypeStruct((modes, snaps_dev), jnp.float32),
-        jax.ShapeDtypeStruct((modes, snaps_dev), jnp.float32),
+        block_shape,
         jax.ShapeDtypeStruct((col_block, row_block), jnp.float32),
         jax.ShapeDtypeStruct((modes, row_block), jnp.float32),
     )
     outs = pl.pallas_call(
-        functools.partial(last_kernel, row_block, col_block, row_chunk, offsets),
+        functools.partial(last_kernel, row_block, col_block, chunks, offsets),
         out_shape=out_shapes,
         in_specs=[smem] + [vmem] * 8,
-        out_specs=(pl.BlockSpec(memory_space=pltpu.HBM),) * 4,
+        out_specs=(hbm,) * 3,
         scratch_shapes=[
             pltpu.VMEM((2 * tm_count, modes, width), jnp.float32),
             pltpu.VMEM((2 * tm_count, modes, width), jnp.float32),
             col_scratch(len(late) * half_snaps),
             *[pltpu.VMEM(shape.shape, shape.dtype) for shape in out_shapes],
-            pltpu.SemaphoreType.DMA((3 + chunks,)),
+            pltpu.SemaphoreType.DMA((1 + 2 * len(chunks),)),
         ],
         compiler_params=params,
         cost_estimate=cost(len(late) * half_snaps),
         name="last_half",
     )(place, left, right, acc, reg_rows, early_stack, early_other, late_stack, late_other)
-    return tuple(out.T for out in outs)
+    return tuple(out.T for out in (reduced, *outs))
 
 
 def solution(mesh):

time: 28.2 us -> 29.8 us (1.057)
  Pallas kernels: 9.92 us -> 11.4 us
    pallas_call x1 -> x2, Pallas kernels: 2.52 us -> 5.24 us  [the longest x1 2.77 us: local(): pl.pallas_call(functools.partial(own_kernel, cols), out_shape=(acc_shape,...]
    pallas_call x3 -> x2, Pallas kernels: 2.94 us -> 1.31 us  [add_terms(): pl.pallas_call(functools.partial(halves_kernel, cols, len(before)), out_s...]
    pallas_call x1, Pallas kernels: 3.33 us -> 3.75 us  [project(): pl.pallas_call(project_kernel, out_shape=(block, block), in_specs=[pl.Blo...]
  transfers between devices with their start and end apart: 9 -> 9, of which waited for: 4 -> 4; matrix products, arithmetic and copies ran while one was open for 3% -> 3% of each run, Pallas kernels for 15% -> 18%
where the time goes in v3:
time: 29.8 us; the launch traced here: 29.5 us
  Pallas kernels  11.4 us (38%)
  starting transfers between devices  9.87 us (33%)
  waiting for transfers between devices  6.53 us (22%)
  local copies, waits for them, and re-layouts  0.78 us (3%)
  between operations  0.77 us (3%)
    ppermute x9, starting transfers between devices, swapped(): lax.ppermute(value, axis, [(i, i ^ distance) for i in range(lax.axis_size...  9.87 us
    ppermute x9, waiting for transfers between devices, swapped(): lax.ppermute(value, axis, [(i, i ^ distance) for i in range(lax.axis_size...  6.53 us
    pallas_call x1, Pallas kernels, project(): pl.pallas_call(project_kernel, out_shape=(block, block), in_specs=[pl.Blo...  3.75 us
    pallas_call x1, Pallas kernels, local(): pl.pallas_call(functools.partial(own_kernel, cols), out_shape=(acc_shape,...  2.77 us
    pallas_call x1, Pallas kernels, local(): pl.pallas_call(functools.partial(last_kernel, row_block, col_block, chunk...  2.47 us
    pallas_call x2, Pallas kernels, add_terms(): pl.pallas_call(functools.partial(halves_kernel, cols, len(before)), out_s...  1.31 us
    pallas_call x1, Pallas kernels, local(): pl.pallas_call(functools.partial(selector_kernel, row_block, col_block, m...  1.14 us
    dynamic_slice x1, local copies, waits for them, and re-layouts, local(): lax.dynamic_slice_in_dim(reg_weights, first_row, row_block, 0)[None]  0.78 us
  transfers between devices with their start and end apart: 9, of which 4 were waited for; matrix products, arithmetic and copies ran while one was open for 3% of the time, Pallas kernels for 18%

profile of v3, /device:TPU:0, one launch (start us, length us, event | category | flops | bytes accessed | tf_op | source)
XLA Modules:
  0.0 29.5 jit_solution(3231830578990885951)
XLA Ops:
  0.6 0.1 pad_add_fusion.place_ref
  0.7 3.7 %project.1 = (f32[64,256]{1,0:T(8,128)S(1)}, f32[64,256]{1,0:T(8,128)S(1)}) custom-call(s32[2]{0:T(128)S(1)} %pad_add_fusion.place_ref, bf16[64,2048]{1,0:T(8,128)(2,1)} %bitcast.16, bf16[512,2048]{1,0:T(8,128)(2,1)} %snaps_ref.1), custom_call_target="tpu_custom_call" | custom-call | tf_op jit(solution)/shard_map/project/pallas_call | solution.py:106
  4.5 0.5 %collective-permute-start = (f32[64,256]{1,0:T(8,128)S(1)}, f32[64,256]{1,0:T(8,128)S(1)}, u32[]{:S(2)}, u32[]{:S(2)}) collective-permute-start(f32[64,256]{1,0:T(8,128)S(1)} %get-tuple-element.23), channel_id=1, source_target_pairs={{0,1},{1,0},{2,3},{3,2},{4,5},{5,4},{6,7},{7,6},{8,9},{9,8},{10,11... | collective-permute-start | bytes 196616 | tf_op jit(solution)/shard_map/ppermute | solution.py:271
  5.0 0.9 %collective-permute-done = f32[64,256]{1,0:T(8,128)S(1)} collective-permute-done((f32[64,256]{1,0:T(8,128)S(1)}, f32[64,256]{1,0:T(8,128)S(1)}, u32[]{:S(2)}, u32[]{:S(2)}) %collective-permute-start) | collective-permute-done | bytes 65568 | tf_op jit(solution)/shard_map/ppermute | solution.py:271
  5.9 5.0 %collective-permute-start.3 = (f32[64,256]{1,0:T(8,128)S(1)}, f32[64,256]{1,0:T(8,128)S(1)}, u32[]{:S(2)}, u32[]{:S(2)}) collective-permute-start(f32[64,256]{1,0:T(8,128)S(1)} %add.15), channel_id=1, source_target_pairs={{0,6},{1,7},{2,4},{3,5},{4,2},{5,3},{6,0},{7,1},{8,14},{9,15},{10,... | collective-permute-start | bytes 196616 | tf_op jit(solution)/shard_map/ppermute | solution.py:271
  10.9 0.0 collective-permute-start.2
  10.9 0.6 %collective-permute-start.1 = (f32[64,256]{1,0:T(8,128)S(1)}, f32[64,256]{1,0:T(8,128)S(1)}, u32[]{:S(2)}, u32[]{:S(2)}) collective-permute-start(f32[64,256]{1,0:T(8,128)S(1)} %add.15), channel_id=1, source_target_pairs={{0,2},{1,3},{2,0},{3,1},{4,6},{5,7},{6,4},{7,5},{8,10},{9,11},{10,... | collective-permute-start | bytes 196616 | tf_op jit(solution)/shard_map/ppermute | solution.py:271
  11.6 0.8 %dynamic_slice.3 = f32[536]{0:T(1024)S(1)} dynamic-slice(f32[2144]{0:T(1024)} %param.5, s32[]{:T(128)S(6)} %select_n.3), dynamic_slice_sizes={536} | dynamic-slice | bytes 4292 | tf_op jit(solution)/shard_map/dynamic_slice | solution.py:307
  12.4 1.1 %selectors.1 = (bf16[816,256]{1,0:T(8,128)(2,1)S(1)}, bf16[816,256]{1,0:T(8,128)(2,1)S(1)}) custom-call(s32[2]{0:T(128)S(1)} %pad_add_fusion.place_ref), custom_call_target="tpu_custom_call" | custom-call | flops 1000000 | bytes 1000000 | tf_op jit(solution)/shard_map/selectors/pallas_call | solution.py:297
  13.5 0.0 collective-permute-done.3
  13.6 3.2 %collective-permute-done.2 = f32[64,256]{1,0:T(8,128)S(1)} collective-permute-done((f32[64,256]{1,0:T(8,128)S(1)}, f32[64,256]{1,0:T(8,128)S(1)}, u32[]{:S(2)}, u32[]{:S(2)}) %collective-permute-start.2) | collective-permute-done | bytes 65568 | tf_op jit(solution)/shard_map/ppermute | solution.py:271
  16.8 0.0 collective-permute-done.1
  16.8 2.5 %collective-permute-start.4 = (f32[64,256]{1,0:T(8,128)S(1)}, f32[64,256]{1,0:T(8,128)S(1)}, u32[]{:S(2)}, u32[]{:S(2)}) collective-permute-start(f32[64,256]{1,0:T(8,128)S(1)} %add_add_fusion.refs_0_), channel_id=1, source_target_pairs={{0,24},{8,16},{16,8},{24,0},{1,25},{9,17},{17,9},{25,1},{2,26},{10... | collective-permute-start | bytes 196616 | tf_op jit(solution)/shard_map/ppermute | solution.py:271
  19.3 0.5 %collective-permute-start.6 = (f32[64,256]{1,0:T(8,128)S(1)}, f32[64,256]{1,0:T(8,128)S(1)}, u32[]{:S(2)}, u32[]{:S(2)}) collective-permute-start(f32[64,256]{1,0:T(8,128)S(1)} %add_add_fusion.refs_0_), channel_id=1, source_target_pairs={{0,8},{8,0},{16,24},{24,16},{1,9},{9,1},{17,25},{25,17},{2,10},{10... | collective-permute-start | bytes 196616 | tf_op jit(solution)/shard_map/ppermute | solution.py:271
  19.9 0.5 %collective-permute-start.5 = (f32[64,256]{1,0:T(8,128)S(1)}, f32[64,256]{1,0:T(8,128)S(1)}, u32[]{:S(2)}, u32[]{:S(2)}) collective-permute-start(f32[64,256]{1,0:T(8,128)S(1)} %add_add_fusion.refs_0_), channel_id=1, source_target_pairs={{0,16},{8,24},{16,0},{24,8},{1,17},{9,25},{17,1},{25,9},{2,18},{10... | collective-permute-start | bytes 196616 | tf_op jit(solution)/shard_map/ppermute | solution.py:271
  20.4 0.6 %halves.2.refs_0_ = f32[336,544]{1,0:T(8,128)S(1)} custom-call(bf16[816,256]{1,0:T(8,128)(2,1)S(1)} %get-tuple-element.28.left_ref, bf16[816,256]{1,0:T(8,128)(2,1)S(1)} %get-tuple-element.29.right_ref, f32[64,256]{1,0:T(8,128)S(1)} %add_add_fusion.refs_0_), custom_call_target="tpu_custom_call" | custom-call | flops 307494912 | bytes 2000000 | tf_op jit(solution)/shard_map/halves/pallas_call | solution.py:328
  21.0 1.8 %collective-permute-done.4.refs_1_ = f32[64,256]{1,0:T(8,128)S(1)} collective-permute-done((f32[64,256]{1,0:T(8,128)S(1)}, f32[64,256]{1,0:T(8,128)S(1)}, u32[]{:S(2)}, u32[]{:S(2)}) %collective-permute-start.4) | collective-permute-done | bytes 65568 | tf_op jit(solution)/shard_map/ppermute | solution.py:271
  22.8 0.1 collective-permute-start.7
  22.9 0.7 %halves.3.before_ref = f32[336,544]{1,0:T(8,128)S(1)} custom-call(bf16[816,256]{1,0:T(8,128)(2,1)S(1)} %get-tuple-element.28.left_ref, bf16[816,256]{1,0:T(8,128)(2,1)S(1)} %get-tuple-element.29.right_ref, f32[336,544]{1,0:T(8,128)S(1)} %halves.2.refs_0_, f32[64,256]{1,0:T(8,128)S(1)} %collective-permute-done.4.refs_1_), custom_call_target="tpu_custom_call", output_to_operand_aliasing={{}: (2, {})} | custom-call | flops 307494912 | bytes 2000000 | tf_op jit(solution)/shard_map/halves/pallas_call | solution.py:328
  23.6 0.0 collective-permute-done.6
  23.6 0.5 %collective-permute-done.5 = f32[64,256]{1,0:T(8,128)S(1)} collective-permute-done((f32[64,256]{1,0:T(8,128)S(1)}, f32[64,256]{1,0:T(8,128)S(1)}, u32[]{:S(2)}, u32[]{:S(2)}) %collective-permute-start.5) | collective-permute-done | bytes 65568 | tf_op jit(solution)/shard_map/ppermute | solution.py:271
  24.2 0.1 collective-permute-start.8
  24.2 0.0 collective-permute-done.7.other_ref.early_other_ref
  24.2 2.8 %own_and_late.1 = (f32[336,544]{1,0:T(8,128)S(1)}, f32[64,512]{1,0:T(8,128)}) custom-call(s32[2]{0:T(128)S(1)} %pad_add_fusion.place_ref, bf16[816,256]{1,0:T(8,128)(2,1)S(1)} %get-tuple-element.28.left_ref, bf16[816,256]{1,0:T(8,128)(2,1)S(1)} %get-tuple-element.29.right_ref, f32[336,544]{1,0:T(8,128)S(1)} %halves.3.before_ref, ...), custom_call_target="tpu_custom_call", output_to_operand_aliasing={{0}: (3, {})} | custom-call | flops 1229979648 | bytes 2000000 | tf_op jit(solution)/shard_map/own_and_late/pallas_call | solution.py:352
  27.0 0.0 collective-permute-done.8.late_other_ref
  27.0 2.5 %last_half.1 = (f32[64,512]{1,0:T(8,128)}, f32[268,536]{1,0:T(8,128)}, f32[64,536]{1,0:T(8,128)}) custom-call(s32[2]{0:T(128)S(1)} %pad_add_fusion.place_ref, bf16[816,256]{1,0:T(8,128)(2,1)S(1)} %get-tuple-element.28.left_ref, bf16[816,256]{1,0:T(8,128)(2,1)S(1)} %get-tuple-element.29.right_ref, f32[336,544]{1,0:T(8,128)S(1)} %get-tuple-element.35.before_ref, ...), custom_call_target="tpu_custom_call" | custom-call | flops 614989824 | bytes 2000000 | tf_op jit(solution)/shard_map/last_half/pallas_call | solution.py:377
  (5 shorter events, 0.1 us)
Async XLA Ops:
  4.5 1.4 %collective-permute-start = (f32[64,256]{1,0:T(8,128)S(1)}, f32[64,256]{1,0:T(8,128)S(1)}, u32[]{:S(2)}, u32[]{:S(2)}) collective-permute-start(f32[64,256]{1,0:T(8,128)S(1)} %get-tuple-element.23), channel_id=1, source_target_pairs={{0,1},{1,0},{2,3},{3,2},{4,5},{5,4},{6,7},{7,6},{8,9},{9,8},{10,11... | collective-permute-start | bytes 196616 | tf_op jit(solution)/shard_map/ppermute | solution.py:271
  5.9 7.7 %collective-permute-start.3 = (f32[64,256]{1,0:T(8,128)S(1)}, f32[64,256]{1,0:T(8,128)S(1)}, u32[]{:S(2)}, u32[]{:S(2)}) collective-permute-start(f32[64,256]{1,0:T(8,128)S(1)} %add.15), channel_id=1, source_target_pairs={{0,6},{1,7},{2,4},{3,5},{4,2},{5,3},{6,0},{7,1},{8,14},{9,15},{10,... | collective-permute-start | bytes 196616 | tf_op jit(solution)/shard_map/ppermute | solution.py:271
  10.9 5.9 %collective-permute-start.2 = (f32[64,256]{1,0:T(8,128)S(1)}, f32[64,256]{1,0:T(8,128)S(1)}, u32[]{:S(2)}, u32[]{:S(2)}) collective-permute-start(f32[64,256]{1,0:T(8,128)S(1)} %add.15), channel_id=1, source_target_pairs={{0,4},{1,5},{2,6},{3,7},{4,0},{5,1},{6,2},{7,3},{8,12},{9,13},{10,... | collective-permute-start | bytes 196616 | tf_op jit(solution)/shard_map/ppermute | solution.py:271
  10.9 5.9 %collective-permute-start.1 = (f32[64,256]{1,0:T(8,128)S(1)}, f32[64,256]{1,0:T(8,128)S(1)}, u32[]{:S(2)}, u32[]{:S(2)}) collective-permute-start(f32[64,256]{1,0:T(8,128)S(1)} %add.15), channel_id=1, source_target_pairs={{0,2},{1,3},{2,0},{3,1},{4,6},{5,7},{6,4},{7,5},{8,10},{9,11},{10,... | collective-permute-start | bytes 196616 | tf_op jit(solution)/shard_map/ppermute | solution.py:271
  16.8 6.0 %collective-permute-start.4 = (f32[64,256]{1,0:T(8,128)S(1)}, f32[64,256]{1,0:T(8,128)S(1)}, u32[]{:S(2)}, u32[]{:S(2)}) collective-permute-start(f32[64,256]{1,0:T(8,128)S(1)} %add_add_fusion.refs_0_), channel_id=1, source_target_pairs={{0,24},{8,16},{16,8},{24,0},{1,25},{9,17},{17,9},{25,1},{2,26},{10... | collective-permute-start | bytes 196616 | tf_op jit(solution)/shard_map/ppermute | solution.py:271
  19.3 4.3 %collective-permute-start.6 = (f32[64,256]{1,0:T(8,128)S(1)}, f32[64,256]{1,0:T(8,128)S(1)}, u32[]{:S(2)}, u32[]{:S(2)}) collective-permute-start(f32[64,256]{1,0:T(8,128)S(1)} %add_add_fusion.refs_0_), channel_id=1, source_target_pairs={{0,8},{8,0},{16,24},{24,16},{1,9},{9,1},{17,25},{25,17},{2,10},{10... | collective-permute-start | bytes 196616 | tf_op jit(solution)/shard_map/ppermute | solution.py:271
  19.9 4.3 %collective-permute-start.5 = (f32[64,256]{1,0:T(8,128)S(1)}, f32[64,256]{1,0:T(8,128)S(1)}, u32[]{:S(2)}, u32[]{:S(2)}) collective-permute-start(f32[64,256]{1,0:T(8,128)S(1)} %add_add_fusion.refs_0_), channel_id=1, source_target_pairs={{0,16},{8,24},{16,0},{24,8},{1,17},{9,25},{17,1},{25,9},{2,18},{10... | collective-permute-start | bytes 196616 | tf_op jit(solution)/shard_map/ppermute | solution.py:271
  22.8 1.4 %collective-permute-start.7 = (f32[2,64,256]{2,1,0:T(8,128)S(1)}, f32[2,64,256]{2,1,0:T(8,128)S(1)}, u32[]{:S(2)}, u32[]{:S(2)}) collective-permute-start(f32[2,64,256]{2,1,0:T(8,128)S(1)} %pad_maximum_fusion.early_ref), channel_id=1, source_target_pairs={{0,1},{1,0},{2,3},{3,2},{4,5},{5,4},{6,7},{7,6},{8,9},{9,8},{10,11... | collective-permute-start | bytes 393224 | tf_op jit(solution)/shard_map/ppermute | solution.py:271
  24.2 2.9 %collective-permute-start.8 = (f32[2,64,256]{2,1,0:T(8,128)S(1)}, f32[2,64,256]{2,1,0:T(8,128)S(1)}, u32[]{:S(2)}, u32[]{:S(2)}) collective-permute-start(f32[2,64,256]{2,1,0:T(8,128)S(1)} %pad_maximum_fusion.1.late_ref), channel_id=1, source_target_pairs={{0,1},{1,0},{2,3},{3,2},{4,5},{5,4},{6,7},{7,6},{8,9},{9,8},{10,11... | collective-permute-start | bytes 393224 | tf_op jit(solution)/shard_map/ppermute | solution.py:271

commit v4 on v2

--- a/solution.py
+++ b/solution.py
@@ -56,8 +56,8 @@
     return (first * second).astype(jnp.bfloat16)
 
 
-def project_kernel(place_ref, basis_ref, snaps_ref, keep_ref, give_ref, basis, held, basis_sem, sems):
-    core = place_ref[1] % 2
+def project_kernel(basis_ref, snaps_ref, keep_ref, give_ref, basis, held, basis_sem, sems):
+    core = lax.axis_index("space") % 2
     chunks, size, states = held.shape
     half = chunks // 2 * size
     basis_copy = pltpu.make_async_copy(basis_ref, basis, basis_sem)
@@ -77,18 +77,18 @@
         copies[chunk].wait()
         terms = [
             lax.dot_general(
+                held[chunk, :, piece * step : (piece + 1) * step],
                 basis[:, piece * step : (piece + 1) * step],
-                held[chunk, :, piece * step : (piece + 1) * step],
                 NT,
                 preferred_element_type=jnp.float32,
             )
             for piece in range(pieces)
         ]
         side, at = divmod(chunk * size, half)
-        (keep_ref if side else give_ref)[:, at : at + size] = tree_sum(terms)
-
-
-def project(place, snapshots, basis):
+        (keep_ref if side else give_ref)[:, at : at + size] = tree_sum(terms).T
+
+
+def project(snapshots, basis):
     snaps, states = snapshots.shape
     modes = basis.shape[0]
     size = 128
@@ -98,7 +98,7 @@
     return pl.pallas_call(
         project_kernel,
         out_shape=(block, block),
-        in_specs=[pl.BlockSpec(memory_space=pltpu.SMEM), hbm, hbm],
+        in_specs=[hbm, hbm],
         out_specs=(vmem, vmem),
         scratch_shapes=[
             pltpu.VMEM(basis.shape, basis.dtype),
@@ -108,16 +108,17 @@
         ],
         compiler_params=pltpu.CompilerParams(vmem_limit_bytes=55000 * 1024),
         name="project",
-    )(place, basis, snapshots)
-
-
-def selector_kernel(row_block, col_block, modes, place_ref, left_ref, right_ref):
+    )(basis, snapshots)
+
+
+def selector_kernel(row_block, col_block, after_ref, left_ref, right_ref):
+    modes = after_ref.shape[0]
     cols = round_up(col_block, 16)
     rows = left_ref.shape[0] - cols
     depth = left_ref.shape[1]
     for at, size, first in (
-        (0, cols, place_ref[1] * col_block),
-        (cols, rows, place_ref[0] * row_block),
+        (0, cols, lax.axis_index("space") * col_block),
+        (cols, rows, lax.axis_index("tm") * row_block),
     ):
         left, right = selectors(first, size, modes, depth)
         left_ref[at : at + size] = left
@@ -155,9 +156,8 @@
 def halves_kernel(cols, has_before, left_ref, right_ref, *refs):
     before_ref, refs = (refs[0], refs[1:]) if has_before else (None, refs)
     block_refs, acc_ref, col_scratch = refs[:-2], refs[-2], refs[-1]
-    half = block_refs[0].shape[-1]
     block = joined(block_refs)
-    term = terms_of(left_ref, right_ref, block, half, cols, col_scratch)
+    term = terms_of(left_ref, right_ref, block, block_refs[0].shape[-1], cols, col_scratch)
     acc_ref[...] = before_ref[...] + term if has_before else term
 
 
@@ -186,12 +186,12 @@
 
 
 def last_kernel(
-    row_block, col_block, row_chunk, offsets, place_ref, left_ref, right_ref, before_ref, reg_ref, early_ref,
+    row_block, col_block, chunks, offsets, left_ref, right_ref, before_ref, reg_ref, early_ref,
     early_other_ref, late_ref, late_other_ref, reduced_ref, rates_ref, normal_ref, right_side_ref, starts,
     ends, col_scratch, reduced_out, rates_out, normal_out, right_side_out, sems,
 ):
-    time_idx = place_ref[0]
-    space_idx = place_ref[1]
+    time_idx = lax.axis_index("tm")
+    space_idx = lax.axis_index("space")
     core = space_idx % 2
     early, modes, half = early_ref.shape
     groups = early + late_ref.shape[0]
@@ -225,7 +225,6 @@
     parts = parts_of(block, depth)
     column_side(left_ref, right_ref, parts, inner_rates(block, half), cols, col_scratch)
     scale = 1.0 / (groups * snaps)
-    chunks = [(at, min(row_chunk, row_block - at)) for at in range(0, row_block, row_chunk)]
     edge_parts = parts_of(edge, depth)
     edge_rates = edge_rates.astype(jnp.bfloat16)
     for at, size in chunks:
@@ -242,7 +241,7 @@
         normal_out[:, at : at + size] = total[:col_block, :size] * scale + diagonal
         right_side_out[:, at : at + size] = (total[cols:] + edge_total)[:, :size] * scale
         send(normal_out.at[:, at : at + size], normal_ref.at[:, at : at + size])
-    send(right_side_out, right_side_ref)
+        send(right_side_out.at[:, at : at + size], right_side_ref.at[:, at : at + size])
     for copy in copies:
         copy.wait()
 
@@ -263,26 +262,24 @@
     cols = round_up(col_block, 16)
     depth = round_up(3 * modes + 1, 128)
     time_idx = lax.axis_index("tm")
-    space_idx = lax.axis_index("space")
-    place = jnp.stack([time_idx, space_idx]).astype(jnp.int32)
-    smem = pl.BlockSpec(memory_space=pltpu.SMEM)
     vmem = pl.BlockSpec(memory_space=pltpu.VMEM)
+    hbm = pl.BlockSpec(memory_space=pltpu.HBM)
     params = pltpu.CompilerParams(vmem_limit_bytes=32 * 1024 * 1024)
 
-    keep, give = project(place, snapshots, modes_basis.T)
+    keep, give = project(snapshots, modes_basis.T)
     half = keep + swapped(give, "space", 1)
-    after, half = lax.optimization_barrier((place, half))
+    after, half = lax.optimization_barrier((time_idx, half))
     selector = jax.ShapeDtypeStruct((cols + rows, depth), jnp.bfloat16)
     left, right = pl.pallas_call(
-        functools.partial(selector_kernel, row_block, col_block, modes),
+        functools.partial(selector_kernel, row_block, col_block),
         out_shape=(selector, selector),
-        in_specs=[smem],
+        in_specs=[vmem],
         out_specs=(vmem, vmem),
         compiler_params=params,
         cost_estimate=pl.CostEstimate(flops=10**6, bytes_accessed=10**6, transcendentals=0),
         name="selectors",
-    )(after)
-    first_row = after[0] * row_block
+    )(half)
+    first_row = after * row_block
     reg_rows = lax.dynamic_slice_in_dim(reg_weights, first_row, row_block, 0)[None]
 
     terms = [half] + [swapped(half, "space", step) for step in range(2, space_count, 2)]
@@ -328,8 +325,10 @@
     late_other = swapped(late_stack, "space", 1)
     acc = add_terms(acc, [early_other, late_stack])
     width = 128
-    row_chunk = 256
-    chunks = pl.cdiv(row_block, row_chunk)
+    starts = list(range(0, row_block - width, 2 * width))
+    starts = [0] + [start - width for start in starts[1:]] if len(starts) > 1 else [0]
+    ends = starts[1:] + [row_block]
+    chunks = [(start, end - start) for start, end in zip(starts, ends)][::-1]
     out_shapes = (
         jax.ShapeDtypeStruct((modes, snaps_dev), jnp.float32),
         jax.ShapeDtypeStruct((modes, snaps_dev), jnp.float32),
@@ -337,21 +336,21 @@
         jax.ShapeDtypeStruct((modes, row_block), jnp.float32),
     )
     outs = pl.pallas_call(
-        functools.partial(last_kernel, row_block, col_block, row_chunk, offsets),
+        functools.partial(last_kernel, row_block, col_block, chunks, offsets),
         out_shape=out_shapes,
-        in_specs=[smem] + [vmem] * 8,
-        out_specs=(pl.BlockSpec(memory_space=pltpu.HBM),) * 4,
+        in_specs=[vmem] * 8,
+        out_specs=(hbm,) * 4,
         scratch_shapes=[
             pltpu.VMEM((2 * tm_count, modes, width), jnp.float32),
             pltpu.VMEM((2 * tm_count, modes, width), jnp.float32),
             col_scratch(len(late) * half_snaps),
             *[pltpu.VMEM(shape.shape, shape.dtype) for shape in out_shapes],
-            pltpu.SemaphoreType.DMA((3 + chunks,)),
+            pltpu.SemaphoreType.DMA((2 + 2 * len(chunks),)),
         ],
         compiler_params=params,
         cost_estimate=cost(len(late) * half_snaps),
         name="last_half",
-    )(place, left, right, acc, reg_rows, early_stack, early_other, late_stack, late_other)
+    )(left, right, acc, reg_rows, early_stack, early_other, late_stack, late_other)
     return tuple(out.T for out in outs)
 
 

time: 28.2 us -> 27.2 us (0.965)
  Pallas kernels: 9.92 us -> 8.44 us
  waiting for transfers between devices: 6.52 us -> 7.13 us
    pallas_call x3, Pallas kernels: 6.98 us -> 5.52 us  [the longest x1 2.98 us: project(): pl.pallas_call(project_kernel, out_shape=(block, block), in_specs=[hbm, h...]
    ppermute x9, waiting for transfers between devices: 6.52 us -> 7.13 us  [swapped(): lax.ppermute(value, axis, [(i, i ^ distance) for i in range(lax.axis_size...]
  transfers between devices with their start and end apart: 9 -> 9, of which waited for: 4 -> 5; matrix products, arithmetic and copies ran while one was open for 3% -> 3% of each run, Pallas kernels for 15% -> 13%
where the time goes in v4:
time: 27.2 us; the launch traced here: 27 us
  starting transfers between devices  9.87 us (36%)
  Pallas kernels  8.44 us (31%)
  waiting for transfers between devices  7.13 us (26%)
  local copies, waits for them, and re-layouts  0.78 us (3%)
  between operations  0.71 us (3%)
    ppermute x9, starting transfers between devices, swapped(): lax.ppermute(value, axis, [(i, i ^ distance) for i in range(lax.axis_size...  9.87 us
    ppermute x9, waiting for transfers between devices, swapped(): lax.ppermute(value, axis, [(i, i ^ distance) for i in range(lax.axis_size...  7.13 us
    pallas_call x1, Pallas kernels, project(): pl.pallas_call(project_kernel, out_shape=(block, block), in_specs=[hbm, h...  2.98 us
    pallas_call x3, Pallas kernels, add_terms(): pl.pallas_call(functools.partial(halves_kernel, cols, len(before)), out_s...  2.92 us
    pallas_call x1, Pallas kernels, local(): pl.pallas_call(functools.partial(last_kernel, row_block, col_block, chunk...  1.94 us
    dynamic_slice x1, local copies, waits for them, and re-layouts, local(): lax.dynamic_slice_in_dim(reg_weights, first_row, row_block, 0)[None]  0.77 us
    pallas_call x1, Pallas kernels, local(): pl.pallas_call(functools.partial(selector_kernel, row_block, col_block),...  0.6 us
  transfers between devices with their start and end apart: 9, of which 5 were waited for; matrix products, arithmetic and copies ran while one was open for 3% of the time, Pallas kernels for 13%

profile of v4, /device:TPU:0, one launch (start us, length us, event | category | flops | bytes accessed | tf_op | source)
XLA Modules:
  0.0 27.0 jit_solution(7874951341751902703)
XLA Ops:
  0.6 3.0 %project.1 = (f32[64,256]{1,0:T(8,128)S(1)}, f32[64,256]{1,0:T(8,128)S(1)}) custom-call(bf16[64,2048]{1,0:T(8,128)(2,1)} %bitcast.11, bf16[512,2048]{1,0:T(8,128)(2,1)} %snaps_ref.1), custom_call_target="tpu_custom_call" | custom-call | tf_op jit(solution)/shard_map/project/pallas_call | solution.py:98
  3.6 0.5 %collective-permute-start = (f32[64,256]{1,0:T(8,128)S(1)}, f32[64,256]{1,0:T(8,128)S(1)}, u32[]{:S(2)}, u32[]{:S(2)}) collective-permute-start(f32[64,256]{1,0:T(8,128)S(1)} %get-tuple-element.22), channel_id=1, source_target_pairs={{0,1},{1,0},{2,3},{3,2},{4,5},{5,4},{6,7},{7,6},{8,9},{9,8},{10,11... | collective-permute-start | bytes 196616 | tf_op jit(solution)/shard_map/ppermute | solution.py:250
  4.1 0.9 %collective-permute-done = f32[64,256]{1,0:T(8,128)S(1)} collective-permute-done((f32[64,256]{1,0:T(8,128)S(1)}, f32[64,256]{1,0:T(8,128)S(1)}, u32[]{:S(2)}, u32[]{:S(2)}) %collective-permute-start) | collective-permute-done | bytes 65568 | tf_op jit(solution)/shard_map/ppermute | solution.py:250
  5.1 5.0 %collective-permute-start.3 = (f32[64,256]{1,0:T(8,128)S(1)}, f32[64,256]{1,0:T(8,128)S(1)}, u32[]{:S(2)}, u32[]{:S(2)}) collective-permute-start(f32[64,256]{1,0:T(8,128)S(1)} %add.15.after_ref), channel_id=1, source_target_pairs={{0,6},{1,7},{2,4},{3,5},{4,2},{5,3},{6,0},{7,1},{8,14},{9,15},{10,... | collective-permute-start | bytes 196616 | tf_op jit(solution)/shard_map/ppermute | solution.py:250
  10.1 0.0 collective-permute-start.2
  10.1 0.6 %collective-permute-start.1 = (f32[64,256]{1,0:T(8,128)S(1)}, f32[64,256]{1,0:T(8,128)S(1)}, u32[]{:S(2)}, u32[]{:S(2)}) collective-permute-start(f32[64,256]{1,0:T(8,128)S(1)} %add.15.after_ref), channel_id=1, source_target_pairs={{0,2},{1,3},{2,0},{3,1},{4,6},{5,7},{6,4},{7,5},{8,10},{9,11},{10,... | collective-permute-start | bytes 196616 | tf_op jit(solution)/shard_map/ppermute | solution.py:250
  10.7 0.8 %dynamic_slice.3 = f32[536]{0:T(1024)S(1)} dynamic-slice(f32[2144]{0:T(1024)} %param.5, s32[]{:T(128)S(6)} %select_n.3), dynamic_slice_sizes={536} | dynamic-slice | bytes 4292 | tf_op jit(solution)/shard_map/dynamic_slice | solution.py:283
  11.5 0.6 %selectors.1 = (bf16[816,256]{1,0:T(8,128)(2,1)S(1)}, bf16[816,256]{1,0:T(8,128)(2,1)S(1)}) custom-call(f32[64,256]{1,0:T(8,128)S(1)} %add.15.after_ref), custom_call_target="tpu_custom_call" | custom-call | flops 1000000 | bytes 1000000 | tf_op jit(solution)/shard_map/selectors/pallas_call | solution.py:273
  12.1 0.6 %collective-permute-done.3 = f32[64,256]{1,0:T(8,128)S(1)} collective-permute-done((f32[64,256]{1,0:T(8,128)S(1)}, f32[64,256]{1,0:T(8,128)S(1)}, u32[]{:S(2)}, u32[]{:S(2)}) %collective-permute-start.3) | collective-permute-done | bytes 65568 | tf_op jit(solution)/shard_map/ppermute | solution.py:250
  12.7 3.2 %collective-permute-done.2 = f32[64,256]{1,0:T(8,128)S(1)} collective-permute-done((f32[64,256]{1,0:T(8,128)S(1)}, f32[64,256]{1,0:T(8,128)S(1)}, u32[]{:S(2)}, u32[]{:S(2)}) %collective-permute-start.2) | collective-permute-done | bytes 65568 | tf_op jit(solution)/shard_map/ppermute | solution.py:250
  16.0 0.0 collective-permute-done.1
  16.0 2.5 %collective-permute-start.4 = (f32[64,256]{1,0:T(8,128)S(1)}, f32[64,256]{1,0:T(8,128)S(1)}, u32[]{:S(2)}, u32[]{:S(2)}) collective-permute-start(f32[64,256]{1,0:T(8,128)S(1)} %add_add_fusion.refs_0_), channel_id=1, source_target_pairs={{0,24},{8,16},{16,8},{24,0},{1,25},{9,17},{17,9},{25,1},{2,26},{10... | collective-permute-start | bytes 196616 | tf_op jit(solution)/shard_map/ppermute | solution.py:250
  18.5 0.5 %collective-permute-start.6 = (f32[64,256]{1,0:T(8,128)S(1)}, f32[64,256]{1,0:T(8,128)S(1)}, u32[]{:S(2)}, u32[]{:S(2)}) collective-permute-start(f32[64,256]{1,0:T(8,128)S(1)} %add_add_fusion.refs_0_), channel_id=1, source_target_pairs={{0,8},{8,0},{16,24},{24,16},{1,9},{9,1},{17,25},{25,17},{2,10},{10... | collective-permute-start | bytes 196616 | tf_op jit(solution)/shard_map/ppermute | solution.py:250
  19.0 0.5 %collective-permute-start.5 = (f32[64,256]{1,0:T(8,128)S(1)}, f32[64,256]{1,0:T(8,128)S(1)}, u32[]{:S(2)}, u32[]{:S(2)}) collective-permute-start(f32[64,256]{1,0:T(8,128)S(1)} %add_add_fusion.refs_0_), channel_id=1, source_target_pairs={{0,16},{8,24},{16,0},{24,8},{1,17},{9,25},{17,1},{25,9},{2,18},{10... | collective-permute-start | bytes 196616 | tf_op jit(solution)/shard_map/ppermute | solution.py:250
  19.5 0.6 %halves.3.refs_0_ = f32[336,544]{1,0:T(8,128)S(1)} custom-call(bf16[816,256]{1,0:T(8,128)(2,1)S(1)} %get-tuple-element.27.left_ref, bf16[816,256]{1,0:T(8,128)(2,1)S(1)} %get-tuple-element.28.right_ref, f32[64,256]{1,0:T(8,128)S(1)} %add_add_fusion.refs_0_), custom_call_target="tpu_custom_call" | custom-call | flops 307494912 | bytes 2000000 | tf_op jit(solution)/shard_map/halves/pallas_call | solution.py:304
  20.2 1.8 %collective-permute-done.4.refs_1_ = f32[64,256]{1,0:T(8,128)S(1)} collective-permute-done((f32[64,256]{1,0:T(8,128)S(1)}, f32[64,256]{1,0:T(8,128)S(1)}, u32[]{:S(2)}, u32[]{:S(2)}) %collective-permute-start.4) | collective-permute-done | bytes 65568 | tf_op jit(solution)/shard_map/ppermute | solution.py:250
  22.0 0.1 collective-permute-start.7
  22.1 0.7 %halves.4.refs_0_ = f32[336,544]{1,0:T(8,128)S(1)} custom-call(bf16[816,256]{1,0:T(8,128)(2,1)S(1)} %get-tuple-element.27.left_ref, bf16[816,256]{1,0:T(8,128)(2,1)S(1)} %get-tuple-element.28.right_ref, f32[336,544]{1,0:T(8,128)S(1)} %halves.3.refs_0_, f32[64,256]{1,0:T(8,128)S(1)} %collective-permute-done.4.refs_1_), custom_call_target="tpu_custom_call", output_to_operand_aliasing={{}: (2, {})} | custom-call | flops 307494912 | bytes 2000000 | tf_op jit(solution)/shard_map/halves/pallas_call | solution.py:304
  22.7 0.0 collective-permute-done.6
  22.8 0.5 %collective-permute-done.5 = f32[64,256]{1,0:T(8,128)S(1)} collective-permute-done((f32[64,256]{1,0:T(8,128)S(1)}, f32[64,256]{1,0:T(8,128)S(1)}, u32[]{:S(2)}, u32[]{:S(2)}) %collective-permute-start.5) | collective-permute-done | bytes 65568 | tf_op jit(solution)/shard_map/ppermute | solution.py:250
  23.3 0.1 collective-permute-start.8
  23.4 0.0 collective-permute-done.7.refs_1_.early_other_ref
  23.4 1.6 %halves.5.before_ref = f32[336,544]{1,0:T(8,128)S(1)} custom-call(bf16[816,256]{1,0:T(8,128)(2,1)S(1)} %get-tuple-element.27.left_ref, bf16[816,256]{1,0:T(8,128)(2,1)S(1)} %get-tuple-element.28.right_ref, f32[336,544]{1,0:T(8,128)S(1)} %halves.4.refs_0_, ...), custom_call_target="tpu_custom_call", output_to_operand_aliasing={{}: (2, {})} | custom-call | flops 1229979648 | bytes 2000000 | tf_op jit(solution)/shard_map/halves/pallas_call | solution.py:304
  25.0 0.0 collective-permute-done.8.late_other_ref
  25.0 1.9 %last_half.1 = (f32[64,512]{1,0:T(8,128)}, f32[64,512]{1,0:T(8,128)}, f32[268,536]{1,0:T(8,128)}, f32[64,536]{1,0:T(8,128)}) custom-call(bf16[816,256]{1,0:T(8,128)(2,1)S(1)} %get-tuple-element.27.left_ref, bf16[816,256]{1,0:T(8,128)(2,1)S(1)} %get-tuple-element.28.right_ref, f32[336,544]{1,0:T(8,128)S(1)} %halves.5.before_ref, ...), custom_call_target="tpu_custom_call" | custom-call | flops 614989824 | bytes 2000000 | tf_op jit(solution)/shard_map/last_half/pallas_call | solution.py:338
  (5 shorter events, 0.1 us)
Async XLA Ops:
  3.6 1.4 %collective-permute-start = (f32[64,256]{1,0:T(8,128)S(1)}, f32[64,256]{1,0:T(8,128)S(1)}, u32[]{:S(2)}, u32[]{:S(2)}) collective-permute-start(f32[64,256]{1,0:T(8,128)S(1)} %get-tuple-element.22), channel_id=1, source_target_pairs={{0,1},{1,0},{2,3},{3,2},{4,5},{5,4},{6,7},{7,6},{8,9},{9,8},{10,11... | collective-permute-start | bytes 196616 | tf_op jit(solution)/shard_map/ppermute | solution.py:250
  5.1 7.7 %collective-permute-start.3 = (f32[64,256]{1,0:T(8,128)S(1)}, f32[64,256]{1,0:T(8,128)S(1)}, u32[]{:S(2)}, u32[]{:S(2)}) collective-permute-start(f32[64,256]{1,0:T(8,128)S(1)} %add.15.after_ref), channel_id=1, source_target_pairs={{0,6},{1,7},{2,4},{3,5},{4,2},{5,3},{6,0},{7,1},{8,14},{9,15},{10,... | collective-permute-start | bytes 196616 | tf_op jit(solution)/shard_map/ppermute | solution.py:250
  10.1 5.9 %collective-permute-start.2 = (f32[64,256]{1,0:T(8,128)S(1)}, f32[64,256]{1,0:T(8,128)S(1)}, u32[]{:S(2)}, u32[]{:S(2)}) collective-permute-start(f32[64,256]{1,0:T(8,128)S(1)} %add.15.after_ref), channel_id=1, source_target_pairs={{0,4},{1,5},{2,6},{3,7},{4,0},{5,1},{6,2},{7,3},{8,12},{9,13},{10,... | collective-permute-start | bytes 196616 | tf_op jit(solution)/shard_map/ppermute | solution.py:250
  10.1 5.9 %collective-permute-start.1 = (f32[64,256]{1,0:T(8,128)S(1)}, f32[64,256]{1,0:T(8,128)S(1)}, u32[]{:S(2)}, u32[]{:S(2)}) collective-permute-start(f32[64,256]{1,0:T(8,128)S(1)} %add.15.after_ref), channel_id=1, source_target_pairs={{0,2},{1,3},{2,0},{3,1},{4,6},{5,7},{6,4},{7,5},{8,10},{9,11},{10,... | collective-permute-start | bytes 196616 | tf_op jit(solution)/shard_map/ppermute | solution.py:250
  16.0 6.0 %collective-permute-start.4 = (f32[64,256]{1,0:T(8,128)S(1)}, f32[64,256]{1,0:T(8,128)S(1)}, u32[]{:S(2)}, u32[]{:S(2)}) collective-permute-start(f32[64,256]{1,0:T(8,128)S(1)} %add_add_fusion.refs_0_), channel_id=1, source_target_pairs={{0,24},{8,16},{16,8},{24,0},{1,25},{9,17},{17,9},{25,1},{2,26},{10... | collective-permute-start | bytes 196616 | tf_op jit(solution)/shard_map/ppermute | solution.py:250
  18.5 4.3 %collective-permute-start.6 = (f32[64,256]{1,0:T(8,128)S(1)}, f32[64,256]{1,0:T(8,128)S(1)}, u32[]{:S(2)}, u32[]{:S(2)}) collective-permute-start(f32[64,256]{1,0:T(8,128)S(1)} %add_add_fusion.refs_0_), channel_id=1, source_target_pairs={{0,8},{8,0},{16,24},{24,16},{1,9},{9,1},{17,25},{25,17},{2,10},{10... | collective-permute-start | bytes 196616 | tf_op jit(solution)/shard_map/ppermute | solution.py:250
  19.0 4.3 %collective-permute-start.5 = (f32[64,256]{1,0:T(8,128)S(1)}, f32[64,256]{1,0:T(8,128)S(1)}, u32[]{:S(2)}, u32[]{:S(2)}) collective-permute-start(f32[64,256]{1,0:T(8,128)S(1)} %add_add_fusion.refs_0_), channel_id=1, source_target_pairs={{0,16},{8,24},{16,0},{24,8},{1,17},{9,25},{17,1},{25,9},{2,18},{10... | collective-permute-start | bytes 196616 | tf_op jit(solution)/shard_map/ppermute | solution.py:250
  22.0 1.4 %collective-permute-start.7 = (f32[2,64,256]{2,1,0:T(8,128)S(1)}, f32[2,64,256]{2,1,0:T(8,128)S(1)}, u32[]{:S(2)}, u32[]{:S(2)}) collective-permute-start(f32[2,64,256]{2,1,0:T(8,128)S(1)} %pad_maximum_fusion.early_ref), channel_id=1, source_target_pairs={{0,1},{1,0},{2,3},{3,2},{4,5},{5,4},{6,7},{7,6},{8,9},{9,8},{10,11... | collective-permute-start | bytes 393224 | tf_op jit(solution)/shard_map/ppermute | solution.py:250
  23.3 1.7 %collective-permute-start.8 = (f32[2,64,256]{2,1,0:T(8,128)S(1)}, f32[2,64,256]{2,1,0:T(8,128)S(1)}, u32[]{:S(2)}, u32[]{:S(2)}) collective-permute-start(f32[2,64,256]{2,1,0:T(8,128)S(1)} %pad_maximum_fusion.1.refs_2_.late_ref), channel_id=1, source_target_pairs={{0,1},{1,0},{2,3},{3,2},{4,5},{5,4},{6,7},{7,6},{8,9},{9,8},{10,11... | collective-permute-start | bytes 393224 | tf_op jit(solution)/shard_map/ppermute | solution.py:250

commit v5 on v4

--- a/solution.py
+++ b/solution.py
@@ -56,19 +56,14 @@
     return (first * second).astype(jnp.bfloat16)
 
 
-def project_kernel(basis_ref, snaps_ref, keep_ref, give_ref, basis, held, basis_sem, sems):
-    core = lax.axis_index("space") % 2
+def project_kernel(basis_ref, snaps_ref, out_ref, basis, held, basis_sem, sems):
     chunks, size, states = held.shape
-    half = chunks // 2 * size
     basis_copy = pltpu.make_async_copy(basis_ref, basis, basis_sem)
     basis_copy.start()
     copies = []
     for chunk in range(chunks):
-        side, at = divmod(chunk * size, half)
-        first = pl.multiple_of((core if side else 1 - core) * half + at, size)
-        copies.append(
-            pltpu.make_async_copy(snaps_ref.at[pl.ds(first, size)], held.at[chunk], sems.at[chunk])
-        )
+        rows = pl.ds(chunk * size, size)
+        copies.append(pltpu.make_async_copy(snaps_ref.at[rows], held.at[chunk], sems.at[chunk]))
         copies[-1].start()
     basis_copy.wait()
     pieces = 4
@@ -77,15 +72,14 @@
         copies[chunk].wait()
         terms = [
             lax.dot_general(
+                basis[:, piece * step : (piece + 1) * step],
                 held[chunk, :, piece * step : (piece + 1) * step],
-                basis[:, piece * step : (piece + 1) * step],
                 NT,
                 preferred_element_type=jnp.float32,
             )
             for piece in range(pieces)
         ]
-        side, at = divmod(chunk * size, half)
-        (keep_ref if side else give_ref)[:, at : at + size] = tree_sum(terms).T
+        out_ref[:, chunk * size : (chunk + 1) * size] = tree_sum(terms)
 
 
 def project(snapshots, basis):
@@ -93,13 +87,11 @@
     modes = basis.shape[0]
     size = 128
     hbm = pl.BlockSpec(memory_space=pltpu.HBM)
-    vmem = pl.BlockSpec(memory_space=pltpu.VMEM)
-    block = jax.ShapeDtypeStruct((modes, snaps // 2), jnp.float32)
     return pl.pallas_call(
         project_kernel,
-        out_shape=(block, block),
+        out_shape=jax.ShapeDtypeStruct((modes, snaps), jnp.float32),
         in_specs=[hbm, hbm],
-        out_specs=(vmem, vmem),
+        out_specs=pl.BlockSpec(memory_space=pltpu.VMEM),
         scratch_shapes=[
             pltpu.VMEM(basis.shape, basis.dtype),
             pltpu.VMEM((snaps // size, size, states), snapshots.dtype),
@@ -146,25 +138,17 @@
     )
 
 
-def joined(refs):
-    halves = []
-    for ref in refs:
-        halves.extend([ref[...]] if len(ref.shape) == 2 else [ref[slot] for slot in range(ref.shape[0])])
-    return jnp.concatenate(halves, axis=1)
-
-
-def halves_kernel(cols, has_before, left_ref, right_ref, *refs):
+def halves_kernel(cols, half, has_before, left_ref, right_ref, *refs):
     before_ref, refs = (refs[0], refs[1:]) if has_before else (None, refs)
     block_refs, acc_ref, col_scratch = refs[:-2], refs[-2], refs[-1]
-    block = joined(block_refs)
-    term = terms_of(left_ref, right_ref, block, block_refs[0].shape[-1], cols, col_scratch)
+    block = jnp.concatenate([ref[...] for ref in block_refs], axis=1)
+    term = terms_of(left_ref, right_ref, block, half, cols, col_scratch)
     acc_ref[...] = before_ref[...] + term if has_before else term
 
 
 def edge_columns(time_idx, core, halves, starts, ends):
     count, modes, width = starts.shape
-    for offset, side, load in halves:
-        block = load()
+    for offset, side, block in halves:
         at = 2 * (time_idx ^ offset) + side
         starts[at] = block[:, :width]
         ends[at] = block[:, block.shape[1] - width :]
@@ -185,17 +169,19 @@
     return jnp.where(inside, edge, 0.0), jnp.where(inside, rates, 0.0)
 
 
-def last_kernel(
-    row_block, col_block, chunks, offsets, left_ref, right_ref, before_ref, reg_ref, early_ref,
-    early_other_ref, late_ref, late_other_ref, reduced_ref, rates_ref, normal_ref, right_side_ref, starts,
-    ends, col_scratch, reduced_out, rates_out, normal_out, right_side_out, sems,
-):
+def last_kernel(row_block, col_block, chunks, shares, left_ref, right_ref, before_ref, reg_ref, *refs):
+    peers = shares.each
+    own_ref = refs[0]
+    got_refs, passed_refs = refs[1 : 1 + peers], refs[1 + peers : 1 + 2 * peers]
+    got_half_ref, passed_half_ref = refs[1 + 2 * peers : 3 + 2 * peers]
+    reduced_ref, rates_ref, normal_ref, right_side_ref = refs[3 + 2 * peers : 7 + 2 * peers]
+    starts, ends, col_scratch, rates_out, normal_out, right_side_out, sems = refs[7 + 2 * peers :]
     time_idx = lax.axis_index("tm")
     space_idx = lax.axis_index("space")
     core = space_idx % 2
-    early, modes, half = early_ref.shape
-    groups = early + late_ref.shape[0]
-    snaps = 2 * half
+    modes, snaps = own_ref.shape
+    half = snaps // 2
+    groups = shares.count
     cols = round_up(col_block, 16)
     depth = left_ref.shape[1]
     copies = []
@@ -204,16 +190,17 @@
         copies.append(pltpu.make_async_copy(source, target, sems.at[len(copies)]))
         copies[-1].start()
 
-    reduced_out[:, pl.ds(pl.multiple_of(core * half, half), half)] = early_ref[0]
-    reduced_out[:, pl.ds(pl.multiple_of((1 - core) * half, half), half)] = early_other_ref[0]
-    send(reduced_out, reduced_ref)
-    halves = []
-    for slot, offset in enumerate(offsets):
-        for side, pair in ((core, (early_ref, late_ref)), (1 - core, (early_other_ref, late_other_ref))):
-            ref, at = (pair[0], slot) if slot < early else (pair[1], slot - early)
-            halves.append((offset, side, functools.partial(lambda ref, at: ref[at], ref, at)))
+    send(own_ref, reduced_ref)
+    wholes = [(0, own_ref)]
+    for step in range(peers):
+        first, second = shares.pair(step)
+        wholes.append((jnp.where(core == 0, first, second), got_refs[step]))
+        wholes.append((jnp.where(core == 0, second, first), passed_refs[step]))
+    halves = [(shares.last, core, got_half_ref[...]), (shares.last, 1 - core, passed_half_ref[...])]
+    for offset, ref in wholes:
+        halves += [(offset, side, ref[:, side * half : (side + 1) * half]) for side in range(2)]
     edge, edge_rates = edge_columns(time_idx, core, halves, starts, ends)
-    own = reduced_out[...]
+    own = own_ref[...]
     width = edge.shape[1]
     own_edges = pltpu.roll(edge_rates, lax.rem(width - 4 * time_idx, width), 1)
     lane = lax.broadcasted_iota(jnp.int32, (1, snaps), 1)
@@ -221,7 +208,7 @@
     rates_out[...] = jnp.where(lane == snaps - 1, own_edges[:, 3:4], rates)
     send(rates_out, rates_ref)
 
-    block = joined([late_other_ref])
+    block = passed_half_ref[...]
     parts = parts_of(block, depth)
     column_side(left_ref, right_ref, parts, inner_rates(block, half), cols, col_scratch)
     scale = 1.0 / (groups * snaps)
@@ -246,8 +233,39 @@
         copy.wait()
 
 
-def swapped(value, axis, distance):
-    return lax.ppermute(value, axis, [(i, i ^ distance) for i in range(lax.axis_size(axis))])
+class Shares:
+    def __init__(self, count):
+        self.count = count
+        self.each = (count - 2) // 2
+        self.last = count - 1
+
+    def pair(self, step):
+        return 1 + step, 1 + self.each + step
+
+
+def swapped(value):
+    return lax.ppermute(value, "space", [(i, i ^ 1) for i in range(lax.axis_size("space"))])
+
+
+def exchanged(value, axis, distances):
+    space_count = lax.axis_size("space")
+    perm = []
+    for time in range(lax.axis_size("tm")):
+        for space in range(space_count):
+            distance = distances[space % 2]
+            if axis == "tm":
+                target = (time ^ distance) * space_count + space
+            else:
+                target = time * space_count + (space ^ (2 * distance))
+            perm.append((time * space_count + space, target))
+    return lax.ppermute(value, ("tm", "space"), perm)
+
+
+def from_partners(value, axis, shares, core):
+    half = value.shape[1] // 2
+    wholes = [exchanged(value, axis, shares.pair(step)) for step in range(shares.each)]
+    part = jnp.where(core == 0, value[:, :half], value[:, half:])
+    return wholes, exchanged(part, axis, (shares.last, shares.last))
 
 
 def local(snapshots, modes_basis, reg_weights):
@@ -266,9 +284,10 @@
     hbm = pl.BlockSpec(memory_space=pltpu.HBM)
     params = pltpu.CompilerParams(vmem_limit_bytes=32 * 1024 * 1024)
 
-    keep, give = project(snapshots, modes_basis.T)
-    half = keep + swapped(give, "space", 1)
-    after, half = lax.optimization_barrier((time_idx, half))
+    core = lax.axis_index("space") % 2
+    chip = project(snapshots, modes_basis.T)
+    chip = chip + swapped(chip)
+    after, chip = lax.optimization_barrier((time_idx, chip))
     selector = jax.ShapeDtypeStruct((cols + rows, depth), jnp.bfloat16)
     left, right = pl.pallas_call(
         functools.partial(selector_kernel, row_block, col_block),
@@ -278,19 +297,27 @@
         compiler_params=params,
         cost_estimate=pl.CostEstimate(flops=10**6, bytes_accessed=10**6, transcendentals=0),
         name="selectors",
-    )(half)
+    )(chip)
     first_row = after * row_block
     reg_rows = lax.dynamic_slice_in_dim(reg_weights, first_row, row_block, 0)[None]
 
-    terms = [half] + [swapped(half, "space", step) for step in range(2, space_count, 2)]
-    while len(terms) > 1:
-        terms = [terms[i] + terms[i + 1] for i in range(0, len(terms), 2)]
-    mine, left, right, reg_rows = lax.optimization_barrier((terms[0], left, right, reg_rows))
-    arriving = [(step, swapped(mine, "tm", step)) for step in range(tm_count - 1, 0, -1)]
+    shares = Shares(space_count // 2)
+    wholes, part = from_partners(chip, "space", shares, core)
+    sent = jnp.concatenate(wholes + [part], axis=1)
+    other = swapped(sent)
+    low, high = [], []
+    for step, whole in enumerate(wholes):
+        passed = other[:, step * snaps_dev : (step + 1) * snaps_dev]
+        low.append(jnp.where(core == 0, whole, passed))
+        high.append(jnp.where(core == 0, passed, whole))
+    passed = other[:, shares.each * snaps_dev :]
+    last = [jnp.where(core == 0, part, passed), jnp.where(core == 0, passed, part)]
+    own = tree_sum([chip] + low + high + [jnp.concatenate(last, axis=1)])
+    own, left, right, reg_rows = lax.optimization_barrier((own, left, right, reg_rows))
     acc_shape = jax.ShapeDtypeStruct((cols + modes, rows), jnp.float32)
 
     def cost(count):
-        flops = 2 * count * (2 * depth * (cols + rows) + (cols + modes) * rows)
+        flops = 8 * count * (2 * depth * (cols + rows) + (cols + modes) * rows)
         return pl.CostEstimate(flops=flops, bytes_accessed=2 * 10**6, transcendentals=0)
 
     def col_scratch(count):
@@ -299,10 +326,10 @@
     half_snaps = snaps_dev // 2
 
     def add_terms(acc, blocks):
-        count = sum(block.size for block in blocks) // modes
+        count = sum(block.shape[1] for block in blocks)
         before = [] if acc is None else [acc]
         return pl.pallas_call(
-            functools.partial(halves_kernel, cols, len(before)),
+            functools.partial(halves_kernel, cols, half_snaps, len(before)),
             out_shape=acc_shape,
             in_specs=[vmem] * (2 + len(before) + len(blocks)),
             out_specs=vmem,
@@ -313,17 +340,14 @@
             name="halves",
         )(left, right, *before, *blocks)
 
-    offsets = [0] + [offset for offset, _ in arriving]
-    early = [mine, arriving[0][1]]
-    late = [got for _, got in arriving[1:]]
-    acc = add_terms(None, [mine])
-    early_stack = jnp.stack(early)
-    early_other = swapped(early_stack, "space", 1)
-    acc = add_terms(acc, early[1:])
-    acc, *late = lax.optimization_barrier((acc, *late))
-    late_stack = jnp.stack(late)
-    late_other = swapped(late_stack, "space", 1)
-    acc = add_terms(acc, [early_other, late_stack])
+    shares = Shares(tm_count)
+    got, got_half = from_partners(own, "tm", shares, core)
+    acc = add_terms(None, [own])
+    passed = [swapped(block) for block in got]
+    acc = add_terms(acc, got)
+    acc, got_half = lax.optimization_barrier((acc, got_half))
+    passed_half = swapped(got_half)
+    acc = add_terms(acc, passed + [got_half])
     width = 128
     starts = list(range(0, row_block - width, 2 * width))
     starts = [0] + [start - width for start in starts[1:]] if len(starts) > 1 else [0]
@@ -336,21 +360,21 @@
         jax.ShapeDtypeStruct((modes, row_block), jnp.float32),
     )
     outs = pl.pallas_call(
-        functools.partial(last_kernel, row_block, col_block, chunks, offsets),
+        functools.partial(last_kernel, row_block, col_block, chunks, shares),
         out_shape=out_shapes,
-        in_specs=[vmem] * 8,
+        in_specs=[vmem] * (7 + 2 * shares.each),
         out_specs=(hbm,) * 4,
         scratch_shapes=[
             pltpu.VMEM((2 * tm_count, modes, width), jnp.float32),
             pltpu.VMEM((2 * tm_count, modes, width), jnp.float32),
-            col_scratch(len(late) * half_snaps),
-            *[pltpu.VMEM(shape.shape, shape.dtype) for shape in out_shapes],
+            col_scratch(half_snaps),
+            *[pltpu.VMEM(shape.shape, shape.dtype) for shape in out_shapes[1:]],
             pltpu.SemaphoreType.DMA((2 + 2 * len(chunks),)),
         ],
         compiler_params=params,
-        cost_estimate=cost(len(late) * half_snaps),
+        cost_estimate=cost(half_snaps),
         name="last_half",
-    )(left, right, acc, reg_rows, early_stack, early_other, late_stack, late_other)
+    )(left, right, acc, reg_rows, own, *got, *passed, got_half, passed_half)
     return tuple(out.T for out in outs)
 
 

time: 27.2 us -> 27.8 us (1.022)
  waiting for transfers between devices: 7.13 us -> 8.16 us
  starting transfers between devices: 9.87 us -> 9.18 us
    ppermute x9 -> x8, waiting for transfers between devices: 7.13 us -> 8.16 us  [the longest x4 7.13 us: exchanged(): return lax.ppermute(value, ('tm', 'space'), perm)]
    ppermute x9 -> x8, starting transfers between devices: 9.87 us -> 9.18 us  [the longest x4 8.59 us: exchanged(): return lax.ppermute(value, ('tm', 'space'), perm)]
    pallas_call x4, Pallas kernels: 5.91 us -> 6.34 us  [the longest x3 3.26 us: add_terms(): pl.pallas_call(functools.partial(halves_kernel, cols, half_snaps, len(bef...]
  transfers between devices with their start and end apart: 9 -> 8, of which waited for: 5 -> 4; matrix products, arithmetic and copies ran while one was open for 3% -> 3% of each run, Pallas kernels for 13% -> 14%
where the time goes in v5:
time: 27.8 us; the launch traced here: 27.6 us
  starting transfers between devices  9.18 us (33%)
  Pallas kernels  8.61 us (31%)
  waiting for transfers between devices  8.16 us (29%)
  local copies, waits for them, and re-layouts  0.78 us (3%)
  between operations  0.72 us (3%)
    ppermute x4, starting transfers between devices, exchanged(): return lax.ppermute(value, ('tm', 'space'), perm)  8.59 us
    ppermute x4, waiting for transfers between devices, exchanged(): return lax.ppermute(value, ('tm', 'space'), perm)  7.13 us
    pallas_call x3, Pallas kernels, add_terms(): pl.pallas_call(functools.partial(halves_kernel, cols, half_snaps, len(bef...  3.26 us
    pallas_call x1, Pallas kernels, project(): pl.pallas_call(project_kernel, out_shape=jax.ShapeDtypeStruct((modes, sna...  3.08 us
    pallas_call x1, Pallas kernels, local(): pl.pallas_call(functools.partial(last_kernel, row_block, col_block, chunk...  1.67 us
    ppermute x4, waiting for transfers between devices, swapped(): lax.ppermute(value, 'space', [(i, i ^ 1) for i in range(lax.axis_size('sp...  1.03 us
    dynamic_slice x1, local copies, waits for them, and re-layouts, local(): lax.dynamic_slice_in_dim(reg_weights, first_row, row_block, 0)[None]  0.78 us
    pallas_call x1, Pallas kernels, local(): pl.pallas_call(functools.partial(selector_kernel, row_block, col_block),...  0.6 us
  transfers between devices with their start and end apart: 8, of which 4 were waited for; matrix products, arithmetic and copies ran while one was open for 3% of the time, Pallas kernels for 14%

profile of v5, /device:TPU:0, one launch (start us, length us, event | category | flops | bytes accessed | tf_op | source)
XLA Modules:
  0.0 27.6 jit_solution(16618569147614065253)
XLA Ops:
  0.6 3.1 %project.1 = f32[64,512]{1,0:T(8,128)S(1)} custom-call(bf16[64,2048]{1,0:T(8,128)(2,1)} %bitcast.5, bf16[512,2048]{1,0:T(8,128)(2,1)} %snaps_ref.1), custom_call_target="tpu_custom_call" | custom-call | tf_op jit(solution)/shard_map/project/pallas_call | solution.py:90
  3.7 0.5 %collective-permute-start = (f32[64,512]{1,0:T(8,128)S(1)}, f32[64,512]{1,0:T(8,128)S(1)}, u32[]{:S(2)}, u32[]{:S(2)}) collective-permute-start(f32[64,512]{1,0:T(8,128)S(1)} %project.1), channel_id=1, source_target_pairs={{0,1},{1,0},{2,3},{3,2},{4,5},{5,4},{6,7},{7,6},{8,9},{9,8},{10,11... | collective-permute-start | bytes 393224 | tf_op jit(solution)/shard_map/ppermute | solution.py:247
  4.2 1.0 %collective-permute-done = f32[64,512]{1,0:T(8,128)S(1)} collective-permute-done((f32[64,512]{1,0:T(8,128)S(1)}, f32[64,512]{1,0:T(8,128)S(1)}, u32[]{:S(2)}, u32[]{:S(2)}) %collective-permute-start) | collective-permute-done | bytes 131104 | tf_op jit(solution)/shard_map/ppermute | solution.py:247
  5.2 3.0 %collective-permute-start.1 = (f32[64,512]{1,0:T(8,128)S(1)}, f32[64,512]{1,0:T(8,128)S(1)}, u32[]{:S(2)}, u32[]{:S(2)}) collective-permute-start(f32[64,512]{1,0:T(8,128)S(1)} %add.19.after_ref), channel_id=1, source_target_pairs={{0,2},{1,5},{2,0},{3,7},{4,6},{5,1},{6,4},{7,3},{8,10},{9,13},{10,... | collective-permute-start | bytes 393224 | tf_op jit(solution)/shard_map/ppermute | solution.py:261
  8.3 2.5 %collective-permute-start.2 = (f32[64,256]{1,0:T(8,128)S(1)}, f32[64,256]{1,0:T(8,128)S(1)}, u32[]{:S(2)}, u32[]{:S(2)}) collective-permute-start(f32[64,256]{1,0:T(8,128)S(1)} %slice_select_fusion.1), channel_id=1, source_target_pairs={{0,6},{1,7},{2,4},{3,5},{4,2},{5,3},{6,0},{7,1},{8,14},{9,15},{10,... | collective-permute-start | bytes 196616 | tf_op jit(solution)/shard_map/ppermute | solution.py:261
  10.8 4.8 %collective-permute-done.2 = f32[64,256]{1,0:T(8,128)S(1)} collective-permute-done((f32[64,256]{1,0:T(8,128)S(1)}, f32[64,256]{1,0:T(8,128)S(1)}, u32[]{:S(2)}, u32[]{:S(2)}) %collective-permute-start.2) | collective-permute-done | bytes 65568 | tf_op jit(solution)/shard_map/ppermute | solution.py:261
  15.6 0.0 collective-permute-done.1
  15.6 0.1 collective-permute-start.3
  15.7 0.8 %dynamic_slice.3 = f32[536]{0:T(1024)S(1)} dynamic-slice(f32[2144]{0:T(1024)} %param.5, s32[]{:T(128)S(6)} %select_n.50), dynamic_slice_sizes={536} | dynamic-slice | bytes 4292 | tf_op jit(solution)/shard_map/dynamic_slice | solution.py:302
  16.5 0.6 %selectors.1 = (bf16[816,256]{1,0:T(8,128)(2,1)S(1)}, bf16[816,256]{1,0:T(8,128)(2,1)S(1)}) custom-call(f32[64,512]{1,0:T(8,128)S(1)} %add.19.after_ref), custom_call_target="tpu_custom_call" | custom-call | flops 1000000 | bytes 1000000 | tf_op jit(solution)/shard_map/selectors/pallas_call | solution.py:292
  17.1 0.0 collective-permute-done.3
  17.2 1.6 %collective-permute-start.4 = (f32[64,512]{1,0:T(8,128)S(1)}, f32[64,512]{1,0:T(8,128)S(1)}, u32[]{:S(2)}, u32[]{:S(2)}) collective-permute-start(f32[64,512]{1,0:T(8,128)S(1)} %fusion.refs_0_), channel_id=1, source_target_pairs={{0,8},{1,17},{2,10},{3,19},{4,12},{5,21},{6,14},{7,23},{8,0},{9,25... | collective-permute-start | bytes 393224 | tf_op jit(solution)/shard_map/ppermute | solution.py:261
  18.8 1.5 %collective-permute-start.5 = (f32[64,256]{1,0:T(8,128)S(1)}, f32[64,256]{1,0:T(8,128)S(1)}, u32[]{:S(2)}, u32[]{:S(2)}) collective-permute-start(f32[64,256]{1,0:T(8,128)S(1)} %slice_select_fusion), channel_id=1, source_target_pairs={{0,24},{1,25},{2,26},{3,27},{4,28},{5,29},{6,30},{7,31},{8,16},{9,... | collective-permute-start | bytes 196616 | tf_op jit(solution)/shard_map/ppermute | solution.py:261
  20.3 1.0 %halves.3.refs_0_ = f32[336,544]{1,0:T(8,128)S(1)} custom-call(bf16[816,256]{1,0:T(8,128)(2,1)S(1)} %get-tuple-element.22.left_ref, bf16[816,256]{1,0:T(8,128)(2,1)S(1)} %get-tuple-element.23.right_ref, f32[64,512]{1,0:T(8,128)S(1)} %fusion.refs_0_), custom_call_target="tpu_custom_call" | custom-call | flops 2459959296 | bytes 2000000 | tf_op jit(solution)/shard_map/halves/pallas_call | solution.py:331
  21.3 1.7 %collective-permute-done.4.refs_1_ = f32[64,512]{1,0:T(8,128)S(1)} collective-permute-done((f32[64,512]{1,0:T(8,128)S(1)}, f32[64,512]{1,0:T(8,128)S(1)}, u32[]{:S(2)}, u32[]{:S(2)}) %collective-permute-start.4) | collective-permute-done | bytes 131104 | tf_op jit(solution)/shard_map/ppermute | solution.py:261
  22.9 0.0 collective-permute-start.6
  22.9 1.0 %halves.4.refs_0_ = f32[336,544]{1,0:T(8,128)S(1)} custom-call(bf16[816,256]{1,0:T(8,128)(2,1)S(1)} %get-tuple-element.22.left_ref, bf16[816,256]{1,0:T(8,128)(2,1)S(1)} %get-tuple-element.23.right_ref, f32[336,544]{1,0:T(8,128)S(1)} %halves.3.refs_0_, f32[64,512]{1,0:T(8,128)S(1)} %collective-permute-done.4.refs_1_), custom_call_target="tpu_custom_call", output_to_operand_aliasing={{}: (2, {})} | custom-call | flops 2459959296 | bytes 2000000 | tf_op jit(solution)/shard_map/halves/pallas_call | solution.py:331
  23.9 0.7 %collective-permute-done.5.refs_2_.refs_3_ = f32[64,256]{1,0:T(8,128)S(1)} collective-permute-done((f32[64,256]{1,0:T(8,128)S(1)}, f32[64,256]{1,0:T(8,128)S(1)}, u32[]{:S(2)}, u32[]{:S(2)}) %collective-permute-start.5) | collective-permute-done | bytes 65568 | tf_op jit(solution)/shard_map/ppermute | solution.py:261
  24.6 0.0 collective-permute-start.7
  24.6 0.0 collective-permute-done.6.refs_1_.refs_2_
  24.6 1.3 %halves.5.before_ref = f32[336,544]{1,0:T(8,128)S(1)} custom-call(bf16[816,256]{1,0:T(8,128)(2,1)S(1)} %get-tuple-element.22.left_ref, bf16[816,256]{1,0:T(8,128)(2,1)S(1)} %get-tuple-element.23.right_ref, f32[336,544]{1,0:T(8,128)S(1)} %halves.4.refs_0_, f32[64,512]{1,0:T(8,128)S(1)} %collective-permute-done.6.refs_1_.refs_2_, ...), custom_call_target="tpu_custom_call", output_to_operand_aliasing={{}: (2, {})} | custom-call | flops 3689938944 | bytes 2000000 | tf_op jit(solution)/shard_map/halves/pallas_call | solution.py:331
  25.9 0.0 collective-permute-done.7.refs_4_
  25.9 1.7 %last_half.1 = (f32[64,512]{1,0:T(8,128)}, f32[64,512]{1,0:T(8,128)}, f32[268,536]{1,0:T(8,128)}, f32[64,536]{1,0:T(8,128)}) custom-call(bf16[816,256]{1,0:T(8,128)(2,1)S(1)} %get-tuple-element.22.left_ref, bf16[816,256]{1,0:T(8,128)(2,1)S(1)} %get-tuple-element.23.right_ref, f32[336,544]{1,0:T(8,128)S(1)} %halves.5.before_ref, ...), custom_call_target="tpu_custom_call" | custom-call | flops 1229979648 | bytes 2000000 | tf_op jit(solution)/shard_map/last_half/pallas_call | solution.py:362
  (7 shorter events, 0.1 us)
Async XLA Ops:
  3.7 1.5 %collective-permute-start = (f32[64,512]{1,0:T(8,128)S(1)}, f32[64,512]{1,0:T(8,128)S(1)}, u32[]{:S(2)}, u32[]{:S(2)}) collective-permute-start(f32[64,512]{1,0:T(8,128)S(1)} %project.1), channel_id=1, source_target_pairs={{0,1},{1,0},{2,3},{3,2},{4,5},{5,4},{6,7},{7,6},{8,9},{9,8},{10,11... | collective-permute-start | bytes 393224 | tf_op jit(solution)/shard_map/ppermute | solution.py:247
  5.2 10.4 %collective-permute-start.1 = (f32[64,512]{1,0:T(8,128)S(1)}, f32[64,512]{1,0:T(8,128)S(1)}, u32[]{:S(2)}, u32[]{:S(2)}) collective-permute-start(f32[64,512]{1,0:T(8,128)S(1)} %add.19.after_ref), channel_id=1, source_target_pairs={{0,2},{1,5},{2,0},{3,7},{4,6},{5,1},{6,4},{7,3},{8,10},{9,13},{10,... | collective-permute-start | bytes 393224 | tf_op jit(solution)/shard_map/ppermute | solution.py:261
  8.3 7.3 %collective-permute-start.2 = (f32[64,256]{1,0:T(8,128)S(1)}, f32[64,256]{1,0:T(8,128)S(1)}, u32[]{:S(2)}, u32[]{:S(2)}) collective-permute-start(f32[64,256]{1,0:T(8,128)S(1)} %slice_select_fusion.1), channel_id=1, source_target_pairs={{0,6},{1,7},{2,4},{3,5},{4,2},{5,3},{6,0},{7,1},{8,14},{9,15},{10,... | collective-permute-start | bytes 196616 | tf_op jit(solution)/shard_map/ppermute | solution.py:261
  15.6 1.5 %collective-permute-start.3 = (f32[64,768]{1,0:T(8,128)S(1)}, f32[64,768]{1,0:T(8,128)S(1)}, u32[]{:S(2)}, u32[]{:S(2)}) collective-permute-start(f32[64,768]{1,0:T(8,128)S(1)} %pad_maximum_fusion), channel_id=1, source_target_pairs={{0,1},{1,0},{2,3},{3,2},{4,5},{5,4},{6,7},{7,6},{8,9},{9,8},{10,11... | collective-permute-start | bytes 589832 | tf_op jit(solution)/shard_map/ppermute | solution.py:247
  17.2 5.7 %collective-permute-start.4 = (f32[64,512]{1,0:T(8,128)S(1)}, f32[64,512]{1,0:T(8,128)S(1)}, u32[]{:S(2)}, u32[]{:S(2)}) collective-permute-start(f32[64,512]{1,0:T(8,128)S(1)} %fusion.refs_0_), channel_id=1, source_target_pairs={{0,8},{1,17},{2,10},{3,19},{4,12},{5,21},{6,14},{7,23},{8,0},{9,25... | collective-permute-start | bytes 393224 | tf_op jit(solution)/shard_map/ppermute | solution.py:261
  18.8 5.8 %collective-permute-start.5 = (f32[64,256]{1,0:T(8,128)S(1)}, f32[64,256]{1,0:T(8,128)S(1)}, u32[]{:S(2)}, u32[]{:S(2)}) collective-permute-start(f32[64,256]{1,0:T(8,128)S(1)} %slice_select_fusion), channel_id=1, source_target_pairs={{0,24},{1,25},{2,26},{3,27},{4,28},{5,29},{6,30},{7,31},{8,16},{9,... | collective-permute-start | bytes 196616 | tf_op jit(solution)/shard_map/ppermute | solution.py:261
  22.9 1.7 %collective-permute-start.6 = (f32[64,512]{1,0:T(8,128)S(1)}, f32[64,512]{1,0:T(8,128)S(1)}, u32[]{:S(2)}, u32[]{:S(2)}) collective-permute-start(f32[64,512]{1,0:T(8,128)S(1)} %collective-permute-done.4.refs_1_), channel_id=1, source_target_pairs={{0,1},{1,0},{2,3},{3,2},{4,5},{5,4},{6,7},{7,6},{8,9},{9,8},{10,11... | collective-permute-start | bytes 393224 | tf_op jit(solution)/shard_map/ppermute | solution.py:247
  24.6 1.3 %collective-permute-start.7 = (f32[64,256]{1,0:T(8,128)S(1)}, f32[64,256]{1,0:T(8,128)S(1)}, u32[]{:S(2)}, u32[]{:S(2)}) collective-permute-start(f32[64,256]{1,0:T(8,128)S(1)} %collective-permute-done.5.refs_2_.refs_3_), channel_id=1, source_target_pairs={{0,1},{1,0},{2,3},{3,2},{4,5},{5,4},{6,7},{7,6},{8,9},{9,8},{10,11... | collective-permute-start | bytes 196616 | tf_op jit(solution)/shard_map/ppermute | solution.py:247

commit v6 on v4

--- a/solution.py
+++ b/solution.py
@@ -77,15 +77,15 @@
         copies[chunk].wait()
         terms = [
             lax.dot_general(
+                basis[:, piece * step : (piece + 1) * step],
                 held[chunk, :, piece * step : (piece + 1) * step],
-                basis[:, piece * step : (piece + 1) * step],
                 NT,
                 preferred_element_type=jnp.float32,
             )
             for piece in range(pieces)
         ]
         side, at = divmod(chunk * size, half)
-        (keep_ref if side else give_ref)[:, at : at + size] = tree_sum(terms).T
+        (keep_ref if side else give_ref)[:, at : at + size] = tree_sum(terms)
 
 
 def project(snapshots, basis):
@@ -286,7 +286,7 @@
     while len(terms) > 1:
         terms = [terms[i] + terms[i + 1] for i in range(0, len(terms), 2)]
     mine, left, right, reg_rows = lax.optimization_barrier((terms[0], left, right, reg_rows))
-    arriving = [(step, swapped(mine, "tm", step)) for step in range(tm_count - 1, 0, -1)]
+    arriving = [(step, swapped(mine, "tm", step)) for step in [1, *range(tm_count - 1, 1, -1)]]
     acc_shape = jax.ShapeDtypeStruct((cols + modes, rows), jnp.float32)
 
     def cost(count):

time: 27.2 us -> 28 us (1.029)
  waiting for transfers between devices: 7.13 us -> 8.06 us
    ppermute x9, waiting for transfers between devices: 7.13 us -> 8.06 us  [swapped(): lax.ppermute(value, axis, [(i, i ^ distance) for i in range(lax.axis_size...]
  transfers between devices with their start and end apart: 9 -> 9, of which waited for: 5 -> 6; matrix products, arithmetic and copies ran while one was open for 3% -> 3% of each run, Pallas kernels for 13% -> 13%
where the time goes in v6:
time: 28 us; the launch traced here: 27.7 us
  starting transfers between devices  9.87 us (35%)
  Pallas kernels  8.25 us (29%)
  waiting for transfers between devices  8.06 us (29%)
  local copies, waits for them, and re-layouts  0.78 us (3%)
  between operations  0.71 us (3%)
    ppermute x9, starting transfers between devices, swapped(): lax.ppermute(value, axis, [(i, i ^ distance) for i in range(lax.axis_size...  9.87 us
    ppermute x9, waiting for transfers between devices, swapped(): lax.ppermute(value, axis, [(i, i ^ distance) for i in range(lax.axis_size...  8.06 us
    pallas_call x3, Pallas kernels, add_terms(): pl.pallas_call(functools.partial(halves_kernel, cols, len(before)), out_s...  2.92 us
    pallas_call x1, Pallas kernels, project(): pl.pallas_call(project_kernel, out_shape=(block, block), in_specs=[hbm, h...  2.79 us
    pallas_call x1, Pallas kernels, local(): pl.pallas_call(functools.partial(last_kernel, row_block, col_block, chunk...  1.94 us
    dynamic_slice x1, local copies, waits for them, and re-layouts, local(): lax.dynamic_slice_in_dim(reg_weights, first_row, row_block, 0)[None]  0.77 us
    pallas_call x1, Pallas kernels, local(): pl.pallas_call(functools.partial(selector_kernel, row_block, col_block),...  0.6 us
  transfers between devices with their start and end apart: 9, of which 6 were waited for; matrix products, arithmetic and copies ran while one was open for 3% of the time, Pallas kernels for 13%

profile of v6, /device:TPU:0, one launch (start us, length us, event | category | flops | bytes accessed | tf_op | source)
XLA Modules:
  0.0 27.7 jit_solution(14734130367886343860)
XLA Ops:
  0.6 2.8 %project.1 = (f32[64,256]{1,0:T(8,128)S(1)}, f32[64,256]{1,0:T(8,128)S(1)}) custom-call(bf16[64,2048]{1,0:T(8,128)(2,1)} %bitcast.11, bf16[512,2048]{1,0:T(8,128)(2,1)} %snaps_ref.1), custom_call_target="tpu_custom_call" | custom-call | tf_op jit(solution)/shard_map/project/pallas_call | solution.py:98
  3.4 0.5 %collective-permute-start = (f32[64,256]{1,0:T(8,128)S(1)}, f32[64,256]{1,0:T(8,128)S(1)}, u32[]{:S(2)}, u32[]{:S(2)}) collective-permute-start(f32[64,256]{1,0:T(8,128)S(1)} %get-tuple-element.22), channel_id=1, source_target_pairs={{0,1},{1,0},{2,3},{3,2},{4,5},{5,4},{6,7},{7,6},{8,9},{9,8},{10,11... | collective-permute-start | bytes 196616 | tf_op jit(solution)/shard_map/ppermute | solution.py:250
  3.9 0.9 %collective-permute-done = f32[64,256]{1,0:T(8,128)S(1)} collective-permute-done((f32[64,256]{1,0:T(8,128)S(1)}, f32[64,256]{1,0:T(8,128)S(1)}, u32[]{:S(2)}, u32[]{:S(2)}) %collective-permute-start) | collective-permute-done | bytes 65568 | tf_op jit(solution)/shard_map/ppermute | solution.py:250
  4.9 5.0 %collective-permute-start.3 = (f32[64,256]{1,0:T(8,128)S(1)}, f32[64,256]{1,0:T(8,128)S(1)}, u32[]{:S(2)}, u32[]{:S(2)}) collective-permute-start(f32[64,256]{1,0:T(8,128)S(1)} %add.15.after_ref), channel_id=1, source_target_pairs={{0,6},{1,7},{2,4},{3,5},{4,2},{5,3},{6,0},{7,1},{8,14},{9,15},{10,... | collective-permute-start | bytes 196616 | tf_op jit(solution)/shard_map/ppermute | solution.py:250
  9.9 0.0 collective-permute-start.2
  9.9 0.6 %collective-permute-start.1 = (f32[64,256]{1,0:T(8,128)S(1)}, f32[64,256]{1,0:T(8,128)S(1)}, u32[]{:S(2)}, u32[]{:S(2)}) collective-permute-start(f32[64,256]{1,0:T(8,128)S(1)} %add.15.after_ref), channel_id=1, source_target_pairs={{0,2},{1,3},{2,0},{3,1},{4,6},{5,7},{6,4},{7,5},{8,10},{9,11},{10,... | collective-permute-start | bytes 196616 | tf_op jit(solution)/shard_map/ppermute | solution.py:250
  10.5 0.8 %dynamic_slice.3 = f32[536]{0:T(1024)S(1)} dynamic-slice(f32[2144]{0:T(1024)} %param.5, s32[]{:T(128)S(6)} %select_n.3), dynamic_slice_sizes={536} | dynamic-slice | bytes 4292 | tf_op jit(solution)/shard_map/dynamic_slice | solution.py:283
  11.3 0.6 %selectors.1 = (bf16[816,256]{1,0:T(8,128)(2,1)S(1)}, bf16[816,256]{1,0:T(8,128)(2,1)S(1)}) custom-call(f32[64,256]{1,0:T(8,128)S(1)} %add.15.after_ref), custom_call_target="tpu_custom_call" | custom-call | flops 1000000 | bytes 1000000 | tf_op jit(solution)/shard_map/selectors/pallas_call | solution.py:273
  11.9 0.6 %collective-permute-done.3 = f32[64,256]{1,0:T(8,128)S(1)} collective-permute-done((f32[64,256]{1,0:T(8,128)S(1)}, f32[64,256]{1,0:T(8,128)S(1)}, u32[]{:S(2)}, u32[]{:S(2)}) %collective-permute-start.3) | collective-permute-done | bytes 65568 | tf_op jit(solution)/shard_map/ppermute | solution.py:250
  12.5 3.2 %collective-permute-done.2 = f32[64,256]{1,0:T(8,128)S(1)} collective-permute-done((f32[64,256]{1,0:T(8,128)S(1)}, f32[64,256]{1,0:T(8,128)S(1)}, u32[]{:S(2)}, u32[]{:S(2)}) %collective-permute-start.2) | collective-permute-done | bytes 65568 | tf_op jit(solution)/shard_map/ppermute | solution.py:250
  15.8 0.0 collective-permute-done.1
  15.8 1.6 %collective-permute-start.4 = (f32[64,256]{1,0:T(8,128)S(1)}, f32[64,256]{1,0:T(8,128)S(1)}, u32[]{:S(2)}, u32[]{:S(2)}) collective-permute-start(f32[64,256]{1,0:T(8,128)S(1)} %add_add_fusion.refs_0_), channel_id=1, source_target_pairs={{0,8},{8,0},{16,24},{24,16},{1,9},{9,1},{17,25},{25,17},{2,10},{10... | collective-permute-start | bytes 196616 | tf_op jit(solution)/shard_map/ppermute | solution.py:250
  17.3 1.5 %collective-permute-start.6 = (f32[64,256]{1,0:T(8,128)S(1)}, f32[64,256]{1,0:T(8,128)S(1)}, u32[]{:S(2)}, u32[]{:S(2)}) collective-permute-start(f32[64,256]{1,0:T(8,128)S(1)} %add_add_fusion.refs_0_), channel_id=1, source_target_pairs={{0,16},{8,24},{16,0},{24,8},{1,17},{9,25},{17,1},{25,9},{2,18},{10... | collective-permute-start | bytes 196616 | tf_op jit(solution)/shard_map/ppermute | solution.py:250
  18.9 0.5 %collective-permute-start.5 = (f32[64,256]{1,0:T(8,128)S(1)}, f32[64,256]{1,0:T(8,128)S(1)}, u32[]{:S(2)}, u32[]{:S(2)}) collective-permute-start(f32[64,256]{1,0:T(8,128)S(1)} %add_add_fusion.refs_0_), channel_id=1, source_target_pairs={{0,24},{8,16},{16,8},{24,0},{1,25},{9,17},{17,9},{25,1},{2,26},{10... | collective-permute-start | bytes 196616 | tf_op jit(solution)/shard_map/ppermute | solution.py:250
  19.3 0.6 %halves.3.refs_0_ = f32[336,544]{1,0:T(8,128)S(1)} custom-call(bf16[816,256]{1,0:T(8,128)(2,1)S(1)} %get-tuple-element.27.left_ref, bf16[816,256]{1,0:T(8,128)(2,1)S(1)} %get-tuple-element.28.right_ref, f32[64,256]{1,0:T(8,128)S(1)} %add_add_fusion.refs_0_), custom_call_target="tpu_custom_call" | custom-call | flops 307494912 | bytes 2000000 | tf_op jit(solution)/shard_map/halves/pallas_call | solution.py:304
  20.0 0.1 collective-permute-done.4.refs_1_
  20.1 0.1 collective-permute-start.7
  20.2 0.7 %halves.4.refs_0_ = f32[336,544]{1,0:T(8,128)S(1)} custom-call(bf16[816,256]{1,0:T(8,128)(2,1)S(1)} %get-tuple-element.27.left_ref, bf16[816,256]{1,0:T(8,128)(2,1)S(1)} %get-tuple-element.28.right_ref, f32[336,544]{1,0:T(8,128)S(1)} %halves.3.refs_0_, f32[64,256]{1,0:T(8,128)S(1)} %collective-permute-done.4.refs_1_), custom_call_target="tpu_custom_call", output_to_operand_aliasing={{}: (2, {})} | custom-call | flops 307494912 | bytes 2000000 | tf_op jit(solution)/shard_map/halves/pallas_call | solution.py:304
  20.9 1.4 %collective-permute-done.6 = f32[64,256]{1,0:T(8,128)S(1)} collective-permute-done((f32[64,256]{1,0:T(8,128)S(1)}, f32[64,256]{1,0:T(8,128)S(1)}, u32[]{:S(2)}, u32[]{:S(2)}) %collective-permute-start.6) | collective-permute-done | bytes 65568 | tf_op jit(solution)/shard_map/ppermute | solution.py:250
  22.3 1.7 %collective-permute-done.5 = f32[64,256]{1,0:T(8,128)S(1)} collective-permute-done((f32[64,256]{1,0:T(8,128)S(1)}, f32[64,256]{1,0:T(8,128)S(1)}, u32[]{:S(2)}, u32[]{:S(2)}) %collective-permute-start.5) | collective-permute-done | bytes 65568 | tf_op jit(solution)/shard_map/ppermute | solution.py:250
  24.0 0.1 collective-permute-start.8
  24.1 0.0 collective-permute-done.7.refs_1_.early_other_ref
  24.1 1.6 %halves.5.before_ref = f32[336,544]{1,0:T(8,128)S(1)} custom-call(bf16[816,256]{1,0:T(8,128)(2,1)S(1)} %get-tuple-element.27.left_ref, bf16[816,256]{1,0:T(8,128)(2,1)S(1)} %get-tuple-element.28.right_ref, f32[336,544]{1,0:T(8,128)S(1)} %halves.4.refs_0_, ...), custom_call_target="tpu_custom_call", output_to_operand_aliasing={{}: (2, {})} | custom-call | flops 1229979648 | bytes 2000000 | tf_op jit(solution)/shard_map/halves/pallas_call | solution.py:304
  25.8 0.0 collective-permute-done.8.late_other_ref
  25.8 1.9 %last_half.1 = (f32[64,512]{1,0:T(8,128)}, f32[64,512]{1,0:T(8,128)}, f32[268,536]{1,0:T(8,128)}, f32[64,536]{1,0:T(8,128)}) custom-call(bf16[816,256]{1,0:T(8,128)(2,1)S(1)} %get-tuple-element.27.left_ref, bf16[816,256]{1,0:T(8,128)(2,1)S(1)} %get-tuple-element.28.right_ref, f32[336,544]{1,0:T(8,128)S(1)} %halves.5.before_ref, ...), custom_call_target="tpu_custom_call" | custom-call | flops 614989824 | bytes 2000000 | tf_op jit(solution)/shard_map/last_half/pallas_call | solution.py:338
  (5 shorter events, 0.1 us)
Async XLA Ops:
  3.4 1.4 %collective-permute-start = (f32[64,256]{1,0:T(8,128)S(1)}, f32[64,256]{1,0:T(8,128)S(1)}, u32[]{:S(2)}, u32[]{:S(2)}) collective-permute-start(f32[64,256]{1,0:T(8,128)S(1)} %get-tuple-element.22), channel_id=1, source_target_pairs={{0,1},{1,0},{2,3},{3,2},{4,5},{5,4},{6,7},{7,6},{8,9},{9,8},{10,11... | collective-permute-start | bytes 196616 | tf_op jit(solution)/shard_map/ppermute | solution.py:250
  4.9 7.7 %collective-permute-start.3 = (f32[64,256]{1,0:T(8,128)S(1)}, f32[64,256]{1,0:T(8,128)S(1)}, u32[]{:S(2)}, u32[]{:S(2)}) collective-permute-start(f32[64,256]{1,0:T(8,128)S(1)} %add.15.after_ref), channel_id=1, source_target_pairs={{0,6},{1,7},{2,4},{3,5},{4,2},{5,3},{6,0},{7,1},{8,14},{9,15},{10,... | collective-permute-start | bytes 196616 | tf_op jit(solution)/shard_map/ppermute | solution.py:250
  9.9 5.9 %collective-permute-start.2 = (f32[64,256]{1,0:T(8,128)S(1)}, f32[64,256]{1,0:T(8,128)S(1)}, u32[]{:S(2)}, u32[]{:S(2)}) collective-permute-start(f32[64,256]{1,0:T(8,128)S(1)} %add.15.after_ref), channel_id=1, source_target_pairs={{0,4},{1,5},{2,6},{3,7},{4,0},{5,1},{6,2},{7,3},{8,12},{9,13},{10,... | collective-permute-start | bytes 196616 | tf_op jit(solution)/shard_map/ppermute | solution.py:250
  9.9 5.9 %collective-permute-start.1 = (f32[64,256]{1,0:T(8,128)S(1)}, f32[64,256]{1,0:T(8,128)S(1)}, u32[]{:S(2)}, u32[]{:S(2)}) collective-permute-start(f32[64,256]{1,0:T(8,128)S(1)} %add.15.after_ref), channel_id=1, source_target_pairs={{0,2},{1,3},{2,0},{3,1},{4,6},{5,7},{6,4},{7,5},{8,10},{9,11},{10,... | collective-permute-start | bytes 196616 | tf_op jit(solution)/shard_map/ppermute | solution.py:250
  15.8 4.3 %collective-permute-start.4 = (f32[64,256]{1,0:T(8,128)S(1)}, f32[64,256]{1,0:T(8,128)S(1)}, u32[]{:S(2)}, u32[]{:S(2)}) collective-permute-start(f32[64,256]{1,0:T(8,128)S(1)} %add_add_fusion.refs_0_), channel_id=1, source_target_pairs={{0,8},{8,0},{16,24},{24,16},{1,9},{9,1},{17,25},{25,17},{2,10},{10... | collective-permute-start | bytes 196616 | tf_op jit(solution)/shard_map/ppermute | solution.py:250
  17.3 5.0 %collective-permute-start.6 = (f32[64,256]{1,0:T(8,128)S(1)}, f32[64,256]{1,0:T(8,128)S(1)}, u32[]{:S(2)}, u32[]{:S(2)}) collective-permute-start(f32[64,256]{1,0:T(8,128)S(1)} %add_add_fusion.refs_0_), channel_id=1, source_target_pairs={{0,16},{8,24},{16,0},{24,8},{1,17},{9,25},{17,1},{25,9},{2,18},{10... | collective-permute-start | bytes 196616 | tf_op jit(solution)/shard_map/ppermute | solution.py:250
  18.9 5.2 %collective-permute-start.5 = (f32[64,256]{1,0:T(8,128)S(1)}, f32[64,256]{1,0:T(8,128)S(1)}, u32[]{:S(2)}, u32[]{:S(2)}) collective-permute-start(f32[64,256]{1,0:T(8,128)S(1)} %add_add_fusion.refs_0_), channel_id=1, source_target_pairs={{0,24},{8,16},{16,8},{24,0},{1,25},{9,17},{17,9},{25,1},{2,26},{10... | collective-permute-start | bytes 196616 | tf_op jit(solution)/shard_map/ppermute | solution.py:250
  20.1 4.0 %collective-permute-start.7 = (f32[2,64,256]{2,1,0:T(8,128)S(1)}, f32[2,64,256]{2,1,0:T(8,128)S(1)}, u32[]{:S(2)}, u32[]{:S(2)}) collective-permute-start(f32[2,64,256]{2,1,0:T(8,128)S(1)} %pad_maximum_fusion.early_ref), channel_id=1, source_target_pairs={{0,1},{1,0},{2,3},{3,2},{4,5},{5,4},{6,7},{7,6},{8,9},{9,8},{10,11... | collective-permute-start | bytes 393224 | tf_op jit(solution)/shard_map/ppermute | solution.py:250
  24.0 1.7 %collective-permute-start.8 = (f32[2,64,256]{2,1,0:T(8,128)S(1)}, f32[2,64,256]{2,1,0:T(8,128)S(1)}, u32[]{:S(2)}, u32[]{:S(2)}) collective-permute-start(f32[2,64,256]{2,1,0:T(8,128)S(1)} %pad_maximum_fusion.1.refs_2_.late_ref), channel_id=1, source_target_pairs={{0,1},{1,0},{2,3},{3,2},{4,5},{5,4},{6,7},{7,6},{8,9},{9,8},{10,11... | collective-permute-start | bytes 393224 | tf_op jit(solution)/shard_map/ppermute | solution.py:250

commit v7 on v6

--- a/solution.py
+++ b/solution.py
@@ -146,11 +146,15 @@
     )
 
 
-def joined(refs):
+def halves_of(refs):
     halves = []
     for ref in refs:
         halves.extend([ref[...]] if len(ref.shape) == 2 else [ref[slot] for slot in range(ref.shape[0])])
-    return jnp.concatenate(halves, axis=1)
+    return halves
+
+
+def joined(refs):
+    return jnp.concatenate(halves_of(refs), axis=1)
 
 
 def halves_kernel(cols, has_before, left_ref, right_ref, *refs):
@@ -163,8 +167,7 @@
 
 def edge_columns(time_idx, core, halves, starts, ends):
     count, modes, width = starts.shape
-    for offset, side, load in halves:
-        block = load()
+    for offset, side, block in halves:
         at = 2 * (time_idx ^ offset) + side
         starts[at] = block[:, :width]
         ends[at] = block[:, block.shape[1] - width :]
@@ -186,15 +189,15 @@
 
 
 def last_kernel(
-    row_block, col_block, chunks, offsets, left_ref, right_ref, before_ref, reg_ref, early_ref,
-    early_other_ref, late_ref, late_other_ref, reduced_ref, rates_ref, normal_ref, right_side_ref, starts,
+    row_block, col_block, chunks, offsets, left_ref, right_ref, before_ref, reg_ref, own_ref, own_other_ref,
+    first_ref, first_other_ref, late_ref, late_other_ref, reduced_ref, rates_ref, normal_ref, right_side_ref, starts,
     ends, col_scratch, reduced_out, rates_out, normal_out, right_side_out, sems,
 ):
     time_idx = lax.axis_index("tm")
     space_idx = lax.axis_index("space")
     core = space_idx % 2
-    early, modes, half = early_ref.shape
-    groups = early + late_ref.shape[0]
+    modes, half = own_ref.shape
+    groups = 2 + late_ref.shape[0]
     snaps = 2 * half
     cols = round_up(col_block, 16)
     depth = left_ref.shape[1]
@@ -204,14 +207,15 @@
         copies.append(pltpu.make_async_copy(source, target, sems.at[len(copies)]))
         copies[-1].start()
 
-    reduced_out[:, pl.ds(pl.multiple_of(core * half, half), half)] = early_ref[0]
-    reduced_out[:, pl.ds(pl.multiple_of((1 - core) * half, half), half)] = early_other_ref[0]
+    reduced_out[:, pl.ds(pl.multiple_of(core * half, half), half)] = own_ref[...]
+    reduced_out[:, pl.ds(pl.multiple_of((1 - core) * half, half), half)] = own_other_ref[...]
     send(reduced_out, reduced_ref)
     halves = []
-    for slot, offset in enumerate(offsets):
-        for side, pair in ((core, (early_ref, late_ref)), (1 - core, (early_other_ref, late_other_ref))):
-            ref, at = (pair[0], slot) if slot < early else (pair[1], slot - early)
-            halves.append((offset, side, functools.partial(lambda ref, at: ref[at], ref, at)))
+    for side, refs in (
+        (core, (own_ref, first_ref, late_ref)),
+        (1 - core, (own_other_ref, first_other_ref, late_other_ref)),
+    ):
+        halves.extend((offset, side, half) for offset, half in zip(offsets, halves_of(refs)))
     edge, edge_rates = edge_columns(time_idx, core, halves, starts, ends)
     own = reduced_out[...]
     width = edge.shape[1]
@@ -286,7 +290,7 @@
     while len(terms) > 1:
         terms = [terms[i] + terms[i + 1] for i in range(0, len(terms), 2)]
     mine, left, right, reg_rows = lax.optimization_barrier((terms[0], left, right, reg_rows))
-    arriving = [(step, swapped(mine, "tm", step)) for step in [1, *range(tm_count - 1, 1, -1)]]
+    arriving = [(step, swapped(mine, "tm", step)) for step in range(tm_count - 1, 0, -1)]
     acc_shape = jax.ShapeDtypeStruct((cols + modes, rows), jnp.float32)
 
     def cost(count):
@@ -314,16 +318,17 @@
         )(left, right, *before, *blocks)
 
     offsets = [0] + [offset for offset, _ in arriving]
-    early = [mine, arriving[0][1]]
+    first = arriving[0][1]
     late = [got for _, got in arriving[1:]]
-    acc = add_terms(None, [mine])
-    early_stack = jnp.stack(early)
-    early_other = swapped(early_stack, "space", 1)
-    acc = add_terms(acc, early[1:])
+    own_other = swapped(mine, "space", 1)
+    acc = add_terms(None, [mine, own_other])
+    acc, first = lax.optimization_barrier((acc, first))
+    first_other = swapped(jnp.stack([mine, first]), "space", 1)[1]
+    acc = add_terms(acc, [first])
     acc, *late = lax.optimization_barrier((acc, *late))
     late_stack = jnp.stack(late)
     late_other = swapped(late_stack, "space", 1)
-    acc = add_terms(acc, [early_other, late_stack])
+    acc = add_terms(acc, [first_other, late_stack])
     width = 128
     starts = list(range(0, row_block - width, 2 * width))
     starts = [0] + [start - width for start in starts[1:]] if len(starts) > 1 else [0]
@@ -338,7 +343,7 @@
     outs = pl.pallas_call(
         functools.partial(last_kernel, row_block, col_block, chunks, offsets),
         out_shape=out_shapes,
-        in_specs=[vmem] * 8,
+        in_specs=[vmem] * 10,
         out_specs=(hbm,) * 4,
         scratch_shapes=[
             pltpu.VMEM((2 * tm_count, modes, width), jnp.float32),
@@ -350,7 +355,7 @@
         compiler_params=params,
         cost_estimate=cost(len(late) * half_snaps),
         name="last_half",
-    )(left, right, acc, reg_rows, early_stack, early_other, late_stack, late_other)
+    )(left, right, acc, reg_rows, mine, own_other, first, first_other, late_stack, late_other)
     return tuple(out.T for out in outs)
 
 

time: 28 us -> 26.8 us (0.957)
  waiting for transfers between devices: 8.06 us -> 6.81 us
    ppermute x9 -> x10, waiting for transfers between devices: 8.06 us -> 6.81 us  [swapped(): lax.ppermute(value, axis, [(i, i ^ distance) for i in range(lax.axis_size...]
    ppermute x9 -> x10, starting transfers between devices: 9.87 us -> 9.94 us  [swapped(): lax.ppermute(value, axis, [(i, i ^ distance) for i in range(lax.axis_size...]
  transfers between devices with their start and end apart: 9 -> 10, of which waited for: 6 -> 6; matrix products, arithmetic and copies ran while one was open for 3% -> 3% of each run, Pallas kernels for 13% -> 13%
where the time goes in v7:
time: 26.8 us; the launch traced here: 26.5 us
  starting transfers between devices  9.94 us (37%)
  Pallas kernels  8.23 us (31%)
  waiting for transfers between devices  6.81 us (25%)
  local copies, waits for them, and re-layouts  0.78 us (3%)
  between operations  0.73 us (3%)
    ppermute x10, starting transfers between devices, swapped(): lax.ppermute(value, axis, [(i, i ^ distance) for i in range(lax.axis_size...  9.94 us
    ppermute x10, waiting for transfers between devices, swapped(): lax.ppermute(value, axis, [(i, i ^ distance) for i in range(lax.axis_size...  6.81 us
    pallas_call x3, Pallas kernels, add_terms(): pl.pallas_call(functools.partial(halves_kernel, cols, len(before)), out_s...  2.92 us
    pallas_call x1, Pallas kernels, project(): pl.pallas_call(project_kernel, out_shape=(block, block), in_specs=[hbm, h...  2.79 us
    pallas_call x1, Pallas kernels, local(): pl.pallas_call(functools.partial(last_kernel, row_block, col_block, chunk...  1.93 us
    dynamic_slice x1, local copies, waits for them, and re-layouts, local(): lax.dynamic_slice_in_dim(reg_weights, first_row, row_block, 0)[None]  0.77 us
    pallas_call x1, Pallas kernels, local(): pl.pallas_call(functools.partial(selector_kernel, row_block, col_block),...  0.6 us
  transfers between devices with their start and end apart: 10, of which 6 were waited for; matrix products, arithmetic and copies ran while one was open for 3% of the time, Pallas kernels for 13%

profile of v7, /device:TPU:0, one launch (start us, length us, event | category | flops | bytes accessed | tf_op | source)
XLA Modules:
  0.0 26.5 jit_solution(17215598766765672914)
XLA Ops:
  0.6 2.8 %project.1 = (f32[64,256]{1,0:T(8,128)S(1)}, f32[64,256]{1,0:T(8,128)S(1)}) custom-call(bf16[64,2048]{1,0:T(8,128)(2,1)} %bitcast.13, bf16[512,2048]{1,0:T(8,128)(2,1)} %snaps_ref.1), custom_call_target="tpu_custom_call" | custom-call | tf_op jit(solution)/shard_map/project/pallas_call | solution.py:98
  3.4 0.5 %collective-permute-start = (f32[64,256]{1,0:T(8,128)S(1)}, f32[64,256]{1,0:T(8,128)S(1)}, u32[]{:S(2)}, u32[]{:S(2)}) collective-permute-start(f32[64,256]{1,0:T(8,128)S(1)} %get-tuple-element.24), channel_id=1, source_target_pairs={{0,1},{1,0},{2,3},{3,2},{4,5},{5,4},{6,7},{7,6},{8,9},{9,8},{10,11... | collective-permute-start | bytes 196616 | tf_op jit(solution)/shard_map/ppermute | solution.py:254
  3.9 0.9 %collective-permute-done = f32[64,256]{1,0:T(8,128)S(1)} collective-permute-done((f32[64,256]{1,0:T(8,128)S(1)}, f32[64,256]{1,0:T(8,128)S(1)}, u32[]{:S(2)}, u32[]{:S(2)}) %collective-permute-start) | collective-permute-done | bytes 65568 | tf_op jit(solution)/shard_map/ppermute | solution.py:254
  4.9 5.0 %collective-permute-start.3 = (f32[64,256]{1,0:T(8,128)S(1)}, f32[64,256]{1,0:T(8,128)S(1)}, u32[]{:S(2)}, u32[]{:S(2)}) collective-permute-start(f32[64,256]{1,0:T(8,128)S(1)} %add.15.after_ref), channel_id=1, source_target_pairs={{0,6},{1,7},{2,4},{3,5},{4,2},{5,3},{6,0},{7,1},{8,14},{9,15},{10,... | collective-permute-start | bytes 196616 | tf_op jit(solution)/shard_map/ppermute | solution.py:254
  9.9 0.0 collective-permute-start.2
  9.9 0.6 %collective-permute-start.1 = (f32[64,256]{1,0:T(8,128)S(1)}, f32[64,256]{1,0:T(8,128)S(1)}, u32[]{:S(2)}, u32[]{:S(2)}) collective-permute-start(f32[64,256]{1,0:T(8,128)S(1)} %add.15.after_ref), channel_id=1, source_target_pairs={{0,2},{1,3},{2,0},{3,1},{4,6},{5,7},{6,4},{7,5},{8,10},{9,11},{10,... | collective-permute-start | bytes 196616 | tf_op jit(solution)/shard_map/ppermute | solution.py:254
  10.5 0.8 %dynamic_slice.3 = f32[536]{0:T(1024)S(1)} dynamic-slice(f32[2144]{0:T(1024)} %param.5, s32[]{:T(128)S(6)} %select_n.3), dynamic_slice_sizes={536} | dynamic-slice | bytes 4292 | tf_op jit(solution)/shard_map/dynamic_slice | solution.py:287
  11.3 0.6 %selectors.1 = (bf16[816,256]{1,0:T(8,128)(2,1)S(1)}, bf16[816,256]{1,0:T(8,128)(2,1)S(1)}) custom-call(f32[64,256]{1,0:T(8,128)S(1)} %add.15.after_ref), custom_call_target="tpu_custom_call" | custom-call | flops 1000000 | bytes 1000000 | tf_op jit(solution)/shard_map/selectors/pallas_call | solution.py:277
  11.9 0.6 %collective-permute-done.3 = f32[64,256]{1,0:T(8,128)S(1)} collective-permute-done((f32[64,256]{1,0:T(8,128)S(1)}, f32[64,256]{1,0:T(8,128)S(1)}, u32[]{:S(2)}, u32[]{:S(2)}) %collective-permute-start.3) | collective-permute-done | bytes 65568 | tf_op jit(solution)/shard_map/ppermute | solution.py:254
  12.5 3.2 %collective-permute-done.2 = f32[64,256]{1,0:T(8,128)S(1)} collective-permute-done((f32[64,256]{1,0:T(8,128)S(1)}, f32[64,256]{1,0:T(8,128)S(1)}, u32[]{:S(2)}, u32[]{:S(2)}) %collective-permute-start.2) | collective-permute-done | bytes 65568 | tf_op jit(solution)/shard_map/ppermute | solution.py:254
  15.8 0.0 collective-permute-done.1
  15.8 0.1 collective-permute-start.4
  15.9 2.5 %collective-permute-start.5 = (f32[64,256]{1,0:T(8,128)S(1)}, f32[64,256]{1,0:T(8,128)S(1)}, u32[]{:S(2)}, u32[]{:S(2)}) collective-permute-start(f32[64,256]{1,0:T(8,128)S(1)} %add_add_fusion.refs_0_.own_ref), channel_id=1, source_target_pairs={{0,24},{8,16},{16,8},{24,0},{1,25},{9,17},{17,9},{25,1},{2,26},{10... | collective-permute-start | bytes 196616 | tf_op jit(solution)/shard_map/ppermute | solution.py:254
  18.4 0.5 %collective-permute-start.7 = (f32[64,256]{1,0:T(8,128)S(1)}, f32[64,256]{1,0:T(8,128)S(1)}, u32[]{:S(2)}, u32[]{:S(2)}) collective-permute-start(f32[64,256]{1,0:T(8,128)S(1)} %add_add_fusion.refs_0_.own_ref), channel_id=1, source_target_pairs={{0,8},{8,0},{16,24},{24,16},{1,9},{9,1},{17,25},{25,17},{2,10},{10... | collective-permute-start | bytes 196616 | tf_op jit(solution)/shard_map/ppermute | solution.py:254
  18.9 0.5 %collective-permute-start.6 = (f32[64,256]{1,0:T(8,128)S(1)}, f32[64,256]{1,0:T(8,128)S(1)}, u32[]{:S(2)}, u32[]{:S(2)}) collective-permute-start(f32[64,256]{1,0:T(8,128)S(1)} %add_add_fusion.refs_0_.own_ref), channel_id=1, source_target_pairs={{0,16},{8,24},{16,0},{24,8},{1,17},{9,25},{17,1},{25,9},{2,18},{10... | collective-permute-start | bytes 196616 | tf_op jit(solution)/shard_map/ppermute | solution.py:254
  19.4 0.0 collective-permute-done.4.refs_1_.own_other_ref
  19.4 1.0 %halves.3.refs_0_ = f32[336,544]{1,0:T(8,128)S(1)} custom-call(bf16[816,256]{1,0:T(8,128)(2,1)S(1)} %get-tuple-element.29.left_ref, bf16[816,256]{1,0:T(8,128)(2,1)S(1)} %get-tuple-element.30.right_ref, f32[64,256]{1,0:T(8,128)S(1)} %add_add_fusion.refs_0_.own_ref, f32[64,256]{1,0:T(8,128)S(1)} %collective-permute-done.4.refs_1_.own_other_ref), custom_call_target="tpu_custom_call" | custom-call | flops 614989824 | bytes 2000000 | tf_op jit(solution)/shard_map/halves/pallas_call | solution.py:308
  20.4 1.1 %collective-permute-done.5.refs_1_.first_ref = f32[64,256]{1,0:T(8,128)S(1)} collective-permute-done((f32[64,256]{1,0:T(8,128)S(1)}, f32[64,256]{1,0:T(8,128)S(1)}, u32[]{:S(2)}, u32[]{:S(2)}) %collective-permute-start.5) | collective-permute-done | bytes 65568 | tf_op jit(solution)/shard_map/ppermute | solution.py:254
  21.5 0.1 collective-permute-start.8
  21.6 0.7 %halves.4.refs_0_ = f32[336,544]{1,0:T(8,128)S(1)} custom-call(bf16[816,256]{1,0:T(8,128)(2,1)S(1)} %get-tuple-element.29.left_ref, bf16[816,256]{1,0:T(8,128)(2,1)S(1)} %get-tuple-element.30.right_ref, f32[336,544]{1,0:T(8,128)S(1)} %halves.3.refs_0_, f32[64,256]{1,0:T(8,128)S(1)} %collective-permute-done.5.refs_1_.first_ref), custom_call_target="tpu_custom_call", output_to_operand_aliasing={{}: (2, {})} | custom-call | flops 307494912 | bytes 2000000 | tf_op jit(solution)/shard_map/halves/pallas_call | solution.py:308
  22.3 0.5 %collective-permute-done.7 = f32[64,256]{1,0:T(8,128)S(1)} collective-permute-done((f32[64,256]{1,0:T(8,128)S(1)}, f32[64,256]{1,0:T(8,128)S(1)}, u32[]{:S(2)}, u32[]{:S(2)}) %collective-permute-start.7) | collective-permute-done | bytes 65568 | tf_op jit(solution)/shard_map/ppermute | solution.py:254
  22.7 0.4 %collective-permute-done.6 = f32[64,256]{1,0:T(8,128)S(1)} collective-permute-done((f32[64,256]{1,0:T(8,128)S(1)}, f32[64,256]{1,0:T(8,128)S(1)}, u32[]{:S(2)}, u32[]{:S(2)}) %collective-permute-start.6) | collective-permute-done | bytes 65568 | tf_op jit(solution)/shard_map/ppermute | solution.py:254
  23.2 0.1 collective-permute-start.9
  23.3 0.0 collective-permute-done.8
  23.3 1.3 %halves.5.before_ref = f32[336,544]{1,0:T(8,128)S(1)} custom-call(bf16[816,256]{1,0:T(8,128)(2,1)S(1)} %get-tuple-element.29.left_ref, bf16[816,256]{1,0:T(8,128)(2,1)S(1)} %get-tuple-element.30.right_ref, f32[336,544]{1,0:T(8,128)S(1)} %halves.4.refs_0_, f32[64,256]{1,0:T(8,128)S(1)} %slice_bitcast_fusion.refs_1_.first_other_ref, ...), custom_call_target="tpu_custom_call", output_to_operand_aliasing={{}: (2, {})} | custom-call | flops 922484736 | bytes 2000000 | tf_op jit(solution)/shard_map/halves/pallas_call | solution.py:308
  24.6 0.0 collective-permute-done.9.late_other_ref
  24.6 1.9 %last_half.1 = (f32[64,512]{1,0:T(8,128)}, f32[64,512]{1,0:T(8,128)}, f32[268,536]{1,0:T(8,128)}, f32[64,536]{1,0:T(8,128)}) custom-call(bf16[816,256]{1,0:T(8,128)(2,1)S(1)} %get-tuple-element.29.left_ref, bf16[816,256]{1,0:T(8,128)(2,1)S(1)} %get-tuple-element.30.right_ref, f32[336,544]{1,0:T(8,128)S(1)} %halves.5.before_ref, ...), custom_call_target="tpu_custom_call" | custom-call | flops 614989824 | bytes 2000000 | tf_op jit(solution)/shard_map/last_half/pallas_call | solution.py:343
  (6 shorter events, 0.1 us)
Async XLA Ops:
  3.4 1.4 %collective-permute-start = (f32[64,256]{1,0:T(8,128)S(1)}, f32[64,256]{1,0:T(8,128)S(1)}, u32[]{:S(2)}, u32[]{:S(2)}) collective-permute-start(f32[64,256]{1,0:T(8,128)S(1)} %get-tuple-element.24), channel_id=1, source_target_pairs={{0,1},{1,0},{2,3},{3,2},{4,5},{5,4},{6,7},{7,6},{8,9},{9,8},{10,11... | collective-permute-start | bytes 196616 | tf_op jit(solution)/shard_map/ppermute | solution.py:254
  4.9 7.7 %collective-permute-start.3 = (f32[64,256]{1,0:T(8,128)S(1)}, f32[64,256]{1,0:T(8,128)S(1)}, u32[]{:S(2)}, u32[]{:S(2)}) collective-permute-start(f32[64,256]{1,0:T(8,128)S(1)} %add.15.after_ref), channel_id=1, source_target_pairs={{0,6},{1,7},{2,4},{3,5},{4,2},{5,3},{6,0},{7,1},{8,14},{9,15},{10,... | collective-permute-start | bytes 196616 | tf_op jit(solution)/shard_map/ppermute | solution.py:254
  9.9 5.9 %collective-permute-start.2 = (f32[64,256]{1,0:T(8,128)S(1)}, f32[64,256]{1,0:T(8,128)S(1)}, u32[]{:S(2)}, u32[]{:S(2)}) collective-permute-start(f32[64,256]{1,0:T(8,128)S(1)} %add.15.after_ref), channel_id=1, source_target_pairs={{0,4},{1,5},{2,6},{3,7},{4,0},{5,1},{6,2},{7,3},{8,12},{9,13},{10,... | collective-permute-start | bytes 196616 | tf_op jit(solution)/shard_map/ppermute | solution.py:254
  9.9 5.9 %collective-permute-start.1 = (f32[64,256]{1,0:T(8,128)S(1)}, f32[64,256]{1,0:T(8,128)S(1)}, u32[]{:S(2)}, u32[]{:S(2)}) collective-permute-start(f32[64,256]{1,0:T(8,128)S(1)} %add.15.after_ref), channel_id=1, source_target_pairs={{0,2},{1,3},{2,0},{3,1},{4,6},{5,7},{6,4},{7,5},{8,10},{9,11},{10,... | collective-permute-start | bytes 196616 | tf_op jit(solution)/shard_map/ppermute | solution.py:254
  15.8 3.6 %collective-permute-start.4 = (f32[64,256]{1,0:T(8,128)S(1)}, f32[64,256]{1,0:T(8,128)S(1)}, u32[]{:S(2)}, u32[]{:S(2)}) collective-permute-start(f32[64,256]{1,0:T(8,128)S(1)} %add_add_fusion.refs_0_.own_ref), channel_id=1, source_target_pairs={{0,1},{1,0},{2,3},{3,2},{4,5},{5,4},{6,7},{7,6},{8,9},{9,8},{10,11... | collective-permute-start | bytes 196616 | tf_op jit(solution)/shard_map/ppermute | solution.py:254
  15.9 5.6 %collective-permute-start.5 = (f32[64,256]{1,0:T(8,128)S(1)}, f32[64,256]{1,0:T(8,128)S(1)}, u32[]{:S(2)}, u32[]{:S(2)}) collective-permute-start(f32[64,256]{1,0:T(8,128)S(1)} %add_add_fusion.refs_0_.own_ref), channel_id=1, source_target_pairs={{0,24},{8,16},{16,8},{24,0},{1,25},{9,17},{17,9},{25,1},{2,26},{10... | collective-permute-start | bytes 196616 | tf_op jit(solution)/shard_map/ppermute | solution.py:254
  18.4 4.4 %collective-permute-start.7 = (f32[64,256]{1,0:T(8,128)S(1)}, f32[64,256]{1,0:T(8,128)S(1)}, u32[]{:S(2)}, u32[]{:S(2)}) collective-permute-start(f32[64,256]{1,0:T(8,128)S(1)} %add_add_fusion.refs_0_.own_ref), channel_id=1, source_target_pairs={{0,8},{8,0},{16,24},{24,16},{1,9},{9,1},{17,25},{25,17},{2,10},{10... | collective-permute-start | bytes 196616 | tf_op jit(solution)/shard_map/ppermute | solution.py:254
  18.9 4.3 %collective-permute-start.6 = (f32[64,256]{1,0:T(8,128)S(1)}, f32[64,256]{1,0:T(8,128)S(1)}, u32[]{:S(2)}, u32[]{:S(2)}) collective-permute-start(f32[64,256]{1,0:T(8,128)S(1)} %add_add_fusion.refs_0_.own_ref), channel_id=1, source_target_pairs={{0,16},{8,24},{16,0},{24,8},{1,17},{9,25},{17,1},{25,9},{2,18},{10... | collective-permute-start | bytes 196616 | tf_op jit(solution)/shard_map/ppermute | solution.py:254
  21.5 1.8 %collective-permute-start.8 = (f32[2,64,256]{2,1,0:T(8,128)S(1)}, f32[2,64,256]{2,1,0:T(8,128)S(1)}, u32[]{:S(2)}, u32[]{:S(2)}) collective-permute-start(f32[2,64,256]{2,1,0:T(8,128)S(1)} %pad_maximum_fusion), channel_id=1, source_target_pairs={{0,1},{1,0},{2,3},{3,2},{4,5},{5,4},{6,7},{7,6},{8,9},{9,8},{10,11... | collective-permute-start | bytes 393224 | tf_op jit(solution)/shard_map/ppermute | solution.py:254
  23.2 1.4 %collective-permute-start.9 = (f32[2,64,256]{2,1,0:T(8,128)S(1)}, f32[2,64,256]{2,1,0:T(8,128)S(1)}, u32[]{:S(2)}, u32[]{:S(2)}) collective-permute-start(f32[2,64,256]{2,1,0:T(8,128)S(1)} %pad_maximum_fusion.1.refs_2_.late_ref), channel_id=1, source_target_pairs={{0,1},{1,0},{2,3},{3,2},{4,5},{5,4},{6,7},{7,6},{8,9},{9,8},{10,11... | collective-permute-start | bytes 393224 | tf_op jit(solution)/shard_map/ppermute | solution.py:254

commit v8 on v7

--- a/solution.py
+++ b/solution.py
@@ -286,7 +286,9 @@
     first_row = after * row_block
     reg_rows = lax.dynamic_slice_in_dim(reg_weights, first_row, row_block, 0)[None]
 
-    terms = [half] + [swapped(half, "space", step) for step in range(2, space_count, 2)]
+    steps = list(range(2, space_count, 2))
+    steps = steps[:-2] + steps[-2:][::-1]
+    terms = [half] + [swapped(half, "space", step) for step in steps]
     while len(terms) > 1:
         terms = [terms[i] + terms[i + 1] for i in range(0, len(terms), 2)]
     mine, left, right, reg_rows = lax.optimization_barrier((terms[0], left, right, reg_rows))

time: 26.8 us -> 26.6 us (level)
  transfers between devices with their start and end apart: 10 -> 10, of which waited for: 6 -> 7; matrix products, arithmetic and copies ran while one was open for 3% -> 3% of each run, Pallas kernels for 13% -> 13%
where the time goes in v8:
time: 26.6 us; the launch traced here: 26.4 us
  starting transfers between devices  9.86 us (37%)
  Pallas kernels  8.24 us (31%)
  waiting for transfers between devices  6.75 us (25%)
  local copies, waits for them, and re-layouts  0.78 us (3%)
  between operations  0.73 us (3%)
    ppermute x10, starting transfers between devices, swapped(): lax.ppermute(value, axis, [(i, i ^ distance) for i in range(lax.axis_size...  9.86 us
    ppermute x10, waiting for transfers between devices, swapped(): lax.ppermute(value, axis, [(i, i ^ distance) for i in range(lax.axis_size...  6.75 us
    pallas_call x3, Pallas kernels, add_terms(): pl.pallas_call(functools.partial(halves_kernel, cols, len(before)), out_s...  2.92 us
    pallas_call x1, Pallas kernels, project(): pl.pallas_call(project_kernel, out_shape=(block, block), in_specs=[hbm, h...  2.79 us
    pallas_call x1, Pallas kernels, local(): pl.pallas_call(functools.partial(last_kernel, row_block, col_block, chunk...  1.94 us
    dynamic_slice x1, local copies, waits for them, and re-layouts, local(): lax.dynamic_slice_in_dim(reg_weights, first_row, row_block, 0)[None]  0.77 us
    pallas_call x1, Pallas kernels, local(): pl.pallas_call(functools.partial(selector_kernel, row_block, col_block),...  0.6 us
  transfers between devices with their start and end apart: 10, of which 7 were waited for; matrix products, arithmetic and copies ran while one was open for 3% of the time, Pallas kernels for 13%

profile of v8, /device:TPU:0, one launch (start us, length us, event | category | flops | bytes accessed | tf_op | source)
XLA Modules:
  0.0 26.4 jit_solution(13176321978833592041)
XLA Ops:
  0.6 2.8 %project.1 = (f32[64,256]{1,0:T(8,128)S(1)}, f32[64,256]{1,0:T(8,128)S(1)}) custom-call(bf16[64,2048]{1,0:T(8,128)(2,1)} %bitcast.13, bf16[512,2048]{1,0:T(8,128)(2,1)} %snaps_ref.1), custom_call_target="tpu_custom_call" | custom-call | tf_op jit(solution)/shard_map/project/pallas_call | solution.py:98
  3.4 0.5 %collective-permute-start = (f32[64,256]{1,0:T(8,128)S(1)}, f32[64,256]{1,0:T(8,128)S(1)}, u32[]{:S(2)}, u32[]{:S(2)}) collective-permute-start(f32[64,256]{1,0:T(8,128)S(1)} %get-tuple-element.24), channel_id=1, source_target_pairs={{0,1},{1,0},{2,3},{3,2},{4,5},{5,4},{6,7},{7,6},{8,9},{9,8},{10,11... | collective-permute-start | bytes 196616 | tf_op jit(solution)/shard_map/ppermute | solution.py:254
  3.9 0.9 %collective-permute-done = f32[64,256]{1,0:T(8,128)S(1)} collective-permute-done((f32[64,256]{1,0:T(8,128)S(1)}, f32[64,256]{1,0:T(8,128)S(1)}, u32[]{:S(2)}, u32[]{:S(2)}) %collective-permute-start) | collective-permute-done | bytes 65568 | tf_op jit(solution)/shard_map/ppermute | solution.py:254
  4.9 4.0 %collective-permute-start.3 = (f32[64,256]{1,0:T(8,128)S(1)}, f32[64,256]{1,0:T(8,128)S(1)}, u32[]{:S(2)}, u32[]{:S(2)}) collective-permute-start(f32[64,256]{1,0:T(8,128)S(1)} %add.15.after_ref), channel_id=1, source_target_pairs={{0,4},{1,5},{2,6},{3,7},{4,0},{5,1},{6,2},{7,3},{8,12},{9,13},{10,... | collective-permute-start | bytes 196616 | tf_op jit(solution)/shard_map/ppermute | solution.py:254
  8.9 1.3 %collective-permute-start.2 = (f32[64,256]{1,0:T(8,128)S(1)}, f32[64,256]{1,0:T(8,128)S(1)}, u32[]{:S(2)}, u32[]{:S(2)}) collective-permute-start(f32[64,256]{1,0:T(8,128)S(1)} %add.15.after_ref), channel_id=1, source_target_pairs={{0,6},{1,7},{2,4},{3,5},{4,2},{5,3},{6,0},{7,1},{8,14},{9,15},{10,... | collective-permute-start | bytes 196616 | tf_op jit(solution)/shard_map/ppermute | solution.py:254
  10.2 0.2 collective-permute-start.1
  10.4 0.8 %dynamic_slice.3 = f32[536]{0:T(1024)S(1)} dynamic-slice(f32[2144]{0:T(1024)} %param.5, s32[]{:T(128)S(6)} %select_n.3), dynamic_slice_sizes={536} | dynamic-slice | bytes 4292 | tf_op jit(solution)/shard_map/dynamic_slice | solution.py:287
  11.2 0.6 %selectors.1 = (bf16[816,256]{1,0:T(8,128)(2,1)S(1)}, bf16[816,256]{1,0:T(8,128)(2,1)S(1)}) custom-call(f32[64,256]{1,0:T(8,128)S(1)} %add.15.after_ref), custom_call_target="tpu_custom_call" | custom-call | flops 1000000 | bytes 1000000 | tf_op jit(solution)/shard_map/selectors/pallas_call | solution.py:277
  11.8 1.0 %collective-permute-done.3 = f32[64,256]{1,0:T(8,128)S(1)} collective-permute-done((f32[64,256]{1,0:T(8,128)S(1)}, f32[64,256]{1,0:T(8,128)S(1)}, u32[]{:S(2)}, u32[]{:S(2)}) %collective-permute-start.3) | collective-permute-done | bytes 65568 | tf_op jit(solution)/shard_map/ppermute | solution.py:254
  12.8 2.4 %collective-permute-done.2 = f32[64,256]{1,0:T(8,128)S(1)} collective-permute-done((f32[64,256]{1,0:T(8,128)S(1)}, f32[64,256]{1,0:T(8,128)S(1)}, u32[]{:S(2)}, u32[]{:S(2)}) %collective-permute-start.2) | collective-permute-done | bytes 65568 | tf_op jit(solution)/shard_map/ppermute | solution.py:254
  15.3 0.2 collective-permute-done.1
  15.5 0.1 collective-permute-start.4
  15.6 2.7 %collective-permute-start.5 = (f32[64,256]{1,0:T(8,128)S(1)}, f32[64,256]{1,0:T(8,128)S(1)}, u32[]{:S(2)}, u32[]{:S(2)}) collective-permute-start(f32[64,256]{1,0:T(8,128)S(1)} %add_add_fusion.refs_0_.own_ref), channel_id=1, source_target_pairs={{0,24},{8,16},{16,8},{24,0},{1,25},{9,17},{17,9},{25,1},{2,26},{10... | collective-permute-start | bytes 196616 | tf_op jit(solution)/shard_map/ppermute | solution.py:254
  18.2 0.5 %collective-permute-start.7 = (f32[64,256]{1,0:T(8,128)S(1)}, f32[64,256]{1,0:T(8,128)S(1)}, u32[]{:S(2)}, u32[]{:S(2)}) collective-permute-start(f32[64,256]{1,0:T(8,128)S(1)} %add_add_fusion.refs_0_.own_ref), channel_id=1, source_target_pairs={{0,8},{8,0},{16,24},{24,16},{1,9},{9,1},{17,25},{25,17},{2,10},{10... | collective-permute-start | bytes 196616 | tf_op jit(solution)/shard_map/ppermute | solution.py:254
  18.8 0.3 %collective-permute-start.6 = (f32[64,256]{1,0:T(8,128)S(1)}, f32[64,256]{1,0:T(8,128)S(1)}, u32[]{:S(2)}, u32[]{:S(2)}) collective-permute-start(f32[64,256]{1,0:T(8,128)S(1)} %add_add_fusion.refs_0_.own_ref), channel_id=1, source_target_pairs={{0,16},{8,24},{16,0},{24,8},{1,17},{9,25},{17,1},{25,9},{2,18},{10... | collective-permute-start | bytes 196616 | tf_op jit(solution)/shard_map/ppermute | solution.py:254
  19.1 0.0 collective-permute-done.4.refs_1_.own_other_ref
  19.1 1.0 %halves.3.refs_0_ = f32[336,544]{1,0:T(8,128)S(1)} custom-call(bf16[816,256]{1,0:T(8,128)(2,1)S(1)} %get-tuple-element.29.left_ref, bf16[816,256]{1,0:T(8,128)(2,1)S(1)} %get-tuple-element.30.right_ref, f32[64,256]{1,0:T(8,128)S(1)} %add_add_fusion.refs_0_.own_ref, f32[64,256]{1,0:T(8,128)S(1)} %collective-permute-done.4.refs_1_.own_other_ref), custom_call_target="tpu_custom_call" | custom-call | flops 614989824 | bytes 2000000 | tf_op jit(solution)/shard_map/halves/pallas_call | solution.py:310
  20.1 0.9 %collective-permute-done.5.refs_1_.first_ref = f32[64,256]{1,0:T(8,128)S(1)} collective-permute-done((f32[64,256]{1,0:T(8,128)S(1)}, f32[64,256]{1,0:T(8,128)S(1)}, u32[]{:S(2)}, u32[]{:S(2)}) %collective-permute-start.5) | collective-permute-done | bytes 65568 | tf_op jit(solution)/shard_map/ppermute | solution.py:254
  21.0 0.1 collective-permute-start.8
  21.1 0.7 %halves.4.refs_0_ = f32[336,544]{1,0:T(8,128)S(1)} custom-call(bf16[816,256]{1,0:T(8,128)(2,1)S(1)} %get-tuple-element.29.left_ref, bf16[816,256]{1,0:T(8,128)(2,1)S(1)} %get-tuple-element.30.right_ref, f32[336,544]{1,0:T(8,128)S(1)} %halves.3.refs_0_, f32[64,256]{1,0:T(8,128)S(1)} %collective-permute-done.5.refs_1_.first_ref), custom_call_target="tpu_custom_call", output_to_operand_aliasing={{}: (2, {})} | custom-call | flops 307494912 | bytes 2000000 | tf_op jit(solution)/shard_map/halves/pallas_call | solution.py:310
  21.8 0.8 %collective-permute-done.7 = f32[64,256]{1,0:T(8,128)S(1)} collective-permute-done((f32[64,256]{1,0:T(8,128)S(1)}, f32[64,256]{1,0:T(8,128)S(1)}, u32[]{:S(2)}, u32[]{:S(2)}) %collective-permute-start.7) | collective-permute-done | bytes 65568 | tf_op jit(solution)/shard_map/ppermute | solution.py:254
  22.6 0.4 %collective-permute-done.6 = f32[64,256]{1,0:T(8,128)S(1)} collective-permute-done((f32[64,256]{1,0:T(8,128)S(1)}, f32[64,256]{1,0:T(8,128)S(1)}, u32[]{:S(2)}, u32[]{:S(2)}) %collective-permute-start.6) | collective-permute-done | bytes 65568 | tf_op jit(solution)/shard_map/ppermute | solution.py:254
  23.1 0.1 collective-permute-start.9
  23.1 0.0 collective-permute-done.8
  23.2 1.3 %halves.5.before_ref = f32[336,544]{1,0:T(8,128)S(1)} custom-call(bf16[816,256]{1,0:T(8,128)(2,1)S(1)} %get-tuple-element.29.left_ref, bf16[816,256]{1,0:T(8,128)(2,1)S(1)} %get-tuple-element.30.right_ref, f32[336,544]{1,0:T(8,128)S(1)} %halves.4.refs_0_, f32[64,256]{1,0:T(8,128)S(1)} %slice_bitcast_fusion.refs_1_.first_other_ref, ...), custom_call_target="tpu_custom_call", output_to_operand_aliasing={{}: (2, {})} | custom-call | flops 922484736 | bytes 2000000 | tf_op jit(solution)/shard_map/halves/pallas_call | solution.py:310
  24.4 0.0 collective-permute-done.9.late_other_ref
  24.5 1.9 %last_half.1 = (f32[64,512]{1,0:T(8,128)}, f32[64,512]{1,0:T(8,128)}, f32[268,536]{1,0:T(8,128)}, f32[64,536]{1,0:T(8,128)}) custom-call(bf16[816,256]{1,0:T(8,128)(2,1)S(1)} %get-tuple-element.29.left_ref, bf16[816,256]{1,0:T(8,128)(2,1)S(1)} %get-tuple-element.30.right_ref, f32[336,544]{1,0:T(8,128)S(1)} %halves.5.before_ref, ...), custom_call_target="tpu_custom_call" | custom-call | flops 614989824 | bytes 2000000 | tf_op jit(solution)/shard_map/last_half/pallas_call | solution.py:345
  (6 shorter events, 0.1 us)
Async XLA Ops:
  3.4 1.4 %collective-permute-start = (f32[64,256]{1,0:T(8,128)S(1)}, f32[64,256]{1,0:T(8,128)S(1)}, u32[]{:S(2)}, u32[]{:S(2)}) collective-permute-start(f32[64,256]{1,0:T(8,128)S(1)} %get-tuple-element.24), channel_id=1, source_target_pairs={{0,1},{1,0},{2,3},{3,2},{4,5},{5,4},{6,7},{7,6},{8,9},{9,8},{10,11... | collective-permute-start | bytes 196616 | tf_op jit(solution)/shard_map/ppermute | solution.py:254
  4.9 8.0 %collective-permute-start.3 = (f32[64,256]{1,0:T(8,128)S(1)}, f32[64,256]{1,0:T(8,128)S(1)}, u32[]{:S(2)}, u32[]{:S(2)}) collective-permute-start(f32[64,256]{1,0:T(8,128)S(1)} %add.15.after_ref), channel_id=1, source_target_pairs={{0,4},{1,5},{2,6},{3,7},{4,0},{5,1},{6,2},{7,3},{8,12},{9,13},{10,... | collective-permute-start | bytes 196616 | tf_op jit(solution)/shard_map/ppermute | solution.py:254
  8.9 6.4 %collective-permute-start.2 = (f32[64,256]{1,0:T(8,128)S(1)}, f32[64,256]{1,0:T(8,128)S(1)}, u32[]{:S(2)}, u32[]{:S(2)}) collective-permute-start(f32[64,256]{1,0:T(8,128)S(1)} %add.15.after_ref), channel_id=1, source_target_pairs={{0,6},{1,7},{2,4},{3,5},{4,2},{5,3},{6,0},{7,1},{8,14},{9,15},{10,... | collective-permute-start | bytes 196616 | tf_op jit(solution)/shard_map/ppermute | solution.py:254
  10.2 5.3 %collective-permute-start.1 = (f32[64,256]{1,0:T(8,128)S(1)}, f32[64,256]{1,0:T(8,128)S(1)}, u32[]{:S(2)}, u32[]{:S(2)}) collective-permute-start(f32[64,256]{1,0:T(8,128)S(1)} %add.15.after_ref), channel_id=1, source_target_pairs={{0,2},{1,3},{2,0},{3,1},{4,6},{5,7},{6,4},{7,5},{8,10},{9,11},{10,... | collective-permute-start | bytes 196616 | tf_op jit(solution)/shard_map/ppermute | solution.py:254
  15.5 3.6 %collective-permute-start.4 = (f32[64,256]{1,0:T(8,128)S(1)}, f32[64,256]{1,0:T(8,128)S(1)}, u32[]{:S(2)}, u32[]{:S(2)}) collective-permute-start(f32[64,256]{1,0:T(8,128)S(1)} %add_add_fusion.refs_0_.own_ref), channel_id=1, source_target_pairs={{0,1},{1,0},{2,3},{3,2},{4,5},{5,4},{6,7},{7,6},{8,9},{9,8},{10,11... | collective-permute-start | bytes 196616 | tf_op jit(solution)/shard_map/ppermute | solution.py:254
  15.6 5.5 %collective-permute-start.5 = (f32[64,256]{1,0:T(8,128)S(1)}, f32[64,256]{1,0:T(8,128)S(1)}, u32[]{:S(2)}, u32[]{:S(2)}) collective-permute-start(f32[64,256]{1,0:T(8,128)S(1)} %add_add_fusion.refs_0_.own_ref), channel_id=1, source_target_pairs={{0,24},{8,16},{16,8},{24,0},{1,25},{9,17},{17,9},{25,1},{2,26},{10... | collective-permute-start | bytes 196616 | tf_op jit(solution)/shard_map/ppermute | solution.py:254
  18.2 4.4 %collective-permute-start.7 = (f32[64,256]{1,0:T(8,128)S(1)}, f32[64,256]{1,0:T(8,128)S(1)}, u32[]{:S(2)}, u32[]{:S(2)}) collective-permute-start(f32[64,256]{1,0:T(8,128)S(1)} %add_add_fusion.refs_0_.own_ref), channel_id=1, source_target_pairs={{0,8},{8,0},{16,24},{24,16},{1,9},{9,1},{17,25},{25,17},{2,10},{10... | collective-permute-start | bytes 196616 | tf_op jit(solution)/shard_map/ppermute | solution.py:254
  18.8 4.3 %collective-permute-start.6 = (f32[64,256]{1,0:T(8,128)S(1)}, f32[64,256]{1,0:T(8,128)S(1)}, u32[]{:S(2)}, u32[]{:S(2)}) collective-permute-start(f32[64,256]{1,0:T(8,128)S(1)} %add_add_fusion.refs_0_.own_ref), channel_id=1, source_target_pairs={{0,16},{8,24},{16,0},{24,8},{1,17},{9,25},{17,1},{25,9},{2,18},{10... | collective-permute-start | bytes 196616 | tf_op jit(solution)/shard_map/ppermute | solution.py:254
  21.0 2.1 %collective-permute-start.8 = (f32[2,64,256]{2,1,0:T(8,128)S(1)}, f32[2,64,256]{2,1,0:T(8,128)S(1)}, u32[]{:S(2)}, u32[]{:S(2)}) collective-permute-start(f32[2,64,256]{2,1,0:T(8,128)S(1)} %pad_maximum_fusion), channel_id=1, source_target_pairs={{0,1},{1,0},{2,3},{3,2},{4,5},{5,4},{6,7},{7,6},{8,9},{9,8},{10,11... | collective-permute-start | bytes 393224 | tf_op jit(solution)/shard_map/ppermute | solution.py:254
  23.1 1.4 %collective-permute-start.9 = (f32[2,64,256]{2,1,0:T(8,128)S(1)}, f32[2,64,256]{2,1,0:T(8,128)S(1)}, u32[]{:S(2)}, u32[]{:S(2)}) collective-permute-start(f32[2,64,256]{2,1,0:T(8,128)S(1)} %pad_maximum_fusion.1.refs_2_.late_ref), channel_id=1, source_target_pairs={{0,1},{1,0},{2,3},{3,2},{4,5},{5,4},{6,7},{7,6},{8,9},{9,8},{10,11... | collective-permute-start | bytes 393224 | tf_op jit(solution)/shard_map/ppermute | solution.py:254

commit v9 on v8

--- a/solution.py
+++ b/solution.py
@@ -91,7 +91,7 @@
 def project(snapshots, basis):
     snaps, states = snapshots.shape
     modes = basis.shape[0]
-    size = 128
+    size = snaps // 2
     hbm = pl.BlockSpec(memory_space=pltpu.HBM)
     vmem = pl.BlockSpec(memory_space=pltpu.VMEM)
     block = jax.ShapeDtypeStruct((modes, snaps // 2), jnp.float32)
@@ -292,7 +292,7 @@
     while len(terms) > 1:
         terms = [terms[i] + terms[i + 1] for i in range(0, len(terms), 2)]
     mine, left, right, reg_rows = lax.optimization_barrier((terms[0], left, right, reg_rows))
-    arriving = [(step, swapped(mine, "tm", step)) for step in range(tm_count - 1, 0, -1)]
+    arriving = [(step, swapped(mine, "tm", step)) for step in [tm_count - 1, *range(1, tm_count - 1)]]
     acc_shape = jax.ShapeDtypeStruct((cols + modes, rows), jnp.float32)
 
     def cost(count):

time: 26.6 us -> 26.5 us (level)
  no operation moved by 1% of the time
where the time goes in v9:
time: 26.5 us; the launch traced here: 26.3 us
  starting transfers between devices  9.87 us (37%)
  Pallas kernels  8.13 us (31%)
  waiting for transfers between devices  6.71 us (25%)
  local copies, waits for them, and re-layouts  0.78 us (3%)
  between operations  0.73 us (3%)
    ppermute x10, starting transfers between devices, swapped(): lax.ppermute(value, axis, [(i, i ^ distance) for i in range(lax.axis_size...  9.87 us
    ppermute x10, waiting for transfers between devices, swapped(): lax.ppermute(value, axis, [(i, i ^ distance) for i in range(lax.axis_size...  6.71 us
    pallas_call x3, Pallas kernels, add_terms(): pl.pallas_call(functools.partial(halves_kernel, cols, len(before)), out_s...  2.92 us
    pallas_call x1, Pallas kernels, project(): pl.pallas_call(project_kernel, out_shape=(block, block), in_specs=[hbm, h...  2.69 us
    pallas_call x1, Pallas kernels, local(): pl.pallas_call(functools.partial(last_kernel, row_block, col_block, chunk...  1.92 us
    dynamic_slice x1, local copies, waits for them, and re-layouts, local(): lax.dynamic_slice_in_dim(reg_weights, first_row, row_block, 0)[None]  0.77 us
    pallas_call x1, Pallas kernels, local(): pl.pallas_call(functools.partial(selector_kernel, row_block, col_block),...  0.6 us
  transfers between devices with their start and end apart: 10, of which 7 were waited for; matrix products, arithmetic and copies ran while one was open for 3% of the time, Pallas kernels for 13%

profile of v9, /device:TPU:0, one launch (start us, length us, event | category | flops | bytes accessed | tf_op | source)
XLA Modules:
  0.0 26.3 jit_solution(17254599179961117422)
XLA Ops:
  0.6 2.7 %project.1 = (f32[64,256]{1,0:T(8,128)S(1)}, f32[64,256]{1,0:T(8,128)S(1)}) custom-call(bf16[64,2048]{1,0:T(8,128)(2,1)} %bitcast.13, bf16[512,2048]{1,0:T(8,128)(2,1)} %snaps_ref.1), custom_call_target="tpu_custom_call" | custom-call | tf_op jit(solution)/shard_map/project/pallas_call | solution.py:98
  3.3 0.5 %collective-permute-start = (f32[64,256]{1,0:T(8,128)S(1)}, f32[64,256]{1,0:T(8,128)S(1)}, u32[]{:S(2)}, u32[]{:S(2)}) collective-permute-start(f32[64,256]{1,0:T(8,128)S(1)} %get-tuple-element.24), channel_id=1, source_target_pairs={{0,1},{1,0},{2,3},{3,2},{4,5},{5,4},{6,7},{7,6},{8,9},{9,8},{10,11... | collective-permute-start | bytes 196616 | tf_op jit(solution)/shard_map/ppermute | solution.py:254
  3.8 0.9 %collective-permute-done = f32[64,256]{1,0:T(8,128)S(1)} collective-permute-done((f32[64,256]{1,0:T(8,128)S(1)}, f32[64,256]{1,0:T(8,128)S(1)}, u32[]{:S(2)}, u32[]{:S(2)}) %collective-permute-start) | collective-permute-done | bytes 65568 | tf_op jit(solution)/shard_map/ppermute | solution.py:254
  4.8 4.0 %collective-permute-start.3 = (f32[64,256]{1,0:T(8,128)S(1)}, f32[64,256]{1,0:T(8,128)S(1)}, u32[]{:S(2)}, u32[]{:S(2)}) collective-permute-start(f32[64,256]{1,0:T(8,128)S(1)} %add.15.after_ref), channel_id=1, source_target_pairs={{0,4},{1,5},{2,6},{3,7},{4,0},{5,1},{6,2},{7,3},{8,12},{9,13},{10,... | collective-permute-start | bytes 196616 | tf_op jit(solution)/shard_map/ppermute | solution.py:254
  8.8 1.3 %collective-permute-start.2 = (f32[64,256]{1,0:T(8,128)S(1)}, f32[64,256]{1,0:T(8,128)S(1)}, u32[]{:S(2)}, u32[]{:S(2)}) collective-permute-start(f32[64,256]{1,0:T(8,128)S(1)} %add.15.after_ref), channel_id=1, source_target_pairs={{0,6},{1,7},{2,4},{3,5},{4,2},{5,3},{6,0},{7,1},{8,14},{9,15},{10,... | collective-permute-start | bytes 196616 | tf_op jit(solution)/shard_map/ppermute | solution.py:254
  10.1 0.2 collective-permute-start.1
  10.3 0.8 %dynamic_slice.3 = f32[536]{0:T(1024)S(1)} dynamic-slice(f32[2144]{0:T(1024)} %param.5, s32[]{:T(128)S(6)} %select_n.3), dynamic_slice_sizes={536} | dynamic-slice | bytes 4292 | tf_op jit(solution)/shard_map/dynamic_slice | solution.py:287
  11.1 0.6 %selectors.1 = (bf16[816,256]{1,0:T(8,128)(2,1)S(1)}, bf16[816,256]{1,0:T(8,128)(2,1)S(1)}) custom-call(f32[64,256]{1,0:T(8,128)S(1)} %add.15.after_ref), custom_call_target="tpu_custom_call" | custom-call | flops 1000000 | bytes 1000000 | tf_op jit(solution)/shard_map/selectors/pallas_call | solution.py:277
  11.7 1.0 %collective-permute-done.3 = f32[64,256]{1,0:T(8,128)S(1)} collective-permute-done((f32[64,256]{1,0:T(8,128)S(1)}, f32[64,256]{1,0:T(8,128)S(1)}, u32[]{:S(2)}, u32[]{:S(2)}) %collective-permute-start.3) | collective-permute-done | bytes 65568 | tf_op jit(solution)/shard_map/ppermute | solution.py:254
  12.8 2.4 %collective-permute-done.2 = f32[64,256]{1,0:T(8,128)S(1)} collective-permute-done((f32[64,256]{1,0:T(8,128)S(1)}, f32[64,256]{1,0:T(8,128)S(1)}, u32[]{:S(2)}, u32[]{:S(2)}) %collective-permute-start.2) | collective-permute-done | bytes 65568 | tf_op jit(solution)/shard_map/ppermute | solution.py:254
  15.2 0.2 collective-permute-done.1
  15.4 0.1 collective-permute-start.4
  15.5 2.7 %collective-permute-start.5 = (f32[64,256]{1,0:T(8,128)S(1)}, f32[64,256]{1,0:T(8,128)S(1)}, u32[]{:S(2)}, u32[]{:S(2)}) collective-permute-start(f32[64,256]{1,0:T(8,128)S(1)} %add_add_fusion.refs_0_.own_ref), channel_id=1, source_target_pairs={{0,24},{8,16},{16,8},{24,0},{1,25},{9,17},{17,9},{25,1},{2,26},{10... | collective-permute-start | bytes 196616 | tf_op jit(solution)/shard_map/ppermute | solution.py:254
  18.1 0.5 %collective-permute-start.7 = (f32[64,256]{1,0:T(8,128)S(1)}, f32[64,256]{1,0:T(8,128)S(1)}, u32[]{:S(2)}, u32[]{:S(2)}) collective-permute-start(f32[64,256]{1,0:T(8,128)S(1)} %add_add_fusion.refs_0_.own_ref), channel_id=1, source_target_pairs={{0,16},{8,24},{16,0},{24,8},{1,17},{9,25},{17,1},{25,9},{2,18},{10... | collective-permute-start | bytes 196616 | tf_op jit(solution)/shard_map/ppermute | solution.py:254
  18.6 0.4 %collective-permute-start.6 = (f32[64,256]{1,0:T(8,128)S(1)}, f32[64,256]{1,0:T(8,128)S(1)}, u32[]{:S(2)}, u32[]{:S(2)}) collective-permute-start(f32[64,256]{1,0:T(8,128)S(1)} %add_add_fusion.refs_0_.own_ref), channel_id=1, source_target_pairs={{0,8},{8,0},{16,24},{24,16},{1,9},{9,1},{17,25},{25,17},{2,10},{10... | collective-permute-start | bytes 196616 | tf_op jit(solution)/shard_map/ppermute | solution.py:254
  19.0 0.0 collective-permute-done.4.refs_1_.own_other_ref
  19.0 1.0 %halves.3.refs_0_ = f32[336,544]{1,0:T(8,128)S(1)} custom-call(bf16[816,256]{1,0:T(8,128)(2,1)S(1)} %get-tuple-element.29.left_ref, bf16[816,256]{1,0:T(8,128)(2,1)S(1)} %get-tuple-element.30.right_ref, f32[64,256]{1,0:T(8,128)S(1)} %add_add_fusion.refs_0_.own_ref, f32[64,256]{1,0:T(8,128)S(1)} %collective-permute-done.4.refs_1_.own_other_ref), custom_call_target="tpu_custom_call" | custom-call | flops 614989824 | bytes 2000000 | tf_op jit(solution)/shard_map/halves/pallas_call | solution.py:310
  20.0 0.8 %collective-permute-done.5.refs_1_.first_ref = f32[64,256]{1,0:T(8,128)S(1)} collective-permute-done((f32[64,256]{1,0:T(8,128)S(1)}, f32[64,256]{1,0:T(8,128)S(1)}, u32[]{:S(2)}, u32[]{:S(2)}) %collective-permute-start.5) | collective-permute-done | bytes 65568 | tf_op jit(solution)/shard_map/ppermute | solution.py:254
  20.9 0.1 collective-permute-start.8
  21.0 0.7 %halves.4.refs_0_ = f32[336,544]{1,0:T(8,128)S(1)} custom-call(bf16[816,256]{1,0:T(8,128)(2,1)S(1)} %get-tuple-element.29.left_ref, bf16[816,256]{1,0:T(8,128)(2,1)S(1)} %get-tuple-element.30.right_ref, f32[336,544]{1,0:T(8,128)S(1)} %halves.3.refs_0_, f32[64,256]{1,0:T(8,128)S(1)} %collective-permute-done.5.refs_1_.first_ref), custom_call_target="tpu_custom_call", output_to_operand_aliasing={{}: (2, {})} | custom-call | flops 307494912 | bytes 2000000 | tf_op jit(solution)/shard_map/halves/pallas_call | solution.py:310
  21.6 0.8 %collective-permute-done.7 = f32[64,256]{1,0:T(8,128)S(1)} collective-permute-done((f32[64,256]{1,0:T(8,128)S(1)}, f32[64,256]{1,0:T(8,128)S(1)}, u32[]{:S(2)}, u32[]{:S(2)}) %collective-permute-start.7) | collective-permute-done | bytes 65568 | tf_op jit(solution)/shard_map/ppermute | solution.py:254
  22.4 0.5 %collective-permute-done.6 = f32[64,256]{1,0:T(8,128)S(1)} collective-permute-done((f32[64,256]{1,0:T(8,128)S(1)}, f32[64,256]{1,0:T(8,128)S(1)}, u32[]{:S(2)}, u32[]{:S(2)}) %collective-permute-start.6) | collective-permute-done | bytes 65568 | tf_op jit(solution)/shard_map/ppermute | solution.py:254
  22.9 0.1 collective-permute-start.9
  23.0 0.0 collective-permute-done.8
  23.0 1.3 %halves.5.before_ref = f32[336,544]{1,0:T(8,128)S(1)} custom-call(bf16[816,256]{1,0:T(8,128)(2,1)S(1)} %get-tuple-element.29.left_ref, bf16[816,256]{1,0:T(8,128)(2,1)S(1)} %get-tuple-element.30.right_ref, f32[336,544]{1,0:T(8,128)S(1)} %halves.4.refs_0_, f32[64,256]{1,0:T(8,128)S(1)} %slice_bitcast_fusion.refs_1_.first_other_ref, ...), custom_call_target="tpu_custom_call", output_to_operand_aliasing={{}: (2, {})} | custom-call | flops 922484736 | bytes 2000000 | tf_op jit(solution)/shard_map/halves/pallas_call | solution.py:310
  24.3 0.0 collective-permute-done.9.late_other_ref
  24.3 1.9 %last_half.1 = (f32[64,512]{1,0:T(8,128)}, f32[64,512]{1,0:T(8,128)}, f32[268,536]{1,0:T(8,128)}, f32[64,536]{1,0:T(8,128)}) custom-call(bf16[816,256]{1,0:T(8,128)(2,1)S(1)} %get-tuple-element.29.left_ref, bf16[816,256]{1,0:T(8,128)(2,1)S(1)} %get-tuple-element.30.right_ref, f32[336,544]{1,0:T(8,128)S(1)} %halves.5.before_ref, ...), custom_call_target="tpu_custom_call" | custom-call | flops 614989824 | bytes 2000000 | tf_op jit(solution)/shard_map/last_half/pallas_call | solution.py:345
  (6 shorter events, 0.1 us)
Async XLA Ops:
  3.3 1.4 %collective-permute-start = (f32[64,256]{1,0:T(8,128)S(1)}, f32[64,256]{1,0:T(8,128)S(1)}, u32[]{:S(2)}, u32[]{:S(2)}) collective-permute-start(f32[64,256]{1,0:T(8,128)S(1)} %get-tuple-element.24), channel_id=1, source_target_pairs={{0,1},{1,0},{2,3},{3,2},{4,5},{5,4},{6,7},{7,6},{8,9},{9,8},{10,11... | collective-permute-start | bytes 196616 | tf_op jit(solution)/shard_map/ppermute | solution.py:254
  4.8 8.0 %collective-permute-start.3 = (f32[64,256]{1,0:T(8,128)S(1)}, f32[64,256]{1,0:T(8,128)S(1)}, u32[]{:S(2)}, u32[]{:S(2)}) collective-permute-start(f32[64,256]{1,0:T(8,128)S(1)} %add.15.after_ref), channel_id=1, source_target_pairs={{0,4},{1,5},{2,6},{3,7},{4,0},{5,1},{6,2},{7,3},{8,12},{9,13},{10,... | collective-permute-start | bytes 196616 | tf_op jit(solution)/shard_map/ppermute | solution.py:254
  8.8 6.4 %collective-permute-start.2 = (f32[64,256]{1,0:T(8,128)S(1)}, f32[64,256]{1,0:T(8,128)S(1)}, u32[]{:S(2)}, u32[]{:S(2)}) collective-permute-start(f32[64,256]{1,0:T(8,128)S(1)} %add.15.after_ref), channel_id=1, source_target_pairs={{0,6},{1,7},{2,4},{3,5},{4,2},{5,3},{6,0},{7,1},{8,14},{9,15},{10,... | collective-permute-start | bytes 196616 | tf_op jit(solution)/shard_map/ppermute | solution.py:254
  10.1 5.3 %collective-permute-start.1 = (f32[64,256]{1,0:T(8,128)S(1)}, f32[64,256]{1,0:T(8,128)S(1)}, u32[]{:S(2)}, u32[]{:S(2)}) collective-permute-start(f32[64,256]{1,0:T(8,128)S(1)} %add.15.after_ref), channel_id=1, source_target_pairs={{0,2},{1,3},{2,0},{3,1},{4,6},{5,7},{6,4},{7,5},{8,10},{9,11},{10,... | collective-permute-start | bytes 196616 | tf_op jit(solution)/shard_map/ppermute | solution.py:254
  15.4 3.6 %collective-permute-start.4 = (f32[64,256]{1,0:T(8,128)S(1)}, f32[64,256]{1,0:T(8,128)S(1)}, u32[]{:S(2)}, u32[]{:S(2)}) collective-permute-start(f32[64,256]{1,0:T(8,128)S(1)} %add_add_fusion.refs_0_.own_ref), channel_id=1, source_target_pairs={{0,1},{1,0},{2,3},{3,2},{4,5},{5,4},{6,7},{7,6},{8,9},{9,8},{10,11... | collective-permute-start | bytes 196616 | tf_op jit(solution)/shard_map/ppermute | solution.py:254
  15.5 5.4 %collective-permute-start.5 = (f32[64,256]{1,0:T(8,128)S(1)}, f32[64,256]{1,0:T(8,128)S(1)}, u32[]{:S(2)}, u32[]{:S(2)}) collective-permute-start(f32[64,256]{1,0:T(8,128)S(1)} %add_add_fusion.refs_0_.own_ref), channel_id=1, source_target_pairs={{0,24},{8,16},{16,8},{24,0},{1,25},{9,17},{17,9},{25,1},{2,26},{10... | collective-permute-start | bytes 196616 | tf_op jit(solution)/shard_map/ppermute | solution.py:254
  18.1 4.3 %collective-permute-start.7 = (f32[64,256]{1,0:T(8,128)S(1)}, f32[64,256]{1,0:T(8,128)S(1)}, u32[]{:S(2)}, u32[]{:S(2)}) collective-permute-start(f32[64,256]{1,0:T(8,128)S(1)} %add_add_fusion.refs_0_.own_ref), channel_id=1, source_target_pairs={{0,16},{8,24},{16,0},{24,8},{1,17},{9,25},{17,1},{25,9},{2,18},{10... | collective-permute-start | bytes 196616 | tf_op jit(solution)/shard_map/ppermute | solution.py:254
  18.6 4.3 %collective-permute-start.6 = (f32[64,256]{1,0:T(8,128)S(1)}, f32[64,256]{1,0:T(8,128)S(1)}, u32[]{:S(2)}, u32[]{:S(2)}) collective-permute-start(f32[64,256]{1,0:T(8,128)S(1)} %add_add_fusion.refs_0_.own_ref), channel_id=1, source_target_pairs={{0,8},{8,0},{16,24},{24,16},{1,9},{9,1},{17,25},{25,17},{2,10},{10... | collective-permute-start | bytes 196616 | tf_op jit(solution)/shard_map/ppermute | solution.py:254
  20.9 2.1 %collective-permute-start.8 = (f32[2,64,256]{2,1,0:T(8,128)S(1)}, f32[2,64,256]{2,1,0:T(8,128)S(1)}, u32[]{:S(2)}, u32[]{:S(2)}) collective-permute-start(f32[2,64,256]{2,1,0:T(8,128)S(1)} %pad_maximum_fusion), channel_id=1, source_target_pairs={{0,1},{1,0},{2,3},{3,2},{4,5},{5,4},{6,7},{7,6},{8,9},{9,8},{10,11... | collective-permute-start | bytes 393224 | tf_op jit(solution)/shard_map/ppermute | solution.py:254
  22.9 1.4 %collective-permute-start.9 = (f32[2,64,256]{2,1,0:T(8,128)S(1)}, f32[2,64,256]{2,1,0:T(8,128)S(1)}, u32[]{:S(2)}, u32[]{:S(2)}) collective-permute-start(f32[2,64,256]{2,1,0:T(8,128)S(1)} %pad_maximum_fusion.1.refs_2_.late_ref), channel_id=1, source_target_pairs={{0,1},{1,0},{2,3},{3,2},{4,5},{5,4},{6,7},{7,6},{8,9},{9,8},{10,11... | collective-permute-start | bytes 393224 | tf_op jit(solution)/shard_map/ppermute | solution.py:254

commit v10 on v9

--- a/solution.py
+++ b/solution.py
@@ -254,6 +254,11 @@
     return lax.ppermute(value, axis, [(i, i ^ distance) for i in range(lax.axis_size(axis))])
 
 
+def shifted(value, distance):
+    count = lax.axis_size("space")
+    return lax.ppermute(value, "space", [(i, (i + distance) % count) for i in range(count)])
+
+
 def local(snapshots, modes_basis, reg_weights):
     feature_count = reg_weights.shape[0]
     snaps_dev = snapshots.shape[0]
@@ -286,11 +291,11 @@
     first_row = after * row_block
     reg_rows = lax.dynamic_slice_in_dim(reg_weights, first_row, row_block, 0)[None]
 
-    steps = list(range(2, space_count, 2))
-    steps = steps[:-2] + steps[-2:][::-1]
-    terms = [half] + [swapped(half, "space", step) for step in steps]
+    terms = [shifted(half, step) for step in range(2, space_count, 2)]
+    terms = [half] + list(lax.optimization_barrier(tuple(terms[::-1]))[::-1])
     while len(terms) > 1:
-        terms = [terms[i] + terms[i + 1] for i in range(0, len(terms), 2)]
+        middle = len(terms) // 2
+        terms = [terms[i] + terms[i + middle] for i in range(middle)]
     mine, left, right, reg_rows = lax.optimization_barrier((terms[0], left, right, reg_rows))
     arriving = [(step, swapped(mine, "tm", step)) for step in [tm_count - 1, *range(1, tm_count - 1)]]
     acc_shape = jax.ShapeDtypeStruct((cols + modes, rows), jnp.float32)

time: 26.5 us -> 26.3 us (level)
  waiting for transfers between devices: 6.71 us -> 5.17 us
  starting transfers between devices: 9.87 us -> 11.2 us
    ppermute x0 -> x3, starting transfers between devices: none -> 6.92 us  [shifted(): lax.ppermute(value, 'space', [(i, (i + distance) % count) for i in range(...]
    ppermute x10 -> x7, starting transfers between devices: 9.87 us -> 4.28 us  [swapped(): lax.ppermute(value, axis, [(i, i ^ distance) for i in range(lax.axis_size...]
    ppermute x10 -> x7, waiting for transfers between devices: 6.71 us -> 2.91 us  [swapped(): lax.ppermute(value, axis, [(i, i ^ distance) for i in range(lax.axis_size...]
    ppermute x0 -> x3, waiting for transfers between devices: none -> 2.26 us  [shifted(): lax.ppermute(value, 'space', [(i, (i + distance) % count) for i in range(...]
  transfers between devices with their start and end apart: 10 -> 10, of which waited for: 7 -> 6; matrix products, arithmetic and copies ran while one was open for 3% -> 3% of each run, Pallas kernels for 13% -> 13%
where the time goes in v10:
time: 26.3 us; the launch traced here: 26.1 us
  starting transfers between devices  11.2 us (43%)
  Pallas kernels  8.13 us (31%)
  waiting for transfers between devices  5.17 us (20%)
  local copies, waits for them, and re-layouts  0.78 us (3%)
  between operations  0.73 us (3%)
    ppermute x3, starting transfers between devices, shifted(): lax.ppermute(value, 'space', [(i, (i + distance) % count) for i in range(...  6.92 us
    ppermute x7, starting transfers between devices, swapped(): lax.ppermute(value, axis, [(i, i ^ distance) for i in range(lax.axis_size...  4.28 us
    pallas_call x3, Pallas kernels, add_terms(): pl.pallas_call(functools.partial(halves_kernel, cols, len(before)), out_s...  2.92 us
    ppermute x7, waiting for transfers between devices, swapped(): lax.ppermute(value, axis, [(i, i ^ distance) for i in range(lax.axis_size...  2.91 us
    pallas_call x1, Pallas kernels, project(): pl.pallas_call(project_kernel, out_shape=(block, block), in_specs=[hbm, h...  2.69 us
    ppermute x3, waiting for transfers between devices, shifted(): lax.ppermute(value, 'space', [(i, (i + distance) % count) for i in range(...  2.26 us
    pallas_call x1, Pallas kernels, local(): pl.pallas_call(functools.partial(last_kernel, row_block, col_block, chunk...  1.92 us
    dynamic_slice x1, local copies, waits for them, and re-layouts, local(): lax.dynamic_slice_in_dim(reg_weights, first_row, row_block, 0)[None]  0.77 us
  transfers between devices with their start and end apart: 10, of which 6 were waited for; matrix products, arithmetic and copies ran while one was open for 3% of the time, Pallas kernels for 13%

profile of v10, /device:TPU:0, one launch (start us, length us, event | category | flops | bytes accessed | tf_op | source)
XLA Modules:
  0.0 26.1 jit_solution(720073383431378616)
XLA Ops:
  0.6 2.7 %project.1 = (f32[64,256]{1,0:T(8,128)S(1)}, f32[64,256]{1,0:T(8,128)S(1)}) custom-call(bf16[64,2048]{1,0:T(8,128)(2,1)} %bitcast.13, bf16[512,2048]{1,0:T(8,128)(2,1)} %snaps_ref.1), custom_call_target="tpu_custom_call" | custom-call | tf_op jit(solution)/shard_map/project/pallas_call | solution.py:98
  3.3 0.5 %collective-permute-start = (f32[64,256]{1,0:T(8,128)S(1)}, f32[64,256]{1,0:T(8,128)S(1)}, u32[]{:S(2)}, u32[]{:S(2)}) collective-permute-start(f32[64,256]{1,0:T(8,128)S(1)} %get-tuple-element.27), channel_id=1, source_target_pairs={{0,1},{1,0},{2,3},{3,2},{4,5},{5,4},{6,7},{7,6},{8,9},{9,8},{10,11... | collective-permute-start | bytes 196616 | tf_op jit(solution)/shard_map/ppermute | solution.py:254
  3.8 0.9 %collective-permute-done = f32[64,256]{1,0:T(8,128)S(1)} collective-permute-done((f32[64,256]{1,0:T(8,128)S(1)}, f32[64,256]{1,0:T(8,128)S(1)}, u32[]{:S(2)}, u32[]{:S(2)}) %collective-permute-start) | collective-permute-done | bytes 65568 | tf_op jit(solution)/shard_map/ppermute | solution.py:254
  4.8 3.0 %collective-permute-start.3 = (f32[64,256]{1,0:T(8,128)S(1)}, f32[64,256]{1,0:T(8,128)S(1)}, u32[]{:S(2)}, u32[]{:S(2)}) collective-permute-start(f32[64,256]{1,0:T(8,128)S(1)} %add.15.after_ref), channel_id=1, source_target_pairs={{0,2},{1,3},{2,4},{3,5},{4,6},{5,7},{6,0},{7,1},{8,10},{9,11},{10,... | collective-permute-start | bytes 196616 | tf_op jit(solution)/shard_map/ppermute | solution.py:259
  7.7 2.6 %collective-permute-start.2 = (f32[64,256]{1,0:T(8,128)S(1)}, f32[64,256]{1,0:T(8,128)S(1)}, u32[]{:S(2)}, u32[]{:S(2)}) collective-permute-start(f32[64,256]{1,0:T(8,128)S(1)} %add.15.after_ref), channel_id=1, source_target_pairs={{0,4},{1,5},{2,6},{3,7},{4,0},{5,1},{6,2},{7,3},{8,12},{9,13},{10,... | collective-permute-start | bytes 196616 | tf_op jit(solution)/shard_map/ppermute | solution.py:259
  10.3 1.3 %collective-permute-start.1 = (f32[64,256]{1,0:T(8,128)S(1)}, f32[64,256]{1,0:T(8,128)S(1)}, u32[]{:S(2)}, u32[]{:S(2)}) collective-permute-start(f32[64,256]{1,0:T(8,128)S(1)} %add.15.after_ref), channel_id=1, source_target_pairs={{0,6},{1,7},{2,0},{3,1},{4,2},{5,3},{6,4},{7,5},{8,14},{9,15},{10,... | collective-permute-start | bytes 196616 | tf_op jit(solution)/shard_map/ppermute | solution.py:259
  11.7 0.8 %dynamic_slice.3 = f32[536]{0:T(1024)S(1)} dynamic-slice(f32[2144]{0:T(1024)} %param.5, s32[]{:T(128)S(6)} %select_n.3), dynamic_slice_sizes={536} | dynamic-slice | bytes 4292 | tf_op jit(solution)/shard_map/dynamic_slice | solution.py:292
  12.5 0.6 %selectors.1 = (bf16[816,256]{1,0:T(8,128)(2,1)S(1)}, bf16[816,256]{1,0:T(8,128)(2,1)S(1)}) custom-call(f32[64,256]{1,0:T(8,128)S(1)} %add.15.after_ref), custom_call_target="tpu_custom_call" | custom-call | flops 1000000 | bytes 1000000 | tf_op jit(solution)/shard_map/selectors/pallas_call | solution.py:282
  13.1 0.0 collective-permute-done.3
  13.1 2.0 %collective-permute-done.2 = f32[64,256]{1,0:T(8,128)S(1)} collective-permute-done((f32[64,256]{1,0:T(8,128)S(1)}, f32[64,256]{1,0:T(8,128)S(1)}, u32[]{:S(2)}, u32[]{:S(2)}) %collective-permute-start.2) | collective-permute-done | bytes 65568 | tf_op jit(solution)/shard_map/ppermute | solution.py:259
  15.1 0.2 collective-permute-done.1
  15.3 0.1 collective-permute-start.4
  15.4 2.5 %collective-permute-start.5 = (f32[64,256]{1,0:T(8,128)S(1)}, f32[64,256]{1,0:T(8,128)S(1)}, u32[]{:S(2)}, u32[]{:S(2)}) collective-permute-start(f32[64,256]{1,0:T(8,128)S(1)} %add_add_fusion.refs_0_.own_ref), channel_id=1, source_target_pairs={{0,24},{8,16},{16,8},{24,0},{1,25},{9,17},{17,9},{25,1},{2,26},{10... | collective-permute-start | bytes 196616 | tf_op jit(solution)/shard_map/ppermute | solution.py:254
  17.9 0.5 %collective-permute-start.7 = (f32[64,256]{1,0:T(8,128)S(1)}, f32[64,256]{1,0:T(8,128)S(1)}, u32[]{:S(2)}, u32[]{:S(2)}) collective-permute-start(f32[64,256]{1,0:T(8,128)S(1)} %add_add_fusion.refs_0_.own_ref), channel_id=1, source_target_pairs={{0,16},{8,24},{16,0},{24,8},{1,17},{9,25},{17,1},{25,9},{2,18},{10... | collective-permute-start | bytes 196616 | tf_op jit(solution)/shard_map/ppermute | solution.py:254
  18.4 0.5 %collective-permute-start.6 = (f32[64,256]{1,0:T(8,128)S(1)}, f32[64,256]{1,0:T(8,128)S(1)}, u32[]{:S(2)}, u32[]{:S(2)}) collective-permute-start(f32[64,256]{1,0:T(8,128)S(1)} %add_add_fusion.refs_0_.own_ref), channel_id=1, source_target_pairs={{0,8},{8,0},{16,24},{24,16},{1,9},{9,1},{17,25},{25,17},{2,10},{10... | collective-permute-start | bytes 196616 | tf_op jit(solution)/shard_map/ppermute | solution.py:254
  19.0 0.0 collective-permute-done.4.refs_1_.own_other_ref
  19.0 1.0 %halves.3.refs_0_ = f32[336,544]{1,0:T(8,128)S(1)} custom-call(bf16[816,256]{1,0:T(8,128)(2,1)S(1)} %get-tuple-element.35.left_ref, bf16[816,256]{1,0:T(8,128)(2,1)S(1)} %get-tuple-element.36.right_ref, f32[64,256]{1,0:T(8,128)S(1)} %add_add_fusion.refs_0_.own_ref, f32[64,256]{1,0:T(8,128)S(1)} %collective-permute-done.4.refs_1_.own_other_ref), custom_call_target="tpu_custom_call" | custom-call | flops 614989824 | bytes 2000000 | tf_op jit(solution)/shard_map/halves/pallas_call | solution.py:315
  20.0 0.9 %collective-permute-done.5.refs_1_.first_ref = f32[64,256]{1,0:T(8,128)S(1)} collective-permute-done((f32[64,256]{1,0:T(8,128)S(1)}, f32[64,256]{1,0:T(8,128)S(1)}, u32[]{:S(2)}, u32[]{:S(2)}) %collective-permute-start.5) | collective-permute-done | bytes 65568 | tf_op jit(solution)/shard_map/ppermute | solution.py:254
  20.9 0.1 collective-permute-start.8
  20.9 0.7 %halves.4.refs_0_ = f32[336,544]{1,0:T(8,128)S(1)} custom-call(bf16[816,256]{1,0:T(8,128)(2,1)S(1)} %get-tuple-element.35.left_ref, bf16[816,256]{1,0:T(8,128)(2,1)S(1)} %get-tuple-element.36.right_ref, f32[336,544]{1,0:T(8,128)S(1)} %halves.3.refs_0_, f32[64,256]{1,0:T(8,128)S(1)} %collective-permute-done.5.refs_1_.first_ref), custom_call_target="tpu_custom_call", output_to_operand_aliasing={{}: (2, {})} | custom-call | flops 307494912 | bytes 2000000 | tf_op jit(solution)/shard_map/halves/pallas_call | solution.py:315
  21.6 0.6 %collective-permute-done.7 = f32[64,256]{1,0:T(8,128)S(1)} collective-permute-done((f32[64,256]{1,0:T(8,128)S(1)}, f32[64,256]{1,0:T(8,128)S(1)}, u32[]{:S(2)}, u32[]{:S(2)}) %collective-permute-start.7) | collective-permute-done | bytes 65568 | tf_op jit(solution)/shard_map/ppermute | solution.py:254
  22.2 0.5 %collective-permute-done.6 = f32[64,256]{1,0:T(8,128)S(1)} collective-permute-done((f32[64,256]{1,0:T(8,128)S(1)}, f32[64,256]{1,0:T(8,128)S(1)}, u32[]{:S(2)}, u32[]{:S(2)}) %collective-permute-start.6) | collective-permute-done | bytes 65568 | tf_op jit(solution)/shard_map/ppermute | solution.py:254
  22.7 0.1 collective-permute-start.9
  22.8 0.0 collective-permute-done.8
  22.8 1.3 %halves.5.before_ref = f32[336,544]{1,0:T(8,128)S(1)} custom-call(bf16[816,256]{1,0:T(8,128)(2,1)S(1)} %get-tuple-element.35.left_ref, bf16[816,256]{1,0:T(8,128)(2,1)S(1)} %get-tuple-element.36.right_ref, f32[336,544]{1,0:T(8,128)S(1)} %halves.4.refs_0_, f32[64,256]{1,0:T(8,128)S(1)} %slice_bitcast_fusion.refs_1_.first_other_ref, ...), custom_call_target="tpu_custom_call", output_to_operand_aliasing={{}: (2, {})} | custom-call | flops 922484736 | bytes 2000000 | tf_op jit(solution)/shard_map/halves/pallas_call | solution.py:315
  24.1 0.0 collective-permute-done.9.late_other_ref
  24.1 1.9 %last_half.1 = (f32[64,512]{1,0:T(8,128)}, f32[64,512]{1,0:T(8,128)}, f32[268,536]{1,0:T(8,128)}, f32[64,536]{1,0:T(8,128)}) custom-call(bf16[816,256]{1,0:T(8,128)(2,1)S(1)} %get-tuple-element.35.left_ref, bf16[816,256]{1,0:T(8,128)(2,1)S(1)} %get-tuple-element.36.right_ref, f32[336,544]{1,0:T(8,128)S(1)} %halves.5.before_ref, ...), custom_call_target="tpu_custom_call" | custom-call | flops 614989824 | bytes 2000000 | tf_op jit(solution)/shard_map/last_half/pallas_call | solution.py:350
  (6 shorter events, 0.1 us)
Async XLA Ops:
  3.3 1.4 %collective-permute-start = (f32[64,256]{1,0:T(8,128)S(1)}, f32[64,256]{1,0:T(8,128)S(1)}, u32[]{:S(2)}, u32[]{:S(2)}) collective-permute-start(f32[64,256]{1,0:T(8,128)S(1)} %get-tuple-element.27), channel_id=1, source_target_pairs={{0,1},{1,0},{2,3},{3,2},{4,5},{5,4},{6,7},{7,6},{8,9},{9,8},{10,11... | collective-permute-start | bytes 196616 | tf_op jit(solution)/shard_map/ppermute | solution.py:254
  4.8 8.3 %collective-permute-start.3 = (f32[64,256]{1,0:T(8,128)S(1)}, f32[64,256]{1,0:T(8,128)S(1)}, u32[]{:S(2)}, u32[]{:S(2)}) collective-permute-start(f32[64,256]{1,0:T(8,128)S(1)} %add.15.after_ref), channel_id=1, source_target_pairs={{0,2},{1,3},{2,4},{3,5},{4,6},{5,7},{6,0},{7,1},{8,10},{9,11},{10,... | collective-permute-start | bytes 196616 | tf_op jit(solution)/shard_map/ppermute | solution.py:259
  7.7 7.3 %collective-permute-start.2 = (f32[64,256]{1,0:T(8,128)S(1)}, f32[64,256]{1,0:T(8,128)S(1)}, u32[]{:S(2)}, u32[]{:S(2)}) collective-permute-start(f32[64,256]{1,0:T(8,128)S(1)} %add.15.after_ref), channel_id=1, source_target_pairs={{0,4},{1,5},{2,6},{3,7},{4,0},{5,1},{6,2},{7,3},{8,12},{9,13},{10,... | collective-permute-start | bytes 196616 | tf_op jit(solution)/shard_map/ppermute | solution.py:259
  10.3 5.0 %collective-permute-start.1 = (f32[64,256]{1,0:T(8,128)S(1)}, f32[64,256]{1,0:T(8,128)S(1)}, u32[]{:S(2)}, u32[]{:S(2)}) collective-permute-start(f32[64,256]{1,0:T(8,128)S(1)} %add.15.after_ref), channel_id=1, source_target_pairs={{0,6},{1,7},{2,0},{3,1},{4,2},{5,3},{6,4},{7,5},{8,14},{9,15},{10,... | collective-permute-start | bytes 196616 | tf_op jit(solution)/shard_map/ppermute | solution.py:259
  15.3 3.6 %collective-permute-start.4 = (f32[64,256]{1,0:T(8,128)S(1)}, f32[64,256]{1,0:T(8,128)S(1)}, u32[]{:S(2)}, u32[]{:S(2)}) collective-permute-start(f32[64,256]{1,0:T(8,128)S(1)} %add_add_fusion.refs_0_.own_ref), channel_id=1, source_target_pairs={{0,1},{1,0},{2,3},{3,2},{4,5},{5,4},{6,7},{7,6},{8,9},{9,8},{10,11... | collective-permute-start | bytes 196616 | tf_op jit(solution)/shard_map/ppermute | solution.py:254
  15.4 5.4 %collective-permute-start.5 = (f32[64,256]{1,0:T(8,128)S(1)}, f32[64,256]{1,0:T(8,128)S(1)}, u32[]{:S(2)}, u32[]{:S(2)}) collective-permute-start(f32[64,256]{1,0:T(8,128)S(1)} %add_add_fusion.refs_0_.own_ref), channel_id=1, source_target_pairs={{0,24},{8,16},{16,8},{24,0},{1,25},{9,17},{17,9},{25,1},{2,26},{10... | collective-permute-start | bytes 196616 | tf_op jit(solution)/shard_map/ppermute | solution.py:254
  17.9 4.3 %collective-permute-start.7 = (f32[64,256]{1,0:T(8,128)S(1)}, f32[64,256]{1,0:T(8,128)S(1)}, u32[]{:S(2)}, u32[]{:S(2)}) collective-permute-start(f32[64,256]{1,0:T(8,128)S(1)} %add_add_fusion.refs_0_.own_ref), channel_id=1, source_target_pairs={{0,16},{8,24},{16,0},{24,8},{1,17},{9,25},{17,1},{25,9},{2,18},{10... | collective-permute-start | bytes 196616 | tf_op jit(solution)/shard_map/ppermute | solution.py:254
  18.4 4.3 %collective-permute-start.6 = (f32[64,256]{1,0:T(8,128)S(1)}, f32[64,256]{1,0:T(8,128)S(1)}, u32[]{:S(2)}, u32[]{:S(2)}) collective-permute-start(f32[64,256]{1,0:T(8,128)S(1)} %add_add_fusion.refs_0_.own_ref), channel_id=1, source_target_pairs={{0,8},{8,0},{16,24},{24,16},{1,9},{9,1},{17,25},{25,17},{2,10},{10... | collective-permute-start | bytes 196616 | tf_op jit(solution)/shard_map/ppermute | solution.py:254
  20.9 1.9 %collective-permute-start.8 = (f32[2,64,256]{2,1,0:T(8,128)S(1)}, f32[2,64,256]{2,1,0:T(8,128)S(1)}, u32[]{:S(2)}, u32[]{:S(2)}) collective-permute-start(f32[2,64,256]{2,1,0:T(8,128)S(1)} %pad_maximum_fusion), channel_id=1, source_target_pairs={{0,1},{1,0},{2,3},{3,2},{4,5},{5,4},{6,7},{7,6},{8,9},{9,8},{10,11... | collective-permute-start | bytes 393224 | tf_op jit(solution)/shard_map/ppermute | solution.py:254
  22.7 1.4 %collective-permute-start.9 = (f32[2,64,256]{2,1,0:T(8,128)S(1)}, f32[2,64,256]{2,1,0:T(8,128)S(1)}, u32[]{:S(2)}, u32[]{:S(2)}) collective-permute-start(f32[2,64,256]{2,1,0:T(8,128)S(1)} %pad_maximum_fusion.1.refs_2_.late_ref), channel_id=1, source_target_pairs={{0,1},{1,0},{2,3},{3,2},{4,5},{5,4},{6,7},{7,6},{8,9},{9,8},{10,11... | collective-permute-start | bytes 393224 | tf_op jit(solution)/shard_map/ppermute | solution.py:254

commit v11 on v10

--- a/solution.py
+++ b/solution.py
@@ -165,10 +165,10 @@
     acc_ref[...] = before_ref[...] + term if has_before else term
 
 
-def edge_columns(time_idx, core, halves, starts, ends):
+def edge_columns(halves, starts, ends):
     count, modes, width = starts.shape
-    for offset, side, block in halves:
-        at = 2 * (time_idx ^ offset) + side
+    for group, side, block in halves:
+        at = 2 * group + side
         starts[at] = block[:, :width]
         ends[at] = block[:, block.shape[1] - width :]
     lane = lax.broadcasted_iota(jnp.int32, (1, width), 1)
@@ -215,8 +215,10 @@
         (core, (own_ref, first_ref, late_ref)),
         (1 - core, (own_other_ref, first_other_ref, late_other_ref)),
     ):
-        halves.extend((offset, side, half) for offset, half in zip(offsets, halves_of(refs)))
-    edge, edge_rates = edge_columns(time_idx, core, halves, starts, ends)
+        for (even, odd), half_block in zip(offsets, halves_of(refs)):
+            group = lax.rem(time_idx + groups - jnp.where(side == 0, even, odd), groups)
+            halves.append((group, side, half_block))
+    edge, edge_rates = edge_columns(halves, starts, ends)
     own = reduced_out[...]
     width = edge.shape[1]
     own_edges = pltpu.roll(edge_rates, lax.rem(width - 4 * time_idx, width), 1)
@@ -259,6 +261,17 @@
     return lax.ppermute(value, "space", [(i, (i + distance) % count) for i in range(count)])
 
 
+def turned(value, distances):
+    tm_count = lax.axis_size("tm")
+    space_count = lax.axis_size("space")
+    perm = []
+    for time in range(tm_count):
+        for space in range(space_count):
+            target = (time + distances[space % 2]) % tm_count
+            perm.append((time * space_count + space, target * space_count + space))
+    return lax.ppermute(value, ("tm", "space"), perm)
+
+
 def local(snapshots, modes_basis, reg_weights):
     feature_count = reg_weights.shape[0]
     snaps_dev = snapshots.shape[0]
@@ -297,7 +310,9 @@
         middle = len(terms) // 2
         terms = [terms[i] + terms[i + middle] for i in range(middle)]
     mine, left, right, reg_rows = lax.optimization_barrier((terms[0], left, right, reg_rows))
-    arriving = [(step, swapped(mine, "tm", step)) for step in [tm_count - 1, *range(1, tm_count - 1)]]
+    orders = list(range(1, tm_count))
+    orders = list(zip(orders[:-2] + orders[-2:][::-1], orders))
+    arriving = [(orders[k], turned(mine, orders[k])) for k in (0, *range(tm_count - 2, 0, -1))]
     acc_shape = jax.ShapeDtypeStruct((cols + modes, rows), jnp.float32)
 
     def cost(count):
@@ -324,7 +339,7 @@
             name="halves",
         )(left, right, *before, *blocks)
 
-    offsets = [0] + [offset for offset, _ in arriving]
+    offsets = [(0, 0)] + [offset for offset, _ in arriving]
     first = arriving[0][1]
     late = [got for _, got in arriving[1:]]
     own_other = swapped(mine, "space", 1)

time: 26.3 us -> 26.3 us (level)
  waiting for transfers between devices: 5.17 us -> 4.14 us
  starting transfers between devices: 11.2 us -> 12.2 us
    ppermute x0 -> x3, starting transfers between devices: none -> 4.53 us  [turned(): return lax.ppermute(value, ('tm', 'space'), perm)]
    ppermute x7 -> x4, starting transfers between devices: 4.28 us -> 0.73 us  [swapped(): lax.ppermute(value, axis, [(i, i ^ distance) for i in range(lax.axis_size...]
    ppermute x7 -> x4, waiting for transfers between devices: 2.91 us -> 0.94 us  [swapped(): lax.ppermute(value, axis, [(i, i ^ distance) for i in range(lax.axis_size...]
    ppermute x0 -> x3, waiting for transfers between devices: none -> 0.94 us  [turned(): return lax.ppermute(value, ('tm', 'space'), perm)]
  transfers between devices with their start and end apart: 10 -> 10, of which waited for: 6 -> 5; matrix products, arithmetic and copies ran while one was open for 3% -> 3% of each run, Pallas kernels for 13% -> 14%
where the time goes in v11:
time: 26.3 us; the launch traced here: 26 us
  starting transfers between devices  12.2 us (46%)
  Pallas kernels  8.12 us (31%)
  waiting for transfers between devices  4.14 us (16%)
  local copies, waits for them, and re-layouts  0.78 us (3%)
  between operations  0.75 us (3%)
    ppermute x3, starting transfers between devices, shifted(): lax.ppermute(value, 'space', [(i, (i + distance) % count) for i in range(...  6.92 us
    ppermute x3, starting transfers between devices, turned(): return lax.ppermute(value, ('tm', 'space'), perm)  4.53 us
    pallas_call x3, Pallas kernels, add_terms(): pl.pallas_call(functools.partial(halves_kernel, cols, len(before)), out_s...  2.92 us
    pallas_call x1, Pallas kernels, project(): pl.pallas_call(project_kernel, out_shape=(block, block), in_specs=[hbm, h...  2.69 us
    ppermute x3, waiting for transfers between devices, shifted(): lax.ppermute(value, 'space', [(i, (i + distance) % count) for i in range(...  2.26 us
    pallas_call x1, Pallas kernels, local(): pl.pallas_call(functools.partial(last_kernel, row_block, col_block, chunk...  1.92 us
    ppermute x4, waiting for transfers between devices, swapped(): lax.ppermute(value, axis, [(i, i ^ distance) for i in range(lax.axis_size...  0.94 us
    ppermute x3, waiting for transfers between devices, turned(): return lax.ppermute(value, ('tm', 'space'), perm)  0.94 us
  transfers between devices with their start and end apart: 10, of which 5 were waited for; matrix products, arithmetic and copies ran while one was open for 3% of the time, Pallas kernels for 14%

profile of v11, /device:TPU:0, one launch (start us, length us, event | category | flops | bytes accessed | tf_op | source)
XLA Modules:
  0.0 26.0 jit_solution(7325890745134939596)
XLA Ops:
  0.6 2.7 %project.1 = (f32[64,256]{1,0:T(8,128)S(1)}, f32[64,256]{1,0:T(8,128)S(1)}) custom-call(bf16[64,2048]{1,0:T(8,128)(2,1)} %bitcast.13, bf16[512,2048]{1,0:T(8,128)(2,1)} %snaps_ref.1), custom_call_target="tpu_custom_call" | custom-call | tf_op jit(solution)/shard_map/project/pallas_call | solution.py:98
  3.3 0.5 %collective-permute-start = (f32[64,256]{1,0:T(8,128)S(1)}, f32[64,256]{1,0:T(8,128)S(1)}, u32[]{:S(2)}, u32[]{:S(2)}) collective-permute-start(f32[64,256]{1,0:T(8,128)S(1)} %get-tuple-element.27), channel_id=1, source_target_pairs={{0,1},{1,0},{2,3},{3,2},{4,5},{5,4},{6,7},{7,6},{8,9},{9,8},{10,11... | collective-permute-start | bytes 196616 | tf_op jit(solution)/shard_map/ppermute | solution.py:256
  3.8 0.9 %collective-permute-done = f32[64,256]{1,0:T(8,128)S(1)} collective-permute-done((f32[64,256]{1,0:T(8,128)S(1)}, f32[64,256]{1,0:T(8,128)S(1)}, u32[]{:S(2)}, u32[]{:S(2)}) %collective-permute-start) | collective-permute-done | bytes 65568 | tf_op jit(solution)/shard_map/ppermute | solution.py:256
  4.8 3.0 %collective-permute-start.3 = (f32[64,256]{1,0:T(8,128)S(1)}, f32[64,256]{1,0:T(8,128)S(1)}, u32[]{:S(2)}, u32[]{:S(2)}) collective-permute-start(f32[64,256]{1,0:T(8,128)S(1)} %add.15.after_ref), channel_id=1, source_target_pairs={{0,2},{1,3},{2,4},{3,5},{4,6},{5,7},{6,0},{7,1},{8,10},{9,11},{10,... | collective-permute-start | bytes 196616 | tf_op jit(solution)/shard_map/ppermute | solution.py:261
  7.7 2.6 %collective-permute-start.2 = (f32[64,256]{1,0:T(8,128)S(1)}, f32[64,256]{1,0:T(8,128)S(1)}, u32[]{:S(2)}, u32[]{:S(2)}) collective-permute-start(f32[64,256]{1,0:T(8,128)S(1)} %add.15.after_ref), channel_id=1, source_target_pairs={{0,4},{1,5},{2,6},{3,7},{4,0},{5,1},{6,2},{7,3},{8,12},{9,13},{10,... | collective-permute-start | bytes 196616 | tf_op jit(solution)/shard_map/ppermute | solution.py:261
  10.3 1.3 %collective-permute-start.1 = (f32[64,256]{1,0:T(8,128)S(1)}, f32[64,256]{1,0:T(8,128)S(1)}, u32[]{:S(2)}, u32[]{:S(2)}) collective-permute-start(f32[64,256]{1,0:T(8,128)S(1)} %add.15.after_ref), channel_id=1, source_target_pairs={{0,6},{1,7},{2,0},{3,1},{4,2},{5,3},{6,4},{7,5},{8,14},{9,15},{10,... | collective-permute-start | bytes 196616 | tf_op jit(solution)/shard_map/ppermute | solution.py:261
  11.7 0.8 %dynamic_slice.3 = f32[536]{0:T(1024)S(1)} dynamic-slice(f32[2144]{0:T(1024)} %param.5, s32[]{:T(128)S(6)} %select_n.3), dynamic_slice_sizes={536} | dynamic-slice | bytes 4292 | tf_op jit(solution)/shard_map/dynamic_slice | solution.py:305
  12.5 0.6 %selectors.1 = (bf16[816,256]{1,0:T(8,128)(2,1)S(1)}, bf16[816,256]{1,0:T(8,128)(2,1)S(1)}) custom-call(f32[64,256]{1,0:T(8,128)S(1)} %add.15.after_ref), custom_call_target="tpu_custom_call" | custom-call | flops 1000000 | bytes 1000000 | tf_op jit(solution)/shard_map/selectors/pallas_call | solution.py:295
  13.1 0.0 collective-permute-done.3
  13.1 2.0 %collective-permute-done.2 = f32[64,256]{1,0:T(8,128)S(1)} collective-permute-done((f32[64,256]{1,0:T(8,128)S(1)}, f32[64,256]{1,0:T(8,128)S(1)}, u32[]{:S(2)}, u32[]{:S(2)}) %collective-permute-start.2) | collective-permute-done | bytes 65568 | tf_op jit(solution)/shard_map/ppermute | solution.py:261
  15.1 0.2 collective-permute-done.1
  15.3 0.1 collective-permute-start.4
  15.4 1.5 %collective-permute-start.5 = (f32[64,256]{1,0:T(8,128)S(1)}, f32[64,256]{1,0:T(8,128)S(1)}, u32[]{:S(2)}, u32[]{:S(2)}) collective-permute-start(f32[64,256]{1,0:T(8,128)S(1)} %add_add_fusion.refs_0_.own_ref), channel_id=1, source_target_pairs={{0,8},{1,9},{2,10},{3,11},{4,12},{5,13},{6,14},{7,15},{8,16},{9,17... | collective-permute-start | bytes 196616 | tf_op jit(solution)/shard_map/ppermute | solution.py:272
  17.0 1.4 %collective-permute-start.7 = (f32[64,256]{1,0:T(8,128)S(1)}, f32[64,256]{1,0:T(8,128)S(1)}, u32[]{:S(2)}, u32[]{:S(2)}) collective-permute-start(f32[64,256]{1,0:T(8,128)S(1)} %add_add_fusion.refs_0_.own_ref), channel_id=1, source_target_pairs={{0,24},{1,17},{2,26},{3,19},{4,28},{5,21},{6,30},{7,23},{8,0},{9,2... | collective-permute-start | bytes 196616 | tf_op jit(solution)/shard_map/ppermute | solution.py:272
  18.4 1.5 %collective-permute-start.6 = (f32[64,256]{1,0:T(8,128)S(1)}, f32[64,256]{1,0:T(8,128)S(1)}, u32[]{:S(2)}, u32[]{:S(2)}) collective-permute-start(f32[64,256]{1,0:T(8,128)S(1)} %add_add_fusion.refs_0_.own_ref), channel_id=1, source_target_pairs={{0,16},{1,25},{2,18},{3,27},{4,20},{5,29},{6,22},{7,31},{8,24},{9,... | collective-permute-start | bytes 196616 | tf_op jit(solution)/shard_map/ppermute | solution.py:272
  20.0 0.0 collective-permute-done.4.refs_1_.own_other_ref
  20.0 1.0 %halves.3.refs_0_ = f32[336,544]{1,0:T(8,128)S(1)} custom-call(bf16[816,256]{1,0:T(8,128)(2,1)S(1)} %get-tuple-element.35.left_ref, bf16[816,256]{1,0:T(8,128)(2,1)S(1)} %get-tuple-element.36.right_ref, f32[64,256]{1,0:T(8,128)S(1)} %add_add_fusion.refs_0_.own_ref, f32[64,256]{1,0:T(8,128)S(1)} %collective-permute-done.4.refs_1_.own_other_ref), custom_call_target="tpu_custom_call" | custom-call | flops 614989824 | bytes 2000000 | tf_op jit(solution)/shard_map/halves/pallas_call | solution.py:330
  21.0 0.0 collective-permute-done.5.refs_1_.first_ref
  21.0 0.1 collective-permute-start.8
  21.1 0.7 %halves.4.refs_0_ = f32[336,544]{1,0:T(8,128)S(1)} custom-call(bf16[816,256]{1,0:T(8,128)(2,1)S(1)} %get-tuple-element.35.left_ref, bf16[816,256]{1,0:T(8,128)(2,1)S(1)} %get-tuple-element.36.right_ref, f32[336,544]{1,0:T(8,128)S(1)} %halves.3.refs_0_, f32[64,256]{1,0:T(8,128)S(1)} %collective-permute-done.5.refs_1_.first_ref), custom_call_target="tpu_custom_call", output_to_operand_aliasing={{}: (2, {})} | custom-call | flops 307494912 | bytes 2000000 | tf_op jit(solution)/shard_map/halves/pallas_call | solution.py:330
  21.7 0.5 %collective-permute-done.7 = f32[64,256]{1,0:T(8,128)S(1)} collective-permute-done((f32[64,256]{1,0:T(8,128)S(1)}, f32[64,256]{1,0:T(8,128)S(1)}, u32[]{:S(2)}, u32[]{:S(2)}) %collective-permute-start.7) | collective-permute-done | bytes 65568 | tf_op jit(solution)/shard_map/ppermute | solution.py:272
  22.2 0.5 %collective-permute-done.6 = f32[64,256]{1,0:T(8,128)S(1)} collective-permute-done((f32[64,256]{1,0:T(8,128)S(1)}, f32[64,256]{1,0:T(8,128)S(1)}, u32[]{:S(2)}, u32[]{:S(2)}) %collective-permute-start.6) | collective-permute-done | bytes 65568 | tf_op jit(solution)/shard_map/ppermute | solution.py:272
  22.7 0.1 collective-permute-start.9
  22.8 0.0 collective-permute-done.8
  22.8 1.3 %halves.5.before_ref = f32[336,544]{1,0:T(8,128)S(1)} custom-call(bf16[816,256]{1,0:T(8,128)(2,1)S(1)} %get-tuple-element.35.left_ref, bf16[816,256]{1,0:T(8,128)(2,1)S(1)} %get-tuple-element.36.right_ref, f32[336,544]{1,0:T(8,128)S(1)} %halves.4.refs_0_, f32[64,256]{1,0:T(8,128)S(1)} %slice_bitcast_fusion.refs_1_.first_other_ref, ...), custom_call_target="tpu_custom_call", output_to_operand_aliasing={{}: (2, {})} | custom-call | flops 922484736 | bytes 2000000 | tf_op jit(solution)/shard_map/halves/pallas_call | solution.py:330
  24.1 0.0 collective-permute-done.9.late_other_ref
  24.1 1.9 %last_half.1 = (f32[64,512]{1,0:T(8,128)}, f32[64,512]{1,0:T(8,128)}, f32[268,536]{1,0:T(8,128)}, f32[64,536]{1,0:T(8,128)}) custom-call(bf16[816,256]{1,0:T(8,128)(2,1)S(1)} %get-tuple-element.35.left_ref, bf16[816,256]{1,0:T(8,128)(2,1)S(1)} %get-tuple-element.36.right_ref, f32[336,544]{1,0:T(8,128)S(1)} %halves.5.before_ref, ...), custom_call_target="tpu_custom_call" | custom-call | flops 614989824 | bytes 2000000 | tf_op jit(solution)/shard_map/last_half/pallas_call | solution.py:365
  (6 shorter events, 0.1 us)
Async XLA Ops:
  3.3 1.4 %collective-permute-start = (f32[64,256]{1,0:T(8,128)S(1)}, f32[64,256]{1,0:T(8,128)S(1)}, u32[]{:S(2)}, u32[]{:S(2)}) collective-permute-start(f32[64,256]{1,0:T(8,128)S(1)} %get-tuple-element.27), channel_id=1, source_target_pairs={{0,1},{1,0},{2,3},{3,2},{4,5},{5,4},{6,7},{7,6},{8,9},{9,8},{10,11... | collective-permute-start | bytes 196616 | tf_op jit(solution)/shard_map/ppermute | solution.py:256
  4.8 8.3 %collective-permute-start.3 = (f32[64,256]{1,0:T(8,128)S(1)}, f32[64,256]{1,0:T(8,128)S(1)}, u32[]{:S(2)}, u32[]{:S(2)}) collective-permute-start(f32[64,256]{1,0:T(8,128)S(1)} %add.15.after_ref), channel_id=1, source_target_pairs={{0,2},{1,3},{2,4},{3,5},{4,6},{5,7},{6,0},{7,1},{8,10},{9,11},{10,... | collective-permute-start | bytes 196616 | tf_op jit(solution)/shard_map/ppermute | solution.py:261
  7.7 7.3 %collective-permute-start.2 = (f32[64,256]{1,0:T(8,128)S(1)}, f32[64,256]{1,0:T(8,128)S(1)}, u32[]{:S(2)}, u32[]{:S(2)}) collective-permute-start(f32[64,256]{1,0:T(8,128)S(1)} %add.15.after_ref), channel_id=1, source_target_pairs={{0,4},{1,5},{2,6},{3,7},{4,0},{5,1},{6,2},{7,3},{8,12},{9,13},{10,... | collective-permute-start | bytes 196616 | tf_op jit(solution)/shard_map/ppermute | solution.py:261
  10.3 5.0 %collective-permute-start.1 = (f32[64,256]{1,0:T(8,128)S(1)}, f32[64,256]{1,0:T(8,128)S(1)}, u32[]{:S(2)}, u32[]{:S(2)}) collective-permute-start(f32[64,256]{1,0:T(8,128)S(1)} %add.15.after_ref), channel_id=1, source_target_pairs={{0,6},{1,7},{2,0},{3,1},{4,2},{5,3},{6,4},{7,5},{8,14},{9,15},{10,... | collective-permute-start | bytes 196616 | tf_op jit(solution)/shard_map/ppermute | solution.py:261
  15.3 4.6 %collective-permute-start.4 = (f32[64,256]{1,0:T(8,128)S(1)}, f32[64,256]{1,0:T(8,128)S(1)}, u32[]{:S(2)}, u32[]{:S(2)}) collective-permute-start(f32[64,256]{1,0:T(8,128)S(1)} %add_add_fusion.refs_0_.own_ref), channel_id=1, source_target_pairs={{0,1},{1,0},{2,3},{3,2},{4,5},{5,4},{6,7},{7,6},{8,9},{9,8},{10,11... | collective-permute-start | bytes 196616 | tf_op jit(solution)/shard_map/ppermute | solution.py:256
  15.4 5.5 %collective-permute-start.5 = (f32[64,256]{1,0:T(8,128)S(1)}, f32[64,256]{1,0:T(8,128)S(1)}, u32[]{:S(2)}, u32[]{:S(2)}) collective-permute-start(f32[64,256]{1,0:T(8,128)S(1)} %add_add_fusion.refs_0_.own_ref), channel_id=1, source_target_pairs={{0,8},{1,9},{2,10},{3,11},{4,12},{5,13},{6,14},{7,15},{8,16},{9,17... | collective-permute-start | bytes 196616 | tf_op jit(solution)/shard_map/ppermute | solution.py:272
  17.0 5.2 %collective-permute-start.7 = (f32[64,256]{1,0:T(8,128)S(1)}, f32[64,256]{1,0:T(8,128)S(1)}, u32[]{:S(2)}, u32[]{:S(2)}) collective-permute-start(f32[64,256]{1,0:T(8,128)S(1)} %add_add_fusion.refs_0_.own_ref), channel_id=1, source_target_pairs={{0,24},{1,17},{2,26},{3,19},{4,28},{5,21},{6,30},{7,23},{8,0},{9,2... | collective-permute-start | bytes 196616 | tf_op jit(solution)/shard_map/ppermute | solution.py:272
  18.4 4.3 %collective-permute-start.6 = (f32[64,256]{1,0:T(8,128)S(1)}, f32[64,256]{1,0:T(8,128)S(1)}, u32[]{:S(2)}, u32[]{:S(2)}) collective-permute-start(f32[64,256]{1,0:T(8,128)S(1)} %add_add_fusion.refs_0_.own_ref), channel_id=1, source_target_pairs={{0,16},{1,25},{2,18},{3,27},{4,20},{5,29},{6,22},{7,31},{8,24},{9,... | collective-permute-start | bytes 196616 | tf_op jit(solution)/shard_map/ppermute | solution.py:272
  21.0 1.8 %collective-permute-start.8 = (f32[2,64,256]{2,1,0:T(8,128)S(1)}, f32[2,64,256]{2,1,0:T(8,128)S(1)}, u32[]{:S(2)}, u32[]{:S(2)}) collective-permute-start(f32[2,64,256]{2,1,0:T(8,128)S(1)} %pad_maximum_fusion), channel_id=1, source_target_pairs={{0,1},{1,0},{2,3},{3,2},{4,5},{5,4},{6,7},{7,6},{8,9},{9,8},{10,11... | collective-permute-start | bytes 393224 | tf_op jit(solution)/shard_map/ppermute | solution.py:256
  22.7 1.4 %collective-permute-start.9 = (f32[2,64,256]{2,1,0:T(8,128)S(1)}, f32[2,64,256]{2,1,0:T(8,128)S(1)}, u32[]{:S(2)}, u32[]{:S(2)}) collective-permute-start(f32[2,64,256]{2,1,0:T(8,128)S(1)} %pad_maximum_fusion.1.refs_2_.late_ref), channel_id=1, source_target_pairs={{0,1},{1,0},{2,3},{3,2},{4,5},{5,4},{6,7},{7,6},{8,9},{9,8},{10,11... | collective-permute-start | bytes 393224 | tf_op jit(solution)/shard_map/ppermute | solution.py:256

commit v12 on v11

--- a/solution.py
+++ b/solution.py
@@ -146,22 +146,11 @@
     )
 
 
-def halves_of(refs):
-    halves = []
-    for ref in refs:
-        halves.extend([ref[...]] if len(ref.shape) == 2 else [ref[slot] for slot in range(ref.shape[0])])
-    return halves
-
-
-def joined(refs):
-    return jnp.concatenate(halves_of(refs), axis=1)
-
-
-def halves_kernel(cols, has_before, left_ref, right_ref, *refs):
+def halves_kernel(cols, half, has_before, left_ref, right_ref, *refs):
     before_ref, refs = (refs[0], refs[1:]) if has_before else (None, refs)
     block_refs, acc_ref, col_scratch = refs[:-2], refs[-2], refs[-1]
-    block = joined(block_refs)
-    term = terms_of(left_ref, right_ref, block, block_refs[0].shape[-1], cols, col_scratch)
+    block = jnp.concatenate([ref[...] for ref in block_refs], axis=1)
+    term = terms_of(left_ref, right_ref, block, half, cols, col_scratch)
     acc_ref[...] = before_ref[...] + term if has_before else term
 
 
@@ -188,17 +177,18 @@
     return jnp.where(inside, edge, 0.0), jnp.where(inside, rates, 0.0)
 
 
-def last_kernel(
-    row_block, col_block, chunks, offsets, left_ref, right_ref, before_ref, reg_ref, own_ref, own_other_ref,
-    first_ref, first_other_ref, late_ref, late_other_ref, reduced_ref, rates_ref, normal_ref, right_side_ref, starts,
-    ends, col_scratch, reduced_out, rates_out, normal_out, right_side_out, sems,
-):
+def last_kernel(row_block, col_block, chunks, wholes, left_ref, right_ref, before_ref, reg_ref, *refs):
+    each = len(wholes)
+    own_ref, got_half_ref, passed_half_ref = refs[:3]
+    got_refs, passed_refs, refs = refs[3 : 3 + each], refs[3 + each : 3 + 2 * each], refs[3 + 2 * each :]
+    reduced_ref, rates_ref, normal_ref, right_side_ref = refs[:4]
+    starts, ends, col_scratch, rates_out, normal_out, right_side_out, sems = refs[4:]
     time_idx = lax.axis_index("tm")
     space_idx = lax.axis_index("space")
     core = space_idx % 2
-    modes, half = own_ref.shape
-    groups = 2 + late_ref.shape[0]
-    snaps = 2 * half
+    modes, snaps = own_ref.shape
+    half = snaps // 2
+    groups = 2 + 2 * each
     cols = round_up(col_block, 16)
     depth = left_ref.shape[1]
     copies = []
@@ -207,19 +197,22 @@
         copies.append(pltpu.make_async_copy(source, target, sems.at[len(copies)]))
         copies[-1].start()
 
-    reduced_out[:, pl.ds(pl.multiple_of(core * half, half), half)] = own_ref[...]
-    reduced_out[:, pl.ds(pl.multiple_of((1 - core) * half, half), half)] = own_other_ref[...]
-    send(reduced_out, reduced_ref)
-    halves = []
-    for side, refs in (
-        (core, (own_ref, first_ref, late_ref)),
-        (1 - core, (own_other_ref, first_other_ref, late_other_ref)),
-    ):
-        for (even, odd), half_block in zip(offsets, halves_of(refs)):
-            group = lax.rem(time_idx + groups - jnp.where(side == 0, even, odd), groups)
-            halves.append((group, side, half_block))
+    send(own_ref, reduced_ref)
+
+    def group_at(steps, side):
+        return lax.rem(time_idx + groups - jnp.where(side == 0, steps[0], steps[1]), groups)
+
+    halves = [
+        (group_at((1, 1), 0), core, got_half_ref[...]),
+        (group_at((1, 1), 0), 1 - core, passed_half_ref[...]),
+    ]
+    blocks = [(time_idx, own_ref)]
+    blocks += [(group_at(steps, core), ref) for steps, ref in zip(wholes, got_refs)]
+    blocks += [(group_at(steps, 1 - core), ref) for steps, ref in zip(wholes, passed_refs)]
+    for group, ref in blocks:
+        halves += [(group, side, ref[:, side * half : (side + 1) * half]) for side in range(2)]
     edge, edge_rates = edge_columns(halves, starts, ends)
-    own = reduced_out[...]
+    own = own_ref[...]
     width = edge.shape[1]
     own_edges = pltpu.roll(edge_rates, lax.rem(width - 4 * time_idx, width), 1)
     lane = lax.broadcasted_iota(jnp.int32, (1, snaps), 1)
@@ -227,7 +220,7 @@
     rates_out[...] = jnp.where(lane == snaps - 1, own_edges[:, 3:4], rates)
     send(rates_out, rates_ref)
 
-    block = joined([late_other_ref])
+    block = jnp.concatenate([ref[...] for ref in passed_refs], axis=1)
     parts = parts_of(block, depth)
     column_side(left_ref, right_ref, parts, inner_rates(block, half), cols, col_scratch)
     scale = 1.0 / (groups * snaps)
@@ -310,9 +303,14 @@
         middle = len(terms) // 2
         terms = [terms[i] + terms[i + middle] for i in range(middle)]
     mine, left, right, reg_rows = lax.optimization_barrier((terms[0], left, right, reg_rows))
-    orders = list(range(1, tm_count))
-    orders = list(zip(orders[:-2] + orders[-2:][::-1], orders))
-    arriving = [(orders[k], turned(mine, orders[k])) for k in (0, *range(tm_count - 2, 0, -1))]
+    core = lax.axis_index("space") % 2
+    own_other = swapped(mine, "space", 1)
+    got_half = turned(mine, (1, 1))
+    own = jnp.concatenate(
+        [jnp.where(core == 0, mine, own_other), jnp.where(core == 0, own_other, mine)], axis=1
+    )
+    wholes = [(tm_count - 1 - k, 2 + k) for k in range((tm_count - 2) // 2)]
+    got = [turned(own, steps) for steps in wholes]
     acc_shape = jax.ShapeDtypeStruct((cols + modes, rows), jnp.float32)
 
     def cost(count):
@@ -328,7 +326,7 @@
         count = sum(block.size for block in blocks) // modes
         before = [] if acc is None else [acc]
         return pl.pallas_call(
-            functools.partial(halves_kernel, cols, len(before)),
+            functools.partial(halves_kernel, cols, half_snaps, len(before)),
             out_shape=acc_shape,
             in_specs=[vmem] * (2 + len(before) + len(blocks)),
             out_specs=vmem,
@@ -339,18 +337,13 @@
             name="halves",
         )(left, right, *before, *blocks)
 
-    offsets = [(0, 0)] + [offset for offset, _ in arriving]
-    first = arriving[0][1]
-    late = [got for _, got in arriving[1:]]
-    own_other = swapped(mine, "space", 1)
-    acc = add_terms(None, [mine, own_other])
-    acc, first = lax.optimization_barrier((acc, first))
-    first_other = swapped(jnp.stack([mine, first]), "space", 1)[1]
-    acc = add_terms(acc, [first])
-    acc, *late = lax.optimization_barrier((acc, *late))
-    late_stack = jnp.stack(late)
-    late_other = swapped(late_stack, "space", 1)
-    acc = add_terms(acc, [first_other, late_stack])
+    acc = add_terms(None, [own])
+    acc, got_half = lax.optimization_barrier((acc, got_half))
+    passed_half = swapped(got_half, "space", 1)
+    acc = add_terms(acc, [got_half, passed_half])
+    acc, *got = lax.optimization_barrier((acc, *got))
+    passed = [swapped(block, "space", 1) for block in got]
+    acc = add_terms(acc, got)
     width = 128
     starts = list(range(0, row_block - width, 2 * width))
     starts = [0] + [start - width for start in starts[1:]] if len(starts) > 1 else [0]
@@ -363,21 +356,21 @@
         jax.ShapeDtypeStruct((modes, row_block), jnp.float32),
     )
     outs = pl.pallas_call(
-        functools.partial(last_kernel, row_block, col_block, chunks, offsets),
+        functools.partial(last_kernel, row_block, col_block, chunks, wholes),
         out_shape=out_shapes,
-        in_specs=[vmem] * 10,
+        in_specs=[vmem] * (7 + 2 * len(wholes)),
         out_specs=(hbm,) * 4,
         scratch_shapes=[
             pltpu.VMEM((2 * tm_count, modes, width), jnp.float32),
             pltpu.VMEM((2 * tm_count, modes, width), jnp.float32),
-            col_scratch(len(late) * half_snaps),
-            *[pltpu.VMEM(shape.shape, shape.dtype) for shape in out_shapes],
+            col_scratch(len(wholes) * snaps_dev),
+            *[pltpu.VMEM(shape.shape, shape.dtype) for shape in out_shapes[1:]],
             pltpu.SemaphoreType.DMA((2 + 2 * len(chunks),)),
         ],
         compiler_params=params,
-        cost_estimate=cost(len(late) * half_snaps),
+        cost_estimate=cost(len(wholes) * snaps_dev),
         name="last_half",
-    )(left, right, acc, reg_rows, mine, own_other, first, first_other, late_stack, late_other)
+    )(left, right, acc, reg_rows, own, got_half, passed_half, *got, *passed)
     return tuple(out.T for out in outs)
 
 

time: 26.3 us -> 26.8 us (1.019)
  waiting for transfers between devices: 4.14 us -> 5.35 us
  starting transfers between devices: 12.2 us -> 11.5 us
    ppermute x4, waiting for transfers between devices: 0.94 us -> 2.35 us  [swapped(): lax.ppermute(value, axis, [(i, i ^ distance) for i in range(lax.axis_size...]
    ppermute x3 -> x2, starting transfers between devices: 4.53 us -> 3.72 us  [turned(): return lax.ppermute(value, ('tm', 'space'), perm)]
    ppermute x3 -> x2, waiting for transfers between devices: 0.94 us -> 0.74 us  [turned(): return lax.ppermute(value, ('tm', 'space'), perm)]
  transfers between devices with their start and end apart: 10 -> 9, of which waited for: 5 -> 6; matrix products, arithmetic and copies ran while one was open for 3% -> 3% of each run, Pallas kernels for 14% -> 13%
where the time goes in v12:
time: 26.8 us; the launch traced here: 26.5 us
  starting transfers between devices  11.5 us (43%)
  Pallas kernels  8.19 us (31%)
  waiting for transfers between devices  5.35 us (20%)
  local copies, waits for them, and re-layouts  0.78 us (3%)
  between operations  0.73 us (3%)
    ppermute x3, starting transfers between devices, shifted(): lax.ppermute(value, 'space', [(i, (i + distance) % count) for i in range(...  6.92 us
    ppermute x2, starting transfers between devices, turned(): return lax.ppermute(value, ('tm', 'space'), perm)  3.72 us
    pallas_call x3, Pallas kernels, add_terms(): pl.pallas_call(functools.partial(halves_kernel, cols, half_snaps, len(bef...  2.98 us
    pallas_call x1, Pallas kernels, project(): pl.pallas_call(project_kernel, out_shape=(block, block), in_specs=[hbm, h...  2.69 us
    ppermute x4, waiting for transfers between devices, swapped(): lax.ppermute(value, axis, [(i, i ^ distance) for i in range(lax.axis_size...  2.35 us
    ppermute x3, waiting for transfers between devices, shifted(): lax.ppermute(value, 'space', [(i, (i + distance) % count) for i in range(...  2.26 us
    pallas_call x1, Pallas kernels, local(): pl.pallas_call(functools.partial(last_kernel, row_block, col_block, chunk...  1.93 us
    ppermute x4, starting transfers between devices, swapped(): lax.ppermute(value, axis, [(i, i ^ distance) for i in range(lax.axis_size...  0.81 us
  transfers between devices with their start and end apart: 9, of which 6 were waited for; matrix products, arithmetic and copies ran while one was open for 3% of the time, Pallas kernels for 13%

profile of v12, /device:TPU:0, one launch (start us, length us, event | category | flops | bytes accessed | tf_op | source)
XLA Modules:
  0.0 26.5 jit_solution(3881250728149344394)
XLA Ops:
  0.6 2.7 %project.1 = (f32[64,256]{1,0:T(8,128)S(1)}, f32[64,256]{1,0:T(8,128)S(1)}) custom-call(bf16[64,2048]{1,0:T(8,128)(2,1)} %bitcast.5, bf16[512,2048]{1,0:T(8,128)(2,1)} %snaps_ref.1), custom_call_target="tpu_custom_call" | custom-call | tf_op jit(solution)/shard_map/project/pallas_call | solution.py:98
  3.3 0.5 %collective-permute-start = (f32[64,256]{1,0:T(8,128)S(1)}, f32[64,256]{1,0:T(8,128)S(1)}, u32[]{:S(2)}, u32[]{:S(2)}) collective-permute-start(f32[64,256]{1,0:T(8,128)S(1)} %get-tuple-element.26), channel_id=1, source_target_pairs={{0,1},{1,0},{2,3},{3,2},{4,5},{5,4},{6,7},{7,6},{8,9},{9,8},{10,11... | collective-permute-start | bytes 196616 | tf_op jit(solution)/shard_map/ppermute | solution.py:249
  3.8 0.9 %collective-permute-done = f32[64,256]{1,0:T(8,128)S(1)} collective-permute-done((f32[64,256]{1,0:T(8,128)S(1)}, f32[64,256]{1,0:T(8,128)S(1)}, u32[]{:S(2)}, u32[]{:S(2)}) %collective-permute-start) | collective-permute-done | bytes 65568 | tf_op jit(solution)/shard_map/ppermute | solution.py:249
  4.8 3.0 %collective-permute-start.3 = (f32[64,256]{1,0:T(8,128)S(1)}, f32[64,256]{1,0:T(8,128)S(1)}, u32[]{:S(2)}, u32[]{:S(2)}) collective-permute-start(f32[64,256]{1,0:T(8,128)S(1)} %add.19.after_ref), channel_id=1, source_target_pairs={{0,2},{1,3},{2,4},{3,5},{4,6},{5,7},{6,0},{7,1},{8,10},{9,11},{10,... | collective-permute-start | bytes 196616 | tf_op jit(solution)/shard_map/ppermute | solution.py:254
  7.7 2.6 %collective-permute-start.2 = (f32[64,256]{1,0:T(8,128)S(1)}, f32[64,256]{1,0:T(8,128)S(1)}, u32[]{:S(2)}, u32[]{:S(2)}) collective-permute-start(f32[64,256]{1,0:T(8,128)S(1)} %add.19.after_ref), channel_id=1, source_target_pairs={{0,4},{1,5},{2,6},{3,7},{4,0},{5,1},{6,2},{7,3},{8,12},{9,13},{10,... | collective-permute-start | bytes 196616 | tf_op jit(solution)/shard_map/ppermute | solution.py:254
  10.3 1.3 %collective-permute-start.1 = (f32[64,256]{1,0:T(8,128)S(1)}, f32[64,256]{1,0:T(8,128)S(1)}, u32[]{:S(2)}, u32[]{:S(2)}) collective-permute-start(f32[64,256]{1,0:T(8,128)S(1)} %add.19.after_ref), channel_id=1, source_target_pairs={{0,6},{1,7},{2,0},{3,1},{4,2},{5,3},{6,4},{7,5},{8,14},{9,15},{10,... | collective-permute-start | bytes 196616 | tf_op jit(solution)/shard_map/ppermute | solution.py:254
  11.7 0.8 %dynamic_slice.3 = f32[536]{0:T(1024)S(1)} dynamic-slice(f32[2144]{0:T(1024)} %param.5, s32[]{:T(128)S(6)} %select_n.22), dynamic_slice_sizes={536} | dynamic-slice | bytes 4292 | tf_op jit(solution)/shard_map/dynamic_slice | solution.py:298
  12.5 0.6 %selectors.1 = (bf16[816,256]{1,0:T(8,128)(2,1)S(1)}, bf16[816,256]{1,0:T(8,128)(2,1)S(1)}) custom-call(f32[64,256]{1,0:T(8,128)S(1)} %add.19.after_ref), custom_call_target="tpu_custom_call" | custom-call | flops 1000000 | bytes 1000000 | tf_op jit(solution)/shard_map/selectors/pallas_call | solution.py:288
  13.1 0.0 collective-permute-done.3
  13.1 2.0 %collective-permute-done.2 = f32[64,256]{1,0:T(8,128)S(1)} collective-permute-done((f32[64,256]{1,0:T(8,128)S(1)}, f32[64,256]{1,0:T(8,128)S(1)}, u32[]{:S(2)}, u32[]{:S(2)}) %collective-permute-start.2) | collective-permute-done | bytes 65568 | tf_op jit(solution)/shard_map/ppermute | solution.py:254
  15.1 0.2 collective-permute-done.1
  15.3 0.1 collective-permute-start.4
  15.4 1.5 %collective-permute-start.5 = (f32[64,256]{1,0:T(8,128)S(1)}, f32[64,256]{1,0:T(8,128)S(1)}, u32[]{:S(2)}, u32[]{:S(2)}) collective-permute-start(f32[64,256]{1,0:T(8,128)S(1)} %add_add_fusion), channel_id=1, source_target_pairs={{0,8},{1,9},{2,10},{3,11},{4,12},{5,13},{6,14},{7,15},{8,16},{9,17... | collective-permute-start | bytes 196616 | tf_op jit(solution)/shard_map/ppermute | solution.py:265
  17.0 0.0 collective-permute-done.4
  17.0 2.2 %collective-permute-start.7 = (f32[64,512]{1,0:T(8,128)S(1)}, f32[64,512]{1,0:T(8,128)S(1)}, u32[]{:S(2)}, u32[]{:S(2)}) collective-permute-start(f32[64,512]{1,0:T(8,128)S(1)} %pad_maximum_fusion.refs_0_), channel_id=1, source_target_pairs={{0,24},{1,17},{2,26},{3,19},{4,28},{5,21},{6,30},{7,23},{8,0},{9,2... | collective-permute-start | bytes 393224 | tf_op jit(solution)/shard_map/ppermute | solution.py:265
  19.2 1.0 %halves.3.refs_0_ = f32[336,544]{1,0:T(8,128)S(1)} custom-call(bf16[816,256]{1,0:T(8,128)(2,1)S(1)} %get-tuple-element.34.left_ref, bf16[816,256]{1,0:T(8,128)(2,1)S(1)} %get-tuple-element.35.right_ref, f32[64,512]{1,0:T(8,128)S(1)} %pad_maximum_fusion.refs_0_), custom_call_target="tpu_custom_call" | custom-call | flops 614989824 | bytes 2000000 | tf_op jit(solution)/shard_map/halves/pallas_call | solution.py:328
  20.2 0.7 %collective-permute-done.5.refs_1_ = f32[64,256]{1,0:T(8,128)S(1)} collective-permute-done((f32[64,256]{1,0:T(8,128)S(1)}, f32[64,256]{1,0:T(8,128)S(1)}, u32[]{:S(2)}, u32[]{:S(2)}) %collective-permute-start.5) | collective-permute-done | bytes 65568 | tf_op jit(solution)/shard_map/ppermute | solution.py:265
  20.9 0.0 collective-permute-start.6
  20.9 1.3 %collective-permute-done.6.refs_2_ = f32[64,256]{1,0:T(8,128)S(1)} collective-permute-done((f32[64,256]{1,0:T(8,128)S(1)}, f32[64,256]{1,0:T(8,128)S(1)}, u32[]{:S(2)}, u32[]{:S(2)}) %collective-permute-start.6) | collective-permute-done | bytes 65568 | tf_op jit(solution)/shard_map/ppermute | solution.py:249
  22.2 1.0 %halves.4.refs_0_ = f32[336,544]{1,0:T(8,128)S(1)} custom-call(bf16[816,256]{1,0:T(8,128)(2,1)S(1)} %get-tuple-element.34.left_ref, bf16[816,256]{1,0:T(8,128)(2,1)S(1)} %get-tuple-element.35.right_ref, f32[336,544]{1,0:T(8,128)S(1)} %halves.3.refs_0_, f32[64,256]{1,0:T(8,128)S(1)} %collective-permute-done.5.refs_1_, ...), custom_call_target="tpu_custom_call", output_to_operand_aliasing={{}: (2, {})} | custom-call | flops 614989824 | bytes 2000000 | tf_op jit(solution)/shard_map/halves/pallas_call | solution.py:328
  23.2 0.0 collective-permute-done.7.refs_1_.refs_3_
  23.2 0.2 collective-permute-start.8
  23.4 1.0 %halves.5.before_ref = f32[336,544]{1,0:T(8,128)S(1)} custom-call(bf16[816,256]{1,0:T(8,128)(2,1)S(1)} %get-tuple-element.34.left_ref, bf16[816,256]{1,0:T(8,128)(2,1)S(1)} %get-tuple-element.35.right_ref, f32[336,544]{1,0:T(8,128)S(1)} %halves.4.refs_0_, f32[64,512]{1,0:T(8,128)S(1)} %collective-permute-done.7.refs_1_.refs_3_), custom_call_target="tpu_custom_call", output_to_operand_aliasing={{}: (2, {})} | custom-call | flops 614989824 | bytes 2000000 | tf_op jit(solution)/shard_map/halves/pallas_call | solution.py:328
  24.4 0.2 collective-permute-done.8.refs_4_
  24.6 1.9 %last_half.1 = (f32[64,512]{1,0:T(8,128)}, f32[64,512]{1,0:T(8,128)}, f32[268,536]{1,0:T(8,128)}, f32[64,536]{1,0:T(8,128)}) custom-call(bf16[816,256]{1,0:T(8,128)(2,1)S(1)} %get-tuple-element.34.left_ref, bf16[816,256]{1,0:T(8,128)(2,1)S(1)} %get-tuple-element.35.right_ref, f32[336,544]{1,0:T(8,128)S(1)} %halves.5.before_ref, ...), custom_call_target="tpu_custom_call" | custom-call | flops 614989824 | bytes 2000000 | tf_op jit(solution)/shard_map/last_half/pallas_call | solution.py:358
  (5 shorter events, 0.1 us)
Async XLA Ops:
  3.3 1.4 %collective-permute-start = (f32[64,256]{1,0:T(8,128)S(1)}, f32[64,256]{1,0:T(8,128)S(1)}, u32[]{:S(2)}, u32[]{:S(2)}) collective-permute-start(f32[64,256]{1,0:T(8,128)S(1)} %get-tuple-element.26), channel_id=1, source_target_pairs={{0,1},{1,0},{2,3},{3,2},{4,5},{5,4},{6,7},{7,6},{8,9},{9,8},{10,11... | collective-permute-start | bytes 196616 | tf_op jit(solution)/shard_map/ppermute | solution.py:249
  4.8 8.3 %collective-permute-start.3 = (f32[64,256]{1,0:T(8,128)S(1)}, f32[64,256]{1,0:T(8,128)S(1)}, u32[]{:S(2)}, u32[]{:S(2)}) collective-permute-start(f32[64,256]{1,0:T(8,128)S(1)} %add.19.after_ref), channel_id=1, source_target_pairs={{0,2},{1,3},{2,4},{3,5},{4,6},{5,7},{6,0},{7,1},{8,10},{9,11},{10,... | collective-permute-start | bytes 196616 | tf_op jit(solution)/shard_map/ppermute | solution.py:254
  7.7 7.3 %collective-permute-start.2 = (f32[64,256]{1,0:T(8,128)S(1)}, f32[64,256]{1,0:T(8,128)S(1)}, u32[]{:S(2)}, u32[]{:S(2)}) collective-permute-start(f32[64,256]{1,0:T(8,128)S(1)} %add.19.after_ref), channel_id=1, source_target_pairs={{0,4},{1,5},{2,6},{3,7},{4,0},{5,1},{6,2},{7,3},{8,12},{9,13},{10,... | collective-permute-start | bytes 196616 | tf_op jit(solution)/shard_map/ppermute | solution.py:254
  10.3 5.0 %collective-permute-start.1 = (f32[64,256]{1,0:T(8,128)S(1)}, f32[64,256]{1,0:T(8,128)S(1)}, u32[]{:S(2)}, u32[]{:S(2)}) collective-permute-start(f32[64,256]{1,0:T(8,128)S(1)} %add.19.after_ref), channel_id=1, source_target_pairs={{0,6},{1,7},{2,0},{3,1},{4,2},{5,3},{6,4},{7,5},{8,14},{9,15},{10,... | collective-permute-start | bytes 196616 | tf_op jit(solution)/shard_map/ppermute | solution.py:254
  15.3 1.6 %collective-permute-start.4 = (f32[64,256]{1,0:T(8,128)S(1)}, f32[64,256]{1,0:T(8,128)S(1)}, u32[]{:S(2)}, u32[]{:S(2)}) collective-permute-start(f32[64,256]{1,0:T(8,128)S(1)} %add_add_fusion), channel_id=1, source_target_pairs={{0,1},{1,0},{2,3},{3,2},{4,5},{5,4},{6,7},{7,6},{8,9},{9,8},{10,11... | collective-permute-start | bytes 196616 | tf_op jit(solution)/shard_map/ppermute | solution.py:249
  15.4 5.5 %collective-permute-start.5 = (f32[64,256]{1,0:T(8,128)S(1)}, f32[64,256]{1,0:T(8,128)S(1)}, u32[]{:S(2)}, u32[]{:S(2)}) collective-permute-start(f32[64,256]{1,0:T(8,128)S(1)} %add_add_fusion), channel_id=1, source_target_pairs={{0,8},{1,9},{2,10},{3,11},{4,12},{5,13},{6,14},{7,15},{8,16},{9,17... | collective-permute-start | bytes 196616 | tf_op jit(solution)/shard_map/ppermute | solution.py:265
  17.0 6.2 %collective-permute-start.7 = (f32[64,512]{1,0:T(8,128)S(1)}, f32[64,512]{1,0:T(8,128)S(1)}, u32[]{:S(2)}, u32[]{:S(2)}) collective-permute-start(f32[64,512]{1,0:T(8,128)S(1)} %pad_maximum_fusion.refs_0_), channel_id=1, source_target_pairs={{0,24},{1,17},{2,26},{3,19},{4,28},{5,21},{6,30},{7,23},{8,0},{9,2... | collective-permute-start | bytes 393224 | tf_op jit(solution)/shard_map/ppermute | solution.py:265
  20.9 1.3 %collective-permute-start.6 = (f32[64,256]{1,0:T(8,128)S(1)}, f32[64,256]{1,0:T(8,128)S(1)}, u32[]{:S(2)}, u32[]{:S(2)}) collective-permute-start(f32[64,256]{1,0:T(8,128)S(1)} %collective-permute-done.5.refs_1_), channel_id=1, source_target_pairs={{0,1},{1,0},{2,3},{3,2},{4,5},{5,4},{6,7},{7,6},{8,9},{9,8},{10,11... | collective-permute-start | bytes 196616 | tf_op jit(solution)/shard_map/ppermute | solution.py:249
  23.2 1.4 %collective-permute-start.8 = (f32[64,512]{1,0:T(8,128)S(1)}, f32[64,512]{1,0:T(8,128)S(1)}, u32[]{:S(2)}, u32[]{:S(2)}) collective-permute-start(f32[64,512]{1,0:T(8,128)S(1)} %collective-permute-done.7.refs_1_.refs_3_), channel_id=1, source_target_pairs={{0,1},{1,0},{2,3},{3,2},{4,5},{5,4},{6,7},{7,6},{8,9},{9,8},{10,11... | collective-permute-start | bytes 393224 | tf_op jit(solution)/shard_map/ppermute | solution.py:249

commit v13 on v12

--- a/solution.py
+++ b/solution.py
@@ -314,7 +314,7 @@
     acc_shape = jax.ShapeDtypeStruct((cols + modes, rows), jnp.float32)
 
     def cost(count):
-        flops = 2 * count * (2 * depth * (cols + rows) + (cols + modes) * rows)
+        flops = 4 * count * (2 * depth * (cols + rows) + (cols + modes) * rows)
         return pl.CostEstimate(flops=flops, bytes_accessed=2 * 10**6, transcendentals=0)
 
     def col_scratch(count):
@@ -340,10 +340,10 @@
     acc = add_terms(None, [own])
     acc, got_half = lax.optimization_barrier((acc, got_half))
     passed_half = swapped(got_half, "space", 1)
-    acc = add_terms(acc, [got_half, passed_half])
+    acc = add_terms(acc, [got_half])
     acc, *got = lax.optimization_barrier((acc, *got))
     passed = [swapped(block, "space", 1) for block in got]
-    acc = add_terms(acc, got)
+    acc = add_terms(acc, [passed_half] + got)
     width = 128
     starts = list(range(0, row_block - width, 2 * width))
     starts = [0] + [start - width for start in starts[1:]] if len(starts) > 1 else [0]

time: 26.8 us -> 25.8 us (0.963)
  waiting for transfers between devices: 5.35 us -> 4.59 us
    ppermute x4, waiting for transfers between devices: 2.35 us -> 0.91 us  [swapped(): lax.ppermute(value, axis, [(i, i ^ distance) for i in range(lax.axis_size...]
    ppermute x2, waiting for transfers between devices: 0.74 us -> 1.42 us  [turned(): return lax.ppermute(value, ('tm', 'space'), perm)]
  transfers between devices with their start and end apart: 9 -> 9, of which waited for: 6 -> 5; matrix products, arithmetic and copies ran while one was open for 3% -> 3% of each run, Pallas kernels for 13% -> 14%
where the time goes in v13:
time: 25.8 us; the launch traced here: 25.6 us
  starting transfers between devices  11.3 us (44%)
  Pallas kernels  8.16 us (32%)
  waiting for transfers between devices  4.59 us (18%)
  local copies, waits for them, and re-layouts  0.78 us (3%)
  between operations  0.73 us (3%)
    ppermute x3, starting transfers between devices, shifted(): lax.ppermute(value, 'space', [(i, (i + distance) % count) for i in range(...  6.92 us
    ppermute x2, starting transfers between devices, turned(): return lax.ppermute(value, ('tm', 'space'), perm)  3.72 us
    pallas_call x3, Pallas kernels, add_terms(): pl.pallas_call(functools.partial(halves_kernel, cols, half_snaps, len(bef...  2.94 us
    pallas_call x1, Pallas kernels, project(): pl.pallas_call(project_kernel, out_shape=(block, block), in_specs=[hbm, h...  2.69 us
    ppermute x3, waiting for transfers between devices, shifted(): lax.ppermute(value, 'space', [(i, (i + distance) % count) for i in range(...  2.26 us
    pallas_call x1, Pallas kernels, local(): pl.pallas_call(functools.partial(last_kernel, row_block, col_block, chunk...  1.93 us
    ppermute x2, waiting for transfers between devices, turned(): return lax.ppermute(value, ('tm', 'space'), perm)  1.42 us
    ppermute x4, waiting for transfers between devices, swapped(): lax.ppermute(value, axis, [(i, i ^ distance) for i in range(lax.axis_size...  0.91 us
  transfers between devices with their start and end apart: 9, of which 5 were waited for; matrix products, arithmetic and copies ran while one was open for 3% of the time, Pallas kernels for 14%

profile of v13, /device:TPU:0, one launch (start us, length us, event | category | flops | bytes accessed | tf_op | source)
XLA Modules:
  0.0 25.6 jit_solution(6506654314515333290)
XLA Ops:
  0.6 2.7 %project.1 = (f32[64,256]{1,0:T(8,128)S(1)}, f32[64,256]{1,0:T(8,128)S(1)}) custom-call(bf16[64,2048]{1,0:T(8,128)(2,1)} %bitcast.5, bf16[512,2048]{1,0:T(8,128)(2,1)} %snaps_ref.1), custom_call_target="tpu_custom_call" | custom-call | tf_op jit(solution)/shard_map/project/pallas_call | solution.py:98
  3.3 0.5 %collective-permute-start = (f32[64,256]{1,0:T(8,128)S(1)}, f32[64,256]{1,0:T(8,128)S(1)}, u32[]{:S(2)}, u32[]{:S(2)}) collective-permute-start(f32[64,256]{1,0:T(8,128)S(1)} %get-tuple-element.26), channel_id=1, source_target_pairs={{0,1},{1,0},{2,3},{3,2},{4,5},{5,4},{6,7},{7,6},{8,9},{9,8},{10,11... | collective-permute-start | bytes 196616 | tf_op jit(solution)/shard_map/ppermute | solution.py:249
  3.8 0.9 %collective-permute-done = f32[64,256]{1,0:T(8,128)S(1)} collective-permute-done((f32[64,256]{1,0:T(8,128)S(1)}, f32[64,256]{1,0:T(8,128)S(1)}, u32[]{:S(2)}, u32[]{:S(2)}) %collective-permute-start) | collective-permute-done | bytes 65568 | tf_op jit(solution)/shard_map/ppermute | solution.py:249
  4.8 3.0 %collective-permute-start.3 = (f32[64,256]{1,0:T(8,128)S(1)}, f32[64,256]{1,0:T(8,128)S(1)}, u32[]{:S(2)}, u32[]{:S(2)}) collective-permute-start(f32[64,256]{1,0:T(8,128)S(1)} %add.19.after_ref), channel_id=1, source_target_pairs={{0,2},{1,3},{2,4},{3,5},{4,6},{5,7},{6,0},{7,1},{8,10},{9,11},{10,... | collective-permute-start | bytes 196616 | tf_op jit(solution)/shard_map/ppermute | solution.py:254
  7.7 2.6 %collective-permute-start.2 = (f32[64,256]{1,0:T(8,128)S(1)}, f32[64,256]{1,0:T(8,128)S(1)}, u32[]{:S(2)}, u32[]{:S(2)}) collective-permute-start(f32[64,256]{1,0:T(8,128)S(1)} %add.19.after_ref), channel_id=1, source_target_pairs={{0,4},{1,5},{2,6},{3,7},{4,0},{5,1},{6,2},{7,3},{8,12},{9,13},{10,... | collective-permute-start | bytes 196616 | tf_op jit(solution)/shard_map/ppermute | solution.py:254
  10.3 1.3 %collective-permute-start.1 = (f32[64,256]{1,0:T(8,128)S(1)}, f32[64,256]{1,0:T(8,128)S(1)}, u32[]{:S(2)}, u32[]{:S(2)}) collective-permute-start(f32[64,256]{1,0:T(8,128)S(1)} %add.19.after_ref), channel_id=1, source_target_pairs={{0,6},{1,7},{2,0},{3,1},{4,2},{5,3},{6,4},{7,5},{8,14},{9,15},{10,... | collective-permute-start | bytes 196616 | tf_op jit(solution)/shard_map/ppermute | solution.py:254
  11.7 0.8 %dynamic_slice.3 = f32[536]{0:T(1024)S(1)} dynamic-slice(f32[2144]{0:T(1024)} %param.5, s32[]{:T(128)S(6)} %select_n.22), dynamic_slice_sizes={536} | dynamic-slice | bytes 4292 | tf_op jit(solution)/shard_map/dynamic_slice | solution.py:298
  12.5 0.6 %selectors.1 = (bf16[816,256]{1,0:T(8,128)(2,1)S(1)}, bf16[816,256]{1,0:T(8,128)(2,1)S(1)}) custom-call(f32[64,256]{1,0:T(8,128)S(1)} %add.19.after_ref), custom_call_target="tpu_custom_call" | custom-call | flops 1000000 | bytes 1000000 | tf_op jit(solution)/shard_map/selectors/pallas_call | solution.py:288
  13.1 0.0 collective-permute-done.3
  13.1 2.0 %collective-permute-done.2 = f32[64,256]{1,0:T(8,128)S(1)} collective-permute-done((f32[64,256]{1,0:T(8,128)S(1)}, f32[64,256]{1,0:T(8,128)S(1)}, u32[]{:S(2)}, u32[]{:S(2)}) %collective-permute-start.2) | collective-permute-done | bytes 65568 | tf_op jit(solution)/shard_map/ppermute | solution.py:254
  15.1 0.2 collective-permute-done.1
  15.3 0.1 collective-permute-start.4
  15.4 1.5 %collective-permute-start.5 = (f32[64,256]{1,0:T(8,128)S(1)}, f32[64,256]{1,0:T(8,128)S(1)}, u32[]{:S(2)}, u32[]{:S(2)}) collective-permute-start(f32[64,256]{1,0:T(8,128)S(1)} %add_add_fusion), channel_id=1, source_target_pairs={{0,8},{1,9},{2,10},{3,11},{4,12},{5,13},{6,14},{7,15},{8,16},{9,17... | collective-permute-start | bytes 196616 | tf_op jit(solution)/shard_map/ppermute | solution.py:265
  17.0 0.0 collective-permute-done.4
  17.0 2.2 %collective-permute-start.6 = (f32[64,512]{1,0:T(8,128)S(1)}, f32[64,512]{1,0:T(8,128)S(1)}, u32[]{:S(2)}, u32[]{:S(2)}) collective-permute-start(f32[64,512]{1,0:T(8,128)S(1)} %pad_maximum_fusion.refs_0_), channel_id=1, source_target_pairs={{0,24},{1,17},{2,26},{3,19},{4,28},{5,21},{6,30},{7,23},{8,0},{9,2... | collective-permute-start | bytes 393224 | tf_op jit(solution)/shard_map/ppermute | solution.py:265
  19.2 1.0 %halves.3.refs_0_ = f32[336,544]{1,0:T(8,128)S(1)} custom-call(bf16[816,256]{1,0:T(8,128)(2,1)S(1)} %get-tuple-element.34.left_ref, bf16[816,256]{1,0:T(8,128)(2,1)S(1)} %get-tuple-element.35.right_ref, f32[64,512]{1,0:T(8,128)S(1)} %pad_maximum_fusion.refs_0_), custom_call_target="tpu_custom_call" | custom-call | flops 1229979648 | bytes 2000000 | tf_op jit(solution)/shard_map/halves/pallas_call | solution.py:328
  20.2 0.7 %collective-permute-done.5.refs_1_ = f32[64,256]{1,0:T(8,128)S(1)} collective-permute-done((f32[64,256]{1,0:T(8,128)S(1)}, f32[64,256]{1,0:T(8,128)S(1)}, u32[]{:S(2)}, u32[]{:S(2)}) %collective-permute-start.5) | collective-permute-done | bytes 65568 | tf_op jit(solution)/shard_map/ppermute | solution.py:265
  20.9 0.0 collective-permute-start.7
  20.9 0.7 %halves.4.refs_0_ = f32[336,544]{1,0:T(8,128)S(1)} custom-call(bf16[816,256]{1,0:T(8,128)(2,1)S(1)} %get-tuple-element.34.left_ref, bf16[816,256]{1,0:T(8,128)(2,1)S(1)} %get-tuple-element.35.right_ref, f32[336,544]{1,0:T(8,128)S(1)} %halves.3.refs_0_, f32[64,256]{1,0:T(8,128)S(1)} %collective-permute-done.5.refs_1_), custom_call_target="tpu_custom_call", output_to_operand_aliasing={{}: (2, {})} | custom-call | flops 614989824 | bytes 2000000 | tf_op jit(solution)/shard_map/halves/pallas_call | solution.py:328
  21.6 0.7 %collective-permute-done.6.refs_2_.refs_3_ = f32[64,512]{1,0:T(8,128)S(1)} collective-permute-done((f32[64,512]{1,0:T(8,128)S(1)}, f32[64,512]{1,0:T(8,128)S(1)}, u32[]{:S(2)}, u32[]{:S(2)}) %collective-permute-start.6) | collective-permute-done | bytes 131104 | tf_op jit(solution)/shard_map/ppermute | solution.py:265
  22.3 0.1 collective-permute-start.8
  22.4 0.0 collective-permute-done.7.refs_1_.refs_2_
  22.4 1.3 %halves.5.before_ref = f32[336,544]{1,0:T(8,128)S(1)} custom-call(bf16[816,256]{1,0:T(8,128)(2,1)S(1)} %get-tuple-element.34.left_ref, bf16[816,256]{1,0:T(8,128)(2,1)S(1)} %get-tuple-element.35.right_ref, f32[336,544]{1,0:T(8,128)S(1)} %halves.4.refs_0_, f32[64,256]{1,0:T(8,128)S(1)} %collective-permute-done.7.refs_1_.refs_2_, ...), custom_call_target="tpu_custom_call", output_to_operand_aliasing={{}: (2, {})} | custom-call | flops 1844969472 | bytes 2000000 | tf_op jit(solution)/shard_map/halves/pallas_call | solution.py:328
  23.6 0.0 collective-permute-done.8.refs_4_
  23.7 1.9 %last_half.1 = (f32[64,512]{1,0:T(8,128)}, f32[64,512]{1,0:T(8,128)}, f32[268,536]{1,0:T(8,128)}, f32[64,536]{1,0:T(8,128)}) custom-call(bf16[816,256]{1,0:T(8,128)(2,1)S(1)} %get-tuple-element.34.left_ref, bf16[816,256]{1,0:T(8,128)(2,1)S(1)} %get-tuple-element.35.right_ref, f32[336,544]{1,0:T(8,128)S(1)} %halves.5.before_ref, ...), custom_call_target="tpu_custom_call" | custom-call | flops 1229979648 | bytes 2000000 | tf_op jit(solution)/shard_map/last_half/pallas_call | solution.py:358
  (5 shorter events, 0.1 us)
Async XLA Ops:
  3.3 1.4 %collective-permute-start = (f32[64,256]{1,0:T(8,128)S(1)}, f32[64,256]{1,0:T(8,128)S(1)}, u32[]{:S(2)}, u32[]{:S(2)}) collective-permute-start(f32[64,256]{1,0:T(8,128)S(1)} %get-tuple-element.26), channel_id=1, source_target_pairs={{0,1},{1,0},{2,3},{3,2},{4,5},{5,4},{6,7},{7,6},{8,9},{9,8},{10,11... | collective-permute-start | bytes 196616 | tf_op jit(solution)/shard_map/ppermute | solution.py:249
  4.8 8.3 %collective-permute-start.3 = (f32[64,256]{1,0:T(8,128)S(1)}, f32[64,256]{1,0:T(8,128)S(1)}, u32[]{:S(2)}, u32[]{:S(2)}) collective-permute-start(f32[64,256]{1,0:T(8,128)S(1)} %add.19.after_ref), channel_id=1, source_target_pairs={{0,2},{1,3},{2,4},{3,5},{4,6},{5,7},{6,0},{7,1},{8,10},{9,11},{10,... | collective-permute-start | bytes 196616 | tf_op jit(solution)/shard_map/ppermute | solution.py:254
  7.7 7.3 %collective-permute-start.2 = (f32[64,256]{1,0:T(8,128)S(1)}, f32[64,256]{1,0:T(8,128)S(1)}, u32[]{:S(2)}, u32[]{:S(2)}) collective-permute-start(f32[64,256]{1,0:T(8,128)S(1)} %add.19.after_ref), channel_id=1, source_target_pairs={{0,4},{1,5},{2,6},{3,7},{4,0},{5,1},{6,2},{7,3},{8,12},{9,13},{10,... | collective-permute-start | bytes 196616 | tf_op jit(solution)/shard_map/ppermute | solution.py:254
  10.3 5.0 %collective-permute-start.1 = (f32[64,256]{1,0:T(8,128)S(1)}, f32[64,256]{1,0:T(8,128)S(1)}, u32[]{:S(2)}, u32[]{:S(2)}) collective-permute-start(f32[64,256]{1,0:T(8,128)S(1)} %add.19.after_ref), channel_id=1, source_target_pairs={{0,6},{1,7},{2,0},{3,1},{4,2},{5,3},{6,4},{7,5},{8,14},{9,15},{10,... | collective-permute-start | bytes 196616 | tf_op jit(solution)/shard_map/ppermute | solution.py:254
  15.3 1.6 %collective-permute-start.4 = (f32[64,256]{1,0:T(8,128)S(1)}, f32[64,256]{1,0:T(8,128)S(1)}, u32[]{:S(2)}, u32[]{:S(2)}) collective-permute-start(f32[64,256]{1,0:T(8,128)S(1)} %add_add_fusion), channel_id=1, source_target_pairs={{0,1},{1,0},{2,3},{3,2},{4,5},{5,4},{6,7},{7,6},{8,9},{9,8},{10,11... | collective-permute-start | bytes 196616 | tf_op jit(solution)/shard_map/ppermute | solution.py:249
  15.4 5.5 %collective-permute-start.5 = (f32[64,256]{1,0:T(8,128)S(1)}, f32[64,256]{1,0:T(8,128)S(1)}, u32[]{:S(2)}, u32[]{:S(2)}) collective-permute-start(f32[64,256]{1,0:T(8,128)S(1)} %add_add_fusion), channel_id=1, source_target_pairs={{0,8},{1,9},{2,10},{3,11},{4,12},{5,13},{6,14},{7,15},{8,16},{9,17... | collective-permute-start | bytes 196616 | tf_op jit(solution)/shard_map/ppermute | solution.py:265
  17.0 5.3 %collective-permute-start.6 = (f32[64,512]{1,0:T(8,128)S(1)}, f32[64,512]{1,0:T(8,128)S(1)}, u32[]{:S(2)}, u32[]{:S(2)}) collective-permute-start(f32[64,512]{1,0:T(8,128)S(1)} %pad_maximum_fusion.refs_0_), channel_id=1, source_target_pairs={{0,24},{1,17},{2,26},{3,19},{4,28},{5,21},{6,30},{7,23},{8,0},{9,2... | collective-permute-start | bytes 393224 | tf_op jit(solution)/shard_map/ppermute | solution.py:265
  20.9 1.4 %collective-permute-start.7 = (f32[64,256]{1,0:T(8,128)S(1)}, f32[64,256]{1,0:T(8,128)S(1)}, u32[]{:S(2)}, u32[]{:S(2)}) collective-permute-start(f32[64,256]{1,0:T(8,128)S(1)} %collective-permute-done.5.refs_1_), channel_id=1, source_target_pairs={{0,1},{1,0},{2,3},{3,2},{4,5},{5,4},{6,7},{7,6},{8,9},{9,8},{10,11... | collective-permute-start | bytes 196616 | tf_op jit(solution)/shard_map/ppermute | solution.py:249
  22.3 1.4 %collective-permute-start.8 = (f32[64,512]{1,0:T(8,128)S(1)}, f32[64,512]{1,0:T(8,128)S(1)}, u32[]{:S(2)}, u32[]{:S(2)}) collective-permute-start(f32[64,512]{1,0:T(8,128)S(1)} %collective-permute-done.6.refs_2_.refs_3_), channel_id=1, source_target_pairs={{0,1},{1,0},{2,3},{3,2},{4,5},{5,4},{6,7},{7,6},{8,9},{9,8},{10,11... | collective-permute-start | bytes 393224 | tf_op jit(solution)/shard_map/ppermute | solution.py:249

commit v14 on v13

--- a/solution.py
+++ b/solution.py
@@ -58,40 +58,39 @@
 
 def project_kernel(basis_ref, snaps_ref, keep_ref, give_ref, basis, held, basis_sem, sems):
     core = lax.axis_index("space") % 2
-    chunks, size, states = held.shape
-    half = chunks // 2 * size
+    half = held.shape[0] // 2
+    states = held.shape[1]
     basis_copy = pltpu.make_async_copy(basis_ref, basis, basis_sem)
     basis_copy.start()
     copies = []
-    for chunk in range(chunks):
-        side, at = divmod(chunk * size, half)
+    for slot, (side, at, size) in enumerate(((0, 0, half), (1, 0, half // 2), (1, half // 2, half // 2))):
         first = pl.multiple_of((core if side else 1 - core) * half + at, size)
+        rows = held.at[pl.ds(side * half + at, size)]
         copies.append(
-            pltpu.make_async_copy(snaps_ref.at[pl.ds(first, size)], held.at[chunk], sems.at[chunk])
+            (side, at, size, pltpu.make_async_copy(snaps_ref.at[pl.ds(first, size)], rows, sems.at[slot]))
         )
-        copies[-1].start()
+        copies[-1][-1].start()
     basis_copy.wait()
     pieces = 4
     step = states // pieces
-    for chunk in range(chunks):
-        copies[chunk].wait()
+    for side, at, size, copy in copies:
+        copy.wait()
+        rows = slice(side * half + at, side * half + at + size)
         terms = [
             lax.dot_general(
                 basis[:, piece * step : (piece + 1) * step],
-                held[chunk, :, piece * step : (piece + 1) * step],
+                held[rows, piece * step : (piece + 1) * step],
                 NT,
                 preferred_element_type=jnp.float32,
             )
             for piece in range(pieces)
         ]
-        side, at = divmod(chunk * size, half)
         (keep_ref if side else give_ref)[:, at : at + size] = tree_sum(terms)
 
 
 def project(snapshots, basis):
     snaps, states = snapshots.shape
     modes = basis.shape[0]
-    size = snaps // 2
     hbm = pl.BlockSpec(memory_space=pltpu.HBM)
     vmem = pl.BlockSpec(memory_space=pltpu.VMEM)
     block = jax.ShapeDtypeStruct((modes, snaps // 2), jnp.float32)
@@ -102,9 +101,9 @@
         out_specs=(vmem, vmem),
         scratch_shapes=[
             pltpu.VMEM(basis.shape, basis.dtype),
-            pltpu.VMEM((snaps // size, size, states), snapshots.dtype),
+            pltpu.VMEM((snaps, states), snapshots.dtype),
             pltpu.SemaphoreType.DMA,
-            pltpu.SemaphoreType.DMA((snaps // size,)),
+            pltpu.SemaphoreType.DMA((3,)),
         ],
         compiler_params=pltpu.CompilerParams(vmem_limit_bytes=55000 * 1024),
         name="project",
@@ -152,6 +151,13 @@
     block = jnp.concatenate([ref[...] for ref in block_refs], axis=1)
     term = terms_of(left_ref, right_ref, block, half, cols, col_scratch)
     acc_ref[...] = before_ref[...] + term if has_before else term
+
+
+def own_kernel(cols, half, left_ref, right_ref, own_ref, acc_ref, reduced_ref, col_scratch, sem):
+    copy = pltpu.make_async_copy(own_ref, reduced_ref, sem)
+    copy.start()
+    acc_ref[...] = terms_of(left_ref, right_ref, own_ref[...], half, cols, col_scratch)
+    copy.wait()
 
 
 def edge_columns(halves, starts, ends):
@@ -181,8 +187,8 @@
     each = len(wholes)
     own_ref, got_half_ref, passed_half_ref = refs[:3]
     got_refs, passed_refs, refs = refs[3 : 3 + each], refs[3 + each : 3 + 2 * each], refs[3 + 2 * each :]
-    reduced_ref, rates_ref, normal_ref, right_side_ref = refs[:4]
-    starts, ends, col_scratch, rates_out, normal_out, right_side_out, sems = refs[4:]
+    rates_ref, normal_ref, right_side_ref = refs[:3]
+    starts, ends, col_scratch, rates_out, normal_out, right_side_out, sems = refs[3:]
     time_idx = lax.axis_index("tm")
     space_idx = lax.axis_index("space")
     core = space_idx % 2
@@ -196,8 +202,6 @@
     def send(source, target):
         copies.append(pltpu.make_async_copy(source, target, sems.at[len(copies)]))
         copies[-1].start()
-
-    send(own_ref, reduced_ref)
 
     def group_at(steps, side):
         return lax.rem(time_idx + groups - jnp.where(side == 0, steps[0], steps[1]), groups)
@@ -337,7 +341,17 @@
             name="halves",
         )(left, right, *before, *blocks)
 
-    acc = add_terms(None, [own])
+    block_shape = jax.ShapeDtypeStruct((modes, snaps_dev), jnp.float32)
+    acc, reduced = pl.pallas_call(
+        functools.partial(own_kernel, cols, half_snaps),
+        out_shape=(acc_shape, block_shape),
+        in_specs=[vmem] * 3,
+        out_specs=(vmem, hbm),
+        scratch_shapes=[col_scratch(snaps_dev), pltpu.SemaphoreType.DMA],
+        compiler_params=params,
+        cost_estimate=cost(snaps_dev),
+        name="own_group",
+    )(left, right, own)
     acc, got_half = lax.optimization_barrier((acc, got_half))
     passed_half = swapped(got_half, "space", 1)
     acc = add_terms(acc, [got_half])
@@ -350,8 +364,7 @@
     ends = starts[1:] + [row_block]
     chunks = [(start, end - start) for start, end in zip(starts, ends)][::-1]
     out_shapes = (
-        jax.ShapeDtypeStruct((modes, snaps_dev), jnp.float32),
-        jax.ShapeDtypeStruct((modes, snaps_dev), jnp.float32),
+        block_shape,
         jax.ShapeDtypeStruct((col_block, row_block), jnp.float32),
         jax.ShapeDtypeStruct((modes, row_block), jnp.float32),
     )
@@ -359,19 +372,19 @@
         functools.partial(last_kernel, row_block, col_block, chunks, wholes),
         out_shape=out_shapes,
         in_specs=[vmem] * (7 + 2 * len(wholes)),
-        out_specs=(hbm,) * 4,
+        out_specs=(hbm,) * 3,
         scratch_shapes=[
             pltpu.VMEM((2 * tm_count, modes, width), jnp.float32),
             pltpu.VMEM((2 * tm_count, modes, width), jnp.float32),
             col_scratch(len(wholes) * snaps_dev),
-            *[pltpu.VMEM(shape.shape, shape.dtype) for shape in out_shapes[1:]],
-            pltpu.SemaphoreType.DMA((2 + 2 * len(chunks),)),
+            *[pltpu.VMEM(shape.shape, shape.dtype) for shape in out_shapes],
+            pltpu.SemaphoreType.DMA((1 + 2 * len(chunks),)),
         ],
         compiler_params=params,
         cost_estimate=cost(len(wholes) * snaps_dev),
         name="last_half",
     )(left, right, acc, reg_rows, own, got_half, passed_half, *got, *passed)
-    return tuple(out.T for out in outs)
+    return tuple(out.T for out in (reduced, *outs))
 
 
 def solution(mesh):

time: 25.8 us -> 25.9 us (level)
    pallas_call x0 -> x1, Pallas kernels: none -> 1.02 us  [local(): pl.pallas_call(functools.partial(own_kernel, cols, half_snaps), out_shape...]
    pallas_call x3 -> x2, Pallas kernels: 2.94 us -> 1.94 us  [add_terms(): pl.pallas_call(functools.partial(halves_kernel, cols, half_snaps, len(bef...]
where the time goes in v14:
time: 25.9 us; the launch traced here: 25.7 us
  starting transfers between devices  11.3 us (44%)
  Pallas kernels  8.32 us (32%)
  waiting for transfers between devices  4.56 us (18%)
  local copies, waits for them, and re-layouts  0.78 us (3%)
  between operations  0.73 us (3%)
    ppermute x3, starting transfers between devices, shifted(): lax.ppermute(value, 'space', [(i, (i + distance) % count) for i in range(...  6.92 us
    ppermute x2, starting transfers between devices, turned(): return lax.ppermute(value, ('tm', 'space'), perm)  3.72 us
    pallas_call x1, Pallas kernels, project(): pl.pallas_call(project_kernel, out_shape=(block, block), in_specs=[hbm, h...  2.83 us
    ppermute x3, waiting for transfers between devices, shifted(): lax.ppermute(value, 'space', [(i, (i + distance) % count) for i in range(...  2.26 us
    pallas_call x2, Pallas kernels, add_terms(): pl.pallas_call(functools.partial(halves_kernel, cols, half_snaps, len(bef...  1.94 us
    pallas_call x1, Pallas kernels, local(): pl.pallas_call(functools.partial(last_kernel, row_block, col_block, chunk...  1.93 us
    ppermute x2, waiting for transfers between devices, turned(): return lax.ppermute(value, ('tm', 'space'), perm)  1.4 us
    pallas_call x1, Pallas kernels, local(): pl.pallas_call(functools.partial(own_kernel, cols, half_snaps), out_shape...  1.02 us
  transfers between devices with their start and end apart: 9, of which 5 were waited for; matrix products, arithmetic and copies ran while one was open for 3% of the time, Pallas kernels for 14%

profile of v14, /device:TPU:0, one launch (start us, length us, event | category | flops | bytes accessed | tf_op | source)
XLA Modules:
  0.0 25.7 jit_solution(338809163476758117)
XLA Ops:
  0.6 2.8 %project.1 = (f32[64,256]{1,0:T(8,128)S(1)}, f32[64,256]{1,0:T(8,128)S(1)}) custom-call(bf16[64,2048]{1,0:T(8,128)(2,1)} %bitcast.5, bf16[512,2048]{1,0:T(8,128)(2,1)} %snaps_ref.1), custom_call_target="tpu_custom_call" | custom-call | tf_op jit(solution)/shard_map/project/pallas_call | solution.py:97
  3.5 0.5 %collective-permute-start = (f32[64,256]{1,0:T(8,128)S(1)}, f32[64,256]{1,0:T(8,128)S(1)}, u32[]{:S(2)}, u32[]{:S(2)}) collective-permute-start(f32[64,256]{1,0:T(8,128)S(1)} %get-tuple-element.27), channel_id=1, source_target_pairs={{0,1},{1,0},{2,3},{3,2},{4,5},{5,4},{6,7},{7,6},{8,9},{9,8},{10,11... | collective-permute-start | bytes 196616 | tf_op jit(solution)/shard_map/ppermute | solution.py:253
  4.0 0.9 %collective-permute-done = f32[64,256]{1,0:T(8,128)S(1)} collective-permute-done((f32[64,256]{1,0:T(8,128)S(1)}, f32[64,256]{1,0:T(8,128)S(1)}, u32[]{:S(2)}, u32[]{:S(2)}) %collective-permute-start) | collective-permute-done | bytes 65568 | tf_op jit(solution)/shard_map/ppermute | solution.py:253
  4.9 3.0 %collective-permute-start.3 = (f32[64,256]{1,0:T(8,128)S(1)}, f32[64,256]{1,0:T(8,128)S(1)}, u32[]{:S(2)}, u32[]{:S(2)}) collective-permute-start(f32[64,256]{1,0:T(8,128)S(1)} %add.19.after_ref), channel_id=1, source_target_pairs={{0,2},{1,3},{2,4},{3,5},{4,6},{5,7},{6,0},{7,1},{8,10},{9,11},{10,... | collective-permute-start | bytes 196616 | tf_op jit(solution)/shard_map/ppermute | solution.py:258
  7.9 2.6 %collective-permute-start.2 = (f32[64,256]{1,0:T(8,128)S(1)}, f32[64,256]{1,0:T(8,128)S(1)}, u32[]{:S(2)}, u32[]{:S(2)}) collective-permute-start(f32[64,256]{1,0:T(8,128)S(1)} %add.19.after_ref), channel_id=1, source_target_pairs={{0,4},{1,5},{2,6},{3,7},{4,0},{5,1},{6,2},{7,3},{8,12},{9,13},{10,... | collective-permute-start | bytes 196616 | tf_op jit(solution)/shard_map/ppermute | solution.py:258
  10.5 1.3 %collective-permute-start.1 = (f32[64,256]{1,0:T(8,128)S(1)}, f32[64,256]{1,0:T(8,128)S(1)}, u32[]{:S(2)}, u32[]{:S(2)}) collective-permute-start(f32[64,256]{1,0:T(8,128)S(1)} %add.19.after_ref), channel_id=1, source_target_pairs={{0,6},{1,7},{2,0},{3,1},{4,2},{5,3},{6,4},{7,5},{8,14},{9,15},{10,... | collective-permute-start | bytes 196616 | tf_op jit(solution)/shard_map/ppermute | solution.py:258
  11.8 0.8 %dynamic_slice.3 = f32[536]{0:T(1024)S(1)} dynamic-slice(f32[2144]{0:T(1024)} %param.5, s32[]{:T(128)S(6)} %select_n.22), dynamic_slice_sizes={536} | dynamic-slice | bytes 4292 | tf_op jit(solution)/shard_map/dynamic_slice | solution.py:302
  12.6 0.6 %selectors.1 = (bf16[816,256]{1,0:T(8,128)(2,1)S(1)}, bf16[816,256]{1,0:T(8,128)(2,1)S(1)}) custom-call(f32[64,256]{1,0:T(8,128)S(1)} %add.19.after_ref), custom_call_target="tpu_custom_call" | custom-call | flops 1000000 | bytes 1000000 | tf_op jit(solution)/shard_map/selectors/pallas_call | solution.py:292
  13.2 0.0 collective-permute-done.3
  13.2 2.0 %collective-permute-done.2 = f32[64,256]{1,0:T(8,128)S(1)} collective-permute-done((f32[64,256]{1,0:T(8,128)S(1)}, f32[64,256]{1,0:T(8,128)S(1)}, u32[]{:S(2)}, u32[]{:S(2)}) %collective-permute-start.2) | collective-permute-done | bytes 65568 | tf_op jit(solution)/shard_map/ppermute | solution.py:258
  15.2 0.2 collective-permute-done.1
  15.5 0.1 collective-permute-start.4
  15.6 1.5 %collective-permute-start.5 = (f32[64,256]{1,0:T(8,128)S(1)}, f32[64,256]{1,0:T(8,128)S(1)}, u32[]{:S(2)}, u32[]{:S(2)}) collective-permute-start(f32[64,256]{1,0:T(8,128)S(1)} %add_add_fusion), channel_id=1, source_target_pairs={{0,8},{1,9},{2,10},{3,11},{4,12},{5,13},{6,14},{7,15},{8,16},{9,17... | collective-permute-start | bytes 196616 | tf_op jit(solution)/shard_map/ppermute | solution.py:269
  17.1 0.0 collective-permute-done.4
  17.2 2.2 %collective-permute-start.6 = (f32[64,512]{1,0:T(8,128)S(1)}, f32[64,512]{1,0:T(8,128)S(1)}, u32[]{:S(2)}, u32[]{:S(2)}) collective-permute-start(f32[64,512]{1,0:T(8,128)S(1)} %pad_maximum_fusion.own_ref.refs_0_), channel_id=1, source_target_pairs={{0,24},{1,17},{2,26},{3,19},{4,28},{5,21},{6,30},{7,23},{8,0},{9,2... | collective-permute-start | bytes 393224 | tf_op jit(solution)/shard_map/ppermute | solution.py:269
  19.3 1.0 %own_group.1 = (f32[336,544]{1,0:T(8,128)S(1)}, f32[64,512]{1,0:T(8,128)}) custom-call(bf16[816,256]{1,0:T(8,128)(2,1)S(1)} %get-tuple-element.35.left_ref, bf16[816,256]{1,0:T(8,128)(2,1)S(1)} %get-tuple-element.36.right_ref, f32[64,512]{1,0:T(8,128)S(1)} %pad_maximum_fusion.own_ref.refs_0_), custom_call_target="tpu_custom_call" | custom-call | flops 1229979648 | bytes 2000000 | tf_op jit(solution)/shard_map/own_group/pallas_call | solution.py:345
  20.4 0.7 %collective-permute-done.5.refs_1_ = f32[64,256]{1,0:T(8,128)S(1)} collective-permute-done((f32[64,256]{1,0:T(8,128)S(1)}, f32[64,256]{1,0:T(8,128)S(1)}, u32[]{:S(2)}, u32[]{:S(2)}) %collective-permute-start.5) | collective-permute-done | bytes 65568 | tf_op jit(solution)/shard_map/ppermute | solution.py:269
  21.1 0.0 collective-permute-start.7
  21.1 0.7 %halves.2.refs_0_ = f32[336,544]{1,0:T(8,128)S(1)} custom-call(bf16[816,256]{1,0:T(8,128)(2,1)S(1)} %get-tuple-element.35.left_ref, bf16[816,256]{1,0:T(8,128)(2,1)S(1)} %get-tuple-element.36.right_ref, f32[336,544]{1,0:T(8,128)S(1)} %get-tuple-element.40.refs_0_, f32[64,256]{1,0:T(8,128)S(1)} %collective-permute-done.5.refs_1_), custom_call_target="tpu_custom_call", output_to_operand_aliasing={{}: (2, {})} | custom-call | flops 614989824 | bytes 2000000 | tf_op jit(solution)/shard_map/halves/pallas_call | solution.py:332
  21.8 0.7 %collective-permute-done.6.refs_2_.refs_3_ = f32[64,512]{1,0:T(8,128)S(1)} collective-permute-done((f32[64,512]{1,0:T(8,128)S(1)}, f32[64,512]{1,0:T(8,128)S(1)}, u32[]{:S(2)}, u32[]{:S(2)}) %collective-permute-start.6) | collective-permute-done | bytes 131104 | tf_op jit(solution)/shard_map/ppermute | solution.py:269
  22.4 0.1 collective-permute-start.8
  22.5 0.0 collective-permute-done.7.refs_1_.refs_2_
  22.5 1.3 %halves.3.before_ref = f32[336,544]{1,0:T(8,128)S(1)} custom-call(bf16[816,256]{1,0:T(8,128)(2,1)S(1)} %get-tuple-element.35.left_ref, bf16[816,256]{1,0:T(8,128)(2,1)S(1)} %get-tuple-element.36.right_ref, f32[336,544]{1,0:T(8,128)S(1)} %halves.2.refs_0_, f32[64,256]{1,0:T(8,128)S(1)} %collective-permute-done.7.refs_1_.refs_2_, ...), custom_call_target="tpu_custom_call", output_to_operand_aliasing={{}: (2, {})} | custom-call | flops 1844969472 | bytes 2000000 | tf_op jit(solution)/shard_map/halves/pallas_call | solution.py:332
  23.8 0.0 collective-permute-done.8.refs_4_
  23.8 1.9 %last_half.1 = (f32[64,512]{1,0:T(8,128)}, f32[268,536]{1,0:T(8,128)}, f32[64,536]{1,0:T(8,128)}) custom-call(bf16[816,256]{1,0:T(8,128)(2,1)S(1)} %get-tuple-element.35.left_ref, bf16[816,256]{1,0:T(8,128)(2,1)S(1)} %get-tuple-element.36.right_ref, f32[336,544]{1,0:T(8,128)S(1)} %halves.3.before_ref, f32[1,536]{1,0:T(1,128)S(1)} %broadcast_in_dim.3.reg_ref, ...), custom_call_target="tpu_custom_call" | custom-call | flops 1229979648 | bytes 2000000 | tf_op jit(solution)/shard_map/last_half/pallas_call | solution.py:371
  (5 shorter events, 0.1 us)
Async XLA Ops:
  3.5 1.4 %collective-permute-start = (f32[64,256]{1,0:T(8,128)S(1)}, f32[64,256]{1,0:T(8,128)S(1)}, u32[]{:S(2)}, u32[]{:S(2)}) collective-permute-start(f32[64,256]{1,0:T(8,128)S(1)} %get-tuple-element.27), channel_id=1, source_target_pairs={{0,1},{1,0},{2,3},{3,2},{4,5},{5,4},{6,7},{7,6},{8,9},{9,8},{10,11... | collective-permute-start | bytes 196616 | tf_op jit(solution)/shard_map/ppermute | solution.py:253
  4.9 8.3 %collective-permute-start.3 = (f32[64,256]{1,0:T(8,128)S(1)}, f32[64,256]{1,0:T(8,128)S(1)}, u32[]{:S(2)}, u32[]{:S(2)}) collective-permute-start(f32[64,256]{1,0:T(8,128)S(1)} %add.19.after_ref), channel_id=1, source_target_pairs={{0,2},{1,3},{2,4},{3,5},{4,6},{5,7},{6,0},{7,1},{8,10},{9,11},{10,... | collective-permute-start | bytes 196616 | tf_op jit(solution)/shard_map/ppermute | solution.py:258
  7.9 7.3 %collective-permute-start.2 = (f32[64,256]{1,0:T(8,128)S(1)}, f32[64,256]{1,0:T(8,128)S(1)}, u32[]{:S(2)}, u32[]{:S(2)}) collective-permute-start(f32[64,256]{1,0:T(8,128)S(1)} %add.19.after_ref), channel_id=1, source_target_pairs={{0,4},{1,5},{2,6},{3,7},{4,0},{5,1},{6,2},{7,3},{8,12},{9,13},{10,... | collective-permute-start | bytes 196616 | tf_op jit(solution)/shard_map/ppermute | solution.py:258
  10.5 5.0 %collective-permute-start.1 = (f32[64,256]{1,0:T(8,128)S(1)}, f32[64,256]{1,0:T(8,128)S(1)}, u32[]{:S(2)}, u32[]{:S(2)}) collective-permute-start(f32[64,256]{1,0:T(8,128)S(1)} %add.19.after_ref), channel_id=1, source_target_pairs={{0,6},{1,7},{2,0},{3,1},{4,2},{5,3},{6,4},{7,5},{8,14},{9,15},{10,... | collective-permute-start | bytes 196616 | tf_op jit(solution)/shard_map/ppermute | solution.py:258
  15.5 1.6 %collective-permute-start.4 = (f32[64,256]{1,0:T(8,128)S(1)}, f32[64,256]{1,0:T(8,128)S(1)}, u32[]{:S(2)}, u32[]{:S(2)}) collective-permute-start(f32[64,256]{1,0:T(8,128)S(1)} %add_add_fusion), channel_id=1, source_target_pairs={{0,1},{1,0},{2,3},{3,2},{4,5},{5,4},{6,7},{7,6},{8,9},{9,8},{10,11... | collective-permute-start | bytes 196616 | tf_op jit(solution)/shard_map/ppermute | solution.py:253
  15.6 5.5 %collective-permute-start.5 = (f32[64,256]{1,0:T(8,128)S(1)}, f32[64,256]{1,0:T(8,128)S(1)}, u32[]{:S(2)}, u32[]{:S(2)}) collective-permute-start(f32[64,256]{1,0:T(8,128)S(1)} %add_add_fusion), channel_id=1, source_target_pairs={{0,8},{1,9},{2,10},{3,11},{4,12},{5,13},{6,14},{7,15},{8,16},{9,17... | collective-permute-start | bytes 196616 | tf_op jit(solution)/shard_map/ppermute | solution.py:269
  17.2 5.3 %collective-permute-start.6 = (f32[64,512]{1,0:T(8,128)S(1)}, f32[64,512]{1,0:T(8,128)S(1)}, u32[]{:S(2)}, u32[]{:S(2)}) collective-permute-start(f32[64,512]{1,0:T(8,128)S(1)} %pad_maximum_fusion.own_ref.refs_0_), channel_id=1, source_target_pairs={{0,24},{1,17},{2,26},{3,19},{4,28},{5,21},{6,30},{7,23},{8,0},{9,2... | collective-permute-start | bytes 393224 | tf_op jit(solution)/shard_map/ppermute | solution.py:269
  21.1 1.4 %collective-permute-start.7 = (f32[64,256]{1,0:T(8,128)S(1)}, f32[64,256]{1,0:T(8,128)S(1)}, u32[]{:S(2)}, u32[]{:S(2)}) collective-permute-start(f32[64,256]{1,0:T(8,128)S(1)} %collective-permute-done.5.refs_1_), channel_id=1, source_target_pairs={{0,1},{1,0},{2,3},{3,2},{4,5},{5,4},{6,7},{7,6},{8,9},{9,8},{10,11... | collective-permute-start | bytes 196616 | tf_op jit(solution)/shard_map/ppermute | solution.py:253
  22.4 1.4 %collective-permute-start.8 = (f32[64,512]{1,0:T(8,128)S(1)}, f32[64,512]{1,0:T(8,128)S(1)}, u32[]{:S(2)}, u32[]{:S(2)}) collective-permute-start(f32[64,512]{1,0:T(8,128)S(1)} %collective-permute-done.6.refs_2_.refs_3_), channel_id=1, source_target_pairs={{0,1},{1,0},{2,3},{3,2},{4,5},{5,4},{6,7},{7,6},{8,9},{9,8},{10,11... | collective-permute-start | bytes 393224 | tf_op jit(solution)/shard_map/ppermute | solution.py:253

commit v15 on v14

--- a/solution.py
+++ b/solution.py
@@ -63,7 +63,7 @@
     basis_copy = pltpu.make_async_copy(basis_ref, basis, basis_sem)
     basis_copy.start()
     copies = []
-    for slot, (side, at, size) in enumerate(((0, 0, half), (1, 0, half // 2), (1, half // 2, half // 2))):
+    for slot, (side, at, size) in enumerate(((0, 0, half), (1, 0, half))):
         first = pl.multiple_of((core if side else 1 - core) * half + at, size)
         rows = held.at[pl.ds(side * half + at, size)]
         copies.append(
@@ -103,7 +103,7 @@
             pltpu.VMEM(basis.shape, basis.dtype),
             pltpu.VMEM((snaps, states), snapshots.dtype),
             pltpu.SemaphoreType.DMA,
-            pltpu.SemaphoreType.DMA((3,)),
+            pltpu.SemaphoreType.DMA((2,)),
         ],
         compiler_params=pltpu.CompilerParams(vmem_limit_bytes=55000 * 1024),
         name="project",
@@ -359,10 +359,7 @@
     passed = [swapped(block, "space", 1) for block in got]
     acc = add_terms(acc, [passed_half] + got)
     width = 128
-    starts = list(range(0, row_block - width, 2 * width))
-    starts = [0] + [start - width for start in starts[1:]] if len(starts) > 1 else [0]
-    ends = starts[1:] + [row_block]
-    chunks = [(start, end - start) for start, end in zip(starts, ends)][::-1]
+    chunks = [(0, row_block)]
     out_shapes = (
         block_shape,
         jax.ShapeDtypeStruct((col_block, row_block), jnp.float32),

time: 25.9 us -> 25.9 us (level)
  no operation moved by 1% of the time
where the time goes in v15:
time: 25.9 us; the launch traced here: 25.7 us
  starting transfers between devices  11.3 us (44%)
  Pallas kernels  8.25 us (32%)
  waiting for transfers between devices  4.56 us (18%)
  local copies, waits for them, and re-layouts  0.78 us (3%)
  between operations  0.73 us (3%)
    ppermute x3, starting transfers between devices, shifted(): lax.ppermute(value, 'space', [(i, (i + distance) % count) for i in range(...  6.92 us
    ppermute x2, starting transfers between devices, turned(): return lax.ppermute(value, ('tm', 'space'), perm)  3.72 us
    pallas_call x1, Pallas kernels, project(): pl.pallas_call(project_kernel, out_shape=(block, block), in_specs=[hbm, h...  2.69 us
    ppermute x3, waiting for transfers between devices, shifted(): lax.ppermute(value, 'space', [(i, (i + distance) % count) for i in range(...  2.26 us
    pallas_call x1, Pallas kernels, local(): pl.pallas_call(functools.partial(last_kernel, row_block, col_block, chunk...  2 us
    pallas_call x2, Pallas kernels, add_terms(): pl.pallas_call(functools.partial(halves_kernel, cols, half_snaps, len(bef...  1.94 us
    ppermute x2, waiting for transfers between devices, turned(): return lax.ppermute(value, ('tm', 'space'), perm)  1.4 us
    pallas_call x1, Pallas kernels, local(): pl.pallas_call(functools.partial(own_kernel, cols, half_snaps), out_shape...  1.02 us
  transfers between devices with their start and end apart: 9, of which 5 were waited for; matrix products, arithmetic and copies ran while one was open for 3% of the time, Pallas kernels for 14%

profile of v15, /device:TPU:0, one launch (start us, length us, event | category | flops | bytes accessed | tf_op | source)
XLA Modules:
  0.0 25.7 jit_solution(4122970086251566605)
XLA Ops:
  0.6 2.7 %project.1 = (f32[64,256]{1,0:T(8,128)S(1)}, f32[64,256]{1,0:T(8,128)S(1)}) custom-call(bf16[64,2048]{1,0:T(8,128)(2,1)} %bitcast.5, bf16[512,2048]{1,0:T(8,128)(2,1)} %snaps_ref.1), custom_call_target="tpu_custom_call" | custom-call | tf_op jit(solution)/shard_map/project/pallas_call | solution.py:97
  3.3 0.5 %collective-permute-start = (f32[64,256]{1,0:T(8,128)S(1)}, f32[64,256]{1,0:T(8,128)S(1)}, u32[]{:S(2)}, u32[]{:S(2)}) collective-permute-start(f32[64,256]{1,0:T(8,128)S(1)} %get-tuple-element.27), channel_id=1, source_target_pairs={{0,1},{1,0},{2,3},{3,2},{4,5},{5,4},{6,7},{7,6},{8,9},{9,8},{10,11... | collective-permute-start | bytes 196616 | tf_op jit(solution)/shard_map/ppermute | solution.py:253
  3.8 0.9 %collective-permute-done = f32[64,256]{1,0:T(8,128)S(1)} collective-permute-done((f32[64,256]{1,0:T(8,128)S(1)}, f32[64,256]{1,0:T(8,128)S(1)}, u32[]{:S(2)}, u32[]{:S(2)}) %collective-permute-start) | collective-permute-done | bytes 65568 | tf_op jit(solution)/shard_map/ppermute | solution.py:253
  4.8 3.0 %collective-permute-start.3 = (f32[64,256]{1,0:T(8,128)S(1)}, f32[64,256]{1,0:T(8,128)S(1)}, u32[]{:S(2)}, u32[]{:S(2)}) collective-permute-start(f32[64,256]{1,0:T(8,128)S(1)} %add.19.after_ref), channel_id=1, source_target_pairs={{0,2},{1,3},{2,4},{3,5},{4,6},{5,7},{6,0},{7,1},{8,10},{9,11},{10,... | collective-permute-start | bytes 196616 | tf_op jit(solution)/shard_map/ppermute | solution.py:258
  7.7 2.6 %collective-permute-start.2 = (f32[64,256]{1,0:T(8,128)S(1)}, f32[64,256]{1,0:T(8,128)S(1)}, u32[]{:S(2)}, u32[]{:S(2)}) collective-permute-start(f32[64,256]{1,0:T(8,128)S(1)} %add.19.after_ref), channel_id=1, source_target_pairs={{0,4},{1,5},{2,6},{3,7},{4,0},{5,1},{6,2},{7,3},{8,12},{9,13},{10,... | collective-permute-start | bytes 196616 | tf_op jit(solution)/shard_map/ppermute | solution.py:258
  10.3 1.3 %collective-permute-start.1 = (f32[64,256]{1,0:T(8,128)S(1)}, f32[64,256]{1,0:T(8,128)S(1)}, u32[]{:S(2)}, u32[]{:S(2)}) collective-permute-start(f32[64,256]{1,0:T(8,128)S(1)} %add.19.after_ref), channel_id=1, source_target_pairs={{0,6},{1,7},{2,0},{3,1},{4,2},{5,3},{6,4},{7,5},{8,14},{9,15},{10,... | collective-permute-start | bytes 196616 | tf_op jit(solution)/shard_map/ppermute | solution.py:258
  11.7 0.8 %dynamic_slice.3 = f32[536]{0:T(1024)S(1)} dynamic-slice(f32[2144]{0:T(1024)} %param.5, s32[]{:T(128)S(6)} %select_n.22), dynamic_slice_sizes={536} | dynamic-slice | bytes 4292 | tf_op jit(solution)/shard_map/dynamic_slice | solution.py:302
  12.5 0.6 %selectors.1 = (bf16[816,256]{1,0:T(8,128)(2,1)S(1)}, bf16[816,256]{1,0:T(8,128)(2,1)S(1)}) custom-call(f32[64,256]{1,0:T(8,128)S(1)} %add.19.after_ref), custom_call_target="tpu_custom_call" | custom-call | flops 1000000 | bytes 1000000 | tf_op jit(solution)/shard_map/selectors/pallas_call | solution.py:292
  13.1 0.0 collective-permute-done.3
  13.1 2.0 %collective-permute-done.2 = f32[64,256]{1,0:T(8,128)S(1)} collective-permute-done((f32[64,256]{1,0:T(8,128)S(1)}, f32[64,256]{1,0:T(8,128)S(1)}, u32[]{:S(2)}, u32[]{:S(2)}) %collective-permute-start.2) | collective-permute-done | bytes 65568 | tf_op jit(solution)/shard_map/ppermute | solution.py:258
  15.1 0.2 collective-permute-done.1
  15.3 0.1 collective-permute-start.4
  15.4 1.5 %collective-permute-start.5 = (f32[64,256]{1,0:T(8,128)S(1)}, f32[64,256]{1,0:T(8,128)S(1)}, u32[]{:S(2)}, u32[]{:S(2)}) collective-permute-start(f32[64,256]{1,0:T(8,128)S(1)} %add_add_fusion), channel_id=1, source_target_pairs={{0,8},{1,9},{2,10},{3,11},{4,12},{5,13},{6,14},{7,15},{8,16},{9,17... | collective-permute-start | bytes 196616 | tf_op jit(solution)/shard_map/ppermute | solution.py:269
  17.0 0.0 collective-permute-done.4
  17.0 2.2 %collective-permute-start.6 = (f32[64,512]{1,0:T(8,128)S(1)}, f32[64,512]{1,0:T(8,128)S(1)}, u32[]{:S(2)}, u32[]{:S(2)}) collective-permute-start(f32[64,512]{1,0:T(8,128)S(1)} %pad_maximum_fusion.own_ref.refs_0_), channel_id=1, source_target_pairs={{0,24},{1,17},{2,26},{3,19},{4,28},{5,21},{6,30},{7,23},{8,0},{9,2... | collective-permute-start | bytes 393224 | tf_op jit(solution)/shard_map/ppermute | solution.py:269
  19.2 1.0 %own_group.1 = (f32[336,544]{1,0:T(8,128)S(1)}, f32[64,512]{1,0:T(8,128)}) custom-call(bf16[816,256]{1,0:T(8,128)(2,1)S(1)} %get-tuple-element.35.left_ref, bf16[816,256]{1,0:T(8,128)(2,1)S(1)} %get-tuple-element.36.right_ref, f32[64,512]{1,0:T(8,128)S(1)} %pad_maximum_fusion.own_ref.refs_0_), custom_call_target="tpu_custom_call" | custom-call | flops 1229979648 | bytes 2000000 | tf_op jit(solution)/shard_map/own_group/pallas_call | solution.py:345
  20.2 0.7 %collective-permute-done.5.refs_1_ = f32[64,256]{1,0:T(8,128)S(1)} collective-permute-done((f32[64,256]{1,0:T(8,128)S(1)}, f32[64,256]{1,0:T(8,128)S(1)}, u32[]{:S(2)}, u32[]{:S(2)}) %collective-permute-start.5) | collective-permute-done | bytes 65568 | tf_op jit(solution)/shard_map/ppermute | solution.py:269
  20.9 0.0 collective-permute-start.7
  20.9 0.7 %halves.2.refs_0_ = f32[336,544]{1,0:T(8,128)S(1)} custom-call(bf16[816,256]{1,0:T(8,128)(2,1)S(1)} %get-tuple-element.35.left_ref, bf16[816,256]{1,0:T(8,128)(2,1)S(1)} %get-tuple-element.36.right_ref, f32[336,544]{1,0:T(8,128)S(1)} %get-tuple-element.40.refs_0_, f32[64,256]{1,0:T(8,128)S(1)} %collective-permute-done.5.refs_1_), custom_call_target="tpu_custom_call", output_to_operand_aliasing={{}: (2, {})} | custom-call | flops 614989824 | bytes 2000000 | tf_op jit(solution)/shard_map/halves/pallas_call | solution.py:332
  21.6 0.7 %collective-permute-done.6.refs_2_.refs_3_ = f32[64,512]{1,0:T(8,128)S(1)} collective-permute-done((f32[64,512]{1,0:T(8,128)S(1)}, f32[64,512]{1,0:T(8,128)S(1)}, u32[]{:S(2)}, u32[]{:S(2)}) %collective-permute-start.6) | collective-permute-done | bytes 131104 | tf_op jit(solution)/shard_map/ppermute | solution.py:269
  22.3 0.1 collective-permute-start.8
  22.4 0.0 collective-permute-done.7.refs_1_.refs_2_
  22.4 1.3 %halves.3.before_ref = f32[336,544]{1,0:T(8,128)S(1)} custom-call(bf16[816,256]{1,0:T(8,128)(2,1)S(1)} %get-tuple-element.35.left_ref, bf16[816,256]{1,0:T(8,128)(2,1)S(1)} %get-tuple-element.36.right_ref, f32[336,544]{1,0:T(8,128)S(1)} %halves.2.refs_0_, f32[64,256]{1,0:T(8,128)S(1)} %collective-permute-done.7.refs_1_.refs_2_, ...), custom_call_target="tpu_custom_call", output_to_operand_aliasing={{}: (2, {})} | custom-call | flops 1844969472 | bytes 2000000 | tf_op jit(solution)/shard_map/halves/pallas_call | solution.py:332
  23.6 0.0 collective-permute-done.8.refs_4_
  23.7 2.0 %last_half.1 = (f32[64,512]{1,0:T(8,128)}, f32[268,536]{1,0:T(8,128)}, f32[64,536]{1,0:T(8,128)}) custom-call(bf16[816,256]{1,0:T(8,128)(2,1)S(1)} %get-tuple-element.35.left_ref, bf16[816,256]{1,0:T(8,128)(2,1)S(1)} %get-tuple-element.36.right_ref, f32[336,544]{1,0:T(8,128)S(1)} %halves.3.before_ref, f32[1,536]{1,0:T(1,128)S(1)} %broadcast_in_dim.3.reg_ref, ...), custom_call_target="tpu_custom_call" | custom-call | flops 1229979648 | bytes 2000000 | tf_op jit(solution)/shard_map/last_half/pallas_call | solution.py:368
  (5 shorter events, 0.1 us)
Async XLA Ops:
  3.3 1.4 %collective-permute-start = (f32[64,256]{1,0:T(8,128)S(1)}, f32[64,256]{1,0:T(8,128)S(1)}, u32[]{:S(2)}, u32[]{:S(2)}) collective-permute-start(f32[64,256]{1,0:T(8,128)S(1)} %get-tuple-element.27), channel_id=1, source_target_pairs={{0,1},{1,0},{2,3},{3,2},{4,5},{5,4},{6,7},{7,6},{8,9},{9,8},{10,11... | collective-permute-start | bytes 196616 | tf_op jit(solution)/shard_map/ppermute | solution.py:253
  4.8 8.3 %collective-permute-start.3 = (f32[64,256]{1,0:T(8,128)S(1)}, f32[64,256]{1,0:T(8,128)S(1)}, u32[]{:S(2)}, u32[]{:S(2)}) collective-permute-start(f32[64,256]{1,0:T(8,128)S(1)} %add.19.after_ref), channel_id=1, source_target_pairs={{0,2},{1,3},{2,4},{3,5},{4,6},{5,7},{6,0},{7,1},{8,10},{9,11},{10,... | collective-permute-start | bytes 196616 | tf_op jit(solution)/shard_map/ppermute | solution.py:258
  7.7 7.3 %collective-permute-start.2 = (f32[64,256]{1,0:T(8,128)S(1)}, f32[64,256]{1,0:T(8,128)S(1)}, u32[]{:S(2)}, u32[]{:S(2)}) collective-permute-start(f32[64,256]{1,0:T(8,128)S(1)} %add.19.after_ref), channel_id=1, source_target_pairs={{0,4},{1,5},{2,6},{3,7},{4,0},{5,1},{6,2},{7,3},{8,12},{9,13},{10,... | collective-permute-start | bytes 196616 | tf_op jit(solution)/shard_map/ppermute | solution.py:258
  10.3 5.0 %collective-permute-start.1 = (f32[64,256]{1,0:T(8,128)S(1)}, f32[64,256]{1,0:T(8,128)S(1)}, u32[]{:S(2)}, u32[]{:S(2)}) collective-permute-start(f32[64,256]{1,0:T(8,128)S(1)} %add.19.after_ref), channel_id=1, source_target_pairs={{0,6},{1,7},{2,0},{3,1},{4,2},{5,3},{6,4},{7,5},{8,14},{9,15},{10,... | collective-permute-start | bytes 196616 | tf_op jit(solution)/shard_map/ppermute | solution.py:258
  15.3 1.6 %collective-permute-start.4 = (f32[64,256]{1,0:T(8,128)S(1)}, f32[64,256]{1,0:T(8,128)S(1)}, u32[]{:S(2)}, u32[]{:S(2)}) collective-permute-start(f32[64,256]{1,0:T(8,128)S(1)} %add_add_fusion), channel_id=1, source_target_pairs={{0,1},{1,0},{2,3},{3,2},{4,5},{5,4},{6,7},{7,6},{8,9},{9,8},{10,11... | collective-permute-start | bytes 196616 | tf_op jit(solution)/shard_map/ppermute | solution.py:253
  15.4 5.5 %collective-permute-start.5 = (f32[64,256]{1,0:T(8,128)S(1)}, f32[64,256]{1,0:T(8,128)S(1)}, u32[]{:S(2)}, u32[]{:S(2)}) collective-permute-start(f32[64,256]{1,0:T(8,128)S(1)} %add_add_fusion), channel_id=1, source_target_pairs={{0,8},{1,9},{2,10},{3,11},{4,12},{5,13},{6,14},{7,15},{8,16},{9,17... | collective-permute-start | bytes 196616 | tf_op jit(solution)/shard_map/ppermute | solution.py:269
  17.0 5.3 %collective-permute-start.6 = (f32[64,512]{1,0:T(8,128)S(1)}, f32[64,512]{1,0:T(8,128)S(1)}, u32[]{:S(2)}, u32[]{:S(2)}) collective-permute-start(f32[64,512]{1,0:T(8,128)S(1)} %pad_maximum_fusion.own_ref.refs_0_), channel_id=1, source_target_pairs={{0,24},{1,17},{2,26},{3,19},{4,28},{5,21},{6,30},{7,23},{8,0},{9,2... | collective-permute-start | bytes 393224 | tf_op jit(solution)/shard_map/ppermute | solution.py:269
  20.9 1.4 %collective-permute-start.7 = (f32[64,256]{1,0:T(8,128)S(1)}, f32[64,256]{1,0:T(8,128)S(1)}, u32[]{:S(2)}, u32[]{:S(2)}) collective-permute-start(f32[64,256]{1,0:T(8,128)S(1)} %collective-permute-done.5.refs_1_), channel_id=1, source_target_pairs={{0,1},{1,0},{2,3},{3,2},{4,5},{5,4},{6,7},{7,6},{8,9},{9,8},{10,11... | collective-permute-start | bytes 196616 | tf_op jit(solution)/shard_map/ppermute | solution.py:253
  22.3 1.4 %collective-permute-start.8 = (f32[64,512]{1,0:T(8,128)S(1)}, f32[64,512]{1,0:T(8,128)S(1)}, u32[]{:S(2)}, u32[]{:S(2)}) collective-permute-start(f32[64,512]{1,0:T(8,128)S(1)} %collective-permute-done.6.refs_2_.refs_3_), channel_id=1, source_target_pairs={{0,1},{1,0},{2,3},{3,2},{4,5},{5,4},{6,7},{7,6},{8,9},{9,8},{10,11... | collective-permute-start | bytes 393224 | tf_op jit(solution)/shard_map/ppermute | solution.py:253

commit v16 on v13

--- a/solution.py
+++ b/solution.py
@@ -309,7 +309,7 @@
     own = jnp.concatenate(
         [jnp.where(core == 0, mine, own_other), jnp.where(core == 0, own_other, mine)], axis=1
     )
-    wholes = [(tm_count - 1 - k, 2 + k) for k in range((tm_count - 2) // 2)]
+    wholes = [(2 + k, tm_count - 1 - k) for k in range((tm_count - 2) // 2)]
     got = [turned(own, steps) for steps in wholes]
     acc_shape = jax.ShapeDtypeStruct((cols + modes, rows), jnp.float32)
 

time: 25.8 us -> 26.2 us (1.016)
  the two profiles are of different devices: /device:TPU:0 before, /device:TPU:11 now
where the time goes in v16:
time: 26.2 us; the launch traced here: 26 us
  starting transfers between devices  9.29 us (35%)
  Pallas kernels  8.16 us (31%)
  waiting for transfers between devices  6.98 us (27%)
  local copies, waits for them, and re-layouts  0.78 us (3%)
  between operations  0.71 us (3%)
    ppermute x4, starting transfers between devices, swapped(): lax.ppermute(value, axis, [(i, i ^ distance) for i in range(lax.axis_size...  3.93 us
    ppermute x3, waiting for transfers between devices, shifted(): lax.ppermute(value, 'space', [(i, (i + distance) % count) for i in range(...  3.91 us
    ppermute x3, starting transfers between devices, shifted(): lax.ppermute(value, 'space', [(i, (i + distance) % count) for i in range(...  3.83 us
    pallas_call x3, Pallas kernels, add_terms(): pl.pallas_call(functools.partial(halves_kernel, cols, half_snaps, len(bef...  2.94 us
    pallas_call x1, Pallas kernels, project(): pl.pallas_call(project_kernel, out_shape=(block, block), in_specs=[hbm, h...  2.69 us
    ppermute x2, waiting for transfers between devices, turned(): return lax.ppermute(value, ('tm', 'space'), perm)  2.16 us
    pallas_call x1, Pallas kernels, local(): pl.pallas_call(functools.partial(last_kernel, row_block, col_block, chunk...  1.93 us
    ppermute x2, starting transfers between devices, turned(): return lax.ppermute(value, ('tm', 'space'), perm)  1.53 us
  transfers between devices with their start and end apart: 9, of which 5 were waited for; matrix products, arithmetic and copies ran while one was open for 3% of the time, Pallas kernels for 14%

profile of v16, /device:TPU:11, one launch (start us, length us, event | category | flops | bytes accessed | tf_op | source)
XLA Modules:
  0.0 26.0 jit_solution(17858010314199014335)
XLA Ops:
  0.6 2.7 %project.1 = (f32[64,256]{1,0:T(8,128)S(1)}, f32[64,256]{1,0:T(8,128)S(1)}) custom-call(bf16[64,2048]{1,0:T(8,128)(2,1)} %bitcast.5, bf16[512,2048]{1,0:T(8,128)(2,1)} %snaps_ref.1), custom_call_target="tpu_custom_call" | custom-call | tf_op jit(solution)/shard_map/project/pallas_call | solution.py:98
  3.3 0.7 %collective-permute-start = (f32[64,256]{1,0:T(8,128)S(1)}, f32[64,256]{1,0:T(8,128)S(1)}, u32[]{:S(2)}, u32[]{:S(2)}) collective-permute-start(f32[64,256]{1,0:T(8,128)S(1)} %get-tuple-element.26), channel_id=1, source_target_pairs={{0,1},{1,0},{2,3},{3,2},{4,5},{5,4},{6,7},{7,6},{8,9},{9,8},{10,11... | collective-permute-start | bytes 196616 | tf_op jit(solution)/shard_map/ppermute | solution.py:249
  4.1 0.9 %collective-permute-done = f32[64,256]{1,0:T(8,128)S(1)} collective-permute-done((f32[64,256]{1,0:T(8,128)S(1)}, f32[64,256]{1,0:T(8,128)S(1)}, u32[]{:S(2)}, u32[]{:S(2)}) %collective-permute-start) | collective-permute-done | bytes 65568 | tf_op jit(solution)/shard_map/ppermute | solution.py:249
  5.0 1.4 %collective-permute-start.3 = (f32[64,256]{1,0:T(8,128)S(1)}, f32[64,256]{1,0:T(8,128)S(1)}, u32[]{:S(2)}, u32[]{:S(2)}) collective-permute-start(f32[64,256]{1,0:T(8,128)S(1)} %add.19.after_ref), channel_id=1, source_target_pairs={{0,2},{1,3},{2,4},{3,5},{4,6},{5,7},{6,0},{7,1},{8,10},{9,11},{10,... | collective-permute-start | bytes 196616 | tf_op jit(solution)/shard_map/ppermute | solution.py:254
  6.3 1.1 %collective-permute-start.2 = (f32[64,256]{1,0:T(8,128)S(1)}, f32[64,256]{1,0:T(8,128)S(1)}, u32[]{:S(2)}, u32[]{:S(2)}) collective-permute-start(f32[64,256]{1,0:T(8,128)S(1)} %add.19.after_ref), channel_id=1, source_target_pairs={{0,4},{1,5},{2,6},{3,7},{4,0},{5,1},{6,2},{7,3},{8,12},{9,13},{10,... | collective-permute-start | bytes 196616 | tf_op jit(solution)/shard_map/ppermute | solution.py:254
  7.4 1.4 %collective-permute-start.1 = (f32[64,256]{1,0:T(8,128)S(1)}, f32[64,256]{1,0:T(8,128)S(1)}, u32[]{:S(2)}, u32[]{:S(2)}) collective-permute-start(f32[64,256]{1,0:T(8,128)S(1)} %add.19.after_ref), channel_id=1, source_target_pairs={{0,6},{1,7},{2,0},{3,1},{4,2},{5,3},{6,4},{7,5},{8,14},{9,15},{10,... | collective-permute-start | bytes 196616 | tf_op jit(solution)/shard_map/ppermute | solution.py:254
  8.8 0.8 %dynamic_slice.3 = f32[536]{0:T(1024)S(1)} dynamic-slice(f32[2144]{0:T(1024)} %param.5, s32[]{:T(128)S(6)} %select_n.22), dynamic_slice_sizes={536} | dynamic-slice | bytes 4292 | tf_op jit(solution)/shard_map/dynamic_slice | solution.py:298
  9.6 0.6 %selectors.1 = (bf16[816,256]{1,0:T(8,128)(2,1)S(1)}, bf16[816,256]{1,0:T(8,128)(2,1)S(1)}) custom-call(f32[64,256]{1,0:T(8,128)S(1)} %add.19.after_ref), custom_call_target="tpu_custom_call" | custom-call | flops 1000000 | bytes 1000000 | tf_op jit(solution)/shard_map/selectors/pallas_call | solution.py:288
  10.2 0.0 collective-permute-done.3
  10.2 0.3 %collective-permute-done.2 = f32[64,256]{1,0:T(8,128)S(1)} collective-permute-done((f32[64,256]{1,0:T(8,128)S(1)}, f32[64,256]{1,0:T(8,128)S(1)}, u32[]{:S(2)}, u32[]{:S(2)}) %collective-permute-start.2) | collective-permute-done | bytes 65568 | tf_op jit(solution)/shard_map/ppermute | solution.py:254
  10.5 3.6 %collective-permute-done.1 = f32[64,256]{1,0:T(8,128)S(1)} collective-permute-done((f32[64,256]{1,0:T(8,128)S(1)}, f32[64,256]{1,0:T(8,128)S(1)}, u32[]{:S(2)}, u32[]{:S(2)}) %collective-permute-start.1) | collective-permute-done | bytes 65568 | tf_op jit(solution)/shard_map/ppermute | solution.py:254
  14.1 0.6 %collective-permute-start.4 = (f32[64,256]{1,0:T(8,128)S(1)}, f32[64,256]{1,0:T(8,128)S(1)}, u32[]{:S(2)}, u32[]{:S(2)}) collective-permute-start(f32[64,256]{1,0:T(8,128)S(1)} %add_add_fusion), channel_id=1, source_target_pairs={{0,1},{1,0},{2,3},{3,2},{4,5},{5,4},{6,7},{7,6},{8,9},{9,8},{10,11... | collective-permute-start | bytes 196616 | tf_op jit(solution)/shard_map/ppermute | solution.py:249
  14.7 1.2 %collective-permute-start.5 = (f32[64,256]{1,0:T(8,128)S(1)}, f32[64,256]{1,0:T(8,128)S(1)}, u32[]{:S(2)}, u32[]{:S(2)}) collective-permute-start(f32[64,256]{1,0:T(8,128)S(1)} %add_add_fusion), channel_id=1, source_target_pairs={{0,8},{1,9},{2,10},{3,11},{4,12},{5,13},{6,14},{7,15},{8,16},{9,17... | collective-permute-start | bytes 196616 | tf_op jit(solution)/shard_map/ppermute | solution.py:265
  15.9 0.0 collective-permute-done.4
  16.0 0.3 %collective-permute-start.6 = (f32[64,512]{1,0:T(8,128)S(1)}, f32[64,512]{1,0:T(8,128)S(1)}, u32[]{:S(2)}, u32[]{:S(2)}) collective-permute-start(f32[64,512]{1,0:T(8,128)S(1)} %pad_maximum_fusion.refs_0_), channel_id=1, source_target_pairs={{0,16},{1,25},{2,18},{3,27},{4,20},{5,29},{6,22},{7,31},{8,24},{9,... | collective-permute-start | bytes 393224 | tf_op jit(solution)/shard_map/ppermute | solution.py:265
  16.3 1.0 %halves.3.refs_0_ = f32[336,544]{1,0:T(8,128)S(1)} custom-call(bf16[816,256]{1,0:T(8,128)(2,1)S(1)} %get-tuple-element.34.left_ref, bf16[816,256]{1,0:T(8,128)(2,1)S(1)} %get-tuple-element.35.right_ref, f32[64,512]{1,0:T(8,128)S(1)} %pad_maximum_fusion.refs_0_), custom_call_target="tpu_custom_call" | custom-call | flops 1229979648 | bytes 2000000 | tf_op jit(solution)/shard_map/halves/pallas_call | solution.py:328
  17.3 1.1 %collective-permute-done.5.refs_1_ = f32[64,256]{1,0:T(8,128)S(1)} collective-permute-done((f32[64,256]{1,0:T(8,128)S(1)}, f32[64,256]{1,0:T(8,128)S(1)}, u32[]{:S(2)}, u32[]{:S(2)}) %collective-permute-start.5) | collective-permute-done | bytes 65568 | tf_op jit(solution)/shard_map/ppermute | solution.py:265
  18.4 0.8 %collective-permute-start.7 = (f32[64,256]{1,0:T(8,128)S(1)}, f32[64,256]{1,0:T(8,128)S(1)}, u32[]{:S(2)}, u32[]{:S(2)}) collective-permute-start(f32[64,256]{1,0:T(8,128)S(1)} %collective-permute-done.5.refs_1_), channel_id=1, source_target_pairs={{0,1},{1,0},{2,3},{3,2},{4,5},{5,4},{6,7},{7,6},{8,9},{9,8},{10,11... | collective-permute-start | bytes 196616 | tf_op jit(solution)/shard_map/ppermute | solution.py:249
  19.2 0.7 %halves.4.refs_0_ = f32[336,544]{1,0:T(8,128)S(1)} custom-call(bf16[816,256]{1,0:T(8,128)(2,1)S(1)} %get-tuple-element.34.left_ref, bf16[816,256]{1,0:T(8,128)(2,1)S(1)} %get-tuple-element.35.right_ref, f32[336,544]{1,0:T(8,128)S(1)} %halves.3.refs_0_, f32[64,256]{1,0:T(8,128)S(1)} %collective-permute-done.5.refs_1_), custom_call_target="tpu_custom_call", output_to_operand_aliasing={{}: (2, {})} | custom-call | flops 614989824 | bytes 2000000 | tf_op jit(solution)/shard_map/halves/pallas_call | solution.py:328
  19.9 1.1 %collective-permute-done.6.refs_2_.refs_3_ = f32[64,512]{1,0:T(8,128)S(1)} collective-permute-done((f32[64,512]{1,0:T(8,128)S(1)}, f32[64,512]{1,0:T(8,128)S(1)}, u32[]{:S(2)}, u32[]{:S(2)}) %collective-permute-start.6) | collective-permute-done | bytes 131104 | tf_op jit(solution)/shard_map/ppermute | solution.py:265
  20.9 1.8 %collective-permute-start.8 = (f32[64,512]{1,0:T(8,128)S(1)}, f32[64,512]{1,0:T(8,128)S(1)}, u32[]{:S(2)}, u32[]{:S(2)}) collective-permute-start(f32[64,512]{1,0:T(8,128)S(1)} %collective-permute-done.6.refs_2_.refs_3_), channel_id=1, source_target_pairs={{0,1},{1,0},{2,3},{3,2},{4,5},{5,4},{6,7},{7,6},{8,9},{9,8},{10,11... | collective-permute-start | bytes 393224 | tf_op jit(solution)/shard_map/ppermute | solution.py:249
  22.7 0.0 collective-permute-done.7.refs_1_.refs_2_
  22.7 1.3 %halves.5.before_ref = f32[336,544]{1,0:T(8,128)S(1)} custom-call(bf16[816,256]{1,0:T(8,128)(2,1)S(1)} %get-tuple-element.34.left_ref, bf16[816,256]{1,0:T(8,128)(2,1)S(1)} %get-tuple-element.35.right_ref, f32[336,544]{1,0:T(8,128)S(1)} %halves.4.refs_0_, f32[64,256]{1,0:T(8,128)S(1)} %collective-permute-done.7.refs_1_.refs_2_, ...), custom_call_target="tpu_custom_call", output_to_operand_aliasing={{}: (2, {})} | custom-call | flops 1844969472 | bytes 2000000 | tf_op jit(solution)/shard_map/halves/pallas_call | solution.py:328
  24.0 0.0 collective-permute-done.8.refs_4_
  24.0 1.9 %last_half.1 = (f32[64,512]{1,0:T(8,128)}, f32[64,512]{1,0:T(8,128)}, f32[268,536]{1,0:T(8,128)}, f32[64,536]{1,0:T(8,128)}) custom-call(bf16[816,256]{1,0:T(8,128)(2,1)S(1)} %get-tuple-element.34.left_ref, bf16[816,256]{1,0:T(8,128)(2,1)S(1)} %get-tuple-element.35.right_ref, f32[336,544]{1,0:T(8,128)S(1)} %halves.5.before_ref, ...), custom_call_target="tpu_custom_call" | custom-call | flops 1229979648 | bytes 2000000 | tf_op jit(solution)/shard_map/last_half/pallas_call | solution.py:358
  (5 shorter events, 0.1 us)
Async XLA Ops:
  3.3 1.6 %collective-permute-start = (f32[64,256]{1,0:T(8,128)S(1)}, f32[64,256]{1,0:T(8,128)S(1)}, u32[]{:S(2)}, u32[]{:S(2)}) collective-permute-start(f32[64,256]{1,0:T(8,128)S(1)} %get-tuple-element.26), channel_id=1, source_target_pairs={{0,1},{1,0},{2,3},{3,2},{4,5},{5,4},{6,7},{7,6},{8,9},{9,8},{10,11... | collective-permute-start | bytes 196616 | tf_op jit(solution)/shard_map/ppermute | solution.py:249
  5.0 5.2 %collective-permute-start.3 = (f32[64,256]{1,0:T(8,128)S(1)}, f32[64,256]{1,0:T(8,128)S(1)}, u32[]{:S(2)}, u32[]{:S(2)}) collective-permute-start(f32[64,256]{1,0:T(8,128)S(1)} %add.19.after_ref), channel_id=1, source_target_pairs={{0,2},{1,3},{2,4},{3,5},{4,6},{5,7},{6,0},{7,1},{8,10},{9,11},{10,... | collective-permute-start | bytes 196616 | tf_op jit(solution)/shard_map/ppermute | solution.py:254
  6.3 4.2 %collective-permute-start.2 = (f32[64,256]{1,0:T(8,128)S(1)}, f32[64,256]{1,0:T(8,128)S(1)}, u32[]{:S(2)}, u32[]{:S(2)}) collective-permute-start(f32[64,256]{1,0:T(8,128)S(1)} %add.19.after_ref), channel_id=1, source_target_pairs={{0,4},{1,5},{2,6},{3,7},{4,0},{5,1},{6,2},{7,3},{8,12},{9,13},{10,... | collective-permute-start | bytes 196616 | tf_op jit(solution)/shard_map/ppermute | solution.py:254
  7.4 6.7 %collective-permute-start.1 = (f32[64,256]{1,0:T(8,128)S(1)}, f32[64,256]{1,0:T(8,128)S(1)}, u32[]{:S(2)}, u32[]{:S(2)}) collective-permute-start(f32[64,256]{1,0:T(8,128)S(1)} %add.19.after_ref), channel_id=1, source_target_pairs={{0,6},{1,7},{2,0},{3,1},{4,2},{5,3},{6,4},{7,5},{8,14},{9,15},{10,... | collective-permute-start | bytes 196616 | tf_op jit(solution)/shard_map/ppermute | solution.py:254
  14.1 1.8 %collective-permute-start.4 = (f32[64,256]{1,0:T(8,128)S(1)}, f32[64,256]{1,0:T(8,128)S(1)}, u32[]{:S(2)}, u32[]{:S(2)}) collective-permute-start(f32[64,256]{1,0:T(8,128)S(1)} %add_add_fusion), channel_id=1, source_target_pairs={{0,1},{1,0},{2,3},{3,2},{4,5},{5,4},{6,7},{7,6},{8,9},{9,8},{10,11... | collective-permute-start | bytes 196616 | tf_op jit(solution)/shard_map/ppermute | solution.py:249
  14.7 3.7 %collective-permute-start.5 = (f32[64,256]{1,0:T(8,128)S(1)}, f32[64,256]{1,0:T(8,128)S(1)}, u32[]{:S(2)}, u32[]{:S(2)}) collective-permute-start(f32[64,256]{1,0:T(8,128)S(1)} %add_add_fusion), channel_id=1, source_target_pairs={{0,8},{1,9},{2,10},{3,11},{4,12},{5,13},{6,14},{7,15},{8,16},{9,17... | collective-permute-start | bytes 196616 | tf_op jit(solution)/shard_map/ppermute | solution.py:265
  16.0 5.0 %collective-permute-start.6 = (f32[64,512]{1,0:T(8,128)S(1)}, f32[64,512]{1,0:T(8,128)S(1)}, u32[]{:S(2)}, u32[]{:S(2)}) collective-permute-start(f32[64,512]{1,0:T(8,128)S(1)} %pad_maximum_fusion.refs_0_), channel_id=1, source_target_pairs={{0,16},{1,25},{2,18},{3,27},{4,20},{5,29},{6,22},{7,31},{8,24},{9,... | collective-permute-start | bytes 393224 | tf_op jit(solution)/shard_map/ppermute | solution.py:265
  18.4 4.4 %collective-permute-start.7 = (f32[64,256]{1,0:T(8,128)S(1)}, f32[64,256]{1,0:T(8,128)S(1)}, u32[]{:S(2)}, u32[]{:S(2)}) collective-permute-start(f32[64,256]{1,0:T(8,128)S(1)} %collective-permute-done.5.refs_1_), channel_id=1, source_target_pairs={{0,1},{1,0},{2,3},{3,2},{4,5},{5,4},{6,7},{7,6},{8,9},{9,8},{10,11... | collective-permute-start | bytes 196616 | tf_op jit(solution)/shard_map/ppermute | solution.py:249
  20.9 3.1 %collective-permute-start.8 = (f32[64,512]{1,0:T(8,128)S(1)}, f32[64,512]{1,0:T(8,128)S(1)}, u32[]{:S(2)}, u32[]{:S(2)}) collective-permute-start(f32[64,512]{1,0:T(8,128)S(1)} %collective-permute-done.6.refs_2_.refs_3_), channel_id=1, source_target_pairs={{0,1},{1,0},{2,3},{3,2},{4,5},{5,4},{6,7},{7,6},{8,9},{9,8},{10,11... | collective-permute-start | bytes 393224 | tf_op jit(solution)/shard_map/ppermute | solution.py:249

commit v17 on v15

--- a/solution.py
+++ b/solution.py
@@ -359,7 +359,9 @@
     passed = [swapped(block, "space", 1) for block in got]
     acc = add_terms(acc, [passed_half] + got)
     width = 128
-    chunks = [(0, row_block)]
+    firsts = list(range(0, row_block - width, 2 * width))
+    firsts = [0] + [first - width for first in firsts[1:]] if len(firsts) > 1 else [0]
+    chunks = [(first, end - first) for first, end in zip(firsts, firsts[1:] + [row_block])][::-1]
     out_shapes = (
         block_shape,
         jax.ShapeDtypeStruct((col_block, row_block), jnp.float32),

time: 25.9 us -> 25.8 us (level)
  no operation moved by 1% of the time
where the time goes in v17:
time: 25.8 us; the launch traced here: 25.6 us
  starting transfers between devices  11.3 us (44%)
  Pallas kernels  8.17 us (32%)
  waiting for transfers between devices  4.56 us (18%)
  local copies, waits for them, and re-layouts  0.78 us (3%)
  between operations  0.73 us (3%)
    ppermute x3, starting transfers between devices, shifted(): lax.ppermute(value, 'space', [(i, (i + distance) % count) for i in range(...  6.92 us
    ppermute x2, starting transfers between devices, turned(): return lax.ppermute(value, ('tm', 'space'), perm)  3.72 us
    pallas_call x1, Pallas kernels, project(): pl.pallas_call(project_kernel, out_shape=(block, block), in_specs=[hbm, h...  2.69 us
    ppermute x3, waiting for transfers between devices, shifted(): lax.ppermute(value, 'space', [(i, (i + distance) % count) for i in range(...  2.26 us
    pallas_call x2, Pallas kernels, add_terms(): pl.pallas_call(functools.partial(halves_kernel, cols, half_snaps, len(bef...  1.94 us
    pallas_call x1, Pallas kernels, local(): pl.pallas_call(functools.partial(last_kernel, row_block, col_block, chunk...  1.93 us
    ppermute x2, waiting for transfers between devices, turned(): return lax.ppermute(value, ('tm', 'space'), perm)  1.4 us
    pallas_call x1, Pallas kernels, local(): pl.pallas_call(functools.partial(own_kernel, cols, half_snaps), out_shape...  1.02 us
  transfers between devices with their start and end apart: 9, of which 5 were waited for; matrix products, arithmetic and copies ran while one was open for 3% of the time, Pallas kernels for 14%

profile of v17, /device:TPU:0, one launch (start us, length us, event | category | flops | bytes accessed | tf_op | source)
XLA Modules:
  0.0 25.6 jit_solution(2863500705600611184)
XLA Ops:
  0.6 2.7 %project.1 = (f32[64,256]{1,0:T(8,128)S(1)}, f32[64,256]{1,0:T(8,128)S(1)}) custom-call(bf16[64,2048]{1,0:T(8,128)(2,1)} %bitcast.5, bf16[512,2048]{1,0:T(8,128)(2,1)} %snaps_ref.1), custom_call_target="tpu_custom_call" | custom-call | tf_op jit(solution)/shard_map/project/pallas_call | solution.py:97
  3.3 0.5 %collective-permute-start = (f32[64,256]{1,0:T(8,128)S(1)}, f32[64,256]{1,0:T(8,128)S(1)}, u32[]{:S(2)}, u32[]{:S(2)}) collective-permute-start(f32[64,256]{1,0:T(8,128)S(1)} %get-tuple-element.27), channel_id=1, source_target_pairs={{0,1},{1,0},{2,3},{3,2},{4,5},{5,4},{6,7},{7,6},{8,9},{9,8},{10,11... | collective-permute-start | bytes 196616 | tf_op jit(solution)/shard_map/ppermute | solution.py:253
  3.8 0.9 %collective-permute-done = f32[64,256]{1,0:T(8,128)S(1)} collective-permute-done((f32[64,256]{1,0:T(8,128)S(1)}, f32[64,256]{1,0:T(8,128)S(1)}, u32[]{:S(2)}, u32[]{:S(2)}) %collective-permute-start) | collective-permute-done | bytes 65568 | tf_op jit(solution)/shard_map/ppermute | solution.py:253
  4.8 3.0 %collective-permute-start.3 = (f32[64,256]{1,0:T(8,128)S(1)}, f32[64,256]{1,0:T(8,128)S(1)}, u32[]{:S(2)}, u32[]{:S(2)}) collective-permute-start(f32[64,256]{1,0:T(8,128)S(1)} %add.19.after_ref), channel_id=1, source_target_pairs={{0,2},{1,3},{2,4},{3,5},{4,6},{5,7},{6,0},{7,1},{8,10},{9,11},{10,... | collective-permute-start | bytes 196616 | tf_op jit(solution)/shard_map/ppermute | solution.py:258
  7.7 2.6 %collective-permute-start.2 = (f32[64,256]{1,0:T(8,128)S(1)}, f32[64,256]{1,0:T(8,128)S(1)}, u32[]{:S(2)}, u32[]{:S(2)}) collective-permute-start(f32[64,256]{1,0:T(8,128)S(1)} %add.19.after_ref), channel_id=1, source_target_pairs={{0,4},{1,5},{2,6},{3,7},{4,0},{5,1},{6,2},{7,3},{8,12},{9,13},{10,... | collective-permute-start | bytes 196616 | tf_op jit(solution)/shard_map/ppermute | solution.py:258
  10.3 1.3 %collective-permute-start.1 = (f32[64,256]{1,0:T(8,128)S(1)}, f32[64,256]{1,0:T(8,128)S(1)}, u32[]{:S(2)}, u32[]{:S(2)}) collective-permute-start(f32[64,256]{1,0:T(8,128)S(1)} %add.19.after_ref), channel_id=1, source_target_pairs={{0,6},{1,7},{2,0},{3,1},{4,2},{5,3},{6,4},{7,5},{8,14},{9,15},{10,... | collective-permute-start | bytes 196616 | tf_op jit(solution)/shard_map/ppermute | solution.py:258
  11.7 0.8 %dynamic_slice.3 = f32[536]{0:T(1024)S(1)} dynamic-slice(f32[2144]{0:T(1024)} %param.5, s32[]{:T(128)S(6)} %select_n.22), dynamic_slice_sizes={536} | dynamic-slice | bytes 4292 | tf_op jit(solution)/shard_map/dynamic_slice | solution.py:302
  12.5 0.6 %selectors.1 = (bf16[816,256]{1,0:T(8,128)(2,1)S(1)}, bf16[816,256]{1,0:T(8,128)(2,1)S(1)}) custom-call(f32[64,256]{1,0:T(8,128)S(1)} %add.19.after_ref), custom_call_target="tpu_custom_call" | custom-call | flops 1000000 | bytes 1000000 | tf_op jit(solution)/shard_map/selectors/pallas_call | solution.py:292
  13.1 0.0 collective-permute-done.3
  13.1 2.0 %collective-permute-done.2 = f32[64,256]{1,0:T(8,128)S(1)} collective-permute-done((f32[64,256]{1,0:T(8,128)S(1)}, f32[64,256]{1,0:T(8,128)S(1)}, u32[]{:S(2)}, u32[]{:S(2)}) %collective-permute-start.2) | collective-permute-done | bytes 65568 | tf_op jit(solution)/shard_map/ppermute | solution.py:258
  15.1 0.2 collective-permute-done.1
  15.3 0.1 collective-permute-start.4
  15.4 1.5 %collective-permute-start.5 = (f32[64,256]{1,0:T(8,128)S(1)}, f32[64,256]{1,0:T(8,128)S(1)}, u32[]{:S(2)}, u32[]{:S(2)}) collective-permute-start(f32[64,256]{1,0:T(8,128)S(1)} %add_add_fusion), channel_id=1, source_target_pairs={{0,8},{1,9},{2,10},{3,11},{4,12},{5,13},{6,14},{7,15},{8,16},{9,17... | collective-permute-start | bytes 196616 | tf_op jit(solution)/shard_map/ppermute | solution.py:269
  17.0 0.0 collective-permute-done.4
  17.0 2.2 %collective-permute-start.6 = (f32[64,512]{1,0:T(8,128)S(1)}, f32[64,512]{1,0:T(8,128)S(1)}, u32[]{:S(2)}, u32[]{:S(2)}) collective-permute-start(f32[64,512]{1,0:T(8,128)S(1)} %pad_maximum_fusion.own_ref.refs_0_), channel_id=1, source_target_pairs={{0,24},{1,17},{2,26},{3,19},{4,28},{5,21},{6,30},{7,23},{8,0},{9,2... | collective-permute-start | bytes 393224 | tf_op jit(solution)/shard_map/ppermute | solution.py:269
  19.2 1.0 %own_group.1 = (f32[336,544]{1,0:T(8,128)S(1)}, f32[64,512]{1,0:T(8,128)}) custom-call(bf16[816,256]{1,0:T(8,128)(2,1)S(1)} %get-tuple-element.35.left_ref, bf16[816,256]{1,0:T(8,128)(2,1)S(1)} %get-tuple-element.36.right_ref, f32[64,512]{1,0:T(8,128)S(1)} %pad_maximum_fusion.own_ref.refs_0_), custom_call_target="tpu_custom_call" | custom-call | flops 1229979648 | bytes 2000000 | tf_op jit(solution)/shard_map/own_group/pallas_call | solution.py:345
  20.2 0.7 %collective-permute-done.5.refs_1_ = f32[64,256]{1,0:T(8,128)S(1)} collective-permute-done((f32[64,256]{1,0:T(8,128)S(1)}, f32[64,256]{1,0:T(8,128)S(1)}, u32[]{:S(2)}, u32[]{:S(2)}) %collective-permute-start.5) | collective-permute-done | bytes 65568 | tf_op jit(solution)/shard_map/ppermute | solution.py:269
  20.9 0.0 collective-permute-start.7
  20.9 0.7 %halves.2.refs_0_ = f32[336,544]{1,0:T(8,128)S(1)} custom-call(bf16[816,256]{1,0:T(8,128)(2,1)S(1)} %get-tuple-element.35.left_ref, bf16[816,256]{1,0:T(8,128)(2,1)S(1)} %get-tuple-element.36.right_ref, f32[336,544]{1,0:T(8,128)S(1)} %get-tuple-element.40.refs_0_, f32[64,256]{1,0:T(8,128)S(1)} %collective-permute-done.5.refs_1_), custom_call_target="tpu_custom_call", output_to_operand_aliasing={{}: (2, {})} | custom-call | flops 614989824 | bytes 2000000 | tf_op jit(solution)/shard_map/halves/pallas_call | solution.py:332
  21.6 0.7 %collective-permute-done.6.refs_2_.refs_3_ = f32[64,512]{1,0:T(8,128)S(1)} collective-permute-done((f32[64,512]{1,0:T(8,128)S(1)}, f32[64,512]{1,0:T(8,128)S(1)}, u32[]{:S(2)}, u32[]{:S(2)}) %collective-permute-start.6) | collective-permute-done | bytes 131104 | tf_op jit(solution)/shard_map/ppermute | solution.py:269
  22.3 0.1 collective-permute-start.8
  22.4 0.0 collective-permute-done.7.refs_1_.refs_2_
  22.4 1.3 %halves.3.before_ref = f32[336,544]{1,0:T(8,128)S(1)} custom-call(bf16[816,256]{1,0:T(8,128)(2,1)S(1)} %get-tuple-element.35.left_ref, bf16[816,256]{1,0:T(8,128)(2,1)S(1)} %get-tuple-element.36.right_ref, f32[336,544]{1,0:T(8,128)S(1)} %halves.2.refs_0_, f32[64,256]{1,0:T(8,128)S(1)} %collective-permute-done.7.refs_1_.refs_2_, ...), custom_call_target="tpu_custom_call", output_to_operand_aliasing={{}: (2, {})} | custom-call | flops 1844969472 | bytes 2000000 | tf_op jit(solution)/shard_map/halves/pallas_call | solution.py:332
  23.6 0.0 collective-permute-done.8.refs_4_
  23.7 1.9 %last_half.1 = (f32[64,512]{1,0:T(8,128)}, f32[268,536]{1,0:T(8,128)}, f32[64,536]{1,0:T(8,128)}) custom-call(bf16[816,256]{1,0:T(8,128)(2,1)S(1)} %get-tuple-element.35.left_ref, bf16[816,256]{1,0:T(8,128)(2,1)S(1)} %get-tuple-element.36.right_ref, f32[336,544]{1,0:T(8,128)S(1)} %halves.3.before_ref, f32[1,536]{1,0:T(1,128)S(1)} %broadcast_in_dim.3.reg_ref, ...), custom_call_target="tpu_custom_call" | custom-call | flops 1229979648 | bytes 2000000 | tf_op jit(solution)/shard_map/last_half/pallas_call | solution.py:370
  (5 shorter events, 0.1 us)
Async XLA Ops:
  3.3 1.4 %collective-permute-start = (f32[64,256]{1,0:T(8,128)S(1)}, f32[64,256]{1,0:T(8,128)S(1)}, u32[]{:S(2)}, u32[]{:S(2)}) collective-permute-start(f32[64,256]{1,0:T(8,128)S(1)} %get-tuple-element.27), channel_id=1, source_target_pairs={{0,1},{1,0},{2,3},{3,2},{4,5},{5,4},{6,7},{7,6},{8,9},{9,8},{10,11... | collective-permute-start | bytes 196616 | tf_op jit(solution)/shard_map/ppermute | solution.py:253
  4.8 8.3 %collective-permute-start.3 = (f32[64,256]{1,0:T(8,128)S(1)}, f32[64,256]{1,0:T(8,128)S(1)}, u32[]{:S(2)}, u32[]{:S(2)}) collective-permute-start(f32[64,256]{1,0:T(8,128)S(1)} %add.19.after_ref), channel_id=1, source_target_pairs={{0,2},{1,3},{2,4},{3,5},{4,6},{5,7},{6,0},{7,1},{8,10},{9,11},{10,... | collective-permute-start | bytes 196616 | tf_op jit(solution)/shard_map/ppermute | solution.py:258
  7.7 7.3 %collective-permute-start.2 = (f32[64,256]{1,0:T(8,128)S(1)}, f32[64,256]{1,0:T(8,128)S(1)}, u32[]{:S(2)}, u32[]{:S(2)}) collective-permute-start(f32[64,256]{1,0:T(8,128)S(1)} %add.19.after_ref), channel_id=1, source_target_pairs={{0,4},{1,5},{2,6},{3,7},{4,0},{5,1},{6,2},{7,3},{8,12},{9,13},{10,... | collective-permute-start | bytes 196616 | tf_op jit(solution)/shard_map/ppermute | solution.py:258
  10.3 5.0 %collective-permute-start.1 = (f32[64,256]{1,0:T(8,128)S(1)}, f32[64,256]{1,0:T(8,128)S(1)}, u32[]{:S(2)}, u32[]{:S(2)}) collective-permute-start(f32[64,256]{1,0:T(8,128)S(1)} %add.19.after_ref), channel_id=1, source_target_pairs={{0,6},{1,7},{2,0},{3,1},{4,2},{5,3},{6,4},{7,5},{8,14},{9,15},{10,... | collective-permute-start | bytes 196616 | tf_op jit(solution)/shard_map/ppermute | solution.py:258
  15.3 1.6 %collective-permute-start.4 = (f32[64,256]{1,0:T(8,128)S(1)}, f32[64,256]{1,0:T(8,128)S(1)}, u32[]{:S(2)}, u32[]{:S(2)}) collective-permute-start(f32[64,256]{1,0:T(8,128)S(1)} %add_add_fusion), channel_id=1, source_target_pairs={{0,1},{1,0},{2,3},{3,2},{4,5},{5,4},{6,7},{7,6},{8,9},{9,8},{10,11... | collective-permute-start | bytes 196616 | tf_op jit(solution)/shard_map/ppermute | solution.py:253
  15.4 5.5 %collective-permute-start.5 = (f32[64,256]{1,0:T(8,128)S(1)}, f32[64,256]{1,0:T(8,128)S(1)}, u32[]{:S(2)}, u32[]{:S(2)}) collective-permute-start(f32[64,256]{1,0:T(8,128)S(1)} %add_add_fusion), channel_id=1, source_target_pairs={{0,8},{1,9},{2,10},{3,11},{4,12},{5,13},{6,14},{7,15},{8,16},{9,17... | collective-permute-start | bytes 196616 | tf_op jit(solution)/shard_map/ppermute | solution.py:269
  17.0 5.3 %collective-permute-start.6 = (f32[64,512]{1,0:T(8,128)S(1)}, f32[64,512]{1,0:T(8,128)S(1)}, u32[]{:S(2)}, u32[]{:S(2)}) collective-permute-start(f32[64,512]{1,0:T(8,128)S(1)} %pad_maximum_fusion.own_ref.refs_0_), channel_id=1, source_target_pairs={{0,24},{1,17},{2,26},{3,19},{4,28},{5,21},{6,30},{7,23},{8,0},{9,2... | collective-permute-start | bytes 393224 | tf_op jit(solution)/shard_map/ppermute | solution.py:269
  20.9 1.4 %collective-permute-start.7 = (f32[64,256]{1,0:T(8,128)S(1)}, f32[64,256]{1,0:T(8,128)S(1)}, u32[]{:S(2)}, u32[]{:S(2)}) collective-permute-start(f32[64,256]{1,0:T(8,128)S(1)} %collective-permute-done.5.refs_1_), channel_id=1, source_target_pairs={{0,1},{1,0},{2,3},{3,2},{4,5},{5,4},{6,7},{7,6},{8,9},{9,8},{10,11... | collective-permute-start | bytes 196616 | tf_op jit(solution)/shard_map/ppermute | solution.py:253
  22.3 1.4 %collective-permute-start.8 = (f32[64,512]{1,0:T(8,128)S(1)}, f32[64,512]{1,0:T(8,128)S(1)}, u32[]{:S(2)}, u32[]{:S(2)}) collective-permute-start(f32[64,512]{1,0:T(8,128)S(1)} %collective-permute-done.6.refs_2_.refs_3_), channel_id=1, source_target_pairs={{0,1},{1,0},{2,3},{3,2},{4,5},{5,4},{6,7},{7,6},{8,9},{9,8},{10,11... | collective-permute-start | bytes 393224 | tf_op jit(solution)/shard_map/ppermute | solution.py:253

commit v18 on v17

--- a/solution.py
+++ b/solution.py
@@ -71,7 +71,7 @@
         )
         copies[-1][-1].start()
     basis_copy.wait()
-    pieces = 4
+    pieces = 8
     step = states // pieces
     for side, at, size, copy in copies:
         copy.wait()

time: 25.8 us -> 25.8 us (level)
  no operation moved by 1% of the time
where the time goes in v18:
time: 25.8 us; the launch traced here: 25.6 us
  starting transfers between devices  11.3 us (44%)
  Pallas kernels  8.17 us (32%)
  waiting for transfers between devices  4.56 us (18%)
  local copies, waits for them, and re-layouts  0.78 us (3%)
  between operations  0.73 us (3%)
    ppermute x3, starting transfers between devices, shifted(): lax.ppermute(value, 'space', [(i, (i + distance) % count) for i in range(...  6.92 us
    ppermute x2, starting transfers between devices, turned(): return lax.ppermute(value, ('tm', 'space'), perm)  3.72 us
    pallas_call x1, Pallas kernels, project(): pl.pallas_call(project_kernel, out_shape=(block, block), in_specs=[hbm, h...  2.69 us
    ppermute x3, waiting for transfers between devices, shifted(): lax.ppermute(value, 'space', [(i, (i + distance) % count) for i in range(...  2.26 us
    pallas_call x2, Pallas kernels, add_terms(): pl.pallas_call(functools.partial(halves_kernel, cols, half_snaps, len(bef...  1.94 us
    pallas_call x1, Pallas kernels, local(): pl.pallas_call(functools.partial(last_kernel, row_block, col_block, chunk...  1.93 us
    ppermute x2, waiting for transfers between devices, turned(): return lax.ppermute(value, ('tm', 'space'), perm)  1.4 us
    pallas_call x1, Pallas kernels, local(): pl.pallas_call(functools.partial(own_kernel, cols, half_snaps), out_shape...  1.02 us
  transfers between devices with their start and end apart: 9, of which 5 were waited for; matrix products, arithmetic and copies ran while one was open for 3% of the time, Pallas kernels for 14%

profile of v18, /device:TPU:0, one launch (start us, length us, event | category | flops | bytes accessed | tf_op | source)
XLA Modules:
  0.0 25.6 jit_solution(3695314813193067452)
XLA Ops:
  0.6 2.7 %project.1 = (f32[64,256]{1,0:T(8,128)S(1)}, f32[64,256]{1,0:T(8,128)S(1)}) custom-call(bf16[64,2048]{1,0:T(8,128)(2,1)} %bitcast.5, bf16[512,2048]{1,0:T(8,128)(2,1)} %snaps_ref.1), custom_call_target="tpu_custom_call" | custom-call | tf_op jit(solution)/shard_map/project/pallas_call | solution.py:97
  3.3 0.5 %collective-permute-start = (f32[64,256]{1,0:T(8,128)S(1)}, f32[64,256]{1,0:T(8,128)S(1)}, u32[]{:S(2)}, u32[]{:S(2)}) collective-permute-start(f32[64,256]{1,0:T(8,128)S(1)} %get-tuple-element.27), channel_id=1, source_target_pairs={{0,1},{1,0},{2,3},{3,2},{4,5},{5,4},{6,7},{7,6},{8,9},{9,8},{10,11... | collective-permute-start | bytes 196616 | tf_op jit(solution)/shard_map/ppermute | solution.py:253
  3.8 0.9 %collective-permute-done = f32[64,256]{1,0:T(8,128)S(1)} collective-permute-done((f32[64,256]{1,0:T(8,128)S(1)}, f32[64,256]{1,0:T(8,128)S(1)}, u32[]{:S(2)}, u32[]{:S(2)}) %collective-permute-start) | collective-permute-done | bytes 65568 | tf_op jit(solution)/shard_map/ppermute | solution.py:253
  4.8 3.0 %collective-permute-start.3 = (f32[64,256]{1,0:T(8,128)S(1)}, f32[64,256]{1,0:T(8,128)S(1)}, u32[]{:S(2)}, u32[]{:S(2)}) collective-permute-start(f32[64,256]{1,0:T(8,128)S(1)} %add.19.after_ref), channel_id=1, source_target_pairs={{0,2},{1,3},{2,4},{3,5},{4,6},{5,7},{6,0},{7,1},{8,10},{9,11},{10,... | collective-permute-start | bytes 196616 | tf_op jit(solution)/shard_map/ppermute | solution.py:258
  7.7 2.6 %collective-permute-start.2 = (f32[64,256]{1,0:T(8,128)S(1)}, f32[64,256]{1,0:T(8,128)S(1)}, u32[]{:S(2)}, u32[]{:S(2)}) collective-permute-start(f32[64,256]{1,0:T(8,128)S(1)} %add.19.after_ref), channel_id=1, source_target_pairs={{0,4},{1,5},{2,6},{3,7},{4,0},{5,1},{6,2},{7,3},{8,12},{9,13},{10,... | collective-permute-start | bytes 196616 | tf_op jit(solution)/shard_map/ppermute | solution.py:258
  10.3 1.3 %collective-permute-start.1 = (f32[64,256]{1,0:T(8,128)S(1)}, f32[64,256]{1,0:T(8,128)S(1)}, u32[]{:S(2)}, u32[]{:S(2)}) collective-permute-start(f32[64,256]{1,0:T(8,128)S(1)} %add.19.after_ref), channel_id=1, source_target_pairs={{0,6},{1,7},{2,0},{3,1},{4,2},{5,3},{6,4},{7,5},{8,14},{9,15},{10,... | collective-permute-start | bytes 196616 | tf_op jit(solution)/shard_map/ppermute | solution.py:258
  11.7 0.8 %dynamic_slice.3 = f32[536]{0:T(1024)S(1)} dynamic-slice(f32[2144]{0:T(1024)} %param.5, s32[]{:T(128)S(6)} %select_n.22), dynamic_slice_sizes={536} | dynamic-slice | bytes 4292 | tf_op jit(solution)/shard_map/dynamic_slice | solution.py:302
  12.5 0.6 %selectors.1 = (bf16[816,256]{1,0:T(8,128)(2,1)S(1)}, bf16[816,256]{1,0:T(8,128)(2,1)S(1)}) custom-call(f32[64,256]{1,0:T(8,128)S(1)} %add.19.after_ref), custom_call_target="tpu_custom_call" | custom-call | flops 1000000 | bytes 1000000 | tf_op jit(solution)/shard_map/selectors/pallas_call | solution.py:292
  13.1 0.0 collective-permute-done.3
  13.1 2.0 %collective-permute-done.2 = f32[64,256]{1,0:T(8,128)S(1)} collective-permute-done((f32[64,256]{1,0:T(8,128)S(1)}, f32[64,256]{1,0:T(8,128)S(1)}, u32[]{:S(2)}, u32[]{:S(2)}) %collective-permute-start.2) | collective-permute-done | bytes 65568 | tf_op jit(solution)/shard_map/ppermute | solution.py:258
  15.1 0.2 collective-permute-done.1
  15.3 0.1 collective-permute-start.4
  15.4 1.5 %collective-permute-start.5 = (f32[64,256]{1,0:T(8,128)S(1)}, f32[64,256]{1,0:T(8,128)S(1)}, u32[]{:S(2)}, u32[]{:S(2)}) collective-permute-start(f32[64,256]{1,0:T(8,128)S(1)} %add_add_fusion), channel_id=1, source_target_pairs={{0,8},{1,9},{2,10},{3,11},{4,12},{5,13},{6,14},{7,15},{8,16},{9,17... | collective-permute-start | bytes 196616 | tf_op jit(solution)/shard_map/ppermute | solution.py:269
  17.0 0.0 collective-permute-done.4
  17.0 2.2 %collective-permute-start.6 = (f32[64,512]{1,0:T(8,128)S(1)}, f32[64,512]{1,0:T(8,128)S(1)}, u32[]{:S(2)}, u32[]{:S(2)}) collective-permute-start(f32[64,512]{1,0:T(8,128)S(1)} %pad_maximum_fusion.own_ref.refs_0_), channel_id=1, source_target_pairs={{0,24},{1,17},{2,26},{3,19},{4,28},{5,21},{6,30},{7,23},{8,0},{9,2... | collective-permute-start | bytes 393224 | tf_op jit(solution)/shard_map/ppermute | solution.py:269
  19.2 1.0 %own_group.1 = (f32[336,544]{1,0:T(8,128)S(1)}, f32[64,512]{1,0:T(8,128)}) custom-call(bf16[816,256]{1,0:T(8,128)(2,1)S(1)} %get-tuple-element.35.left_ref, bf16[816,256]{1,0:T(8,128)(2,1)S(1)} %get-tuple-element.36.right_ref, f32[64,512]{1,0:T(8,128)S(1)} %pad_maximum_fusion.own_ref.refs_0_), custom_call_target="tpu_custom_call" | custom-call | flops 1229979648 | bytes 2000000 | tf_op jit(solution)/shard_map/own_group/pallas_call | solution.py:345
  20.2 0.7 %collective-permute-done.5.refs_1_ = f32[64,256]{1,0:T(8,128)S(1)} collective-permute-done((f32[64,256]{1,0:T(8,128)S(1)}, f32[64,256]{1,0:T(8,128)S(1)}, u32[]{:S(2)}, u32[]{:S(2)}) %collective-permute-start.5) | collective-permute-done | bytes 65568 | tf_op jit(solution)/shard_map/ppermute | solution.py:269
  20.9 0.0 collective-permute-start.7
  20.9 0.7 %halves.2.refs_0_ = f32[336,544]{1,0:T(8,128)S(1)} custom-call(bf16[816,256]{1,0:T(8,128)(2,1)S(1)} %get-tuple-element.35.left_ref, bf16[816,256]{1,0:T(8,128)(2,1)S(1)} %get-tuple-element.36.right_ref, f32[336,544]{1,0:T(8,128)S(1)} %get-tuple-element.40.refs_0_, f32[64,256]{1,0:T(8,128)S(1)} %collective-permute-done.5.refs_1_), custom_call_target="tpu_custom_call", output_to_operand_aliasing={{}: (2, {})} | custom-call | flops 614989824 | bytes 2000000 | tf_op jit(solution)/shard_map/halves/pallas_call | solution.py:332
  21.6 0.7 %collective-permute-done.6.refs_2_.refs_3_ = f32[64,512]{1,0:T(8,128)S(1)} collective-permute-done((f32[64,512]{1,0:T(8,128)S(1)}, f32[64,512]{1,0:T(8,128)S(1)}, u32[]{:S(2)}, u32[]{:S(2)}) %collective-permute-start.6) | collective-permute-done | bytes 131104 | tf_op jit(solution)/shard_map/ppermute | solution.py:269
  22.3 0.1 collective-permute-start.8
  22.4 0.0 collective-permute-done.7.refs_1_.refs_2_
  22.4 1.3 %halves.3.before_ref = f32[336,544]{1,0:T(8,128)S(1)} custom-call(bf16[816,256]{1,0:T(8,128)(2,1)S(1)} %get-tuple-element.35.left_ref, bf16[816,256]{1,0:T(8,128)(2,1)S(1)} %get-tuple-element.36.right_ref, f32[336,544]{1,0:T(8,128)S(1)} %halves.2.refs_0_, f32[64,256]{1,0:T(8,128)S(1)} %collective-permute-done.7.refs_1_.refs_2_, ...), custom_call_target="tpu_custom_call", output_to_operand_aliasing={{}: (2, {})} | custom-call | flops 1844969472 | bytes 2000000 | tf_op jit(solution)/shard_map/halves/pallas_call | solution.py:332
  23.6 0.0 collective-permute-done.8.refs_4_
  23.7 1.9 %last_half.1 = (f32[64,512]{1,0:T(8,128)}, f32[268,536]{1,0:T(8,128)}, f32[64,536]{1,0:T(8,128)}) custom-call(bf16[816,256]{1,0:T(8,128)(2,1)S(1)} %get-tuple-element.35.left_ref, bf16[816,256]{1,0:T(8,128)(2,1)S(1)} %get-tuple-element.36.right_ref, f32[336,544]{1,0:T(8,128)S(1)} %halves.3.before_ref, f32[1,536]{1,0:T(1,128)S(1)} %broadcast_in_dim.3.reg_ref, ...), custom_call_target="tpu_custom_call" | custom-call | flops 1229979648 | bytes 2000000 | tf_op jit(solution)/shard_map/last_half/pallas_call | solution.py:370
  (5 shorter events, 0.1 us)
Async XLA Ops:
  3.3 1.4 %collective-permute-start = (f32[64,256]{1,0:T(8,128)S(1)}, f32[64,256]{1,0:T(8,128)S(1)}, u32[]{:S(2)}, u32[]{:S(2)}) collective-permute-start(f32[64,256]{1,0:T(8,128)S(1)} %get-tuple-element.27), channel_id=1, source_target_pairs={{0,1},{1,0},{2,3},{3,2},{4,5},{5,4},{6,7},{7,6},{8,9},{9,8},{10,11... | collective-permute-start | bytes 196616 | tf_op jit(solution)/shard_map/ppermute | solution.py:253
  4.8 8.3 %collective-permute-start.3 = (f32[64,256]{1,0:T(8,128)S(1)}, f32[64,256]{1,0:T(8,128)S(1)}, u32[]{:S(2)}, u32[]{:S(2)}) collective-permute-start(f32[64,256]{1,0:T(8,128)S(1)} %add.19.after_ref), channel_id=1, source_target_pairs={{0,2},{1,3},{2,4},{3,5},{4,6},{5,7},{6,0},{7,1},{8,10},{9,11},{10,... | collective-permute-start | bytes 196616 | tf_op jit(solution)/shard_map/ppermute | solution.py:258
  7.7 7.3 %collective-permute-start.2 = (f32[64,256]{1,0:T(8,128)S(1)}, f32[64,256]{1,0:T(8,128)S(1)}, u32[]{:S(2)}, u32[]{:S(2)}) collective-permute-start(f32[64,256]{1,0:T(8,128)S(1)} %add.19.after_ref), channel_id=1, source_target_pairs={{0,4},{1,5},{2,6},{3,7},{4,0},{5,1},{6,2},{7,3},{8,12},{9,13},{10,... | collective-permute-start | bytes 196616 | tf_op jit(solution)/shard_map/ppermute | solution.py:258
  10.3 5.0 %collective-permute-start.1 = (f32[64,256]{1,0:T(8,128)S(1)}, f32[64,256]{1,0:T(8,128)S(1)}, u32[]{:S(2)}, u32[]{:S(2)}) collective-permute-start(f32[64,256]{1,0:T(8,128)S(1)} %add.19.after_ref), channel_id=1, source_target_pairs={{0,6},{1,7},{2,0},{3,1},{4,2},{5,3},{6,4},{7,5},{8,14},{9,15},{10,... | collective-permute-start | bytes 196616 | tf_op jit(solution)/shard_map/ppermute | solution.py:258
  15.3 1.6 %collective-permute-start.4 = (f32[64,256]{1,0:T(8,128)S(1)}, f32[64,256]{1,0:T(8,128)S(1)}, u32[]{:S(2)}, u32[]{:S(2)}) collective-permute-start(f32[64,256]{1,0:T(8,128)S(1)} %add_add_fusion), channel_id=1, source_target_pairs={{0,1},{1,0},{2,3},{3,2},{4,5},{5,4},{6,7},{7,6},{8,9},{9,8},{10,11... | collective-permute-start | bytes 196616 | tf_op jit(solution)/shard_map/ppermute | solution.py:253
  15.4 5.5 %collective-permute-start.5 = (f32[64,256]{1,0:T(8,128)S(1)}, f32[64,256]{1,0:T(8,128)S(1)}, u32[]{:S(2)}, u32[]{:S(2)}) collective-permute-start(f32[64,256]{1,0:T(8,128)S(1)} %add_add_fusion), channel_id=1, source_target_pairs={{0,8},{1,9},{2,10},{3,11},{4,12},{5,13},{6,14},{7,15},{8,16},{9,17... | collective-permute-start | bytes 196616 | tf_op jit(solution)/shard_map/ppermute | solution.py:269
  17.0 5.3 %collective-permute-start.6 = (f32[64,512]{1,0:T(8,128)S(1)}, f32[64,512]{1,0:T(8,128)S(1)}, u32[]{:S(2)}, u32[]{:S(2)}) collective-permute-start(f32[64,512]{1,0:T(8,128)S(1)} %pad_maximum_fusion.own_ref.refs_0_), channel_id=1, source_target_pairs={{0,24},{1,17},{2,26},{3,19},{4,28},{5,21},{6,30},{7,23},{8,0},{9,2... | collective-permute-start | bytes 393224 | tf_op jit(solution)/shard_map/ppermute | solution.py:269
  20.9 1.4 %collective-permute-start.7 = (f32[64,256]{1,0:T(8,128)S(1)}, f32[64,256]{1,0:T(8,128)S(1)}, u32[]{:S(2)}, u32[]{:S(2)}) collective-permute-start(f32[64,256]{1,0:T(8,128)S(1)} %collective-permute-done.5.refs_1_), channel_id=1, source_target_pairs={{0,1},{1,0},{2,3},{3,2},{4,5},{5,4},{6,7},{7,6},{8,9},{9,8},{10,11... | collective-permute-start | bytes 196616 | tf_op jit(solution)/shard_map/ppermute | solution.py:253
  22.3 1.4 %collective-permute-start.8 = (f32[64,512]{1,0:T(8,128)S(1)}, f32[64,512]{1,0:T(8,128)S(1)}, u32[]{:S(2)}, u32[]{:S(2)}) collective-permute-start(f32[64,512]{1,0:T(8,128)S(1)} %collective-permute-done.6.refs_2_.refs_3_), channel_id=1, source_target_pairs={{0,1},{1,0},{2,3},{3,2},{4,5},{5,4},{6,7},{7,6},{8,9},{9,8},{10,11... | collective-permute-start | bytes 393224 | tf_op jit(solution)/shard_map/ppermute | solution.py:253

commit v19 on v18

--- a/solution.py
+++ b/solution.py
@@ -359,8 +359,7 @@
     passed = [swapped(block, "space", 1) for block in got]
     acc = add_terms(acc, [passed_half] + got)
     width = 128
-    firsts = list(range(0, row_block - width, 2 * width))
-    firsts = [0] + [first - width for first in firsts[1:]] if len(firsts) > 1 else [0]
+    firsts = [0, 2 * width] if row_block > 3 * width else [0]
     chunks = [(first, end - first) for first, end in zip(firsts, firsts[1:] + [row_block])][::-1]
     out_shapes = (
         block_shape,

time: 25.8 us -> 26 us (level)
  no operation moved by 1% of the time
where the time goes in v19:
time: 26 us; the launch traced here: 25.7 us
  starting transfers between devices  11.3 us (43%)
  Pallas kernels  8.32 us (32%)
  waiting for transfers between devices  4.56 us (18%)
  local copies, waits for them, and re-layouts  0.78 us (3%)
  between operations  0.73 us (3%)
    ppermute x3, starting transfers between devices, shifted(): lax.ppermute(value, 'space', [(i, (i + distance) % count) for i in range(...  6.92 us
    ppermute x2, starting transfers between devices, turned(): return lax.ppermute(value, ('tm', 'space'), perm)  3.72 us
    pallas_call x1, Pallas kernels, project(): pl.pallas_call(project_kernel, out_shape=(block, block), in_specs=[hbm, h...  2.69 us
    ppermute x3, waiting for transfers between devices, shifted(): lax.ppermute(value, 'space', [(i, (i + distance) % count) for i in range(...  2.26 us
    pallas_call x1, Pallas kernels, local(): pl.pallas_call(functools.partial(last_kernel, row_block, col_block, chunk...  2.07 us
    pallas_call x2, Pallas kernels, add_terms(): pl.pallas_call(functools.partial(halves_kernel, cols, half_snaps, len(bef...  1.94 us
    ppermute x2, waiting for transfers between devices, turned(): return lax.ppermute(value, ('tm', 'space'), perm)  1.4 us
    pallas_call x1, Pallas kernels, local(): pl.pallas_call(functools.partial(own_kernel, cols, half_snaps), out_shape...  1.02 us
  transfers between devices with their start and end apart: 9, of which 5 were waited for; matrix products, arithmetic and copies ran while one was open for 3% of the time, Pallas kernels for 14%

profile of v19, /device:TPU:0, one launch (start us, length us, event | category | flops | bytes accessed | tf_op | source)
XLA Modules:
  0.0 25.7 jit_solution(158450175625105326)
XLA Ops:
  0.6 2.7 %project.1 = (f32[64,256]{1,0:T(8,128)S(1)}, f32[64,256]{1,0:T(8,128)S(1)}) custom-call(bf16[64,2048]{1,0:T(8,128)(2,1)} %bitcast.5, bf16[512,2048]{1,0:T(8,128)(2,1)} %snaps_ref.1), custom_call_target="tpu_custom_call" | custom-call | tf_op jit(solution)/shard_map/project/pallas_call | solution.py:97
  3.3 0.5 %collective-permute-start = (f32[64,256]{1,0:T(8,128)S(1)}, f32[64,256]{1,0:T(8,128)S(1)}, u32[]{:S(2)}, u32[]{:S(2)}) collective-permute-start(f32[64,256]{1,0:T(8,128)S(1)} %get-tuple-element.27), channel_id=1, source_target_pairs={{0,1},{1,0},{2,3},{3,2},{4,5},{5,4},{6,7},{7,6},{8,9},{9,8},{10,11... | collective-permute-start | bytes 196616 | tf_op jit(solution)/shard_map/ppermute | solution.py:253
  3.8 0.9 %collective-permute-done = f32[64,256]{1,0:T(8,128)S(1)} collective-permute-done((f32[64,256]{1,0:T(8,128)S(1)}, f32[64,256]{1,0:T(8,128)S(1)}, u32[]{:S(2)}, u32[]{:S(2)}) %collective-permute-start) | collective-permute-done | bytes 65568 | tf_op jit(solution)/shard_map/ppermute | solution.py:253
  4.8 3.0 %collective-permute-start.3 = (f32[64,256]{1,0:T(8,128)S(1)}, f32[64,256]{1,0:T(8,128)S(1)}, u32[]{:S(2)}, u32[]{:S(2)}) collective-permute-start(f32[64,256]{1,0:T(8,128)S(1)} %add.19.after_ref), channel_id=1, source_target_pairs={{0,2},{1,3},{2,4},{3,5},{4,6},{5,7},{6,0},{7,1},{8,10},{9,11},{10,... | collective-permute-start | bytes 196616 | tf_op jit(solution)/shard_map/ppermute | solution.py:258
  7.7 2.6 %collective-permute-start.2 = (f32[64,256]{1,0:T(8,128)S(1)}, f32[64,256]{1,0:T(8,128)S(1)}, u32[]{:S(2)}, u32[]{:S(2)}) collective-permute-start(f32[64,256]{1,0:T(8,128)S(1)} %add.19.after_ref), channel_id=1, source_target_pairs={{0,4},{1,5},{2,6},{3,7},{4,0},{5,1},{6,2},{7,3},{8,12},{9,13},{10,... | collective-permute-start | bytes 196616 | tf_op jit(solution)/shard_map/ppermute | solution.py:258
  10.3 1.3 %collective-permute-start.1 = (f32[64,256]{1,0:T(8,128)S(1)}, f32[64,256]{1,0:T(8,128)S(1)}, u32[]{:S(2)}, u32[]{:S(2)}) collective-permute-start(f32[64,256]{1,0:T(8,128)S(1)} %add.19.after_ref), channel_id=1, source_target_pairs={{0,6},{1,7},{2,0},{3,1},{4,2},{5,3},{6,4},{7,5},{8,14},{9,15},{10,... | collective-permute-start | bytes 196616 | tf_op jit(solution)/shard_map/ppermute | solution.py:258
  11.7 0.8 %dynamic_slice.3 = f32[536]{0:T(1024)S(1)} dynamic-slice(f32[2144]{0:T(1024)} %param.5, s32[]{:T(128)S(6)} %select_n.22), dynamic_slice_sizes={536} | dynamic-slice | bytes 4292 | tf_op jit(solution)/shard_map/dynamic_slice | solution.py:302
  12.5 0.6 %selectors.1 = (bf16[816,256]{1,0:T(8,128)(2,1)S(1)}, bf16[816,256]{1,0:T(8,128)(2,1)S(1)}) custom-call(f32[64,256]{1,0:T(8,128)S(1)} %add.19.after_ref), custom_call_target="tpu_custom_call" | custom-call | flops 1000000 | bytes 1000000 | tf_op jit(solution)/shard_map/selectors/pallas_call | solution.py:292
  13.1 0.0 collective-permute-done.3
  13.1 2.0 %collective-permute-done.2 = f32[64,256]{1,0:T(8,128)S(1)} collective-permute-done((f32[64,256]{1,0:T(8,128)S(1)}, f32[64,256]{1,0:T(8,128)S(1)}, u32[]{:S(2)}, u32[]{:S(2)}) %collective-permute-start.2) | collective-permute-done | bytes 65568 | tf_op jit(solution)/shard_map/ppermute | solution.py:258
  15.1 0.2 collective-permute-done.1
  15.3 0.1 collective-permute-start.4
  15.4 1.5 %collective-permute-start.5 = (f32[64,256]{1,0:T(8,128)S(1)}, f32[64,256]{1,0:T(8,128)S(1)}, u32[]{:S(2)}, u32[]{:S(2)}) collective-permute-start(f32[64,256]{1,0:T(8,128)S(1)} %add_add_fusion), channel_id=1, source_target_pairs={{0,8},{1,9},{2,10},{3,11},{4,12},{5,13},{6,14},{7,15},{8,16},{9,17... | collective-permute-start | bytes 196616 | tf_op jit(solution)/shard_map/ppermute | solution.py:269
  17.0 0.0 collective-permute-done.4
  17.0 2.2 %collective-permute-start.6 = (f32[64,512]{1,0:T(8,128)S(1)}, f32[64,512]{1,0:T(8,128)S(1)}, u32[]{:S(2)}, u32[]{:S(2)}) collective-permute-start(f32[64,512]{1,0:T(8,128)S(1)} %pad_maximum_fusion.own_ref.refs_0_), channel_id=1, source_target_pairs={{0,24},{1,17},{2,26},{3,19},{4,28},{5,21},{6,30},{7,23},{8,0},{9,2... | collective-permute-start | bytes 393224 | tf_op jit(solution)/shard_map/ppermute | solution.py:269
  19.2 1.0 %own_group.1 = (f32[336,544]{1,0:T(8,128)S(1)}, f32[64,512]{1,0:T(8,128)}) custom-call(bf16[816,256]{1,0:T(8,128)(2,1)S(1)} %get-tuple-element.35.left_ref, bf16[816,256]{1,0:T(8,128)(2,1)S(1)} %get-tuple-element.36.right_ref, f32[64,512]{1,0:T(8,128)S(1)} %pad_maximum_fusion.own_ref.refs_0_), custom_call_target="tpu_custom_call" | custom-call | flops 1229979648 | bytes 2000000 | tf_op jit(solution)/shard_map/own_group/pallas_call | solution.py:345
  20.2 0.7 %collective-permute-done.5.refs_1_ = f32[64,256]{1,0:T(8,128)S(1)} collective-permute-done((f32[64,256]{1,0:T(8,128)S(1)}, f32[64,256]{1,0:T(8,128)S(1)}, u32[]{:S(2)}, u32[]{:S(2)}) %collective-permute-start.5) | collective-permute-done | bytes 65568 | tf_op jit(solution)/shard_map/ppermute | solution.py:269
  20.9 0.0 collective-permute-start.7
  20.9 0.7 %halves.2.refs_0_ = f32[336,544]{1,0:T(8,128)S(1)} custom-call(bf16[816,256]{1,0:T(8,128)(2,1)S(1)} %get-tuple-element.35.left_ref, bf16[816,256]{1,0:T(8,128)(2,1)S(1)} %get-tuple-element.36.right_ref, f32[336,544]{1,0:T(8,128)S(1)} %get-tuple-element.40.refs_0_, f32[64,256]{1,0:T(8,128)S(1)} %collective-permute-done.5.refs_1_), custom_call_target="tpu_custom_call", output_to_operand_aliasing={{}: (2, {})} | custom-call | flops 614989824 | bytes 2000000 | tf_op jit(solution)/shard_map/halves/pallas_call | solution.py:332
  21.6 0.7 %collective-permute-done.6.refs_2_.refs_3_ = f32[64,512]{1,0:T(8,128)S(1)} collective-permute-done((f32[64,512]{1,0:T(8,128)S(1)}, f32[64,512]{1,0:T(8,128)S(1)}, u32[]{:S(2)}, u32[]{:S(2)}) %collective-permute-start.6) | collective-permute-done | bytes 131104 | tf_op jit(solution)/shard_map/ppermute | solution.py:269
  22.3 0.1 collective-permute-start.8
  22.4 0.0 collective-permute-done.7.refs_1_.refs_2_
  22.4 1.3 %halves.3.before_ref = f32[336,544]{1,0:T(8,128)S(1)} custom-call(bf16[816,256]{1,0:T(8,128)(2,1)S(1)} %get-tuple-element.35.left_ref, bf16[816,256]{1,0:T(8,128)(2,1)S(1)} %get-tuple-element.36.right_ref, f32[336,544]{1,0:T(8,128)S(1)} %halves.2.refs_0_, f32[64,256]{1,0:T(8,128)S(1)} %collective-permute-done.7.refs_1_.refs_2_, ...), custom_call_target="tpu_custom_call", output_to_operand_aliasing={{}: (2, {})} | custom-call | flops 1844969472 | bytes 2000000 | tf_op jit(solution)/shard_map/halves/pallas_call | solution.py:332
  23.6 0.0 collective-permute-done.8.refs_4_
  23.7 2.1 %last_half.1 = (f32[64,512]{1,0:T(8,128)}, f32[268,536]{1,0:T(8,128)}, f32[64,536]{1,0:T(8,128)}) custom-call(bf16[816,256]{1,0:T(8,128)(2,1)S(1)} %get-tuple-element.35.left_ref, bf16[816,256]{1,0:T(8,128)(2,1)S(1)} %get-tuple-element.36.right_ref, f32[336,544]{1,0:T(8,128)S(1)} %halves.3.before_ref, f32[1,536]{1,0:T(1,128)S(1)} %broadcast_in_dim.3.reg_ref, ...), custom_call_target="tpu_custom_call" | custom-call | flops 1229979648 | bytes 2000000 | tf_op jit(solution)/shard_map/last_half/pallas_call | solution.py:369
  (5 shorter events, 0.1 us)
Async XLA Ops:
  3.3 1.4 %collective-permute-start = (f32[64,256]{1,0:T(8,128)S(1)}, f32[64,256]{1,0:T(8,128)S(1)}, u32[]{:S(2)}, u32[]{:S(2)}) collective-permute-start(f32[64,256]{1,0:T(8,128)S(1)} %get-tuple-element.27), channel_id=1, source_target_pairs={{0,1},{1,0},{2,3},{3,2},{4,5},{5,4},{6,7},{7,6},{8,9},{9,8},{10,11... | collective-permute-start | bytes 196616 | tf_op jit(solution)/shard_map/ppermute | solution.py:253
  4.8 8.3 %collective-permute-start.3 = (f32[64,256]{1,0:T(8,128)S(1)}, f32[64,256]{1,0:T(8,128)S(1)}, u32[]{:S(2)}, u32[]{:S(2)}) collective-permute-start(f32[64,256]{1,0:T(8,128)S(1)} %add.19.after_ref), channel_id=1, source_target_pairs={{0,2},{1,3},{2,4},{3,5},{4,6},{5,7},{6,0},{7,1},{8,10},{9,11},{10,... | collective-permute-start | bytes 196616 | tf_op jit(solution)/shard_map/ppermute | solution.py:258
  7.7 7.3 %collective-permute-start.2 = (f32[64,256]{1,0:T(8,128)S(1)}, f32[64,256]{1,0:T(8,128)S(1)}, u32[]{:S(2)}, u32[]{:S(2)}) collective-permute-start(f32[64,256]{1,0:T(8,128)S(1)} %add.19.after_ref), channel_id=1, source_target_pairs={{0,4},{1,5},{2,6},{3,7},{4,0},{5,1},{6,2},{7,3},{8,12},{9,13},{10,... | collective-permute-start | bytes 196616 | tf_op jit(solution)/shard_map/ppermute | solution.py:258
  10.3 5.0 %collective-permute-start.1 = (f32[64,256]{1,0:T(8,128)S(1)}, f32[64,256]{1,0:T(8,128)S(1)}, u32[]{:S(2)}, u32[]{:S(2)}) collective-permute-start(f32[64,256]{1,0:T(8,128)S(1)} %add.19.after_ref), channel_id=1, source_target_pairs={{0,6},{1,7},{2,0},{3,1},{4,2},{5,3},{6,4},{7,5},{8,14},{9,15},{10,... | collective-permute-start | bytes 196616 | tf_op jit(solution)/shard_map/ppermute | solution.py:258
  15.3 1.6 %collective-permute-start.4 = (f32[64,256]{1,0:T(8,128)S(1)}, f32[64,256]{1,0:T(8,128)S(1)}, u32[]{:S(2)}, u32[]{:S(2)}) collective-permute-start(f32[64,256]{1,0:T(8,128)S(1)} %add_add_fusion), channel_id=1, source_target_pairs={{0,1},{1,0},{2,3},{3,2},{4,5},{5,4},{6,7},{7,6},{8,9},{9,8},{10,11... | collective-permute-start | bytes 196616 | tf_op jit(solution)/shard_map/ppermute | solution.py:253
  15.4 5.5 %collective-permute-start.5 = (f32[64,256]{1,0:T(8,128)S(1)}, f32[64,256]{1,0:T(8,128)S(1)}, u32[]{:S(2)}, u32[]{:S(2)}) collective-permute-start(f32[64,256]{1,0:T(8,128)S(1)} %add_add_fusion), channel_id=1, source_target_pairs={{0,8},{1,9},{2,10},{3,11},{4,12},{5,13},{6,14},{7,15},{8,16},{9,17... | collective-permute-start | bytes 196616 | tf_op jit(solution)/shard_map/ppermute | solution.py:269
  17.0 5.3 %collective-permute-start.6 = (f32[64,512]{1,0:T(8,128)S(1)}, f32[64,512]{1,0:T(8,128)S(1)}, u32[]{:S(2)}, u32[]{:S(2)}) collective-permute-start(f32[64,512]{1,0:T(8,128)S(1)} %pad_maximum_fusion.own_ref.refs_0_), channel_id=1, source_target_pairs={{0,24},{1,17},{2,26},{3,19},{4,28},{5,21},{6,30},{7,23},{8,0},{9,2... | collective-permute-start | bytes 393224 | tf_op jit(solution)/shard_map/ppermute | solution.py:269
  20.9 1.4 %collective-permute-start.7 = (f32[64,256]{1,0:T(8,128)S(1)}, f32[64,256]{1,0:T(8,128)S(1)}, u32[]{:S(2)}, u32[]{:S(2)}) collective-permute-start(f32[64,256]{1,0:T(8,128)S(1)} %collective-permute-done.5.refs_1_), channel_id=1, source_target_pairs={{0,1},{1,0},{2,3},{3,2},{4,5},{5,4},{6,7},{7,6},{8,9},{9,8},{10,11... | collective-permute-start | bytes 196616 | tf_op jit(solution)/shard_map/ppermute | solution.py:253
  22.3 1.4 %collective-permute-start.8 = (f32[64,512]{1,0:T(8,128)S(1)}, f32[64,512]{1,0:T(8,128)S(1)}, u32[]{:S(2)}, u32[]{:S(2)}) collective-permute-start(f32[64,512]{1,0:T(8,128)S(1)} %collective-permute-done.6.refs_2_.refs_3_), channel_id=1, source_target_pairs={{0,1},{1,0},{2,3},{3,2},{4,5},{5,4},{6,7},{7,6},{8,9},{9,8},{10,11... | collective-permute-start | bytes 393224 | tf_op jit(solution)/shard_map/ppermute | solution.py:253
